TPU v7x, 32 devices: a whole 2x2x4 slice. The times are simulated.
32 devices in a mesh: orb: 4 (over y, core), aux: 8 (over z, x).
Axes of the slice: x: 2, y: 2, z: 4, core: 2. Of those that a mesh axis runs over, the one named last changes fastest.
Arguments:
- factors: bfloat16 [192, 128, 2048], P('orb', None, 'aux'), may hold values from -6 to 6
- amplitudes: bfloat16 [192, 12, 128, 128], P('orb'), may hold values from -0.15625 to 0.15625
- partners: int32 [192, 12], P('orb'), may hold values from 0 to 191, as said below
- metric_tiles: bfloat16 [128, 128, 128], P('aux'), may hold values from -0.1875 to 0.1875
- tile_pos: int32 [128, 2], P('aux'), may hold values from 0 to 15, as said below
Outputs:
- density: bfloat16 [192, 128, 2048], P('orb', 'aux')
Inputs may be any that keep to these rules, and one draw needn't show every extreme that they name: partners[i, 0] = i for every orbital i; the other partners of an orbital are any orbitals, repeats allowed. `tile_pos`: the listed positions (row block, column block) are all distinct, and each of the 16 diagonal positions is listed.
All inputs are finite; a program needn't handle non-finite values.
Results may differ from a plain program's by a relative error of at most 0.0049.
Values may be sent and summed in bfloat16 or wider, within the bound.
No kernel may reach another device: no remote copies, remote signals or barrier semaphores. Data moves between devices by JAX's collectives and lax.ppermute only.
A program may use at most 192 MiB of HBM per device.

v0:
```python
import jax
import jax.numpy as jnp
from jax import lax
from jax.sharding import PartitionSpec as P


def placed_terms(tile_set, positions, block_count):
    levels = jnp.arange(block_count, dtype=jnp.int32)
    row_hits = (positions[:, 0:1] == levels[None, :]).astype(jnp.bfloat16)
    col_hits = (positions[:, 1:2] == levels[None, :]).astype(jnp.bfloat16)
    pair_table = (row_hits[:, :, None] * col_hits[:, None, :]).reshape(
        tile_set.shape[0], block_count * block_count
    )
    flat_tiles = tile_set.reshape(tile_set.shape[0], tile_set.shape[1] * tile_set.shape[2])
    return lax.dot_general(
        pair_table, flat_tiles, (((0,), (0,)), ((), ())), preferred_element_type=jnp.float32
    )


def apply_metric(row_block, placed, block_count, span):
    blocks = placed.astype(jnp.bfloat16).reshape(block_count, block_count, span, span)
    rows_split = row_block.reshape(row_block.shape[0], block_count, span)
    result = jnp.einsum("ars,rcsu->acu", rows_split, blocks, preferred_element_type=jnp.float32)
    return result.reshape(row_block.shape[0], block_count * span)


def shards(factors, amplitudes, partners, metric_tiles, tile_pos):
    group_size, domain, aux_part = factors.shape
    flat_factors = factors.reshape(group_size, domain * aux_part)
    gathered = lax.all_gather(flat_factors, "orb", axis=0, tiled=True)
    picked = jnp.take(gathered, partners.reshape(-1), axis=0)
    picked = picked.reshape(partners.shape[0], partners.shape[1], domain, aux_part)
    gammas = jnp.einsum("ikab,ikbp->iap", amplitudes, picked, preferred_element_type=jnp.float32)
    gammas = gammas.astype(jnp.bfloat16)
    owned_rows = lax.all_to_all(gammas, "aux", split_axis=1, concat_axis=2, tiled=True)
    row_block = owned_rows.reshape(owned_rows.shape[0] * owned_rows.shape[1], owned_rows.shape[2])
    span = metric_tiles.shape[1]
    block_count = row_block.shape[1] // span
    placed = placed_terms(
        lax.all_gather(metric_tiles, "aux", axis=0, tiled=True),
        lax.all_gather(tile_pos, "aux", axis=0, tiled=True),
        block_count,
    )
    result = apply_metric(row_block, placed, block_count, span)
    return result.reshape(owned_rows.shape).astype(jnp.bfloat16)


def solution(mesh):
    in_specs = (
        P("orb", None, "aux"),
        P("orb", None, None, None),
        P("orb", None),
        P("aux", None, None),
        P("aux", None),
    )
    out_specs = P("orb", "aux", None)
    return jax.shard_map(shards, mesh=mesh, in_specs=in_specs, out_specs=out_specs, check_vma=False)
```

profile of v0, /device:TPU:8, one launch (start us, length us, event | category | flops | bytes accessed | tf_op | source)
XLA Modules:
  0.0 413.3 jit_solution(9337204679267441884)
XLA Ops:
  6.5 5.4 %copy.29 = bf16[6,8,128,256]{3,1,2,0:T(8,128)(2,1)} copy(bf16[6,8,128,256]{3,2,1,0:T(8,128)(2,1)} %bitcast.53) | data formatting | bytes 6291456
  12.0 0.0 all-gather.4.cloned.1.call-update
  12.0 0.0 all-gather.6.cloned.1.call-start
  12.1 0.7 all-gather.6.cloned.1.call-update
  12.8 0.1 copy.18
  12.9 0.1 reshape.112
  13.0 0.1 copy.17
  13.1 82.3 %all-gather.4.cloned.1.call-done = bf16[192,32768]{1,0:T(8,128)(2,1)} async-done(((bf16[48,32768]{1,0:T(8,128)(2,1)}), bf16[192,32768]{1,0:T(8,128)(2,1)}) %all-gather.4.cloned.1.call-update) | async-done | bytes 12582928 | tf_op jit(solution)/shard_map/all_gather | solution.py:30
  95.4 74.0 %gather_fusion = bf16[576,32768]{1,0:T(8,128)(2,1)} fusion(bf16[192,32768]{1,0:T(8,128)(2,1)} %all-gather.4.cloned.1.call-done, s32[1024]{0:T(1024)S(1)} %pad_clamp_fusion), kind=kCustom, calls=%fused_computation | custom fusion | bytes 75499776 | tf_op jit(solution)/shard_map/jit(_take)/gather | solution.py:31
  169.4 25.5 %copy.30 = bf16[72,8,128,256]{3,2,1,0:T(8,128)(2,1)} copy(bf16[72,8,128,256]{3,1,2,0:T(8,128)(2,1)} %bitcast.47) | data formatting | bytes 75497472
  194.9 45.2 %copy.19 = bf16[48,12,128,256]{2,3,1,0:T(8,128)(2,1)} copy(bf16[48,12,128,256]{3,2,1,0:T(8,128)(2,1)} %bitcast.46) | data formatting | bytes 75497472 | tf_op jit(solution)/shard_map/jit(_take)/gather | solution.py:31
  240.0 20.4 %fusion.7 = bf16[48,128,256]{1,2,0:T(8,128)(2,1)S(1)} fusion(bf16[48,12,128,128]{3,2,1,0:T(8,128)(2,1)} %param.6, bf16[48,12,128,256]{2,3,1,0:T(8,128)(2,1)} %copy.19, pred[48,12]{1,0:T(8,128)(4,1)S(1)} %copy.17), kind=kOutput, calls=%fused_computation.12 | convolution fusion | flops 4852285440 | bytes 59769408 | tf_op jit(solution)/shard_map/ikab,ikbp->iap/dot_general | solution.py:33
  260.4 3.0 copy.20
  263.4 6.0 %all-to-all-start = ((bf16[48,128,256]{2,0,1:T(8,128)(2,1)}), bf16[48,128,256]{2,0,1:T(8,128)(2,1)S(1)}, u32[]{:S(2)}, u32[]{:S(2)}) async-start(bf16[48,128,256]{2,0,1:T(8,128)(2,1)} %copy.20), calls=%async_computation | async-start | bytes 6291456 | tf_op jit(solution)/shard_map/all_to_all | solution.py:35
  269.5 78.5 %all-gather = s32[8,16,2]{1,2,0:T(2,128)S(1)} all-gather(s32[1,16,2]{1,2,0:T(2,128)S(1)} %bitcast.55), channel_id=1, replica_groups=mesh['orb'=4,'aux'=8] {'aux'}, dimensions={0}, use_global_device_ids=true | all-gather | bytes 1152 | tf_op jit(solution)/shard_map/all_gather | solution.py:41
  348.0 0.1 reshape.124
  348.2 0.0 all-gather.6.cloned.1.call-done
  348.2 8.8 %fusion.4 = bf16[32,8,128,128]{3,1,2,0:T(8,128)(2,1)} fusion(bf16[128,256]{0,1:T(8,128)(2,1)S(1)} %bitcast.54, bf16[16,8,128,128]{3,2,1,0:T(8,128)(2,1)} %bitcast.52), kind=kOutput, calls=%fused_computation.9 | convolution fusion | flops 1077936128 | bytes 12648448 | tf_op jit(solution)/shard_map/dot_general | solution.py:15
  357.0 9.2 %copy.32 = bf16[32,8,128,128]{3,2,1,0:T(8,128)(2,1)} copy(bf16[32,8,128,128]{3,1,2,0:T(8,128)(2,1)} %fusion.4) | data formatting | bytes 16777216
  366.2 10.3 %bitcast_bitcast_fusion = bf16[16,128,16,128]{1,3,0,2:T(8,128)(2,1)} fusion(bf16[16,16,128,128]{3,2,1,0:T(8,128)(2,1)} %bitcast.48), kind=kLoop, calls=%fused_computation.6 | loop fusion | bytes 16777216 | tf_op jit(solution)/shard_map/ars,rcsu->acu/dot_general | solution.py:23
  376.5 12.3 %copy.24 = bf16[16,128,16,128]{3,1,0,2:T(8,128)(2,1)} copy(bf16[16,128,16,128]{1,3,0,2:T(8,128)(2,1)} %bitcast_bitcast_fusion) | data formatting | bytes 16777216 | tf_op jit(solution)/shard_map/ars,rcsu->acu/dot_general | solution.py:23
  388.8 3.4 copy.22
  392.3 3.9 dot_general.16
  396.2 10.3 %bitcast_convert_fusion = bf16[48,16,2048]{2,1,0:T(8,128)(2,1)} fusion(bf16[2048,16,128,1]{2,0,1,3:T(8,128)(2,1)} %bitcast.51, bf16[48,16,16,128]{3,2,1,0:T(8,128)(2,1)S(1)} %dot_general.16), kind=kOutput, calls=%fused_computation.7 | convolution fusion | flops 6444023808 | bytes 14680064 | tf_op jit(solution)/shard_map/ars,rcsu->acu/dot_general | solution.py:23
  (13 shorter events, 0.1 us)
Async XLA Ops:
  6.5 6.2 %copy-start = (s32[48,12]{0,1:T(8,128)S(1)}, s32[48,12]{0,1:T(8,128)}, u32[]{:S(2)}) copy-start(s32[48,12]{0,1:T(8,128)} %param.7) | copy-start | bytes 6916
  6.5 88.9 %all-gather.4.cloned.1.call-start = ((), (), s32[]{:S(2)}) async-start(), calls=%async_computation.1 | async-start | bytes 15728640 | tf_op jit(solution)/shard_map/all_gather | solution.py:30
  12.0 336.2 %all-gather.6.cloned.1.call-start = ((), (), s32[]{:S(2)}) async-start(), calls=%async_computation.2 | async-start | bytes 4718592 | tf_op jit(solution)/shard_map/all_gather | solution.py:40
  260.4 9.1 %copy-start.1 = (s32[16,2]{0,1:T(2,128)S(1)}, s32[16,2]{0,1:T(2,128)}, u32[]{:S(2)}) copy-start(s32[16,2]{0,1:T(2,128)} %param.9) | copy-start | bytes 388
  263.4 125.4 %all-to-all-start = ((bf16[48,128,256]{2,0,1:T(8,128)(2,1)}), bf16[48,128,256]{2,0,1:T(8,128)(2,1)S(1)}, u32[]{:S(2)}, u32[]{:S(2)}) async-start(bf16[48,128,256]{2,0,1:T(8,128)(2,1)} %copy.20), calls=%async_computation | async-start | bytes 6291456 | tf_op jit(solution)/shard_map/all_to_all | solution.py:35
Sparse Core Ops, SparseCore 0:
  12.1 83.2 all-gather.3
  97.6 72.7 all-gather.5
where the time goes:
time: 415 us; the launch traced here: 413 us
  local copies, waits for them, and re-layouts  193 us (47%)
  waiting for transfers between devices  83.1 us (20%)
  blocking collectives  78.5 us (19%)
  matrix products  39.4 us (9%)
  between operations  13.5 us (3%)
  starting transfers between devices  6.09 us (1%)
    gather x2, local copies, waits for them, and re-layouts, shards(): picked = jnp.take(gathered, partners.reshape(-1), axis=0)  119 us
    all_gather x1, waiting for transfers between devices, shards(): gathered = lax.all_gather(flat_factors, 'orb', axis=0, tiled=True)  82.3 us
    all_gather x1, blocking collectives, shards(): lax.all_gather(tile_pos, 'aux', axis=0, tiled=True)  78.5 us
    unnamed x9, local copies, waits for them, and re-layouts  40.3 us
    dot_general x3, local copies, waits for them, and re-layouts, apply_metric(): jnp.einsum('ars,rcsu->acu', rows_split, blocks, preferred_element_type=jn...  26.6 us
    dot_general x1, matrix products, shards(): jnp.einsum('ikab,ikbp->iap', amplitudes, picked, preferred_element_type=j...  20.4 us
    dot_general x1, matrix products, apply_metric(): jnp.einsum('ars,rcsu->acu', rows_split, blocks, preferred_element_type=jn...  10.3 us
    dot_general x1, matrix products, placed_terms(): lax.dot_general(pair_table, flat_tiles, (((0,), (0,)), ((), ())), preferr...  8.8 us
  transfers between devices with their start and end apart: 3, of which 1 were waited for; matrix products, arithmetic and copies ran while one was open for 51% of the time, Pallas kernels for 0%

commit v1 on v0

v1 whole, which is shorter than its diff:
```python
import functools

import jax
import jax.numpy as jnp
from jax import lax
from jax.experimental import pallas as pl
from jax.experimental.pallas import tpu as pltpu
from jax.sharding import PartitionSpec as P

VMEM_LIMIT = 40 * 1024 * 1024


def largest_divisor(total, most):
    return max(size for size in range(1, most + 1) if total % size == 0)


def pack_kernel(width, source, *chunks):
    half = source.shape[1] // 2
    for at, chunk in enumerate(chunks):
        columns = slice(at * width, (at + 1) * width)
        chunk[...] = jnp.concatenate([source[:, :half, columns], source[:, half:, columns]], axis=-1)


def pack_chunks(factors, width):
    orbitals, domain, part = factors.shape
    count = part // width
    step = largest_divisor(orbitals, 8)
    packed = (step, domain // 2, 2 * width)
    return pl.pallas_call(
        functools.partial(pack_kernel, width),
        grid=(orbitals // step,),
        in_specs=[pl.BlockSpec((step, domain, part), lambda i: (i, 0, 0))],
        out_specs=[pl.BlockSpec(packed, lambda i: (i, 0, 0))] * count,
        out_shape=[jax.ShapeDtypeStruct((orbitals,) + packed[1:], factors.dtype)] * count,
        cost_estimate=pl.CostEstimate(flops=0, bytes_accessed=4 * factors.size, transcendentals=0),
        compiler_params=pltpu.CompilerParams(vmem_limit_bytes=VMEM_LIMIT),
        name="pack_chunks",
    )(factors)


def product_kernel(pairs, split_rows, slots, amplitudes, *refs):
    pieces = refs[: -4]
    out, staged, table, arrived = refs[-4:]
    group, half_domain, lanes = pieces[0].shape
    width = lanes // 2
    here = pl.program_id(0)

    @pl.when(here == 0)
    def _():
        copies = [
            pltpu.make_async_copy(piece, staged.at[pl.ds(at * group, group)], arrived.at[at])
            for at, piece in enumerate(pieces)
        ]
        for copy in copies:
            copy.start()
        for at, copy in enumerate(copies):
            copy.wait()

            @pl.loop(at * group, (at + 1) * group, unroll=4)
            def _(row):
                block = staged[row]
                table[row, :half_domain, :] = block[:, :width]
                table[row, half_domain:, :] = block[:, width:]

    step = amplitudes.shape[1]
    half_count = pl.num_programs(0) * step

    @pl.loop(0, step)
    def _(q):
        sums = []
        for side in range(2):
            base = (side * half_count + here * step + q) * pairs
            left = jnp.concatenate([amplitudes[side, q, k] for k in range(pairs)], axis=1)
            right = jnp.concatenate([table[slots[base + k]] for k in range(pairs)], axis=0)
            sums.append(jnp.dot(left, right, preferred_element_type=jnp.float32))
        both = jnp.concatenate(sums, axis=1).astype(out.dtype)
        if split_rows:
            owners, rows = out.shape[0], both.shape[0] // out.shape[0]
            out[:, pl.ds(pl.multiple_of(q * rows, rows), rows), :] = both.reshape(owners, rows, lanes)
        else:
            out[q] = both


def chunk_products(slots, amplitudes, pieces, owners):
    orbitals, pairs, domain, _ = amplitudes.shape
    group, half_domain, lanes = pieces[0].shape
    total = group * len(pieces)
    half = orbitals // 2
    rows = domain // owners
    split_rows = rows % 16 == 0
    step = largest_divisor(half, 4)
    if split_rows:
        out_shape, out_block, out_at = (owners, half * rows, lanes), (owners, step * rows, lanes), lambda i, s: (0, i, 0)
    else:
        out_shape, out_block, out_at = (half, domain, lanes), (step, domain, lanes), lambda i, s: (i, 0, 0)
    result = pl.pallas_call(
        functools.partial(product_kernel, pairs, split_rows),
        grid_spec=pltpu.PrefetchScalarGridSpec(
            num_scalar_prefetch=1,
            grid=(half // step,),
            in_specs=[pl.BlockSpec((2, step, pairs, domain, domain), lambda i, s: (0, i, 0, 0, 0))]
            + [pl.BlockSpec(memory_space=pl.ANY)] * len(pieces),
            out_specs=pl.BlockSpec(out_block, out_at),
            scratch_shapes=[
                pltpu.VMEM((total, half_domain, lanes), jnp.bfloat16),
                pltpu.VMEM((total, domain, lanes // 2), jnp.bfloat16),
                pltpu.SemaphoreType.DMA((len(pieces),)),
            ],
        ),
        out_shape=jax.ShapeDtypeStruct(out_shape, jnp.bfloat16),
        cost_estimate=pl.CostEstimate(
            flops=4 * amplitudes.size * (lanes // 2),
            bytes_accessed=2 * amplitudes.size + 2 * total * half_domain * lanes,
            transcendentals=0,
        ),
        compiler_params=pltpu.CompilerParams(vmem_limit_bytes=VMEM_LIMIT),
        name="chunk_products",
    )(slots, amplitudes.reshape(2, half, pairs, domain, domain), *pieces)
    if split_rows:
        return result
    result = result.reshape(half, owners, rows, lanes).transpose(1, 0, 2, 3)
    return result.reshape(owners, half * rows, lanes)


def place_kernel(chunks, owners, tiles_each, positions, first, second, out):
    span = first.shape[2]
    width = span // 2
    out[...] = jnp.zeros_like(out)
    for which, source in enumerate((first, second)):

        @pl.loop(0, source.shape[0])
        def _(device):
            @pl.loop(0, tiles_each)
            def _(at):
                number = (which * owners + device) * tiles_each + at
                column = pl.multiple_of(positions[2 * number + 1] * span, span)
                for side in range(2):
                    block = 2 * positions[2 * number] + side
                    row = ((block % chunks) * owners + block // chunks) * width
                    begin = pl.multiple_of(at * span + side * width, width)
                    out[pl.ds(pl.multiple_of(row, width), width), pl.ds(column, span)] = source[
                        device, pl.ds(begin, width), :
                    ]


def place_tiles(positions, first, second, tiles_each, chunks, size):
    owners = first.shape[0]
    return pl.pallas_call(
        functools.partial(place_kernel, chunks, owners, tiles_each),
        grid_spec=pltpu.PrefetchScalarGridSpec(
            num_scalar_prefetch=1,
            grid=(1,),
            in_specs=[pl.BlockSpec(first.shape, lambda i, s: (0, 0, 0))] * 2,
            out_specs=pl.BlockSpec((size, size), lambda i, s: (0, 0)),
        ),
        out_shape=jax.ShapeDtypeStruct((size, size), first.dtype),
        cost_estimate=pl.CostEstimate(flops=0, bytes_accessed=4 * first.size + 2 * size * size, transcendentals=0),
        compiler_params=pltpu.CompilerParams(vmem_limit_bytes=VMEM_LIMIT),
        name="place_tiles",
    )(positions, first, second)


def metric_kernel(*refs):
    chunks = refs[:-3]
    metric, out, rows = refs[-3], refs[-2], refs[-1]
    owners, height, lanes = chunks[0].shape
    width = lanes // 2

    @pl.when(pl.program_id(0) == 0)
    def _():
        for at, chunk in enumerate(chunks):
            for owner in range(0, owners, 2):
                one, two = chunk[owner], chunk[owner + 1]
                columns = pl.ds((at * owners + owner) * width, lanes)
                rows[:height, columns] = jnp.concatenate([one[:, :width], two[:, :width]], axis=1)
                rows[height:, columns] = jnp.concatenate([one[:, width:], two[:, width:]], axis=1)

    sums = jnp.dot(rows[...], metric[...], preferred_element_type=jnp.float32).astype(out.dtype)
    out[0] = sums[:height]
    out[1] = sums[height:]


def apply_metric(chunks, metric):
    owners, height, lanes = chunks[0].shape
    size = metric.shape[0]
    step = largest_divisor(size, 256)
    return pl.pallas_call(
        metric_kernel,
        grid=(size // step,),
        in_specs=[pl.BlockSpec((owners, height, lanes), lambda j: (0, 0, 0))] * len(chunks)
        + [pl.BlockSpec((size, step), lambda j: (0, j))],
        out_specs=pl.BlockSpec((2, height, step), lambda j: (0, 0, j)),
        out_shape=jax.ShapeDtypeStruct((2, height, size), jnp.bfloat16),
        scratch_shapes=[pltpu.VMEM((2 * height, size), jnp.bfloat16)],
        cost_estimate=pl.CostEstimate(
            flops=4 * height * size * size,
            bytes_accessed=2 * size * size + 8 * height * size,
            transcendentals=0,
        ),
        compiler_params=pltpu.CompilerParams(vmem_limit_bytes=VMEM_LIMIT),
        name="apply_metric",
    )(*chunks, metric)


def shards(orb_count, aux_count, factors, amplitudes, partners, metric_tiles, tile_pos):
    group, domain, part = factors.shape
    span = metric_tiles.shape[1]
    width = span // 2
    chunk_count = part // width
    far_count = orb_count // 2
    me = lax.axis_index("orb")

    def to_far(array, shift):
        moves = [(g, (g + 2 * shift) % orb_count) for g in range(orb_count)]
        return lax.ppermute(array, "orb", moves)

    def to_mate(array):
        return lax.ppermute(array, "orb", [(g, g ^ 1) for g in range(orb_count)])

    owner, place = partners // group, partners % group
    far = (me // 2 - owner // 2) % far_count
    slots = ((far * 2 + (me % 2 + owner) % 2) * group + place).reshape(-1)

    half_tiles = metric_tiles.shape[0] // 2
    mine = (me % 2) * half_tiles
    tiles = lax.dynamic_slice_in_dim(metric_tiles, mine, half_tiles, axis=0).reshape(half_tiles * span, span)
    spots = lax.dynamic_slice_in_dim(tile_pos, mine, half_tiles, axis=0).reshape(-1).astype(tiles.dtype)
    spot_rows = -(-spots.size // (16 * span)) * 16
    spots = jnp.pad(spots, (0, spot_rows * span - spots.size)).reshape(spot_rows, span)
    load = jnp.concatenate([tiles, spots], axis=0)

    packed = pack_chunks(factors, width)
    sent = []
    products = []
    last = None
    for at in range(chunk_count):
        own = packed[at]
        if last is not None:
            own, last = lax.optimization_barrier((own, last))
        far_pieces = [to_far(own, shift) for shift in range(1, far_count)]
        last = far_pieces[-1] if far_pieces else None
        pieces = []
        for piece in [own] + far_pieces:
            pieces += [piece, to_mate(piece)]
        made = chunk_products(slots, amplitudes, pieces, aux_count)
        products.append(lax.all_to_all(made, "aux", split_axis=0, concat_axis=0, tiled=True))

    parts = [load[None]]
    for shift in range(1, aux_count // 2):
        moves = [(g, (g + 2 * shift) % aux_count) for g in range(aux_count)]
        parts.append(lax.ppermute(load[None], "aux", moves))
    column = jnp.concatenate(parts, axis=0)
    beside = lax.ppermute(column, "aux", [(g, g ^ 1) for g in range(aux_count)])
    first = jnp.concatenate([column, beside], axis=0)
    second = to_mate(first)
    positions = jnp.stack([first[:, half_tiles * span :], second[:, half_tiles * span :]])
    positions = positions.reshape(2 * aux_count, -1)[:, : 2 * half_tiles].astype(jnp.int32).reshape(-1)
    metric = place_tiles(positions, first, second, half_tiles, chunk_count, part * aux_count)

    result = apply_metric(products, metric)
    return result.reshape(group, domain // aux_count, part * aux_count)


def solution(mesh):
    in_specs = (
        P("orb", None, "aux"),
        P("orb", None, None, None),
        P("orb", None),
        P("aux", None, None),
        P("aux", None),
    )
    body = functools.partial(shards, mesh.shape["orb"], mesh.shape["aux"])
    return jax.shard_map(body, mesh=mesh, in_specs=in_specs, out_specs=P("orb", "aux", None), check_vma=False)
```

time: 415 us -> 210 us (0.51)
  the two profiles are of different devices: /device:TPU:8 before, /device:TPU:0 now
where the time goes in v1:
time: 210 us; the launch traced here: 209 us
  Pallas kernels  98.8 us (47%)
  waiting for transfers between devices  51.8 us (25%)
  starting transfers between devices  40.5 us (19%)
  local copies, waits for them, and re-layouts  14.2 us (7%)
  other arithmetic  3.09 us (1%)
    pallas_call x4, Pallas kernels, chunk_products(): pl.pallas_call(functools.partial(product_kernel, pairs, split_rows), grid...  77.6 us
    all_to_all x4, starting transfers between devices, shards(): lax.all_to_all(made, 'aux', split_axis=0, concat_axis=0, tiled=True)  24.7 us
    ppermute x4, waiting for transfers between devices, to_far(): return lax.ppermute(array, 'orb', moves)  17.6 us
    ppermute x3, waiting for transfers between devices, shards(): parts.append(lax.ppermute(load[None], 'aux', moves))  17.3 us
    pallas_call x1, Pallas kernels, apply_metric(): pl.pallas_call(metric_kernel, grid=(size // step,), in_specs=[pl.BlockSpe...  12.4 us
    unnamed x22, local copies, waits for them, and re-layouts  11.6 us
    all_to_all x4, waiting for transfers between devices, shards(): lax.all_to_all(made, 'aux', split_axis=0, concat_axis=0, tiled=True)  10.1 us
    ppermute x4, starting transfers between devices, to_far(): return lax.ppermute(array, 'orb', moves)  7.88 us
  transfers between devices with their start and end apart: 21, of which 6 were waited for; matrix products, arithmetic and copies ran while one was open for 4% of the time, Pallas kernels for 40%

profile of v1, /device:TPU:0, one launch (start us, length us, event | category | flops | bytes accessed | tf_op | source)
XLA Modules:
  0.0 208.6 jit_solution(947252035806839989)
XLA Ops:
  0.0 1.9 copy-done.3
  2.0 2.7 %pack_chunks.1 = (bf16[48,64,128]{2,1,0:T(8,128)(2,1)S(1)}, bf16[48,64,128]{2,1,0:T(8,128)(2,1)S(1)}, bf16[48,64,128]{2,1,0:T(8,128)(2,1)}, bf16[48,64,128]{2,1,0:T(8,128)(2,1)S(1)}) custom-call(bf16[48,128,256]{2,1,0:T(8,128)(2,1)S(1)} %copy-done.3), custom_call_target="tpu_custom_call" | custom-call | bytes 6291456 | tf_op jit(solution)/shard_map/pack_chunks/pallas_call | solution.py:29
  4.6 3.0 %collective-permute-start.1 = (bf16[48,64,128]{2,1,0:T(8,128)(2,1)S(1)}, bf16[48,64,128]{2,1,0:T(8,128)(2,1)}, u32[]{:S(2)}, u32[]{:S(2)}) collective-permute-start(bf16[48,64,128]{2,1,0:T(8,128)(2,1)S(1)} %get-tuple-element.12.refs_0_), channel_id=1, source_target_pairs={{0,16},{8,24},{16,0},{24,8},{1,17},{9,25},{17,1},{25,9},{2,18},{10... | collective-permute-start | bytes 2359304 | tf_op jit(solution)/shard_map/ppermute | solution.py:215
  7.6 17.6 %collective-permute-done.1.refs_2_ = bf16[48,64,128]{2,1,0:T(8,128)(2,1)} collective-permute-done((bf16[48,64,128]{2,1,0:T(8,128)(2,1)S(1)}, bf16[48,64,128]{2,1,0:T(8,128)(2,1)}, u32[]{:S(2)}, u32[]{:S(2)}) %collective-permute-start.1) | collective-permute-done | bytes 786464 | tf_op jit(solution)/shard_map/ppermute | solution.py:215
  25.3 1.7 collective-permute-start.4
  27.9 19.1 %chunk_products.4 = bf16[8,384,128]{2,1,0:T(8,128)(2,1)} custom-call(s32[576]{0:T(1024)S(1)} %reshape.28.slots, bf16[2,24,12,128,128]{4,3,2,1,0:T(8,128)(2,1)} %bitcast.19, bf16[48,64,128]{2,1,0:T(8,128)(2,1)S(1)} %get-tuple-element.12.refs_0_, bf16[48,64,128]{2,1,0:T(8,128)(2,1)} %collective-permute-done.refs_1_, ...), custom_call_target="tpu_custom_call" | custom-call | flops 2415919104 | bytes 22020096 | tf_op jit(solution)/shard_map/chunk_products/pallas_call | solution.py:96
  47.0 6.0 %all-to-all-start = ((bf16[8,384,128]{2,1,0:T(8,128)(2,1)}), bf16[8,384,128]{2,1,0:T(8,128)(2,1)}, u32[]{:S(2)}, u32[]{:S(2)}) async-start(bf16[8,384,128]{2,1,0:T(8,128)(2,1)} %chunk_products.4), calls=%async_computation | async-start | bytes 1572864 | tf_op jit(solution)/shard_map/all_to_all | solution.py:246
  53.9 1.6 collective-permute-start.7
  56.2 3.8 %collective-permute-start.14 = (bf16[1,1040,128]{2,1,0:T(8,128)(2,1)}, bf16[1,1040,128]{2,1,0:T(8,128)(2,1)S(1)}, u32[]{:S(2)}, u32[]{:S(2)}) collective-permute-start(bf16[1,1040,128]{2,1,0:T(8,128)(2,1)} %maximum_bitcast_fusion), channel_id=1, source_target_pairs={{0,6},{1,7},{2,0},{3,1},{4,2},{5,3},{6,4},{7,5},{8,14},{9,15},{10,... | collective-permute-start | bytes 798728 | tf_op jit(solution)/shard_map/ppermute | solution.py:251
  61.2 19.1 %chunk_products.5 = bf16[8,384,128]{2,1,0:T(8,128)(2,1)} custom-call(s32[576]{0:T(1024)S(1)} %reshape.28.slots, bf16[2,24,12,128,128]{4,3,2,1,0:T(8,128)(2,1)} %bitcast.20, bf16[48,64,128]{2,1,0:T(8,128)(2,1)S(1)} %get-tuple-element.14.refs_0_, bf16[48,64,128]{2,1,0:T(8,128)(2,1)S(1)} %collective-permute-done.3.refs_1_, ...), custom_call_target="tpu_custom_call" | custom-call | flops 2415919104 | bytes 22020096 | tf_op jit(solution)/shard_map/chunk_products/pallas_call | solution.py:96
  80.2 8.5 %all-to-all-start.1 = ((bf16[8,384,128]{2,1,0:T(8,128)(2,1)}), bf16[8,384,128]{2,1,0:T(8,128)(2,1)}, u32[]{:S(2)}, u32[]{:S(2)}) async-start(bf16[8,384,128]{2,1,0:T(8,128)(2,1)} %chunk_products.5), calls=%async_computation.1 | async-start | bytes 1572864 | tf_op jit(solution)/shard_map/all_to_all | solution.py:246
  88.7 17.3 %collective-permute-done.13 = bf16[1,1040,128]{2,1,0:T(8,128)(2,1)} collective-permute-done((bf16[1,1040,128]{2,1,0:T(8,128)(2,1)}, bf16[1,1040,128]{2,1,0:T(8,128)(2,1)}, u32[]{:S(2)}, u32[]{:S(2)}) %collective-permute-start.13) | collective-permute-done | bytes 266272 | tf_op jit(solution)/shard_map/ppermute | solution.py:251
  106.0 2.2 %pad_maximum_fusion = bf16[4,1040,128]{2,1,0:T(8,128)(2,1)} fusion(bf16[1,1040,128]{2,1,0:T(8,128)(2,1)S(1)} %collective-permute-done.14, bf16[1,1040,128]{2,1,0:T(8,128)(2,1)} %collective-permute-done.13, bf16[1,1040,128]{2,1,0:T(8,128)(2,1)} %collective-permute-done.12, bf16[1,1040,128]{2,1,0:T(8,128)(2,1)} %maximum_bitcast_fusion), kind=kLoop, calls=%fused_computation | loop fusion | flops 1597440 | bytes 2129920 | tf_op jit(solution)/shard_map/concatenate | solution.py:252
  113.1 1.6 collective-permute-start.10
  114.7 20.3 %chunk_products.6 = bf16[8,384,128]{2,1,0:T(8,128)(2,1)} custom-call(s32[576]{0:T(1024)S(1)} %reshape.28.slots, bf16[2,24,12,128,128]{4,3,2,1,0:T(8,128)(2,1)} %bitcast.21, bf16[48,64,128]{2,1,0:T(8,128)(2,1)} %get-tuple-element.16.refs_0_, bf16[48,64,128]{2,1,0:T(8,128)(2,1)S(1)} %collective-permute-done.6.refs_1_, ...), custom_call_target="tpu_custom_call" | custom-call | flops 2415919104 | bytes 22020096 | tf_op jit(solution)/shard_map/chunk_products/pallas_call | solution.py:96
  135.0 4.2 %all-to-all-start.2 = ((bf16[8,384,128]{2,1,0:T(8,128)(2,1)}), bf16[8,384,128]{2,1,0:T(8,128)(2,1)}, u32[]{:S(2)}, u32[]{:S(2)}) async-start(bf16[8,384,128]{2,1,0:T(8,128)(2,1)} %chunk_products.6), calls=%async_computation.2 | async-start | bytes 1572864 | tf_op jit(solution)/shard_map/all_to_all | solution.py:246
  141.3 5.5 %collective-permute-done.9.refs_1_ = bf16[48,64,128]{2,1,0:T(8,128)(2,1)S(1)} collective-permute-done((bf16[48,64,128]{2,1,0:T(8,128)(2,1)S(1)}, bf16[48,64,128]{2,1,0:T(8,128)(2,1)S(1)}, u32[]{:S(2)}, u32[]{:S(2)}) %collective-permute-start.9) | collective-permute-done | bytes 786464 | tf_op jit(solution)/shard_map/ppermute | solution.py:218
  147.3 19.1 %chunk_products.7 = bf16[8,384,128]{2,1,0:T(8,128)(2,1)} custom-call(s32[576]{0:T(1024)S(1)} %reshape.28.slots, bf16[2,24,12,128,128]{4,3,2,1,0:T(8,128)(2,1)} %bitcast.22, bf16[48,64,128]{2,1,0:T(8,128)(2,1)S(1)} %get-tuple-element.18.refs_0_, bf16[48,64,128]{2,1,0:T(8,128)(2,1)S(1)} %collective-permute-done.9.refs_1_, ...), custom_call_target="tpu_custom_call" | custom-call | flops 2415919104 | bytes 22020096 | tf_op jit(solution)/shard_map/chunk_products/pallas_call | solution.py:96
  166.4 5.9 %all-to-all-start.3 = ((bf16[8,384,128]{2,1,0:T(8,128)(2,1)}), bf16[8,384,128]{2,1,0:T(8,128)(2,1)S(1)}, u32[]{:S(2)}, u32[]{:S(2)}) async-start(bf16[8,384,128]{2,1,0:T(8,128)(2,1)} %chunk_products.7), calls=%async_computation.3 | async-start | bytes 1572864 | tf_op jit(solution)/shard_map/all_to_all | solution.py:246
  173.3 6.2 %place_tiles.1.refs_4_ = bf16[2048,2048]{1,0:T(8,128)(2,1)S(1)} custom-call(s32[256]{0:T(256)S(1)} %reshape.37.positions, bf16[8,1040,128]{2,1,0:T(8,128)(2,1)S(1)} %constant_dynamic-update-slice_fusion.first, bf16[8,1040,128]{2,1,0:T(8,128)(2,1)} %collective-permute-done.16.second), custom_call_target="tpu_custom_call" | custom-call | bytes 12648448 | tf_op jit(solution)/shard_map/place_tiles/pallas_call | solution.py:148
  179.4 3.3 %copy-done.1 = bf16[2048,2048]{1,0:T(8,128)(2,1)} copy-done((bf16[2048,2048]{1,0:T(8,128)(2,1)}, bf16[2048,2048]{1,0:T(8,128)(2,1)S(1)}, u32[]{:S(2)}) %copy-start.1) | copy-done | bytes 8388632
  182.7 10.1 %all-to-all-done.3.refs_3_ = bf16[8,384,128]{2,1,0:T(8,128)(2,1)S(1)} async-done(((bf16[8,384,128]{2,1,0:T(8,128)(2,1)}), bf16[8,384,128]{2,1,0:T(8,128)(2,1)S(1)}, u32[]{:S(2)}, u32[]{:S(2)}) %all-to-all-start.3) | async-done | bytes 786464 | tf_op jit(solution)/shard_map/all_to_all | solution.py:246
  192.8 3.4 %copy-done.2 = bf16[2048,2048]{1,0:T(8,128)(2,1)S(1)} copy-done((bf16[2048,2048]{1,0:T(8,128)(2,1)S(1)}, bf16[2048,2048]{1,0:T(8,128)(2,1)}, u32[]{:S(2)}) %copy-start.2) | copy-done | bytes 8388632
  196.2 12.4 %apply_metric.1 = bf16[2,384,2048]{2,1,0:T(8,128)(2,1)} custom-call(bf16[8,384,128]{2,1,0:T(8,128)(2,1)} %all-to-all-done.refs_0_, bf16[8,384,128]{2,1,0:T(8,128)(2,1)} %all-to-all-done.1.refs_1_, bf16[8,384,128]{2,1,0:T(8,128)(2,1)} %all-to-all-done.2.refs_2_, bf16[8,384,128]{2,1,0:T(8,128)(2,1)S(1)} %all-to-all-done.3.refs_3_, bf16[2048,2048]{1,0:T(8,128)(2,1)S(1)} %copy-done.2), custom_call_target="tpu_custom_call" | custom-call | flops 6442450944 | bytes 14680064 | tf_op jit(solution)/shard_map/apply_metric/pallas_call | solution.py:187
  (64 shorter events, 11.8 us)
Async XLA Ops:
  0.0 53.8 %copy-start = (bf16[16,128,128]{2,1,0:T(8,128)(2,1)S(1)}, bf16[16,128,128]{2,1,0:T(8,128)(2,1)}, u32[]{:S(2)}) copy-start(bf16[16,128,128]{2,1,0:T(8,128)(2,1)} %param.8) | copy-start | bytes 1572868
  4.6 20.6 %collective-permute-start.1 = (bf16[48,64,128]{2,1,0:T(8,128)(2,1)S(1)}, bf16[48,64,128]{2,1,0:T(8,128)(2,1)}, u32[]{:S(2)}, u32[]{:S(2)}) collective-permute-start(bf16[48,64,128]{2,1,0:T(8,128)(2,1)S(1)} %get-tuple-element.12.refs_0_), channel_id=1, source_target_pairs={{0,16},{8,24},{16,0},{24,8},{1,17},{9,25},{17,1},{25,9},{2,18},{10... | collective-permute-start | bytes 2359304 | tf_op jit(solution)/shard_map/ppermute | solution.py:215
  7.6 19.6 %collective-permute-start = (bf16[48,64,128]{2,1,0:T(8,128)(2,1)S(1)}, bf16[48,64,128]{2,1,0:T(8,128)(2,1)}, u32[]{:S(2)}, u32[]{:S(2)}) collective-permute-start(bf16[48,64,128]{2,1,0:T(8,128)(2,1)S(1)} %get-tuple-element.12.refs_0_), channel_id=1, source_target_pairs={{0,8},{8,0},{16,24},{24,16},{1,9},{9,1},{17,25},{25,17},{2,10},{10... | collective-permute-start | bytes 2359304 | tf_op jit(solution)/shard_map/ppermute | solution.py:218
  25.2 2.6 %collective-permute-start.2 = (bf16[48,64,128]{2,1,0:T(8,128)(2,1)}, bf16[48,64,128]{2,1,0:T(8,128)(2,1)}, u32[]{:S(2)}, u32[]{:S(2)}) collective-permute-start(bf16[48,64,128]{2,1,0:T(8,128)(2,1)} %collective-permute-done.1.refs_2_), channel_id=1, source_target_pairs={{0,8},{8,0},{16,24},{24,16},{1,9},{9,1},{17,25},{25,17},{2,10},{10... | collective-permute-start | bytes 2359304 | tf_op jit(solution)/shard_map/ppermute | solution.py:218
  25.3 27.8 %collective-permute-start.4 = (bf16[48,64,128]{2,1,0:T(8,128)(2,1)S(1)}, bf16[48,64,128]{2,1,0:T(8,128)(2,1)}, u32[]{:S(2)}, u32[]{:S(2)}) collective-permute-start(bf16[48,64,128]{2,1,0:T(8,128)(2,1)S(1)} %get-tuple-element.14.refs_0_), channel_id=1, source_target_pairs={{0,16},{8,24},{16,0},{24,8},{1,17},{9,25},{17,1},{25,9},{2,18},{10... | collective-permute-start | bytes 2359304 | tf_op jit(solution)/shard_map/ppermute | solution.py:215
  27.9 25.7 %copy-start.8 = (s32[16,2]{0,1:T(2,128)S(1)}, s32[16,2]{0,1:T(2,128)}, u32[]{:S(2)}) copy-start(s32[16,2]{0,1:T(2,128)} %param.9) | copy-start | bytes 388
  47.0 33.2 %all-to-all-start = ((bf16[8,384,128]{2,1,0:T(8,128)(2,1)}), bf16[8,384,128]{2,1,0:T(8,128)(2,1)}, u32[]{:S(2)}, u32[]{:S(2)}) async-start(bf16[8,384,128]{2,1,0:T(8,128)(2,1)} %chunk_products.4), calls=%async_computation | async-start | bytes 1572864 | tf_op jit(solution)/shard_map/all_to_all | solution.py:246
  53.1 7.0 %collective-permute-start.3 = (bf16[48,64,128]{2,1,0:T(8,128)(2,1)S(1)}, bf16[48,64,128]{2,1,0:T(8,128)(2,1)S(1)}, u32[]{:S(2)}, u32[]{:S(2)}) collective-permute-start(bf16[48,64,128]{2,1,0:T(8,128)(2,1)S(1)} %get-tuple-element.14.refs_0_), channel_id=1, source_target_pairs={{0,8},{8,0},{16,24},{24,16},{1,9},{9,1},{17,25},{25,17},{2,10},{10... | collective-permute-start | bytes 2359304 | tf_op jit(solution)/shard_map/ppermute | solution.py:218
  53.1 8.1 %collective-permute-start.5 = (bf16[48,64,128]{2,1,0:T(8,128)(2,1)}, bf16[48,64,128]{2,1,0:T(8,128)(2,1)}, u32[]{:S(2)}, u32[]{:S(2)}) collective-permute-start(bf16[48,64,128]{2,1,0:T(8,128)(2,1)} %collective-permute-done.4.refs_2_), channel_id=1, source_target_pairs={{0,8},{8,0},{16,24},{24,16},{1,9},{9,1},{17,25},{25,17},{2,10},{10... | collective-permute-start | bytes 2359304 | tf_op jit(solution)/shard_map/ppermute | solution.py:218
  53.9 26.4 %copy-start.4 = (bf16[8,128,128]{2,1,0:T(8,128)(2,1)}, bf16[8,128,128]{2,1,0:T(8,128)(2,1)S(1)}, u32[]{:S(2)}) copy-start(bf16[8,128,128]{2,1,0:T(8,128)(2,1)S(1)} %constant_dynamic-slice_fusion) | copy-start | bytes 786436
  53.9 55.7 %collective-permute-start.7 = (bf16[48,64,128]{2,1,0:T(8,128)(2,1)}, bf16[48,64,128]{2,1,0:T(8,128)(2,1)}, u32[]{:S(2)}, u32[]{:S(2)}) collective-permute-start(bf16[48,64,128]{2,1,0:T(8,128)(2,1)} %get-tuple-element.16.refs_0_), channel_id=1, source_target_pairs={{0,16},{8,24},{16,0},{24,8},{1,17},{9,25},{17,1},{25,9},{2,18},{10... | collective-permute-start | bytes 2359304 | tf_op jit(solution)/shard_map/ppermute | solution.py:215
  56.2 32.5 %collective-permute-start.14 = (bf16[1,1040,128]{2,1,0:T(8,128)(2,1)}, bf16[1,1040,128]{2,1,0:T(8,128)(2,1)S(1)}, u32[]{:S(2)}, u32[]{:S(2)}) collective-permute-start(bf16[1,1040,128]{2,1,0:T(8,128)(2,1)} %maximum_bitcast_fusion), channel_id=1, source_target_pairs={{0,6},{1,7},{2,0},{3,1},{4,2},{5,3},{6,4},{7,5},{8,14},{9,15},{10,... | collective-permute-start | bytes 798728 | tf_op jit(solution)/shard_map/ppermute | solution.py:251
  60.0 46.0 %collective-permute-start.13 = (bf16[1,1040,128]{2,1,0:T(8,128)(2,1)}, bf16[1,1040,128]{2,1,0:T(8,128)(2,1)}, u32[]{:S(2)}, u32[]{:S(2)}) collective-permute-start(bf16[1,1040,128]{2,1,0:T(8,128)(2,1)} %maximum_bitcast_fusion), channel_id=1, source_target_pairs={{0,4},{1,5},{2,6},{3,7},{4,0},{5,1},{6,2},{7,3},{8,12},{9,13},{10,... | collective-permute-start | bytes 798728 | tf_op jit(solution)/shard_map/ppermute | solution.py:251
  60.0 46.0 %collective-permute-start.12 = (bf16[1,1040,128]{2,1,0:T(8,128)(2,1)}, bf16[1,1040,128]{2,1,0:T(8,128)(2,1)}, u32[]{:S(2)}, u32[]{:S(2)}) collective-permute-start(bf16[1,1040,128]{2,1,0:T(8,128)(2,1)} %maximum_bitcast_fusion), channel_id=1, source_target_pairs={{0,2},{1,3},{2,4},{3,5},{4,6},{5,7},{6,0},{7,1},{8,10},{9,11},{10,... | collective-permute-start | bytes 798728 | tf_op jit(solution)/shard_map/ppermute | solution.py:251
  80.2 54.7 %all-to-all-start.1 = ((bf16[8,384,128]{2,1,0:T(8,128)(2,1)}), bf16[8,384,128]{2,1,0:T(8,128)(2,1)}, u32[]{:S(2)}, u32[]{:S(2)}) async-start(bf16[8,384,128]{2,1,0:T(8,128)(2,1)} %chunk_products.5), calls=%async_computation.1 | async-start | bytes 1572864 | tf_op jit(solution)/shard_map/all_to_all | solution.py:246
  108.3 31.0 %collective-permute-start.15 = (bf16[4,1040,128]{2,1,0:T(8,128)(2,1)}, bf16[4,1040,128]{2,1,0:T(8,128)(2,1)}, u32[]{:S(2)}, u32[]{:S(2)}) collective-permute-start(bf16[4,1040,128]{2,1,0:T(8,128)(2,1)} %pad_maximum_fusion), channel_id=1, source_target_pairs={{0,1},{1,0},{2,3},{3,2},{4,5},{5,4},{6,7},{7,6},{8,9},{9,8},{10,11... | collective-permute-start | bytes 3194888 | tf_op jit(solution)/shard_map/ppermute | solution.py:253
  109.6 5.1 %collective-permute-start.6 = (bf16[48,64,128]{2,1,0:T(8,128)(2,1)}, bf16[48,64,128]{2,1,0:T(8,128)(2,1)S(1)}, u32[]{:S(2)}, u32[]{:S(2)}) collective-permute-start(bf16[48,64,128]{2,1,0:T(8,128)(2,1)} %get-tuple-element.16.refs_0_), channel_id=1, source_target_pairs={{0,8},{8,0},{16,24},{24,16},{1,9},{9,1},{17,25},{25,17},{2,10},{10... | collective-permute-start | bytes 2359304 | tf_op jit(solution)/shard_map/ppermute | solution.py:218
  109.6 5.1 %collective-permute-start.8 = (bf16[48,64,128]{2,1,0:T(8,128)(2,1)}, bf16[48,64,128]{2,1,0:T(8,128)(2,1)S(1)}, u32[]{:S(2)}, u32[]{:S(2)}) collective-permute-start(bf16[48,64,128]{2,1,0:T(8,128)(2,1)} %collective-permute-done.7.refs_2_), channel_id=1, source_target_pairs={{0,8},{8,0},{16,24},{24,16},{1,9},{9,1},{17,25},{25,17},{2,10},{10... | collective-permute-start | bytes 2359304 | tf_op jit(solution)/shard_map/ppermute | solution.py:218
  113.1 28.1 %collective-permute-start.10 = (bf16[48,64,128]{2,1,0:T(8,128)(2,1)S(1)}, bf16[48,64,128]{2,1,0:T(8,128)(2,1)}, u32[]{:S(2)}, u32[]{:S(2)}) collective-permute-start(bf16[48,64,128]{2,1,0:T(8,128)(2,1)S(1)} %get-tuple-element.18.refs_0_), channel_id=1, source_target_pairs={{0,16},{8,24},{16,0},{24,8},{1,17},{9,25},{17,1},{25,9},{2,18},{10... | collective-permute-start | bytes 2359304 | tf_op jit(solution)/shard_map/ppermute | solution.py:215
  135.0 31.5 %all-to-all-start.2 = ((bf16[8,384,128]{2,1,0:T(8,128)(2,1)}), bf16[8,384,128]{2,1,0:T(8,128)(2,1)}, u32[]{:S(2)}, u32[]{:S(2)}) async-start(bf16[8,384,128]{2,1,0:T(8,128)(2,1)} %chunk_products.6), calls=%async_computation.2 | async-start | bytes 1572864 | tf_op jit(solution)/shard_map/all_to_all | solution.py:246
  140.6 31.8 %collective-permute-start.16 = (bf16[8,1040,128]{2,1,0:T(8,128)(2,1)S(1)}, bf16[8,1040,128]{2,1,0:T(8,128)(2,1)}, u32[]{:S(2)}, u32[]{:S(2)}) collective-permute-start(bf16[8,1040,128]{2,1,0:T(8,128)(2,1)S(1)} %constant_dynamic-update-slice_fusion.first), channel_id=1, source_target_pairs={{0,8},{8,0},{16,24},{24,16},{1,9},{9,1},{17,25},{25,17},{2,10},{10... | collective-permute-start | bytes 6389768 | tf_op jit(solution)/shard_map/ppermute | solution.py:218
  140.7 6.1 %collective-permute-start.9 = (bf16[48,64,128]{2,1,0:T(8,128)(2,1)S(1)}, bf16[48,64,128]{2,1,0:T(8,128)(2,1)S(1)}, u32[]{:S(2)}, u32[]{:S(2)}) collective-permute-start(bf16[48,64,128]{2,1,0:T(8,128)(2,1)S(1)} %get-tuple-element.18.refs_0_), channel_id=1, source_target_pairs={{0,8},{8,0},{16,24},{24,16},{1,9},{9,1},{17,25},{25,17},{2,10},{10... | collective-permute-start | bytes 2359304 | tf_op jit(solution)/shard_map/ppermute | solution.py:218
  141.2 6.2 %collective-permute-start.11 = (bf16[48,64,128]{2,1,0:T(8,128)(2,1)}, bf16[48,64,128]{2,1,0:T(8,128)(2,1)S(1)}, u32[]{:S(2)}, u32[]{:S(2)}) collective-permute-start(bf16[48,64,128]{2,1,0:T(8,128)(2,1)} %collective-permute-done.10.refs_2_), channel_id=1, source_target_pairs={{0,8},{8,0},{16,24},{24,16},{1,9},{9,1},{17,25},{25,17},{2,10},{10... | collective-permute-start | bytes 2359304 | tf_op jit(solution)/shard_map/ppermute | solution.py:218
  166.4 26.4 %all-to-all-start.3 = ((bf16[8,384,128]{2,1,0:T(8,128)(2,1)}), bf16[8,384,128]{2,1,0:T(8,128)(2,1)S(1)}, u32[]{:S(2)}, u32[]{:S(2)}) async-start(bf16[8,384,128]{2,1,0:T(8,128)(2,1)} %chunk_products.7), calls=%async_computation.3 | async-start | bytes 1572864 | tf_op jit(solution)/shard_map/all_to_all | solution.py:246
  (6 other events, 75.9 us)

commit v2 on v1

v2 whole, which is shorter than its diff:
```python
import functools

import jax
import jax.numpy as jnp
from jax import lax
from jax.experimental import pallas as pl
from jax.experimental.pallas import tpu as pltpu
from jax.sharding import PartitionSpec as P

VMEM_LIMIT = 40 * 1024 * 1024
VMEM_WHOLE = 58 * 1024 * 1024


def largest_divisor(total, most):
    return max(size for size in range(1, most + 1) if total % size == 0)


def pack_kernel(first, width, source, chunk):
    half = source.shape[1] // 2
    columns = slice(first, first + width)
    chunk[...] = jnp.concatenate([source[:, :half, columns], source[:, half:, columns]], axis=-1)


def pack_chunk(factors, width, at):
    orbitals, domain, part = factors.shape
    lanes = 2 * width if part % (2 * width) == 0 else part
    step = largest_divisor(orbitals, 16)
    first = at * width
    return pl.pallas_call(
        functools.partial(pack_kernel, first % lanes, width),
        grid=(orbitals // step,),
        in_specs=[pl.BlockSpec((step, domain, lanes), lambda i: (i, 0, first // lanes))],
        out_specs=pl.BlockSpec((step, domain // 2, 2 * width), lambda i: (i, 0, 0)),
        out_shape=jax.ShapeDtypeStruct((orbitals, domain // 2, 2 * width), factors.dtype),
        cost_estimate=pl.CostEstimate(flops=0, bytes_accessed=6 * orbitals * domain * width, transcendentals=0),
        compiler_params=pltpu.CompilerParams(vmem_limit_bytes=VMEM_WHOLE),
        name="pack_chunk",
    )(factors)


def product_kernel(pairs, split_rows, slots, amplitudes, *refs):
    pieces = refs[:-3]
    out, table, arrived = refs[-3:]
    group, half_domain, lanes = pieces[0].shape
    here = pl.program_id(0)

    @pl.when(here == 0)
    def _():
        copies = [
            pltpu.make_async_copy(piece, table.at[pl.ds(at * group, group), pl.ds(0, half_domain)], arrived.at[at])
            for at, piece in enumerate(pieces)
        ]
        for copy in copies:
            copy.start()
        for at, copy in enumerate(copies):
            copy.wait()

            @pl.loop(at * group, (at + 1) * group, unroll=8)
            def _(row):
                block = table[row, :half_domain, :]
                table[row, half_domain:, :] = jnp.concatenate([block[:, lanes // 2 :], block[:, : lanes // 2]], axis=1)

    step = amplitudes.shape[1]
    half_count = pl.num_programs(0) * step
    lower = lax.broadcasted_iota(jnp.int32, (amplitudes.shape[3], lanes), 1) < lanes // 2
    for q in range(step):
        sums = []
        for side in range(2):
            base = (side * half_count + here * step + q) * pairs
            left = jnp.concatenate([amplitudes[side, q, k] for k in range(pairs)], axis=1)
            right = []
            for k in range(pairs):
                slot = slots[base + k]
                if side:
                    right += [table[slot, half_domain:, :], table[slot, :half_domain, :]]
                else:
                    right += [table[slot]]
            sums.append(jnp.dot(left, jnp.concatenate(right, axis=0), preferred_element_type=jnp.float32))
        both = jnp.where(lower, sums[0], sums[1]).astype(out.dtype)
        if split_rows:
            owners, rows = out.shape[0], both.shape[0] // out.shape[0]
            out[:, q * rows : (q + 1) * rows, :] = both.reshape(owners, rows, lanes)
        else:
            out[q] = both


def chunk_products(slots, amplitudes, pieces, owners):
    orbitals, pairs, domain, _ = amplitudes.shape
    group, half_domain, lanes = pieces[0].shape
    total = group * len(pieces)
    half = orbitals // 2
    rows = domain // owners
    split_rows = rows % 16 == 0
    step = largest_divisor(half, 4)
    if split_rows:
        out_shape, out_block, out_at = (owners, half * rows, lanes), (owners, step * rows, lanes), lambda i, s: (0, i, 0)
    else:
        out_shape, out_block, out_at = (half, domain, lanes), (step, domain, lanes), lambda i, s: (i, 0, 0)
    result = pl.pallas_call(
        functools.partial(product_kernel, pairs, split_rows),
        grid_spec=pltpu.PrefetchScalarGridSpec(
            num_scalar_prefetch=1,
            grid=(half // step,),
            in_specs=[pl.BlockSpec((2, step, pairs, domain, domain), lambda i, s: (0, i, 0, 0, 0))]
            + [pl.BlockSpec(memory_space=pl.ANY)] * len(pieces),
            out_specs=pl.BlockSpec(out_block, out_at),
            scratch_shapes=[
                pltpu.VMEM((total, domain, lanes), jnp.bfloat16),
                pltpu.SemaphoreType.DMA((len(pieces),)),
            ],
        ),
        out_shape=jax.ShapeDtypeStruct(out_shape, jnp.bfloat16),
        cost_estimate=pl.CostEstimate(
            flops=8 * amplitudes.size * lanes,
            bytes_accessed=2 * amplitudes.size + 2 * total * half_domain * lanes,
            transcendentals=0,
        ),
        compiler_params=pltpu.CompilerParams(vmem_limit_bytes=VMEM_LIMIT),
        name="chunk_products",
    )(slots, amplitudes.reshape(2, half, pairs, domain, domain), *pieces)
    if split_rows:
        return result
    result = result.reshape(half, owners, rows, lanes).transpose(1, 0, 2, 3)
    return result.reshape(owners, half * rows, lanes)


def join_kernel(*refs):
    pieces = refs[:-2]
    out, arrived = refs[-2:]
    copies = [pltpu.make_async_copy(piece, out.at[at], arrived.at[at]) for at, piece in enumerate(pieces)]
    for copy in copies:
        copy.start()
    for copy in copies:
        copy.wait()


def join(pieces):
    shape = (len(pieces),) + pieces[0].shape
    return pl.pallas_call(
        join_kernel,
        in_specs=[pl.BlockSpec(memory_space=pl.ANY)] * len(pieces),
        out_specs=pl.BlockSpec(memory_space=pl.ANY),
        out_shape=jax.ShapeDtypeStruct(shape, pieces[0].dtype),
        scratch_shapes=[pltpu.SemaphoreType.DMA((len(pieces),))],
        cost_estimate=pl.CostEstimate(flops=0, bytes_accessed=4 * len(pieces) * pieces[0].size, transcendentals=0),
        name="join",
    )(*pieces)


def place_kernel(chunks, owners, tiles_each, positions, *refs):
    sources, out = refs[:-1], refs[-1]
    devices, _, span = sources[0].shape
    width = span // 2
    out[...] = jnp.zeros_like(out)
    for which, source in enumerate(sources):

        @pl.loop(0, devices)
        def _(device):
            for at in range(tiles_each):
                number = (which * devices + device) * tiles_each + at
                column = pl.multiple_of(positions[2 * number + 1] * span, span)
                for side in range(2):
                    block = 2 * positions[2 * number] + side
                    row = ((block % chunks) * owners + block // chunks) * width
                    begin = at * span + side * width
                    out[pl.ds(pl.multiple_of(row, width), width), pl.ds(column, span)] = source[
                        device, begin : begin + width, :
                    ]


def place_tiles(positions, sources, tiles_each, chunks, owners, size):
    shape = sources[0].shape
    return pl.pallas_call(
        functools.partial(place_kernel, chunks, owners, tiles_each),
        grid_spec=pltpu.PrefetchScalarGridSpec(
            num_scalar_prefetch=1,
            grid=(1,),
            in_specs=[pl.BlockSpec(shape, lambda i, s: (0, 0, 0))] * len(sources),
            out_specs=pl.BlockSpec((size, size), lambda i, s: (0, 0)),
        ),
        out_shape=jax.ShapeDtypeStruct((size, size), sources[0].dtype),
        cost_estimate=pl.CostEstimate(
            flops=0, bytes_accessed=2 * len(sources) * sources[0].size + 2 * size * size, transcendentals=0
        ),
        compiler_params=pltpu.CompilerParams(vmem_limit_bytes=VMEM_LIMIT),
        name="place_tiles",
    )(positions, *sources)


def metric_kernel(count, has_before, *refs):
    chunks, metric, before = refs[:count], refs[count], refs[count + 1]
    out, rows = refs[-2:]
    owners, height, lanes = chunks[0].shape
    width = lanes // 2

    @pl.when(pl.program_id(0) == 0)
    def _():
        for at, chunk in enumerate(chunks):
            for owner in range(0, owners, 2):
                one, two = chunk[owner], chunk[owner + 1]
                columns = pl.ds((at * owners + owner) * width, lanes)
                rows[:height, columns] = jnp.concatenate([one[:, :width], two[:, :width]], axis=1)
                rows[height:, columns] = jnp.concatenate([one[:, width:], two[:, width:]], axis=1)

    for side in range(2):
        sums = jnp.dot(rows[side * height : (side + 1) * height], metric[...], preferred_element_type=jnp.float32)
        if has_before:
            sums += before[side]
        out[side] = sums.astype(out.dtype)


def apply_metric(chunks, metric, begin, before, dtype):
    owners, height, lanes = chunks[0].shape
    size = metric.shape[0]
    depth = len(chunks) * owners * lanes // 2
    step = largest_divisor(size, 256)
    sums = [] if before is None else [before]
    block = pl.BlockSpec((2, height, step), lambda j: (0, 0, j))
    return pl.pallas_call(
        functools.partial(metric_kernel, len(chunks), before is not None),
        grid=(size // step,),
        in_specs=[pl.BlockSpec((owners, height, lanes), lambda j: (0, 0, 0))] * len(chunks)
        + [pl.BlockSpec((depth, step), lambda j: (begin // len(chunks), j))]
        + [block] * len(sums),
        out_specs=block,
        out_shape=jax.ShapeDtypeStruct((2, height, size), dtype),
        scratch_shapes=[pltpu.VMEM((2 * height, depth), jnp.bfloat16)],
        cost_estimate=pl.CostEstimate(
            flops=4 * height * depth * size,
            bytes_accessed=2 * depth * size + 12 * height * size,
            transcendentals=0,
        ),
        compiler_params=pltpu.CompilerParams(vmem_limit_bytes=VMEM_LIMIT),
        name="apply_metric",
    )(*chunks, metric, *sums)


def after(value, others):
    return lax.optimization_barrier((value, others))[0]


def shards(orb_count, aux_count, factors, amplitudes, partners, metric_tiles, tile_pos):
    group, domain, part = factors.shape
    span = metric_tiles.shape[1]
    width = span // 2
    chunk_count = part // width
    far_count = orb_count // 2
    me = lax.axis_index("orb")

    def to_far(array, shift):
        moves = [(g, (g + 2 * shift) % orb_count) for g in range(orb_count)]
        return lax.ppermute(array, "orb", moves)

    def to_mate(array):
        return lax.ppermute(array, "orb", [(g, g ^ 1) for g in range(orb_count)])

    owner, place = partners // group, partners % group
    far = (me // 2 - owner // 2) % far_count
    slots = ((far * 2 + (me % 2 + owner) % 2) * group + place).reshape(-1)

    half_tiles = metric_tiles.shape[0] // 2
    mine = (me % 2) * half_tiles
    tiles = lax.dynamic_slice_in_dim(metric_tiles, mine, half_tiles, axis=0).reshape(half_tiles * span, span)
    spots = lax.dynamic_slice_in_dim(tile_pos, mine, half_tiles, axis=0).reshape(-1).astype(tiles.dtype)
    spot_rows = -(-spots.size // (16 * span)) * 16
    spots = jnp.pad(spots, (0, spot_rows * span - spots.size)).reshape(spot_rows, span)
    load = jnp.concatenate([tiles, spots], axis=0)
    parts = [load]
    for shift in range(1, aux_count // 2):
        moves = [(g, (g + 2 * shift) % aux_count) for g in range(aux_count)]
        parts.append(lax.ppermute(load, "aux", moves))

    products = []
    last = None
    for at in range(chunk_count):
        own = pack_chunk(factors, width, at)
        if last is not None:
            own = after(own, last)
        far_pieces = [to_far(own, shift) for shift in range(1, far_count)]
        last = far_pieces[-1] if far_pieces else None
        pieces = []
        for piece in [own] + far_pieces:
            pieces += [piece, to_mate(piece)]
        made = chunk_products(slots, amplitudes, pieces, aux_count)
        if at == 0:
            made = after(made, parts)
        products.append(lax.all_to_all(made, "aux", split_axis=0, concat_axis=0, tiled=True))

    column = join(parts)
    beside = lax.ppermute(column, "aux", [(g, g ^ 1) for g in range(aux_count)])
    sources = [column, beside, to_mate(column), to_mate(beside)]
    positions = jnp.concatenate([source[:, half_tiles * span, : 2 * half_tiles] for source in sources])
    positions = positions.astype(jnp.int32).reshape(-1)
    metric = place_tiles(positions, sources, half_tiles, chunk_count, aux_count, part * aux_count)

    before = None
    if chunk_count > 1:
        before = apply_metric(after(products[:-1], made), metric, 0, None, jnp.float32)
    result = apply_metric(products[-1:], metric, chunk_count - 1, before, jnp.bfloat16)
    return result.reshape(group, domain // aux_count, part * aux_count)


def solution(mesh):
    in_specs = (
        P("orb", None, "aux"),
        P("orb", None, None, None),
        P("orb", None),
        P("aux", None, None),
        P("aux", None),
    )
    body = functools.partial(shards, mesh.shape["orb"], mesh.shape["aux"])
    return jax.shard_map(body, mesh=mesh, in_specs=in_specs, out_specs=P("orb", "aux", None), check_vma=False)
```

time: 210 us -> 211 us (level)
  Pallas kernels: 98.8 us -> 126 us
  waiting for transfers between devices: 51.8 us -> 33 us
  starting transfers between devices: 40.5 us -> 35.9 us
  other arithmetic: 3.09 us -> 0.14 us
    pallas_call x2 -> x7, Pallas kernels: 15.1 us -> 63.7 us  [the longest x1 33.4 us: join(): pl.pallas_call(join_kernel, in_specs=[pl.BlockSpec(memory_space=pl.ANY)]...]
    pallas_call x4, Pallas kernels: 77.6 us -> 57.8 us  [chunk_products(): pl.pallas_call(functools.partial(product_kernel, pairs, split_rows), grid...]
    ppermute x3, waiting for transfers between devices: 17.3 us -> 0.01 us  [shards(): parts.append(lax.ppermute(load, 'aux', moves))]
    all_to_all x4, waiting for transfers between devices: 10.1 us -> 1.97 us  [shards(): lax.all_to_all(made, 'aux', split_axis=0, concat_axis=0, tiled=True)]
    ppermute x1, waiting for transfers between devices: 0.01 us -> 6.74 us  [shards(): beside = lax.ppermute(column, 'aux', [(g, g ^ 1) for g in range(aux_count)])]
    ppermute x9 -> x10, waiting for transfers between devices: 6.72 us -> 0.03 us  [to_mate(): return lax.ppermute(array, 'orb', [(g, g ^ 1) for g in range(orb_count)])]
    ppermute x4, waiting for transfers between devices: 17.6 us -> 24.3 us  [to_far(): return lax.ppermute(array, 'orb', moves)]
    all_to_all x4, starting transfers between devices: 24.7 us -> 20.8 us  [shards(): lax.all_to_all(made, 'aux', split_axis=0, concat_axis=0, tiled=True)]
  transfers between devices with their start and end apart: 21 -> 22, of which waited for: 6 -> 4; matrix products, arithmetic and copies ran while one was open for 4% -> 1% of each run, Pallas kernels for 40% -> 55%
where the time goes in v2:
time: 211 us; the launch traced here: 209 us
  Pallas kernels  126 us (60%)
  starting transfers between devices  35.9 us (17%)
  waiting for transfers between devices  33 us (16%)
  local copies, waits for them, and re-layouts  13.6 us (6%)
    pallas_call x4, Pallas kernels, chunk_products(): pl.pallas_call(functools.partial(product_kernel, pairs, split_rows), grid...  57.8 us
    pallas_call x1, Pallas kernels, join(): pl.pallas_call(join_kernel, in_specs=[pl.BlockSpec(memory_space=pl.ANY)]...  33.4 us
    ppermute x4, waiting for transfers between devices, to_far(): return lax.ppermute(array, 'orb', moves)  24.3 us
    all_to_all x4, starting transfers between devices, shards(): lax.all_to_all(made, 'aux', split_axis=0, concat_axis=0, tiled=True)  20.8 us
    pallas_call x2, Pallas kernels, apply_metric(): pl.pallas_call(functools.partial(metric_kernel, len(chunks), before is no...  17.2 us
    pallas_call x4, Pallas kernels, pack_chunk(): pl.pallas_call(functools.partial(pack_kernel, first % lanes, width), grid...  13.1 us
    unnamed x40, local copies, waits for them, and re-layouts  11.7 us
    ppermute x4, starting transfers between devices, to_far(): return lax.ppermute(array, 'orb', moves)  6.8 us
  transfers between devices with their start and end apart: 22, of which 4 were waited for; matrix products, arithmetic and copies ran while one was open for 1% of the time, Pallas kernels for 55%

profile of v2, /device:TPU:0, one launch (start us, length us, event | category | flops | bytes accessed | tf_op | source)
XLA Modules:
  0.0 209.4 jit_solution(1787512012088609855)
XLA Ops:
  0.0 3.3 %pack_chunk.7.refs_0_ = bf16[48,64,128]{2,1,0:T(8,128)(2,1)} custom-call(bf16[48,128,256]{2,1,0:T(8,128)(2,1)} %source.7), custom_call_target="tpu_custom_call" | custom-call | bytes 2359296 | tf_op jit(solution)/shard_map/pack_chunk/pallas_call | solution.py:29
  3.3 3.0 %collective-permute-start = (bf16[48,64,128]{2,1,0:T(8,128)(2,1)}, bf16[48,64,128]{2,1,0:T(8,128)(2,1)S(1)}, u32[]{:S(2)}, u32[]{:S(2)}) collective-permute-start(bf16[48,64,128]{2,1,0:T(8,128)(2,1)} %pack_chunk.7.refs_0_), channel_id=1, source_target_pairs={{0,16},{8,24},{16,0},{24,8},{1,17},{9,25},{17,1},{25,9},{2,18},{10... | collective-permute-start | bytes 2359304 | tf_op jit(solution)/shard_map/ppermute | solution.py:252
  6.3 3.3 %pack_chunk.6.refs_0_ = bf16[48,64,128]{2,1,0:T(8,128)(2,1)} custom-call(bf16[48,128,256]{2,1,0:T(8,128)(2,1)} %source.7), custom_call_target="tpu_custom_call" | custom-call | bytes 2359296 | tf_op jit(solution)/shard_map/pack_chunk/pallas_call | solution.py:29
  9.6 14.5 %collective-permute-done.refs_2_ = bf16[48,64,128]{2,1,0:T(8,128)(2,1)S(1)} collective-permute-done((bf16[48,64,128]{2,1,0:T(8,128)(2,1)}, bf16[48,64,128]{2,1,0:T(8,128)(2,1)S(1)}, u32[]{:S(2)}, u32[]{:S(2)}) %collective-permute-start) | collective-permute-done | bytes 786464 | tf_op jit(solution)/shard_map/ppermute | solution.py:252
  26.1 3.7 %collective-permute-start.8 = (bf16[1040,128]{1,0:T(8,128)(2,1)S(1)}, bf16[1040,128]{1,0:T(8,128)(2,1)S(1)}, u32[]{:S(2)}, u32[]{:S(2)}) collective-permute-start(bf16[1040,128]{1,0:T(8,128)(2,1)S(1)} %pad_maximum_fusion.refs_0_), channel_id=1, source_target_pairs={{0,6},{1,7},{2,0},{3,1},{4,2},{5,3},{6,4},{7,5},{8,14},{9,15},{10,... | collective-permute-start | bytes 798728 | tf_op jit(solution)/shard_map/ppermute | solution.py:271
  29.8 3.3 %pack_chunk.5.refs_0_ = bf16[48,64,128]{2,1,0:T(8,128)(2,1)} custom-call(bf16[48,128,256]{2,1,0:T(8,128)(2,1)} %source.7), custom_call_target="tpu_custom_call" | custom-call | bytes 2359296 | tf_op jit(solution)/shard_map/pack_chunk/pallas_call | solution.py:29
  33.3 9.8 %collective-permute-done.1.refs_2_ = bf16[48,64,128]{2,1,0:T(8,128)(2,1)} collective-permute-done((bf16[48,64,128]{2,1,0:T(8,128)(2,1)}, bf16[48,64,128]{2,1,0:T(8,128)(2,1)}, u32[]{:S(2)}, u32[]{:S(2)}) %collective-permute-start.1) | collective-permute-done | bytes 786464 | tf_op jit(solution)/shard_map/ppermute | solution.py:252
  46.4 14.7 %chunk_products.5 = bf16[8,384,128]{2,1,0:T(8,128)(2,1)} custom-call(s32[576]{0:T(1024)S(1)} %reshape.24.slots, bf16[2,24,12,128,128]{4,3,2,1,0:T(8,128)(2,1)} %bitcast.22, bf16[48,64,128]{2,1,0:T(8,128)(2,1)S(1)} %copy-done.12, bf16[48,64,128]{2,1,0:T(8,128)(2,1)} %collective-permute-done.12.refs_1_, bf16[48,64,128]{2,1,0:T(8,128)(2,1)S(1)} %collective-permute-done.refs_2_, ...), custom_call_target="tpu_custom_call" | custom-call | flops 9663676416 | bytes 22020096 | tf_op jit(solution)/shard_map/chunk_products/pallas_call | solution.py:99
  61.2 4.8 %all-to-all-start.1 = ((bf16[8,384,128]{2,1,0:T(8,128)(2,1)}), bf16[8,384,128]{2,1,0:T(8,128)(2,1)S(1)}, u32[]{:S(2)}, u32[]{:S(2)}) async-start(bf16[8,384,128]{2,1,0:T(8,128)(2,1)} %chunk_products.5), calls=%async_computation.1 | async-start | bytes 1572864 | tf_op jit(solution)/shard_map/all_to_all | solution.py:287
  66.0 3.3 %pack_chunk.4.refs_0_ = bf16[48,64,128]{2,1,0:T(8,128)(2,1)} custom-call(bf16[48,128,256]{2,1,0:T(8,128)(2,1)} %source.7), custom_call_target="tpu_custom_call" | custom-call | bytes 2359296 | tf_op jit(solution)/shard_map/pack_chunk/pallas_call | solution.py:29
  70.0 14.7 %chunk_products.6 = bf16[8,384,128]{2,1,0:T(8,128)(2,1)} custom-call(s32[576]{0:T(1024)S(1)} %reshape.24.slots, bf16[2,24,12,128,128]{4,3,2,1,0:T(8,128)(2,1)} %bitcast.23, bf16[48,64,128]{2,1,0:T(8,128)(2,1)S(1)} %copy-done.11, bf16[48,64,128]{2,1,0:T(8,128)(2,1)} %collective-permute-done.14.refs_1_, bf16[48,64,128]{2,1,0:T(8,128)(2,1)} %collective-permute-done.1.refs_2_, ...), custom_call_target="tpu_custom_call" | custom-call | flops 9663676416 | bytes 22020096 | tf_op jit(solution)/shard_map/chunk_products/pallas_call | solution.py:99
  86.6 4.1 %all-to-all-start.2 = ((bf16[8,384,128]{2,1,0:T(8,128)(2,1)}), bf16[8,384,128]{2,1,0:T(8,128)(2,1)S(1)}, u32[]{:S(2)}, u32[]{:S(2)}) async-start(bf16[8,384,128]{2,1,0:T(8,128)(2,1)} %chunk_products.6), calls=%async_computation.2 | async-start | bytes 1572864 | tf_op jit(solution)/shard_map/all_to_all | solution.py:287
  90.7 33.4 %join.1.refs_0_ = bf16[4,1040,128]{2,1,0:T(8,128)(2,1)} custom-call(bf16[1040,128]{1,0:T(8,128)(2,1)} %copy-done.14, bf16[1040,128]{1,0:T(8,128)(2,1)} %collective-permute-done.6.refs_1_, bf16[1040,128]{1,0:T(8,128)(2,1)} %collective-permute-done.7.refs_2_, bf16[1040,128]{1,0:T(8,128)(2,1)} %copy-done.15), custom_call_target="tpu_custom_call" | custom-call | bytes 2129920 | tf_op jit(solution)/shard_map/join/pallas_call | solution.py:139
  126.7 14.5 %chunk_products.7 = bf16[8,384,128]{2,1,0:T(8,128)(2,1)S(1)} custom-call(s32[576]{0:T(1024)S(1)} %reshape.24.slots, bf16[2,24,12,128,128]{4,3,2,1,0:T(8,128)(2,1)} %bitcast.24, bf16[48,64,128]{2,1,0:T(8,128)(2,1)} %pack_chunk.5.refs_0_, bf16[48,64,128]{2,1,0:T(8,128)(2,1)} %collective-permute-done.16.refs_1_, ...), custom_call_target="tpu_custom_call" | custom-call | flops 9663676416 | bytes 22020096 | tf_op jit(solution)/shard_map/chunk_products/pallas_call | solution.py:99
  142.1 4.5 %all-to-all-start.3 = ((bf16[8,384,128]{2,1,0:T(8,128)(2,1)}), bf16[8,384,128]{2,1,0:T(8,128)(2,1)}, u32[]{:S(2)}, u32[]{:S(2)}) async-start(bf16[8,384,128]{2,1,0:T(8,128)(2,1)} %copy-done.10), calls=%async_computation.3 | async-start | bytes 1572864 | tf_op jit(solution)/shard_map/all_to_all | solution.py:287
  146.7 6.7 %collective-permute-done.9.refs_1_ = bf16[4,1040,128]{2,1,0:T(8,128)(2,1)S(1)} collective-permute-done((bf16[4,1040,128]{2,1,0:T(8,128)(2,1)}, bf16[4,1040,128]{2,1,0:T(8,128)(2,1)S(1)}, u32[]{:S(2)}, u32[]{:S(2)}) %collective-permute-start.9) | collective-permute-done | bytes 1064992 | tf_op jit(solution)/shard_map/ppermute | solution.py:290
  154.6 13.9 %chunk_products.4 = bf16[8,384,128]{2,1,0:T(8,128)(2,1)S(1)} custom-call(s32[576]{0:T(1024)S(1)} %reshape.24.slots, bf16[2,24,12,128,128]{4,3,2,1,0:T(8,128)(2,1)} %bitcast.25, bf16[48,64,128]{2,1,0:T(8,128)(2,1)S(1)} %copy-done.13, bf16[48,64,128]{2,1,0:T(8,128)(2,1)} %collective-permute-done.3.refs_1_, ...), custom_call_target="tpu_custom_call" | custom-call | flops 9663676416 | bytes 22020096 | tf_op jit(solution)/shard_map/chunk_products/pallas_call | solution.py:99
  169.4 7.4 %all-to-all-start = ((bf16[8,384,128]{2,1,0:T(8,128)(2,1)}), bf16[8,384,128]{2,1,0:T(8,128)(2,1)S(1)}, u32[]{:S(2)}, u32[]{:S(2)}) async-start(bf16[8,384,128]{2,1,0:T(8,128)(2,1)} %copy-done.9), calls=%async_computation | async-start | bytes 1572864 | tf_op jit(solution)/shard_map/all_to_all | solution.py:287
  178.4 5.0 %place_tiles.1.refs_3_.refs_1_ = bf16[2048,2048]{1,0:T(8,128)(2,1)S(1)} custom-call(s32[256]{0:T(256)S(1)} %reshape.29.positions, bf16[4,1040,128]{2,1,0:T(8,128)(2,1)S(1)} %copy-done.4, bf16[4,1040,128]{2,1,0:T(8,128)(2,1)S(1)} %collective-permute-done.9.refs_1_, bf16[4,1040,128]{2,1,0:T(8,128)(2,1)} %collective-permute-done.10.refs_2_, ...), custom_call_target="tpu_custom_call" | custom-call | bytes 12648448 | tf_op jit(solution)/shard_map/place_tiles/pallas_call | solution.py:173
  183.4 3.3 %copy-done.1 = bf16[2048,2048]{1,0:T(8,128)(2,1)} copy-done((bf16[2048,2048]{1,0:T(8,128)(2,1)}, bf16[2048,2048]{1,0:T(8,128)(2,1)S(1)}, u32[]{:S(2)}) %copy-start.1) | copy-done | bytes 8388632
  186.7 9.8 %apply_metric.2.refs_2_ = f32[2,384,2048]{2,1,0:T(8,128)S(1)} custom-call(bf16[8,384,128]{2,1,0:T(8,128)(2,1)S(1)} %copy-done.6, bf16[8,384,128]{2,1,0:T(8,128)(2,1)S(1)} %copy-done.8, bf16[8,384,128]{2,1,0:T(8,128)(2,1)} %all-to-all-done.3.refs_2_, bf16[2048,2048]{1,0:T(8,128)(2,1)} %copy-done.1), custom_call_target="tpu_custom_call" | custom-call | flops 4831838208 | bytes 15728640 | tf_op jit(solution)/shard_map/apply_metric/pallas_call | solution.py:219
  196.5 2.7 %copy-done.2 = f32[2,384,2048]{2,1,0:T(8,128)} copy-done((f32[2,384,2048]{2,1,0:T(8,128)}, f32[2,384,2048]{2,1,0:T(8,128)S(1)}, u32[]{:S(2)}) %copy-start.2) | copy-done | bytes 6291480
  199.2 2.8 %copy-done.3 = f32[2,384,2048]{2,1,0:T(8,128)S(1)} copy-done((f32[2,384,2048]{2,1,0:T(8,128)S(1)}, f32[2,384,2048]{2,1,0:T(8,128)}, u32[]{:S(2)}) %copy-start.3) | copy-done | bytes 6291480
  202.0 7.4 %apply_metric.3 = bf16[2,384,2048]{2,1,0:T(8,128)(2,1)} custom-call(bf16[8,384,128]{2,1,0:T(8,128)(2,1)S(1)} %all-to-all-done.refs_0_, bf16[2048,2048]{1,0:T(8,128)(2,1)} %copy-done.1, f32[2,384,2048]{2,1,0:T(8,128)S(1)} %copy-done.3), custom_call_target="tpu_custom_call" | custom-call | flops 1610612736 | bytes 11534336 | tf_op jit(solution)/shard_map/apply_metric/pallas_call | solution.py:219
  (87 shorter events, 15.5 us)
Async XLA Ops:
  3.3 20.7 %collective-permute-start = (bf16[48,64,128]{2,1,0:T(8,128)(2,1)}, bf16[48,64,128]{2,1,0:T(8,128)(2,1)S(1)}, u32[]{:S(2)}, u32[]{:S(2)}) collective-permute-start(bf16[48,64,128]{2,1,0:T(8,128)(2,1)} %pack_chunk.7.refs_0_), channel_id=1, source_target_pairs={{0,16},{8,24},{16,0},{24,8},{1,17},{9,25},{17,1},{25,9},{2,18},{10... | collective-permute-start | bytes 2359304 | tf_op jit(solution)/shard_map/ppermute | solution.py:252
  6.3 38.4 %collective-permute-start.12 = (bf16[48,64,128]{2,1,0:T(8,128)(2,1)}, bf16[48,64,128]{2,1,0:T(8,128)(2,1)}, u32[]{:S(2)}, u32[]{:S(2)}) collective-permute-start(bf16[48,64,128]{2,1,0:T(8,128)(2,1)} %pack_chunk.7.refs_0_), channel_id=1, source_target_pairs={{0,8},{8,0},{16,24},{24,16},{1,9},{9,1},{17,25},{25,17},{2,10},{10... | collective-permute-start | bytes 2359304 | tf_op jit(solution)/shard_map/ppermute | solution.py:255
  9.6 35.0 %copy-start.11 = (bf16[48,64,128]{2,1,0:T(8,128)(2,1)S(1)}, bf16[48,64,128]{2,1,0:T(8,128)(2,1)}, u32[]{:S(2)}) copy-start(bf16[48,64,128]{2,1,0:T(8,128)(2,1)} %pack_chunk.6.refs_0_) | copy-start | bytes 2359300
  9.6 36.8 %copy-start.12 = (bf16[48,64,128]{2,1,0:T(8,128)(2,1)S(1)}, bf16[48,64,128]{2,1,0:T(8,128)(2,1)}, u32[]{:S(2)}) copy-start(bf16[48,64,128]{2,1,0:T(8,128)(2,1)} %pack_chunk.7.refs_0_) | copy-start | bytes 2359300
  24.0 19.0 %collective-permute-start.1 = (bf16[48,64,128]{2,1,0:T(8,128)(2,1)}, bf16[48,64,128]{2,1,0:T(8,128)(2,1)}, u32[]{:S(2)}, u32[]{:S(2)}) collective-permute-start(bf16[48,64,128]{2,1,0:T(8,128)(2,1)} %pack_chunk.6.refs_0_), channel_id=1, source_target_pairs={{0,16},{8,24},{16,0},{24,8},{1,17},{9,25},{17,1},{25,9},{2,18},{10... | collective-permute-start | bytes 2359304 | tf_op jit(solution)/shard_map/ppermute | solution.py:252
  25.8 20.5 %collective-permute-start.13 = (bf16[48,64,128]{2,1,0:T(8,128)(2,1)S(1)}, bf16[48,64,128]{2,1,0:T(8,128)(2,1)}, u32[]{:S(2)}, u32[]{:S(2)}) collective-permute-start(bf16[48,64,128]{2,1,0:T(8,128)(2,1)S(1)} %collective-permute-done.refs_2_), channel_id=1, source_target_pairs={{0,8},{8,0},{16,24},{24,16},{1,9},{9,1},{17,25},{25,17},{2,10},{10... | collective-permute-start | bytes 2359304 | tf_op jit(solution)/shard_map/ppermute | solution.py:255
  26.1 18.4 %collective-permute-start.8 = (bf16[1040,128]{1,0:T(8,128)(2,1)S(1)}, bf16[1040,128]{1,0:T(8,128)(2,1)S(1)}, u32[]{:S(2)}, u32[]{:S(2)}) collective-permute-start(bf16[1040,128]{1,0:T(8,128)(2,1)S(1)} %pad_maximum_fusion.refs_0_), channel_id=1, source_target_pairs={{0,6},{1,7},{2,0},{3,1},{4,2},{5,3},{6,4},{7,5},{8,14},{9,15},{10,... | collective-permute-start | bytes 798728 | tf_op jit(solution)/shard_map/ppermute | solution.py:271
  29.8 31.3 %collective-permute-start.7 = (bf16[1040,128]{1,0:T(8,128)(2,1)S(1)}, bf16[1040,128]{1,0:T(8,128)(2,1)}, u32[]{:S(2)}, u32[]{:S(2)}) collective-permute-start(bf16[1040,128]{1,0:T(8,128)(2,1)S(1)} %pad_maximum_fusion.refs_0_), channel_id=1, source_target_pairs={{0,4},{1,5},{2,6},{3,7},{4,0},{5,1},{6,2},{7,3},{8,12},{9,13},{10,... | collective-permute-start | bytes 798728 | tf_op jit(solution)/shard_map/ppermute | solution.py:271
  43.1 18.1 %collective-permute-start.6 = (bf16[1040,128]{1,0:T(8,128)(2,1)S(1)}, bf16[1040,128]{1,0:T(8,128)(2,1)}, u32[]{:S(2)}, u32[]{:S(2)}) collective-permute-start(bf16[1040,128]{1,0:T(8,128)(2,1)S(1)} %pad_maximum_fusion.refs_0_), channel_id=1, source_target_pairs={{0,2},{1,3},{2,4},{3,5},{4,6},{5,7},{6,0},{7,1},{8,10},{9,11},{10,... | collective-permute-start | bytes 798728 | tf_op jit(solution)/shard_map/ppermute | solution.py:271
  44.6 25.4 %collective-permute-start.14 = (bf16[48,64,128]{2,1,0:T(8,128)(2,1)S(1)}, bf16[48,64,128]{2,1,0:T(8,128)(2,1)}, u32[]{:S(2)}, u32[]{:S(2)}) collective-permute-start(bf16[48,64,128]{2,1,0:T(8,128)(2,1)S(1)} %copy-done.11), channel_id=1, source_target_pairs={{0,8},{8,0},{16,24},{24,16},{1,9},{9,1},{17,25},{25,17},{2,10},{10... | collective-permute-start | bytes 2359304 | tf_op jit(solution)/shard_map/ppermute | solution.py:255
  44.7 24.6 %collective-permute-start.2 = (bf16[48,64,128]{2,1,0:T(8,128)(2,1)}, bf16[48,64,128]{2,1,0:T(8,128)(2,1)}, u32[]{:S(2)}, u32[]{:S(2)}) collective-permute-start(bf16[48,64,128]{2,1,0:T(8,128)(2,1)} %pack_chunk.5.refs_0_), channel_id=1, source_target_pairs={{0,16},{8,24},{16,0},{24,8},{1,17},{9,25},{17,1},{25,9},{2,18},{10... | collective-permute-start | bytes 2359304 | tf_op jit(solution)/shard_map/ppermute | solution.py:252
  46.3 23.7 %collective-permute-start.15 = (bf16[48,64,128]{2,1,0:T(8,128)(2,1)}, bf16[48,64,128]{2,1,0:T(8,128)(2,1)}, u32[]{:S(2)}, u32[]{:S(2)}) collective-permute-start(bf16[48,64,128]{2,1,0:T(8,128)(2,1)} %collective-permute-done.1.refs_2_), channel_id=1, source_target_pairs={{0,8},{8,0},{16,24},{24,16},{1,9},{9,1},{17,25},{25,17},{2,10},{10... | collective-permute-start | bytes 2359304 | tf_op jit(solution)/shard_map/ppermute | solution.py:255
  61.2 25.5 %all-to-all-start.1 = ((bf16[8,384,128]{2,1,0:T(8,128)(2,1)}), bf16[8,384,128]{2,1,0:T(8,128)(2,1)S(1)}, u32[]{:S(2)}, u32[]{:S(2)}) async-start(bf16[8,384,128]{2,1,0:T(8,128)(2,1)} %chunk_products.5), calls=%async_computation.1 | async-start | bytes 1572864 | tf_op jit(solution)/shard_map/all_to_all | solution.py:287
  69.2 57.5 %collective-permute-start.16 = (bf16[48,64,128]{2,1,0:T(8,128)(2,1)}, bf16[48,64,128]{2,1,0:T(8,128)(2,1)}, u32[]{:S(2)}, u32[]{:S(2)}) collective-permute-start(bf16[48,64,128]{2,1,0:T(8,128)(2,1)} %pack_chunk.5.refs_0_), channel_id=1, source_target_pairs={{0,8},{8,0},{16,24},{24,16},{1,9},{9,1},{17,25},{25,17},{2,10},{10... | collective-permute-start | bytes 2359304 | tf_op jit(solution)/shard_map/ppermute | solution.py:255
  69.3 56.9 %collective-permute-start.4 = (bf16[48,64,128]{2,1,0:T(8,128)(2,1)}, bf16[48,64,128]{2,1,0:T(8,128)(2,1)}, u32[]{:S(2)}, u32[]{:S(2)}) collective-permute-start(bf16[48,64,128]{2,1,0:T(8,128)(2,1)} %pack_chunk.4.refs_0_), channel_id=1, source_target_pairs={{0,16},{8,24},{16,0},{24,8},{1,17},{9,25},{17,1},{25,9},{2,18},{10... | collective-permute-start | bytes 2359304 | tf_op jit(solution)/shard_map/ppermute | solution.py:252
  69.8 56.9 %collective-permute-start.17 = (bf16[48,64,128]{2,1,0:T(8,128)(2,1)}, bf16[48,64,128]{2,1,0:T(8,128)(2,1)}, u32[]{:S(2)}, u32[]{:S(2)}) collective-permute-start(bf16[48,64,128]{2,1,0:T(8,128)(2,1)} %collective-permute-done.2.refs_2_), channel_id=1, source_target_pairs={{0,8},{8,0},{16,24},{24,16},{1,9},{9,1},{17,25},{25,17},{2,10},{10... | collective-permute-start | bytes 2359304 | tf_op jit(solution)/shard_map/ppermute | solution.py:255
  86.6 55.4 %all-to-all-start.2 = ((bf16[8,384,128]{2,1,0:T(8,128)(2,1)}), bf16[8,384,128]{2,1,0:T(8,128)(2,1)S(1)}, u32[]{:S(2)}, u32[]{:S(2)}) async-start(bf16[8,384,128]{2,1,0:T(8,128)(2,1)} %chunk_products.6), calls=%async_computation.2 | async-start | bytes 1572864 | tf_op jit(solution)/shard_map/all_to_all | solution.py:287
  124.1 29.3 %collective-permute-start.9 = (bf16[4,1040,128]{2,1,0:T(8,128)(2,1)}, bf16[4,1040,128]{2,1,0:T(8,128)(2,1)S(1)}, u32[]{:S(2)}, u32[]{:S(2)}) collective-permute-start(bf16[4,1040,128]{2,1,0:T(8,128)(2,1)} %join.1.refs_0_), channel_id=1, source_target_pairs={{0,1},{1,0},{2,3},{3,2},{4,5},{5,4},{6,7},{7,6},{8,9},{9,8},{10,11... | collective-permute-start | bytes 3194888 | tf_op jit(solution)/shard_map/ppermute | solution.py:290
  126.2 27.3 %collective-permute-start.3 = (bf16[48,64,128]{2,1,0:T(8,128)(2,1)}, bf16[48,64,128]{2,1,0:T(8,128)(2,1)}, u32[]{:S(2)}, u32[]{:S(2)}) collective-permute-start(bf16[48,64,128]{2,1,0:T(8,128)(2,1)} %pack_chunk.4.refs_0_), channel_id=1, source_target_pairs={{0,8},{8,0},{16,24},{24,16},{1,9},{9,1},{17,25},{25,17},{2,10},{10... | collective-permute-start | bytes 2359304 | tf_op jit(solution)/shard_map/ppermute | solution.py:255
  126.2 27.3 %collective-permute-start.5 = (bf16[48,64,128]{2,1,0:T(8,128)(2,1)}, bf16[48,64,128]{2,1,0:T(8,128)(2,1)}, u32[]{:S(2)}, u32[]{:S(2)}) collective-permute-start(bf16[48,64,128]{2,1,0:T(8,128)(2,1)} %collective-permute-done.4.refs_2_), channel_id=1, source_target_pairs={{0,8},{8,0},{16,24},{24,16},{1,9},{9,1},{17,25},{25,17},{2,10},{10... | collective-permute-start | bytes 2359304 | tf_op jit(solution)/shard_map/ppermute | solution.py:255
  142.1 27.3 %all-to-all-start.3 = ((bf16[8,384,128]{2,1,0:T(8,128)(2,1)}), bf16[8,384,128]{2,1,0:T(8,128)(2,1)}, u32[]{:S(2)}, u32[]{:S(2)}) async-start(bf16[8,384,128]{2,1,0:T(8,128)(2,1)} %copy-done.10), calls=%async_computation.3 | async-start | bytes 1572864 | tf_op jit(solution)/shard_map/all_to_all | solution.py:287
  146.6 30.2 %collective-permute-start.10 = (bf16[4,1040,128]{2,1,0:T(8,128)(2,1)S(1)}, bf16[4,1040,128]{2,1,0:T(8,128)(2,1)}, u32[]{:S(2)}, u32[]{:S(2)}) collective-permute-start(bf16[4,1040,128]{2,1,0:T(8,128)(2,1)S(1)} %copy-done.4), channel_id=1, source_target_pairs={{0,8},{8,0},{16,24},{24,16},{1,9},{9,1},{17,25},{25,17},{2,10},{10... | collective-permute-start | bytes 3194888 | tf_op jit(solution)/shard_map/ppermute | solution.py:255
  153.4 24.1 %collective-permute-start.11 = (bf16[4,1040,128]{2,1,0:T(8,128)(2,1)S(1)}, bf16[4,1040,128]{2,1,0:T(8,128)(2,1)}, u32[]{:S(2)}, u32[]{:S(2)}) collective-permute-start(bf16[4,1040,128]{2,1,0:T(8,128)(2,1)S(1)} %collective-permute-done.9.refs_1_), channel_id=1, source_target_pairs={{0,8},{8,0},{16,24},{24,16},{1,9},{9,1},{17,25},{25,17},{2,10},{10... | collective-permute-start | bytes 3194888 | tf_op jit(solution)/shard_map/ppermute | solution.py:255
  169.4 29.8 %all-to-all-start = ((bf16[8,384,128]{2,1,0:T(8,128)(2,1)}), bf16[8,384,128]{2,1,0:T(8,128)(2,1)S(1)}, u32[]{:S(2)}, u32[]{:S(2)}) async-start(bf16[8,384,128]{2,1,0:T(8,128)(2,1)} %copy-done.9), calls=%async_computation | async-start | bytes 1572864 | tf_op jit(solution)/shard_map/all_to_all | solution.py:287
  (16 other events, 208.2 us)

commit v3 on v2

--- a/solution.py
+++ b/solution.py
@@ -15,27 +15,34 @@
     return max(size for size in range(1, most + 1) if total % size == 0)
 
 
-def pack_kernel(first, width, source, chunk):
+def pack_kernel(width, source, *chunks):
     half = source.shape[1] // 2
-    columns = slice(first, first + width)
-    chunk[...] = jnp.concatenate([source[:, :half, columns], source[:, half:, columns]], axis=-1)
-
-
-def pack_chunk(factors, width, at):
+    for at, chunk in enumerate(chunks):
+        columns = slice(at * width, (at + 1) * width)
+        chunk[...] = jnp.concatenate([source[:, :half, columns], source[:, half:, columns]], axis=-1)
+
+
+def pack_chunks(factors, width):
     orbitals, domain, part = factors.shape
-    lanes = 2 * width if part % (2 * width) == 0 else part
-    step = largest_divisor(orbitals, 16)
-    first = at * width
+    count = part // width
+    step = largest_divisor(orbitals, 12)
+    packed = (step, domain // 2, 2 * width)
     return pl.pallas_call(
-        functools.partial(pack_kernel, first % lanes, width),
+        functools.partial(pack_kernel, width),
         grid=(orbitals // step,),
-        in_specs=[pl.BlockSpec((step, domain, lanes), lambda i: (i, 0, first // lanes))],
-        out_specs=pl.BlockSpec((step, domain // 2, 2 * width), lambda i: (i, 0, 0)),
-        out_shape=jax.ShapeDtypeStruct((orbitals, domain // 2, 2 * width), factors.dtype),
-        cost_estimate=pl.CostEstimate(flops=0, bytes_accessed=6 * orbitals * domain * width, transcendentals=0),
+        in_specs=[pl.BlockSpec((step, domain, part), lambda i: (i, 0, 0))],
+        out_specs=[pl.BlockSpec(packed, lambda i: (i, 0, 0))] * count,
+        out_shape=[jax.ShapeDtypeStruct((orbitals,) + packed[1:], factors.dtype)] * count,
+        cost_estimate=pl.CostEstimate(flops=0, bytes_accessed=4 * factors.size, transcendentals=0),
         compiler_params=pltpu.CompilerParams(vmem_limit_bytes=VMEM_WHOLE),
-        name="pack_chunk",
+        name="pack_chunks",
     )(factors)
+
+
+def halves_apart(one, two, half):
+    lower = jnp.concatenate([one[:, :half], two[:, :half]], axis=1)
+    upper = jnp.concatenate([one[:, half:], two[:, half:]], axis=1)
+    return lower, upper
 
 
 def product_kernel(pairs, split_rows, slots, amplitudes, *refs):
@@ -47,38 +54,34 @@
     @pl.when(here == 0)
     def _():
         copies = [
-            pltpu.make_async_copy(piece, table.at[pl.ds(at * group, group), pl.ds(0, half_domain)], arrived.at[at])
+            pltpu.make_async_copy(piece, table.at[pl.ds(at * group, group)], arrived.at[at])
             for at, piece in enumerate(pieces)
         ]
         for copy in copies:
             copy.start()
-        for at, copy in enumerate(copies):
+        for copy in copies:
             copy.wait()
 
-            @pl.loop(at * group, (at + 1) * group, unroll=8)
-            def _(row):
-                block = table[row, :half_domain, :]
-                table[row, half_domain:, :] = jnp.concatenate([block[:, lanes // 2 :], block[:, : lanes // 2]], axis=1)
-
-    step = amplitudes.shape[1]
+    step, domain = amplitudes.shape[1], amplitudes.shape[3]
     half_count = pl.num_programs(0) * step
-    lower = lax.broadcasted_iota(jnp.int32, (amplitudes.shape[3], lanes), 1) < lanes // 2
+    first = lax.broadcasted_iota(jnp.int32, (domain, lanes), 1) < lanes // 2
     for q in range(step):
         sums = []
         for side in range(2):
             base = (side * half_count + here * step + q) * pairs
-            left = jnp.concatenate([amplitudes[side, q, k] for k in range(pairs)], axis=1)
-            right = []
-            for k in range(pairs):
-                slot = slots[base + k]
-                if side:
-                    right += [table[slot, half_domain:, :], table[slot, :half_domain, :]]
-                else:
-                    right += [table[slot]]
-            sums.append(jnp.dot(left, jnp.concatenate(right, axis=0), preferred_element_type=jnp.float32))
-        both = jnp.where(lower, sums[0], sums[1]).astype(out.dtype)
+            lower, upper = [], []
+            for k in range(0, pairs, 2):
+                low, high = halves_apart(amplitudes[side, q, k], amplitudes[side, q, k + 1], half_domain)
+                lower.append(low)
+                upper.append(high)
+            left = jnp.concatenate([jnp.concatenate(lower, axis=1), jnp.concatenate(upper, axis=1)], axis=0)
+            right = jnp.concatenate([table[slots[base + k]] for k in range(pairs)], axis=0)
+            sums.append(jnp.dot(left, right, preferred_element_type=jnp.float32))
+        placed = jnp.where(first, sums[0][:domain], sums[1][domain:])
+        moved = jnp.where(first, sums[1][:domain], sums[0][domain:])
+        both = (placed + pltpu.roll(moved, lanes // 2, 1)).astype(out.dtype)
         if split_rows:
-            owners, rows = out.shape[0], both.shape[0] // out.shape[0]
+            owners, rows = out.shape[0], domain // out.shape[0]
             out[:, q * rows : (q + 1) * rows, :] = both.reshape(owners, rows, lanes)
         else:
             out[q] = both
@@ -105,7 +108,7 @@
             + [pl.BlockSpec(memory_space=pl.ANY)] * len(pieces),
             out_specs=pl.BlockSpec(out_block, out_at),
             scratch_shapes=[
-                pltpu.VMEM((total, domain, lanes), jnp.bfloat16),
+                pltpu.VMEM((total, half_domain, lanes), jnp.bfloat16),
                 pltpu.SemaphoreType.DMA((len(pieces),)),
             ],
         ),
@@ -125,24 +128,17 @@
 
 
 def join_kernel(*refs):
-    pieces = refs[:-2]
-    out, arrived = refs[-2:]
-    copies = [pltpu.make_async_copy(piece, out.at[at], arrived.at[at]) for at, piece in enumerate(pieces)]
-    for copy in copies:
-        copy.start()
-    for copy in copies:
-        copy.wait()
+    for at, piece in enumerate(refs[:-1]):
+        refs[-1][at] = piece[...]
 
 
 def join(pieces):
     shape = (len(pieces),) + pieces[0].shape
     return pl.pallas_call(
         join_kernel,
-        in_specs=[pl.BlockSpec(memory_space=pl.ANY)] * len(pieces),
-        out_specs=pl.BlockSpec(memory_space=pl.ANY),
         out_shape=jax.ShapeDtypeStruct(shape, pieces[0].dtype),
-        scratch_shapes=[pltpu.SemaphoreType.DMA((len(pieces),))],
         cost_estimate=pl.CostEstimate(flops=0, bytes_accessed=4 * len(pieces) * pieces[0].size, transcendentals=0),
+        compiler_params=pltpu.CompilerParams(vmem_limit_bytes=VMEM_LIMIT),
         name="join",
     )(*pieces)
 
@@ -230,7 +226,7 @@
             bytes_accessed=2 * depth * size + 12 * height * size,
             transcendentals=0,
         ),
-        compiler_params=pltpu.CompilerParams(vmem_limit_bytes=VMEM_LIMIT),
+        compiler_params=pltpu.CompilerParams(vmem_limit_bytes=VMEM_WHOLE),
         name="apply_metric",
     )(*chunks, metric, *sums)
 
@@ -270,25 +266,29 @@
         moves = [(g, (g + 2 * shift) % aux_count) for g in range(aux_count)]
         parts.append(lax.ppermute(load, "aux", moves))
 
-    products = []
-    last = None
-    for at in range(chunk_count):
-        own = pack_chunk(factors, width, at)
-        if last is not None:
-            own = after(own, last)
-        far_pieces = [to_far(own, shift) for shift in range(1, far_count)]
-        last = far_pieces[-1] if far_pieces else None
-        pieces = []
-        for piece in [own] + far_pieces:
-            pieces += [piece, to_mate(piece)]
-        made = chunk_products(slots, amplitudes, pieces, aux_count)
-        if at == 0:
-            made = after(made, parts)
-        products.append(lax.all_to_all(made, "aux", split_axis=0, concat_axis=0, tiled=True))
-
     column = join(parts)
     beside = lax.ppermute(column, "aux", [(g, g ^ 1) for g in range(aux_count)])
     sources = [column, beside, to_mate(column), to_mate(beside)]
+
+    packed = pack_chunks(factors, width)
+    before_far = {1: parts[1::2]}
+    before_rows = {0: parts, 1: beside, 2: sources[2:]}
+    products = []
+    far_pieces, made = [], None
+    for at in range(chunk_count):
+        own = packed[at]
+        if at:
+            own = after(own, [far_pieces, before_far.get(at, [])])
+        far_pieces = [to_far(own, shift) for shift in range(1, far_count)]
+        if at:
+            far_pieces = after(far_pieces, made)
+        pieces = []
+        for piece in [packed[at]] + far_pieces:
+            pieces += [piece, to_mate(piece)]
+        made = chunk_products(slots, amplitudes, pieces, aux_count)
+        rows = after(made, before_rows[at]) if at in before_rows and chunk_count > 1 else made
+        products.append(lax.all_to_all(rows, "aux", split_axis=0, concat_axis=0, tiled=True))
+
     positions = jnp.concatenate([source[:, half_tiles * span, : 2 * half_tiles] for source in sources])
     positions = positions.astype(jnp.int32).reshape(-1)
     metric = place_tiles(positions, sources, half_tiles, chunk_count, aux_count, part * aux_count)

time: 211 us -> 201 us (0.953)
  Pallas kernels: 126 us -> 84.3 us
  waiting for transfers between devices: 33 us -> 72.1 us
  starting transfers between devices: 35.9 us -> 32.5 us
  local copies, waits for them, and re-layouts: 13.6 us -> 10.6 us
    pallas_call x5 -> x2, Pallas kernels: 46.5 us -> 4.54 us  [the longest x1 4.47 us: pack_chunks(): pl.pallas_call(functools.partial(pack_kernel, width), grid=(orbitals // s...]
    ppermute x3, waiting for transfers between devices: 0.01 us -> 27.2 us  [shards(): parts.append(lax.ppermute(load, 'aux', moves))]
    all_to_all x4, waiting for transfers between devices: 1.97 us -> 8.43 us  [shards(): lax.all_to_all(rows, 'aux', split_axis=0, concat_axis=0, tiled=True)]
    ppermute x4, waiting for transfers between devices: 24.3 us -> 28.9 us  [to_far(): return lax.ppermute(array, 'orb', moves)]
    pallas_call x2, Pallas kernels: 17.2 us -> 20.8 us  [apply_metric(): pl.pallas_call(functools.partial(metric_kernel, len(chunks), before is no...]
    pallas_call x4, Pallas kernels: 57.8 us -> 54.3 us  [chunk_products(): pl.pallas_call(functools.partial(product_kernel, pairs, split_rows), grid...]
    unnamed x40 -> x24, local copies, waits for them, and re-layouts: 11.7 us -> 8.69 us
    all_to_all x4, starting transfers between devices: 20.8 us -> 17.9 us  [shards(): lax.all_to_all(rows, 'aux', split_axis=0, concat_axis=0, tiled=True)]
  transfers between devices with their start and end apart: 22 -> 22, of which waited for: 4 -> 10; matrix products, arithmetic and copies ran while one was open for 1% -> 1% of each run, Pallas kernels for 55% -> 35%
where the time goes in v3:
time: 201 us; the launch traced here: 200 us
  Pallas kernels  84.3 us (42%)
  waiting for transfers between devices  72.1 us (36%)
  starting transfers between devices  32.5 us (16%)
  local copies, waits for them, and re-layouts  10.6 us (5%)
    pallas_call x4, Pallas kernels, chunk_products(): pl.pallas_call(functools.partial(product_kernel, pairs, split_rows), grid...  54.3 us
    ppermute x4, waiting for transfers between devices, to_far(): return lax.ppermute(array, 'orb', moves)  28.9 us
    ppermute x3, waiting for transfers between devices, shards(): parts.append(lax.ppermute(load, 'aux', moves))  27.2 us
    pallas_call x2, Pallas kernels, apply_metric(): pl.pallas_call(functools.partial(metric_kernel, len(chunks), before is no...  20.8 us
    all_to_all x4, starting transfers between devices, shards(): lax.all_to_all(rows, 'aux', split_axis=0, concat_axis=0, tiled=True)  17.9 us
    unnamed x24, local copies, waits for them, and re-layouts  8.69 us
    all_to_all x4, waiting for transfers between devices, shards(): lax.all_to_all(rows, 'aux', split_axis=0, concat_axis=0, tiled=True)  8.43 us
    ppermute x4, starting transfers between devices, to_far(): return lax.ppermute(array, 'orb', moves)  7.59 us
  transfers between devices with their start and end apart: 22, of which 10 were waited for; matrix products, arithmetic and copies ran while one was open for 1% of the time, Pallas kernels for 35%

profile of v3, /device:TPU:0, one launch (start us, length us, event | category | flops | bytes accessed | tf_op | source)
XLA Modules:
  0.0 199.8 jit_solution(4260440523557450056)
XLA Ops:
  0.0 4.5 %pack_chunks.1 = (bf16[48,64,128]{2,1,0:T(8,128)(2,1)}, bf16[48,64,128]{2,1,0:T(8,128)(2,1)}, bf16[48,64,128]{2,1,0:T(8,128)(2,1)}, bf16[48,64,128]{2,1,0:T(8,128)(2,1)}) custom-call(bf16[48,128,256]{2,1,0:T(8,128)(2,1)} %source.1), custom_call_target="tpu_custom_call" | custom-call | bytes 6291456 | tf_op jit(solution)/shard_map/pack_chunks/pallas_call | solution.py:30
  4.5 3.0 %collective-permute-start.1 = (bf16[48,64,128]{2,1,0:T(8,128)(2,1)}, bf16[48,64,128]{2,1,0:T(8,128)(2,1)S(1)}, u32[]{:S(2)}, u32[]{:S(2)}) collective-permute-start(bf16[48,64,128]{2,1,0:T(8,128)(2,1)} %get-tuple-element.24.refs_0_), channel_id=1, source_target_pairs={{0,16},{8,24},{16,0},{24,8},{1,17},{9,25},{17,1},{25,9},{2,18},{10... | collective-permute-start | bytes 2359304 | tf_op jit(solution)/shard_map/ppermute | solution.py:248
  7.4 17.7 %collective-permute-done.1.refs_2_ = bf16[48,64,128]{2,1,0:T(8,128)(2,1)S(1)} collective-permute-done((bf16[48,64,128]{2,1,0:T(8,128)(2,1)}, bf16[48,64,128]{2,1,0:T(8,128)(2,1)S(1)}, u32[]{:S(2)}, u32[]{:S(2)}) %collective-permute-start.1) | collective-permute-done | bytes 786464 | tf_op jit(solution)/shard_map/ppermute | solution.py:248
  25.5 3.9 %collective-permute-start.3 = (bf16[1040,128]{1,0:T(8,128)(2,1)S(1)}, bf16[1040,128]{1,0:T(8,128)(2,1)S(1)}, u32[]{:S(2)}, u32[]{:S(2)}) collective-permute-start(bf16[1040,128]{1,0:T(8,128)(2,1)S(1)} %pad_maximum_fusion.refs_0_), channel_id=1, source_target_pairs={{0,6},{1,7},{2,0},{3,1},{4,2},{5,3},{6,4},{7,5},{8,14},{9,15},{10,... | collective-permute-start | bytes 798728 | tf_op jit(solution)/shard_map/ppermute | solution.py:267
  29.9 6.3 %collective-permute-done.3.refs_3_ = bf16[1040,128]{1,0:T(8,128)(2,1)S(1)} collective-permute-done((bf16[1040,128]{1,0:T(8,128)(2,1)S(1)}, bf16[1040,128]{1,0:T(8,128)(2,1)S(1)}, u32[]{:S(2)}, u32[]{:S(2)}) %collective-permute-start.3) | collective-permute-done | bytes 266272 | tf_op jit(solution)/shard_map/ppermute | solution.py:267
  36.2 6.2 %collective-permute-done.2.refs_1_ = bf16[1040,128]{1,0:T(8,128)(2,1)S(1)} collective-permute-done((bf16[1040,128]{1,0:T(8,128)(2,1)S(1)}, bf16[1040,128]{1,0:T(8,128)(2,1)S(1)}, u32[]{:S(2)}, u32[]{:S(2)}) %collective-permute-start.2) | collective-permute-done | bytes 266272 | tf_op jit(solution)/shard_map/ppermute | solution.py:267
  45.0 13.2 %chunk_products.4 = bf16[8,384,128]{2,1,0:T(8,128)(2,1)} custom-call(s32[576]{0:T(1024)S(1)} %reshape.24.slots, bf16[2,24,12,128,128]{4,3,2,1,0:T(8,128)(2,1)} %bitcast.22, bf16[48,64,128]{2,1,0:T(8,128)(2,1)S(1)} %copy-done.6, bf16[48,64,128]{2,1,0:T(8,128)(2,1)S(1)} %collective-permute-done.5.refs_1_, ...), custom_call_target="tpu_custom_call" | custom-call | flops 9663676416 | bytes 22020096 | tf_op jit(solution)/shard_map/chunk_products/pallas_call | solution.py:102
  58.3 3.6 %collective-permute-done.4.refs_2_ = bf16[48,64,128]{2,1,0:T(8,128)(2,1)} collective-permute-done((bf16[48,64,128]{2,1,0:T(8,128)(2,1)}, bf16[48,64,128]{2,1,0:T(8,128)(2,1)}, u32[]{:S(2)}, u32[]{:S(2)}) %collective-permute-start.4) | collective-permute-done | bytes 786464 | tf_op jit(solution)/shard_map/ppermute | solution.py:248
  62.5 14.8 %collective-permute-done.14.refs_2_ = bf16[1040,128]{1,0:T(8,128)(2,1)S(1)} collective-permute-done((bf16[1040,128]{1,0:T(8,128)(2,1)S(1)}, bf16[1040,128]{1,0:T(8,128)(2,1)S(1)}, u32[]{:S(2)}, u32[]{:S(2)}) %collective-permute-start.14) | collective-permute-done | bytes 266272 | tf_op jit(solution)/shard_map/ppermute | solution.py:267
  78.9 4.2 %all-to-all-start.1 = ((bf16[8,384,128]{2,1,0:T(8,128)(2,1)}), bf16[8,384,128]{2,1,0:T(8,128)(2,1)}, u32[]{:S(2)}, u32[]{:S(2)}) async-start(bf16[8,384,128]{2,1,0:T(8,128)(2,1)} %chunk_products.4), calls=%async_computation.1 | async-start | bytes 1572864 | tf_op jit(solution)/shard_map/all_to_all | solution.py:290
  85.8 13.6 %chunk_products.5 = bf16[8,384,128]{2,1,0:T(8,128)(2,1)} custom-call(s32[576]{0:T(1024)S(1)} %reshape.24.slots, bf16[2,24,12,128,128]{4,3,2,1,0:T(8,128)(2,1)} %bitcast.23, bf16[48,64,128]{2,1,0:T(8,128)(2,1)S(1)} %copy-done.5, bf16[48,64,128]{2,1,0:T(8,128)(2,1)} %collective-permute-done.8.refs_1_, bf16[48,64,128]{2,1,0:T(8,128)(2,1)} %collective-permute-done.4.refs_2_, ...), custom_call_target="tpu_custom_call" | custom-call | flops 9663676416 | bytes 22020096 | tf_op jit(solution)/shard_map/chunk_products/pallas_call | solution.py:102
  99.5 2.9 %collective-permute-done.7.refs_2_ = bf16[48,64,128]{2,1,0:T(8,128)(2,1)} collective-permute-done((bf16[48,64,128]{2,1,0:T(8,128)(2,1)}, bf16[48,64,128]{2,1,0:T(8,128)(2,1)}, u32[]{:S(2)}, u32[]{:S(2)}) %collective-permute-start.7) | collective-permute-done | bytes 786464 | tf_op jit(solution)/shard_map/ppermute | solution.py:248
  102.4 7.5 %collective-permute-done.15.refs_1_ = bf16[4,1040,128]{2,1,0:T(8,128)(2,1)S(1)} collective-permute-done((bf16[4,1040,128]{2,1,0:T(8,128)(2,1)S(1)}, bf16[4,1040,128]{2,1,0:T(8,128)(2,1)S(1)}, u32[]{:S(2)}, u32[]{:S(2)}) %collective-permute-start.15) | collective-permute-done | bytes 1064992 | tf_op jit(solution)/shard_map/ppermute | solution.py:270
  111.1 4.2 %all-to-all-start.2 = ((bf16[8,384,128]{2,1,0:T(8,128)(2,1)}), bf16[8,384,128]{2,1,0:T(8,128)(2,1)}, u32[]{:S(2)}, u32[]{:S(2)}) async-start(bf16[8,384,128]{2,1,0:T(8,128)(2,1)} %chunk_products.5), calls=%async_computation.2 | async-start | bytes 1572864 | tf_op jit(solution)/shard_map/all_to_all | solution.py:290
  117.5 13.8 %chunk_products.6 = bf16[8,384,128]{2,1,0:T(8,128)(2,1)} custom-call(s32[576]{0:T(1024)S(1)} %reshape.24.slots, bf16[2,24,12,128,128]{4,3,2,1,0:T(8,128)(2,1)} %bitcast.24, bf16[48,64,128]{2,1,0:T(8,128)(2,1)} %get-tuple-element.27.refs_0_, bf16[48,64,128]{2,1,0:T(8,128)(2,1)} %collective-permute-done.11.refs_1_, ...), custom_call_target="tpu_custom_call" | custom-call | flops 9663676416 | bytes 22020096 | tf_op jit(solution)/shard_map/chunk_products/pallas_call | solution.py:102
  131.3 4.7 %collective-permute-done.10.refs_2_ = bf16[48,64,128]{2,1,0:T(8,128)(2,1)} collective-permute-done((bf16[48,64,128]{2,1,0:T(8,128)(2,1)S(1)}, bf16[48,64,128]{2,1,0:T(8,128)(2,1)}, u32[]{:S(2)}, u32[]{:S(2)}) %collective-permute-start.10) | collective-permute-done | bytes 786464 | tf_op jit(solution)/shard_map/ppermute | solution.py:248
  136.9 5.8 %all-to-all-start.3 = ((bf16[8,384,128]{2,1,0:T(8,128)(2,1)}), bf16[8,384,128]{2,1,0:T(8,128)(2,1)}, u32[]{:S(2)}, u32[]{:S(2)}) async-start(bf16[8,384,128]{2,1,0:T(8,128)(2,1)} %chunk_products.6), calls=%async_computation.3 | async-start | bytes 1572864 | tf_op jit(solution)/shard_map/all_to_all | solution.py:290
  142.8 13.6 %chunk_products.7 = bf16[8,384,128]{2,1,0:T(8,128)(2,1)} custom-call(s32[576]{0:T(1024)S(1)} %reshape.24.slots, bf16[2,24,12,128,128]{4,3,2,1,0:T(8,128)(2,1)} %bitcast.25, bf16[48,64,128]{2,1,0:T(8,128)(2,1)S(1)} %copy-done.4, bf16[48,64,128]{2,1,0:T(8,128)(2,1)} %collective-permute-done.refs_1_, bf16[48,64,128]{2,1,0:T(8,128)(2,1)} %collective-permute-done.10.refs_2_, ...), custom_call_target="tpu_custom_call" | custom-call | flops 9663676416 | bytes 22020096 | tf_op jit(solution)/shard_map/chunk_products/pallas_call | solution.py:102
  156.4 7.3 %all-to-all-done.3.refs_2_ = bf16[8,384,128]{2,1,0:T(8,128)(2,1)} async-done(((bf16[8,384,128]{2,1,0:T(8,128)(2,1)}), bf16[8,384,128]{2,1,0:T(8,128)(2,1)}, u32[]{:S(2)}, u32[]{:S(2)}) %all-to-all-start.3) | async-done | bytes 786464 | tf_op jit(solution)/shard_map/all_to_all | solution.py:290
  163.7 3.6 %all-to-all-start = ((bf16[8,384,128]{2,1,0:T(8,128)(2,1)}), bf16[8,384,128]{2,1,0:T(8,128)(2,1)S(1)}, u32[]{:S(2)}, u32[]{:S(2)}) async-start(bf16[8,384,128]{2,1,0:T(8,128)(2,1)} %chunk_products.7), calls=%async_computation | async-start | bytes 1572864 | tf_op jit(solution)/shard_map/all_to_all | solution.py:290
  170.1 4.7 %place_tiles.1.refs_3_.refs_1_ = bf16[2048,2048]{1,0:T(8,128)(2,1)S(1)} custom-call(s32[256]{0:T(256)S(1)} %reshape.29.positions, bf16[4,1040,128]{2,1,0:T(8,128)(2,1)S(1)} %join.1.refs_0_, bf16[4,1040,128]{2,1,0:T(8,128)(2,1)S(1)} %collective-permute-done.15.refs_1_, bf16[4,1040,128]{2,1,0:T(8,128)(2,1)S(1)} %copy-done.3, ...), custom_call_target="tpu_custom_call" | custom-call | bytes 12648448 | tf_op jit(solution)/shard_map/place_tiles/pallas_call | solution.py:169
  174.8 3.3 %copy-done.1 = bf16[2048,2048]{1,0:T(8,128)(2,1)} copy-done((bf16[2048,2048]{1,0:T(8,128)(2,1)}, bf16[2048,2048]{1,0:T(8,128)(2,1)S(1)}, u32[]{:S(2)}) %copy-start.1) | copy-done | bytes 8388632
  178.1 11.8 %apply_metric.2.refs_2_ = f32[2,384,2048]{2,1,0:T(8,128)} custom-call(bf16[8,384,128]{2,1,0:T(8,128)(2,1)} %all-to-all-done.1.refs_0_, bf16[8,384,128]{2,1,0:T(8,128)(2,1)} %all-to-all-done.2.refs_1_, bf16[8,384,128]{2,1,0:T(8,128)(2,1)} %all-to-all-done.3.refs_2_, bf16[2048,2048]{1,0:T(8,128)(2,1)} %copy-done.1), custom_call_target="tpu_custom_call" | custom-call | flops 4831838208 | bytes 15728640 | tf_op jit(solution)/shard_map/apply_metric/pallas_call | solution.py:215
  190.8 9.0 %apply_metric.3 = bf16[2,384,2048]{2,1,0:T(8,128)(2,1)} custom-call(bf16[8,384,128]{2,1,0:T(8,128)(2,1)} %copy-done.7, bf16[2048,2048]{1,0:T(8,128)(2,1)} %copy-done.1, f32[2,384,2048]{2,1,0:T(8,128)} %apply_metric.2.refs_2_), custom_call_target="tpu_custom_call" | custom-call | flops 1610612736 | bytes 11534336 | tf_op jit(solution)/shard_map/apply_metric/pallas_call | solution.py:215
  (68 shorter events, 16.5 us)
Async XLA Ops:
  0.0 29.6 %copy-start.8 = (s32[48,12]{0,1:T(8,128)S(1)}, s32[48,12]{0,1:T(8,128)}, u32[]{:S(2)}) copy-start(s32[48,12]{0,1:T(8,128)} %param.7) | copy-start | bytes 6916
  4.5 20.7 %collective-permute-start.1 = (bf16[48,64,128]{2,1,0:T(8,128)(2,1)}, bf16[48,64,128]{2,1,0:T(8,128)(2,1)S(1)}, u32[]{:S(2)}, u32[]{:S(2)}) collective-permute-start(bf16[48,64,128]{2,1,0:T(8,128)(2,1)} %get-tuple-element.24.refs_0_), channel_id=1, source_target_pairs={{0,16},{8,24},{16,0},{24,8},{1,17},{9,25},{17,1},{25,9},{2,18},{10... | collective-permute-start | bytes 2359304 | tf_op jit(solution)/shard_map/ppermute | solution.py:248
  7.4 36.4 %collective-permute-start.5 = (bf16[48,64,128]{2,1,0:T(8,128)(2,1)}, bf16[48,64,128]{2,1,0:T(8,128)(2,1)S(1)}, u32[]{:S(2)}, u32[]{:S(2)}) collective-permute-start(bf16[48,64,128]{2,1,0:T(8,128)(2,1)} %get-tuple-element.24.refs_0_), channel_id=1, source_target_pairs={{0,8},{8,0},{16,24},{24,16},{1,9},{9,1},{17,25},{25,17},{2,10},{10... | collective-permute-start | bytes 2359304 | tf_op jit(solution)/shard_map/ppermute | solution.py:251
  25.2 18.7 %collective-permute-start.6 = (bf16[48,64,128]{2,1,0:T(8,128)(2,1)S(1)}, bf16[48,64,128]{2,1,0:T(8,128)(2,1)}, u32[]{:S(2)}, u32[]{:S(2)}) collective-permute-start(bf16[48,64,128]{2,1,0:T(8,128)(2,1)S(1)} %collective-permute-done.1.refs_2_), channel_id=1, source_target_pairs={{0,8},{8,0},{16,24},{24,16},{1,9},{9,1},{17,25},{25,17},{2,10},{10... | collective-permute-start | bytes 2359304 | tf_op jit(solution)/shard_map/ppermute | solution.py:251
  25.5 10.6 %collective-permute-start.3 = (bf16[1040,128]{1,0:T(8,128)(2,1)S(1)}, bf16[1040,128]{1,0:T(8,128)(2,1)S(1)}, u32[]{:S(2)}, u32[]{:S(2)}) collective-permute-start(bf16[1040,128]{1,0:T(8,128)(2,1)S(1)} %pad_maximum_fusion.refs_0_), channel_id=1, source_target_pairs={{0,6},{1,7},{2,0},{3,1},{4,2},{5,3},{6,4},{7,5},{8,14},{9,15},{10,... | collective-permute-start | bytes 798728 | tf_op jit(solution)/shard_map/ppermute | solution.py:267
  29.4 12.9 %collective-permute-start.2 = (bf16[1040,128]{1,0:T(8,128)(2,1)S(1)}, bf16[1040,128]{1,0:T(8,128)(2,1)S(1)}, u32[]{:S(2)}, u32[]{:S(2)}) collective-permute-start(bf16[1040,128]{1,0:T(8,128)(2,1)S(1)} %pad_maximum_fusion.refs_0_), channel_id=1, source_target_pairs={{0,2},{1,3},{2,4},{3,5},{4,6},{5,7},{6,0},{7,1},{8,10},{9,11},{10,... | collective-permute-start | bytes 798728 | tf_op jit(solution)/shard_map/ppermute | solution.py:267
  29.4 55.3 %collective-permute-start.8 = (bf16[48,64,128]{2,1,0:T(8,128)(2,1)}, bf16[48,64,128]{2,1,0:T(8,128)(2,1)}, u32[]{:S(2)}, u32[]{:S(2)}) collective-permute-start(bf16[48,64,128]{2,1,0:T(8,128)(2,1)} %get-tuple-element.25.refs_0_), channel_id=1, source_target_pairs={{0,8},{8,0},{16,24},{24,16},{1,9},{9,1},{17,25},{25,17},{2,10},{10... | collective-permute-start | bytes 2359304 | tf_op jit(solution)/shard_map/ppermute | solution.py:251
  42.4 19.5 %collective-permute-start.4 = (bf16[48,64,128]{2,1,0:T(8,128)(2,1)}, bf16[48,64,128]{2,1,0:T(8,128)(2,1)}, u32[]{:S(2)}, u32[]{:S(2)}) collective-permute-start(bf16[48,64,128]{2,1,0:T(8,128)(2,1)} %get-tuple-element.25.refs_0_), channel_id=1, source_target_pairs={{0,16},{8,24},{16,0},{24,8},{1,17},{9,25},{17,1},{25,9},{2,18},{10... | collective-permute-start | bytes 2359304 | tf_op jit(solution)/shard_map/ppermute | solution.py:248
  61.8 22.9 %collective-permute-start.9 = (bf16[48,64,128]{2,1,0:T(8,128)(2,1)}, bf16[48,64,128]{2,1,0:T(8,128)(2,1)}, u32[]{:S(2)}, u32[]{:S(2)}) collective-permute-start(bf16[48,64,128]{2,1,0:T(8,128)(2,1)} %collective-permute-done.4.refs_2_), channel_id=1, source_target_pairs={{0,8},{8,0},{16,24},{24,16},{1,9},{9,1},{17,25},{25,17},{2,10},{10... | collective-permute-start | bytes 2359304 | tf_op jit(solution)/shard_map/ppermute | solution.py:251
  61.8 15.4 %collective-permute-start.14 = (bf16[1040,128]{1,0:T(8,128)(2,1)S(1)}, bf16[1040,128]{1,0:T(8,128)(2,1)S(1)}, u32[]{:S(2)}, u32[]{:S(2)}) collective-permute-start(bf16[1040,128]{1,0:T(8,128)(2,1)S(1)} %pad_maximum_fusion.refs_0_), channel_id=1, source_target_pairs={{0,4},{1,5},{2,6},{3,7},{4,0},{5,1},{6,2},{7,3},{8,12},{9,13},{10,... | collective-permute-start | bytes 798728 | tf_op jit(solution)/shard_map/ppermute | solution.py:267
  62.3 53.7 %collective-permute-start.11 = (bf16[48,64,128]{2,1,0:T(8,128)(2,1)}, bf16[48,64,128]{2,1,0:T(8,128)(2,1)}, u32[]{:S(2)}, u32[]{:S(2)}) collective-permute-start(bf16[48,64,128]{2,1,0:T(8,128)(2,1)} %get-tuple-element.27.refs_0_), channel_id=1, source_target_pairs={{0,8},{8,0},{16,24},{24,16},{1,9},{9,1},{17,25},{25,17},{2,10},{10... | collective-permute-start | bytes 2359304 | tf_op jit(solution)/shard_map/ppermute | solution.py:251
  77.3 32.6 %collective-permute-start.15 = (bf16[4,1040,128]{2,1,0:T(8,128)(2,1)S(1)}, bf16[4,1040,128]{2,1,0:T(8,128)(2,1)S(1)}, u32[]{:S(2)}, u32[]{:S(2)}) collective-permute-start(bf16[4,1040,128]{2,1,0:T(8,128)(2,1)S(1)} %join.1.refs_0_), channel_id=1, source_target_pairs={{0,1},{1,0},{2,3},{3,2},{4,5},{5,4},{6,7},{7,6},{8,9},{9,8},{10,11... | collective-permute-start | bytes 3194888 | tf_op jit(solution)/shard_map/ppermute | solution.py:270
  78.9 32.2 %all-to-all-start.1 = ((bf16[8,384,128]{2,1,0:T(8,128)(2,1)}), bf16[8,384,128]{2,1,0:T(8,128)(2,1)}, u32[]{:S(2)}, u32[]{:S(2)}) async-start(bf16[8,384,128]{2,1,0:T(8,128)(2,1)} %chunk_products.4), calls=%async_computation.1 | async-start | bytes 1572864 | tf_op jit(solution)/shard_map/all_to_all | solution.py:290
  83.1 32.2 %copy-start.4 = (bf16[48,64,128]{2,1,0:T(8,128)(2,1)S(1)}, bf16[48,64,128]{2,1,0:T(8,128)(2,1)}, u32[]{:S(2)}) copy-start(bf16[48,64,128]{2,1,0:T(8,128)(2,1)} %get-tuple-element.29.refs_0_) | copy-start | bytes 2359300
  83.1 19.3 %collective-permute-start.7 = (bf16[48,64,128]{2,1,0:T(8,128)(2,1)}, bf16[48,64,128]{2,1,0:T(8,128)(2,1)}, u32[]{:S(2)}, u32[]{:S(2)}) collective-permute-start(bf16[48,64,128]{2,1,0:T(8,128)(2,1)} %get-tuple-element.27.refs_0_), channel_id=1, source_target_pairs={{0,16},{8,24},{16,0},{24,8},{1,17},{9,25},{17,1},{25,9},{2,18},{10... | collective-permute-start | bytes 2359304 | tf_op jit(solution)/shard_map/ppermute | solution.py:248
  102.4 15.1 %collective-permute-start.12 = (bf16[48,64,128]{2,1,0:T(8,128)(2,1)}, bf16[48,64,128]{2,1,0:T(8,128)(2,1)}, u32[]{:S(2)}, u32[]{:S(2)}) collective-permute-start(bf16[48,64,128]{2,1,0:T(8,128)(2,1)} %collective-permute-done.7.refs_2_), channel_id=1, source_target_pairs={{0,8},{8,0},{16,24},{24,16},{1,9},{9,1},{17,25},{25,17},{2,10},{10... | collective-permute-start | bytes 2359304 | tf_op jit(solution)/shard_map/ppermute | solution.py:251
  111.1 25.9 %all-to-all-start.2 = ((bf16[8,384,128]{2,1,0:T(8,128)(2,1)}), bf16[8,384,128]{2,1,0:T(8,128)(2,1)}, u32[]{:S(2)}, u32[]{:S(2)}) async-start(bf16[8,384,128]{2,1,0:T(8,128)(2,1)} %chunk_products.5), calls=%async_computation.2 | async-start | bytes 1572864 | tf_op jit(solution)/shard_map/all_to_all | solution.py:290
  115.3 27.5 %collective-permute-start = (bf16[48,64,128]{2,1,0:T(8,128)(2,1)S(1)}, bf16[48,64,128]{2,1,0:T(8,128)(2,1)}, u32[]{:S(2)}, u32[]{:S(2)}) collective-permute-start(bf16[48,64,128]{2,1,0:T(8,128)(2,1)S(1)} %copy-done.4), channel_id=1, source_target_pairs={{0,8},{8,0},{16,24},{24,16},{1,9},{9,1},{17,25},{25,17},{2,10},{10... | collective-permute-start | bytes 2359304 | tf_op jit(solution)/shard_map/ppermute | solution.py:251
  115.4 20.6 %collective-permute-start.16 = (bf16[4,1040,128]{2,1,0:T(8,128)(2,1)S(1)}, bf16[4,1040,128]{2,1,0:T(8,128)(2,1)S(1)}, u32[]{:S(2)}, u32[]{:S(2)}) collective-permute-start(bf16[4,1040,128]{2,1,0:T(8,128)(2,1)S(1)} %join.1.refs_0_), channel_id=1, source_target_pairs={{0,8},{8,0},{16,24},{24,16},{1,9},{9,1},{17,25},{25,17},{2,10},{10... | collective-permute-start | bytes 3194888 | tf_op jit(solution)/shard_map/ppermute | solution.py:251
  115.9 21.1 %collective-permute-start.17 = (bf16[4,1040,128]{2,1,0:T(8,128)(2,1)S(1)}, bf16[4,1040,128]{2,1,0:T(8,128)(2,1)}, u32[]{:S(2)}, u32[]{:S(2)}) collective-permute-start(bf16[4,1040,128]{2,1,0:T(8,128)(2,1)S(1)} %collective-permute-done.15.refs_1_), channel_id=1, source_target_pairs={{0,8},{8,0},{16,24},{24,16},{1,9},{9,1},{17,25},{25,17},{2,10},{10... | collective-permute-start | bytes 3194888 | tf_op jit(solution)/shard_map/ppermute | solution.py:251
  116.0 20.0 %collective-permute-start.10 = (bf16[48,64,128]{2,1,0:T(8,128)(2,1)S(1)}, bf16[48,64,128]{2,1,0:T(8,128)(2,1)}, u32[]{:S(2)}, u32[]{:S(2)}) collective-permute-start(bf16[48,64,128]{2,1,0:T(8,128)(2,1)S(1)} %copy-done.4), channel_id=1, source_target_pairs={{0,16},{8,24},{16,0},{24,8},{1,17},{9,25},{17,1},{25,9},{2,18},{10... | collective-permute-start | bytes 2359304 | tf_op jit(solution)/shard_map/ppermute | solution.py:248
  136.0 6.8 %collective-permute-start.13 = (bf16[48,64,128]{2,1,0:T(8,128)(2,1)}, bf16[48,64,128]{2,1,0:T(8,128)(2,1)}, u32[]{:S(2)}, u32[]{:S(2)}) collective-permute-start(bf16[48,64,128]{2,1,0:T(8,128)(2,1)} %collective-permute-done.10.refs_2_), channel_id=1, source_target_pairs={{0,8},{8,0},{16,24},{24,16},{1,9},{9,1},{17,25},{25,17},{2,10},{10... | collective-permute-start | bytes 2359304 | tf_op jit(solution)/shard_map/ppermute | solution.py:251
  136.9 26.8 %all-to-all-start.3 = ((bf16[8,384,128]{2,1,0:T(8,128)(2,1)}), bf16[8,384,128]{2,1,0:T(8,128)(2,1)}, u32[]{:S(2)}, u32[]{:S(2)}) async-start(bf16[8,384,128]{2,1,0:T(8,128)(2,1)} %chunk_products.6), calls=%async_computation.3 | async-start | bytes 1572864 | tf_op jit(solution)/shard_map/all_to_all | solution.py:290
  163.7 26.2 %all-to-all-start = ((bf16[8,384,128]{2,1,0:T(8,128)(2,1)}), bf16[8,384,128]{2,1,0:T(8,128)(2,1)S(1)}, u32[]{:S(2)}, u32[]{:S(2)}) async-start(bf16[8,384,128]{2,1,0:T(8,128)(2,1)} %chunk_products.7), calls=%async_computation | async-start | bytes 1572864 | tf_op jit(solution)/shard_map/all_to_all | solution.py:290
  (8 other events, 59.3 us)

commit v4 on v3

v4 whole, which is shorter than its diff:
```python
import functools

import jax
import jax.numpy as jnp
from jax import lax
from jax.experimental import pallas as pl
from jax.experimental.pallas import tpu as pltpu
from jax.sharding import PartitionSpec as P

VMEM_LIMIT = 40 * 1024 * 1024
VMEM_WHOLE = 58 * 1024 * 1024


def largest_divisor(total, most):
    return max(size for size in range(1, most + 1) if total % size == 0)


def pack_kernel(width, first, source, *chunks):
    half = source.shape[1] // 2
    for at, chunk in enumerate(chunks):
        columns = slice(first + at * width, first + (at + 1) * width)
        chunk[...] = jnp.concatenate([source[:, :half, columns], source[:, half:, columns]], axis=-1)


def pack_chunks(factors, width, begin, count, cost):
    orbitals, domain, part = factors.shape
    first = begin * width
    step = largest_divisor(orbitals, 12)
    packed = (step, domain // 2, 2 * width)
    return pl.pallas_call(
        functools.partial(pack_kernel, width, first),
        grid=(orbitals // step,),
        in_specs=[pl.BlockSpec((step, domain, part), lambda i: (i, 0, 0))],
        out_specs=[pl.BlockSpec(packed, lambda i: (i, 0, 0))] * count,
        out_shape=[jax.ShapeDtypeStruct((orbitals,) + packed[1:], factors.dtype)] * count,
        cost_estimate=pl.CostEstimate(flops=0, bytes_accessed=cost * factors.size, transcendentals=0),
        compiler_params=pltpu.CompilerParams(vmem_limit_bytes=VMEM_WHOLE),
        name="pack_chunks",
    )(factors)


def halves_apart(one, two, half):
    lower = jnp.concatenate([one[:, :half], two[:, :half]], axis=1)
    upper = jnp.concatenate([one[:, half:], two[:, half:]], axis=1)
    return lower, upper


def product_kernel(pairs, split_rows, streams, slots, *refs):
    amplitudes, pieces = refs[: 2 * streams], refs[2 * streams : -3]
    out, table, arrived = refs[-3:]
    group, half_domain, lanes = pieces[0].shape
    here = pl.program_id(0)

    @pl.when(here == 0)
    def _():
        copies = [
            pltpu.make_async_copy(piece, table.at[pl.ds(at * group, group)], arrived.at[at])
            for at, piece in enumerate(pieces)
        ]
        for copy in copies:
            copy.start()
        for copy in copies:
            copy.wait()

    step, domain = amplitudes[0].shape[1], amplitudes[0].shape[3]
    each = pairs // streams
    half_count = pl.num_programs(0) * step
    first = lax.broadcasted_iota(jnp.int32, (domain, lanes), 1) < lanes // 2
    for q in range(step):
        sums = []
        for side in range(2):
            base = (side * half_count + here * step + q) * pairs
            lower, upper = [], []
            for k in range(0, pairs, 2):
                tiles = amplitudes[side * streams + k // each]
                low, high = halves_apart(tiles[0, q, k % each], tiles[0, q, k % each + 1], half_domain)
                lower.append(low)
                upper.append(high)
            left = jnp.concatenate([jnp.concatenate(lower, axis=1), jnp.concatenate(upper, axis=1)], axis=0)
            right = jnp.concatenate([table[slots[base + k]] for k in range(pairs)], axis=0)
            sums.append(jnp.dot(left, right, preferred_element_type=jnp.float32))
        placed = jnp.where(first, sums[0][:domain], sums[1][domain:])
        moved = jnp.where(first, sums[1][:domain], sums[0][domain:])
        both = (placed + pltpu.roll(moved, lanes // 2, 1)).astype(out.dtype)
        if split_rows:
            owners, rows = out.shape[0], domain // out.shape[0]
            out[:, q * rows : (q + 1) * rows, :] = both.reshape(owners, rows, lanes)
        else:
            out[q] = both


def chunk_products(slots, amplitudes, pieces, owners):
    orbitals, pairs, domain, _ = amplitudes.shape
    group, half_domain, lanes = pieces[0].shape
    total = group * len(pieces)
    half = orbitals // 2
    rows = domain // owners
    split_rows = rows % 16 == 0
    step = largest_divisor(half, 4)
    streams = 2 if pairs % 4 == 0 else 1
    tiles = (1, step, pairs // streams, domain, domain)
    if split_rows:
        out_shape, out_block, out_at = (owners, half * rows, lanes), (owners, step * rows, lanes), lambda i, s: (0, i, 0)
    else:
        out_shape, out_block, out_at = (half, domain, lanes), (step, domain, lanes), lambda i, s: (i, 0, 0)
    result = pl.pallas_call(
        functools.partial(product_kernel, pairs, split_rows, streams),
        grid_spec=pltpu.PrefetchScalarGridSpec(
            num_scalar_prefetch=1,
            grid=(half // step,),
            in_specs=[
                pl.BlockSpec(tiles, lambda i, s, side=side, part=part: (side, i, part, 0, 0))
                for side in range(2)
                for part in range(streams)
            ]
            + [pl.BlockSpec(memory_space=pl.ANY)] * len(pieces),
            out_specs=pl.BlockSpec(out_block, out_at),
            scratch_shapes=[
                pltpu.VMEM((total, half_domain, lanes), jnp.bfloat16),
                pltpu.SemaphoreType.DMA((len(pieces),)),
            ],
        ),
        out_shape=jax.ShapeDtypeStruct(out_shape, jnp.bfloat16),
        cost_estimate=pl.CostEstimate(
            flops=8 * amplitudes.size * lanes,
            bytes_accessed=2 * amplitudes.size + 2 * total * half_domain * lanes,
            transcendentals=0,
        ),
        compiler_params=pltpu.CompilerParams(vmem_limit_bytes=VMEM_LIMIT),
        name="chunk_products",
    )(slots, *[amplitudes.reshape(2, half, pairs, domain, domain)] * (2 * streams), *pieces)
    if split_rows:
        return result
    result = result.reshape(half, owners, rows, lanes).transpose(1, 0, 2, 3)
    return result.reshape(owners, half * rows, lanes)


def join_kernel(*refs):
    for at, piece in enumerate(refs[:-1]):
        refs[-1][at] = piece[...]


def join(pieces):
    shape = (len(pieces),) + pieces[0].shape
    return pl.pallas_call(
        join_kernel,
        out_shape=jax.ShapeDtypeStruct(shape, pieces[0].dtype),
        cost_estimate=pl.CostEstimate(flops=0, bytes_accessed=4 * len(pieces) * pieces[0].size, transcendentals=0),
        compiler_params=pltpu.CompilerParams(vmem_limit_bytes=VMEM_LIMIT),
        name="join",
    )(*pieces)


def place_tiles(chunks, owners, tiles_each, positions, sources, dense):
    devices, _, span = sources[0].shape
    width = span // 2
    dense[...] = jnp.zeros_like(dense)
    for which, source in enumerate(sources):

        @pl.loop(0, devices)
        def _(device):
            for at in range(tiles_each):
                number = (which * devices + device) * tiles_each + at
                column = pl.multiple_of(positions[2 * number + 1] * span, span)
                for side in range(2):
                    block = 2 * positions[2 * number] + side
                    row = ((block % chunks) * owners + block // chunks) * width
                    begin = at * span + side * width
                    dense[pl.ds(pl.multiple_of(row, width), width), pl.ds(column, span)] = source[
                        device, begin : begin + width, :
                    ]


def unpack_rows(chunks, rows):
    owners, height, lanes = chunks[0].shape
    width = lanes // 2
    for at, chunk in enumerate(chunks):
        for owner in range(0, owners, 2):
            one, two = chunk[owner], chunk[owner + 1]
            columns = pl.ds((at * owners + owner) * width, lanes)
            rows[:height, columns] = jnp.concatenate([one[:, :width], two[:, :width]], axis=1)
            rows[height:, columns] = jnp.concatenate([one[:, width:], two[:, width:]], axis=1)


def first_kernel(count, source_count, tiles_each, positions, *refs):
    chunks, sources = refs[:count], refs[count : count + source_count]
    *outs, dense, rows = refs[count + source_count :]
    owners, height, _ = chunks[0].shape
    depth = rows.shape[1]

    @pl.when(pl.program_id(0) == 0)
    def _():
        place_tiles(dense.shape[0] // (depth // count), owners, tiles_each, positions, sources, dense)
        unpack_rows(chunks, rows)

    step = outs[0].shape[-1]
    columns = pl.ds(pl.multiple_of(pl.program_id(0) * step, step), step)
    if len(outs) > 2:
        outs[2][...] = dense[depth:, columns]
    for side in range(2):
        part = rows[side * height : (side + 1) * height]
        sums = jnp.dot(part, dense[:depth, columns], preferred_element_type=jnp.float32)
        outs[side][...] = sums.astype(outs[side].dtype)


def first_shares(chunks, positions, sources, tiles_each, size, dtype):
    owners, height, lanes = chunks[0].shape
    depth = len(chunks) * owners * lanes // 2
    step = largest_divisor(size, 256)
    whole = lambda j, s: (0, 0, 0)
    heights = [height] * 2 + ([size - depth] if depth < size else [])
    kinds = [dtype] * 2 + [sources[0].dtype]
    return pl.pallas_call(
        functools.partial(first_kernel, len(chunks), len(sources), tiles_each),
        grid_spec=pltpu.PrefetchScalarGridSpec(
            num_scalar_prefetch=1,
            grid=(size // step,),
            in_specs=[pl.BlockSpec(array.shape, whole) for array in [*chunks, *sources]],
            out_specs=[pl.BlockSpec((tall, step), lambda j, s: (0, j)) for tall in heights],
            scratch_shapes=[
                pltpu.VMEM((size, size), sources[0].dtype),
                pltpu.VMEM((2 * height, depth), jnp.bfloat16),
            ],
        ),
        out_shape=[jax.ShapeDtypeStruct((tall, size), kind) for tall, kind in zip(heights, kinds)],
        cost_estimate=pl.CostEstimate(
            flops=4 * height * depth * size,
            bytes_accessed=2 * depth * size + 8 * height * size,
            transcendentals=0,
        ),
        compiler_params=pltpu.CompilerParams(vmem_limit_bytes=VMEM_WHOLE),
        name="first_shares",
    )(positions, *chunks, *sources)


def last_kernel(chunk, metric, one, two, out, rows):
    height = chunk.shape[1]

    @pl.when(pl.program_id(0) == 0)
    def _():
        unpack_rows([chunk], rows)

    for side, before in enumerate((one, two)):
        part = rows[side * height : (side + 1) * height]
        sums = jnp.dot(part, metric[...], preferred_element_type=jnp.float32)
        out[side] = (sums + before[...]).astype(out.dtype)


def last_share(chunk, metric, one, two):
    owners, height, lanes = chunk.shape
    depth, size = metric.shape
    step = largest_divisor(size, 256)
    tall = pl.BlockSpec((height, step), lambda j: (0, j))
    return pl.pallas_call(
        last_kernel,
        grid=(size // step,),
        in_specs=[
            pl.BlockSpec(chunk.shape, lambda j: (0, 0, 0)),
            pl.BlockSpec((depth, step), lambda j: (0, j)),
            tall,
            tall,
        ],
        out_specs=pl.BlockSpec((2, height, step), lambda j: (0, 0, j)),
        out_shape=jax.ShapeDtypeStruct((2, height, size), jnp.bfloat16),
        scratch_shapes=[pltpu.VMEM((2 * height, depth), jnp.bfloat16)],
        cost_estimate=pl.CostEstimate(
            flops=4 * height * depth * size,
            bytes_accessed=2 * depth * size + 12 * height * size,
            transcendentals=0,
        ),
        compiler_params=pltpu.CompilerParams(vmem_limit_bytes=VMEM_WHOLE),
        name="last_share",
    )(chunk, metric, one, two)


def after(value, others):
    return lax.optimization_barrier((value, others))[0]


def shards(orb_count, aux_count, factors, amplitudes, partners, metric_tiles, tile_pos):
    group, domain, part = factors.shape
    span = metric_tiles.shape[1]
    width = span // 2
    chunk_count = part // width
    far_count = orb_count // 2
    me = lax.axis_index("orb")

    def to_far(array, shift):
        moves = [(g, (g + 2 * shift) % orb_count) for g in range(orb_count)]
        return lax.ppermute(array, "orb", moves)

    def to_mate(array):
        return lax.ppermute(array, "orb", [(g, g ^ 1) for g in range(orb_count)])

    owner, place = partners // group, partners % group
    far = (me // 2 - owner // 2) % far_count
    slots = ((far * 2 + (me % 2 + owner) % 2) * group + place).reshape(-1)

    half_tiles = metric_tiles.shape[0] // 2
    mine = (me % 2) * half_tiles
    tiles = lax.dynamic_slice_in_dim(metric_tiles, mine, half_tiles, axis=0).reshape(half_tiles * span, span)
    spots = lax.dynamic_slice_in_dim(tile_pos, mine, half_tiles, axis=0).reshape(-1).astype(tiles.dtype)
    spot_rows = -(-spots.size // (16 * span)) * 16
    spots = jnp.pad(spots, (0, spot_rows * span - spots.size)).reshape(spot_rows, span)
    load = jnp.concatenate([tiles, spots], axis=0)
    parts = [load]
    for shift in range(1, aux_count // 2):
        moves = [(g, (g + 2 * shift) % aux_count) for g in range(aux_count)]
        parts.append(lax.ppermute(load, "aux", moves))

    packed = list(pack_chunks(factors, width, 0, 1, 2))
    if chunk_count > 1:
        packed += pack_chunks(factors, width, 1, chunk_count - 1, 40)
        parts = after(parts, packed[1:])

    column = join(parts)
    beside = lax.ppermute(column, "aux", [(g, g ^ 1) for g in range(aux_count)])
    sources = [column, beside, to_mate(column), to_mate(beside)]

    before_far = {1: parts}
    before_products = {1: beside, 2: sources[2:]}
    products = []
    far_pieces, made = [], None
    for at in range(chunk_count):
        own = packed[at]
        if at:
            own = after(own, [far_pieces, before_far.get(at, [])])
        far_pieces = [to_far(own, shift) for shift in range(1, far_count)]
        if chunk_count > 1:
            far_pieces = after(far_pieces, made if at else packed[1:])
        pieces = []
        for piece in [packed[at]] + far_pieces:
            pieces += [piece, to_mate(piece)]
        places = after(slots, before_products[at]) if at in before_products else slots
        made = chunk_products(places, amplitudes, pieces, aux_count)
        products.append(lax.all_to_all(made, "aux", split_axis=0, concat_axis=0, tiled=True))

    positions = jnp.concatenate([source[:, half_tiles * span, : 2 * half_tiles] for source in sources])
    positions = positions.astype(jnp.int32).reshape(-1)
    size = part * aux_count
    if chunk_count > 1:
        ready = after(products[:-1], made)
        one, two, metric = first_shares(ready, positions, sources, half_tiles, size, jnp.float32)
        result = last_share(products[-1], metric, one, two)
    else:
        result = jnp.stack(first_shares(products, positions, sources, half_tiles, size, jnp.bfloat16))
    return result.reshape(group, domain // aux_count, size)


def solution(mesh):
    in_specs = (
        P("orb", None, "aux"),
        P("orb", None, None, None),
        P("orb", None),
        P("aux", None, None),
        P("aux", None),
    )
    body = functools.partial(shards, mesh.shape["orb"], mesh.shape["aux"])
    return jax.shard_map(body, mesh=mesh, in_specs=in_specs, out_specs=P("orb", "aux", None), check_vma=False)
```

time: 201 us -> 194 us (0.965)
  waiting for transfers between devices: 72.1 us -> 63.3 us
  Pallas kernels: 84.3 us -> 86.5 us
    ppermute x3, waiting for transfers between devices: 27.2 us -> 21.4 us  [shards(): parts.append(lax.ppermute(load, 'aux', moves))]
    ppermute x1, waiting for transfers between devices: 7.51 us -> 4.03 us  [shards(): beside = lax.ppermute(column, 'aux', [(g, g ^ 1) for g in range(aux_count)])]
    all_to_all x4, waiting for transfers between devices: 8.43 us -> 11.6 us  [shards(): lax.all_to_all(made, 'aux', split_axis=0, concat_axis=0, tiled=True)]
    ppermute x4, waiting for transfers between devices: 28.9 us -> 26.3 us  [to_far(): return lax.ppermute(array, 'orb', moves)]
    pallas_call x8, Pallas kernels: 84.2 us -> 86.4 us  [the longest x4 53.7 us: chunk_products(): pl.pallas_call(functools.partial(product_kernel, pairs, split_rows, strea...]
    unnamed x24 -> x36, local copies, waits for them, and re-layouts: 8.69 us -> 7.09 us
  transfers between devices with their start and end apart: 22 -> 22, of which waited for: 10 -> 11; matrix products, arithmetic and copies ran while one was open for 1% -> 2% of each run, Pallas kernels for 35% -> 38%
where the time goes in v4:
time: 194 us; the launch traced here: 193 us
  Pallas kernels  86.5 us (45%)
  waiting for transfers between devices  63.3 us (33%)
  starting transfers between devices  32.6 us (17%)
  local copies, waits for them, and re-layouts  10.2 us (5%)
    pallas_call x4, Pallas kernels, chunk_products(): pl.pallas_call(functools.partial(product_kernel, pairs, split_rows, strea...  53.7 us
    ppermute x4, waiting for transfers between devices, to_far(): return lax.ppermute(array, 'orb', moves)  26.3 us
    ppermute x3, waiting for transfers between devices, shards(): parts.append(lax.ppermute(load, 'aux', moves))  21.4 us
    all_to_all x4, starting transfers between devices, shards(): lax.all_to_all(made, 'aux', split_axis=0, concat_axis=0, tiled=True)  17.7 us
    pallas_call x1, Pallas kernels, first_shares(): pl.pallas_call(functools.partial(first_kernel, len(chunks), len(sources),...  15.4 us
    all_to_all x4, waiting for transfers between devices, shards(): lax.all_to_all(made, 'aux', split_axis=0, concat_axis=0, tiled=True)  11.6 us
    pallas_call x1, Pallas kernels, last_share(): pl.pallas_call(last_kernel, grid=(size // step,), in_specs=[pl.BlockSpec(...  9.04 us
    pallas_call x2, Pallas kernels, pack_chunks(): pl.pallas_call(functools.partial(pack_kernel, width, first), grid=(orbita...  8.26 us
  transfers between devices with their start and end apart: 22, of which 11 were waited for; matrix products, arithmetic and copies ran while one was open for 2% of the time, Pallas kernels for 38%

profile of v4, /device:TPU:0, one launch (start us, length us, event | category | flops | bytes accessed | tf_op | source)
XLA Modules:
  0.0 193.0 jit_solution(7853986893671716388)
XLA Ops:
  0.0 4.0 %pack_chunks.3.refs_4_ = bf16[48,64,128]{2,1,0:T(8,128)(2,1)} custom-call(bf16[48,128,256]{2,1,0:T(8,128)(2,1)} %source.3), custom_call_target="tpu_custom_call" | custom-call | bytes 3145728 | tf_op jit(solution)/shard_map/pack_chunks/pallas_call | solution.py:30
  4.0 3.0 %collective-permute-start.1 = (bf16[48,64,128]{2,1,0:T(8,128)(2,1)}, bf16[48,64,128]{2,1,0:T(8,128)(2,1)S(1)}, u32[]{:S(2)}, u32[]{:S(2)}) collective-permute-start(bf16[48,64,128]{2,1,0:T(8,128)(2,1)} %pack_chunks.3.refs_4_), channel_id=1, source_target_pairs={{0,16},{8,24},{16,0},{24,8},{1,17},{9,25},{17,1},{25,9},{2,18},{10... | collective-permute-start | bytes 2359304 | tf_op jit(solution)/shard_map/ppermute | solution.py:290
  7.0 4.3 %pack_chunks.2 = (bf16[48,64,128]{2,1,0:T(8,128)(2,1)}, bf16[48,64,128]{2,1,0:T(8,128)(2,1)}, bf16[48,64,128]{2,1,0:T(8,128)(2,1)}) custom-call(bf16[48,128,256]{2,1,0:T(8,128)(2,1)} %source.3), custom_call_target="tpu_custom_call" | custom-call | bytes 62914560 | tf_op jit(solution)/shard_map/pack_chunks/pallas_call | solution.py:30
  11.2 13.5 %collective-permute-done.1.refs_6_ = bf16[48,64,128]{2,1,0:T(8,128)(2,1)S(1)} collective-permute-done((bf16[48,64,128]{2,1,0:T(8,128)(2,1)}, bf16[48,64,128]{2,1,0:T(8,128)(2,1)S(1)}, u32[]{:S(2)}, u32[]{:S(2)}) %collective-permute-start.1) | collective-permute-done | bytes 786464 | tf_op jit(solution)/shard_map/ppermute | solution.py:290
  25.1 3.9 %collective-permute-start.4 = (bf16[1040,128]{1,0:T(8,128)(2,1)S(1)}, bf16[1040,128]{1,0:T(8,128)(2,1)S(1)}, u32[]{:S(2)}, u32[]{:S(2)}) collective-permute-start(bf16[1040,128]{1,0:T(8,128)(2,1)S(1)} %pad_maximum_fusion.refs_0_), channel_id=1, source_target_pairs={{0,6},{1,7},{2,0},{3,1},{4,2},{5,3},{6,4},{7,5},{8,14},{9,15},{10,... | collective-permute-start | bytes 798728 | tf_op jit(solution)/shard_map/ppermute | solution.py:309
  30.2 5.5 %collective-permute-done.4.refs_3_ = bf16[1040,128]{1,0:T(8,128)(2,1)S(1)} collective-permute-done((bf16[1040,128]{1,0:T(8,128)(2,1)S(1)}, bf16[1040,128]{1,0:T(8,128)(2,1)S(1)}, u32[]{:S(2)}, u32[]{:S(2)}) %collective-permute-start.4) | collective-permute-done | bytes 266272 | tf_op jit(solution)/shard_map/ppermute | solution.py:309
  36.5 15.8 %collective-permute-done.3.refs_2_ = bf16[1040,128]{1,0:T(8,128)(2,1)S(1)} collective-permute-done((bf16[1040,128]{1,0:T(8,128)(2,1)S(1)}, bf16[1040,128]{1,0:T(8,128)(2,1)S(1)}, u32[]{:S(2)}, u32[]{:S(2)}) %collective-permute-start.3) | collective-permute-done | bytes 266272 | tf_op jit(solution)/shard_map/ppermute | solution.py:309
  60.9 13.2 %chunk_products.4 = bf16[8,384,128]{2,1,0:T(8,128)(2,1)} custom-call(s32[576]{0:T(1024)S(1)} %reshape.24.slots, bf16[2,24,12,128,128]{4,3,2,1,0:T(8,128)(2,1)} %bitcast.17, bf16[2,24,12,128,128]{4,3,2,1,0:T(8,128)(2,1)} %bitcast.18, bf16[2,24,12,128,128]{4,3,2,1,0:T(8,128)(2,1)} %bitcast.19, bf16[2,24,12,128,128]{4,3,2,1,0:T(8,128)(2,1)} %bitcast.20, ...), custom_call_target="tpu_custom_call" | custom-call | flops 9663676416 | bytes 22020096 | tf_op jit(solution)/shard_map/chunk_products/pallas_call | solution.py:106
  74.1 3.3 %collective-permute-done.5.refs_6_ = bf16[48,64,128]{2,1,0:T(8,128)(2,1)} collective-permute-done((bf16[48,64,128]{2,1,0:T(8,128)(2,1)}, bf16[48,64,128]{2,1,0:T(8,128)(2,1)}, u32[]{:S(2)}, u32[]{:S(2)}) %collective-permute-start.5) | collective-permute-done | bytes 786464 | tf_op jit(solution)/shard_map/ppermute | solution.py:290
  77.9 4.0 %collective-permute-done.9.refs_4_ = bf16[4,1040,128]{2,1,0:T(8,128)(2,1)} collective-permute-done((bf16[4,1040,128]{2,1,0:T(8,128)(2,1)S(1)}, bf16[4,1040,128]{2,1,0:T(8,128)(2,1)}, u32[]{:S(2)}, u32[]{:S(2)}) %collective-permute-start.9) | collective-permute-done | bytes 1064992 | tf_op jit(solution)/shard_map/ppermute | solution.py:317
  82.0 4.2 %all-to-all-start.1 = ((bf16[8,384,128]{2,1,0:T(8,128)(2,1)}), bf16[8,384,128]{2,1,0:T(8,128)(2,1)}, u32[]{:S(2)}, u32[]{:S(2)}) async-start(bf16[8,384,128]{2,1,0:T(8,128)(2,1)} %chunk_products.4), calls=%async_computation.1 | async-start | bytes 1572864 | tf_op jit(solution)/shard_map/all_to_all | solution.py:336
  86.2 1.6 collective-permute-start.8
  87.8 13.7 %chunk_products.5 = bf16[8,384,128]{2,1,0:T(8,128)(2,1)} custom-call(s32[576]{0:T(1024)S(1)} %reshape.24.slots, bf16[2,24,12,128,128]{4,3,2,1,0:T(8,128)(2,1)} %bitcast.21, bf16[2,24,12,128,128]{4,3,2,1,0:T(8,128)(2,1)} %bitcast.22, bf16[2,24,12,128,128]{4,3,2,1,0:T(8,128)(2,1)} %bitcast.23, bf16[2,24,12,128,128]{4,3,2,1,0:T(8,128)(2,1)} %bitcast.24, ...), custom_call_target="tpu_custom_call" | custom-call | flops 9663676416 | bytes 22020096 | tf_op jit(solution)/shard_map/chunk_products/pallas_call | solution.py:106
  101.5 4.8 %collective-permute-done.8.refs_6_ = bf16[48,64,128]{2,1,0:T(8,128)(2,1)} collective-permute-done((bf16[48,64,128]{2,1,0:T(8,128)(2,1)S(1)}, bf16[48,64,128]{2,1,0:T(8,128)(2,1)}, u32[]{:S(2)}, u32[]{:S(2)}) %collective-permute-start.8) | collective-permute-done | bytes 786464 | tf_op jit(solution)/shard_map/ppermute | solution.py:290
  107.3 4.7 %all-to-all-start.2 = ((bf16[8,384,128]{2,1,0:T(8,128)(2,1)}), bf16[8,384,128]{2,1,0:T(8,128)(2,1)}, u32[]{:S(2)}, u32[]{:S(2)}) async-start(bf16[8,384,128]{2,1,0:T(8,128)(2,1)} %chunk_products.5), calls=%async_computation.2 | async-start | bytes 1572864 | tf_op jit(solution)/shard_map/all_to_all | solution.py:336
  113.8 13.5 %chunk_products.6 = bf16[8,384,128]{2,1,0:T(8,128)(2,1)} custom-call(s32[576]{0:T(1024)S(1)} %reshape.24.slots, bf16[2,24,12,128,128]{4,3,2,1,0:T(8,128)(2,1)} %bitcast.25, bf16[2,24,12,128,128]{4,3,2,1,0:T(8,128)(2,1)} %bitcast.26, bf16[2,24,12,128,128]{4,3,2,1,0:T(8,128)(2,1)} %bitcast.27, bf16[2,24,12,128,128]{4,3,2,1,0:T(8,128)(2,1)} %bitcast.28, ...), custom_call_target="tpu_custom_call" | custom-call | flops 9663676416 | bytes 22020096 | tf_op jit(solution)/shard_map/chunk_products/pallas_call | solution.py:106
  127.3 4.8 %collective-permute-done.12.refs_6_ = bf16[48,64,128]{2,1,0:T(8,128)(2,1)} collective-permute-done((bf16[48,64,128]{2,1,0:T(8,128)(2,1)S(1)}, bf16[48,64,128]{2,1,0:T(8,128)(2,1)}, u32[]{:S(2)}, u32[]{:S(2)}) %collective-permute-start.12) | collective-permute-done | bytes 786464 | tf_op jit(solution)/shard_map/ppermute | solution.py:290
  132.9 5.2 %all-to-all-start.3 = ((bf16[8,384,128]{2,1,0:T(8,128)(2,1)}), bf16[8,384,128]{2,1,0:T(8,128)(2,1)}, u32[]{:S(2)}, u32[]{:S(2)}) async-start(bf16[8,384,128]{2,1,0:T(8,128)(2,1)} %chunk_products.6), calls=%async_computation.3 | async-start | bytes 1572864 | tf_op jit(solution)/shard_map/all_to_all | solution.py:336
  138.1 13.3 %chunk_products.7 = bf16[8,384,128]{2,1,0:T(8,128)(2,1)} custom-call(s32[576]{0:T(1024)S(1)} %reshape.24.slots, bf16[2,24,12,128,128]{4,3,2,1,0:T(8,128)(2,1)} %bitcast.29, bf16[2,24,12,128,128]{4,3,2,1,0:T(8,128)(2,1)} %bitcast.30, bf16[2,24,12,128,128]{4,3,2,1,0:T(8,128)(2,1)} %bitcast.31, bf16[2,24,12,128,128]{4,3,2,1,0:T(8,128)(2,1)} %bitcast.32, ...), custom_call_target="tpu_custom_call" | custom-call | flops 9663676416 | bytes 22020096 | tf_op jit(solution)/shard_map/chunk_products/pallas_call | solution.py:106
  151.3 7.6 %all-to-all-done.3.refs_2_ = bf16[8,384,128]{2,1,0:T(8,128)(2,1)} async-done(((bf16[8,384,128]{2,1,0:T(8,128)(2,1)}), bf16[8,384,128]{2,1,0:T(8,128)(2,1)}, u32[]{:S(2)}, u32[]{:S(2)}) %all-to-all-start.3) | async-done | bytes 786464 | tf_op jit(solution)/shard_map/all_to_all | solution.py:336
  159.0 3.6 %all-to-all-start = ((bf16[8,384,128]{2,1,0:T(8,128)(2,1)}), bf16[8,384,128]{2,1,0:T(8,128)(2,1)S(1)}, u32[]{:S(2)}, u32[]{:S(2)}) async-start(bf16[8,384,128]{2,1,0:T(8,128)(2,1)} %chunk_products.7), calls=%async_computation | async-start | bytes 1572864 | tf_op jit(solution)/shard_map/all_to_all | solution.py:336
  165.4 15.4 %first_shares.1 = (f32[384,2048]{1,0:T(8,128)}, f32[384,2048]{1,0:T(8,128)}, bf16[512,2048]{1,0:T(8,128)(2,1)}) custom-call(s32[256]{0:T(256)} %reshape.29.positions, bf16[8,384,128]{2,1,0:T(8,128)(2,1)} %all-to-all-done.1.refs_0_, bf16[8,384,128]{2,1,0:T(8,128)(2,1)} %all-to-all-done.2.refs_1_, bf16[8,384,128]{2,1,0:T(8,128)(2,1)} %all-to-all-done.3.refs_2_, ...), custom_call_target="tpu_custom_call" | custom-call | flops 4831838208 | bytes 12582912 | tf_op jit(solution)/shard_map/first_shares/pallas_call | solution.py:213
  180.8 2.2 %all-to-all-done.chunk = bf16[8,384,128]{2,1,0:T(8,128)(2,1)S(1)} async-done(((bf16[8,384,128]{2,1,0:T(8,128)(2,1)}), bf16[8,384,128]{2,1,0:T(8,128)(2,1)S(1)}, u32[]{:S(2)}, u32[]{:S(2)}) %all-to-all-start) | async-done | bytes 786464 | tf_op jit(solution)/shard_map/all_to_all | solution.py:336
  183.9 9.0 %last_share.1 = bf16[2,384,2048]{2,1,0:T(8,128)(2,1)} custom-call(bf16[8,384,128]{2,1,0:T(8,128)(2,1)} %copy-done.13, bf16[512,2048]{1,0:T(8,128)(2,1)} %get-tuple-element.46.metric, f32[384,2048]{1,0:T(8,128)} %get-tuple-element.47.one, f32[384,2048]{1,0:T(8,128)} %get-tuple-element.48.two), custom_call_target="tpu_custom_call" | custom-call | flops 1610612736 | bytes 11534336 | tf_op jit(solution)/shard_map/last_share/pallas_call | solution.py:254
  (80 shorter events, 18.7 us)
Async XLA Ops:
  4.0 20.7 %collective-permute-start.1 = (bf16[48,64,128]{2,1,0:T(8,128)(2,1)}, bf16[48,64,128]{2,1,0:T(8,128)(2,1)S(1)}, u32[]{:S(2)}, u32[]{:S(2)}) collective-permute-start(bf16[48,64,128]{2,1,0:T(8,128)(2,1)} %pack_chunks.3.refs_4_), channel_id=1, source_target_pairs={{0,16},{8,24},{16,0},{24,8},{1,17},{9,25},{17,1},{25,9},{2,18},{10... | collective-permute-start | bytes 2359304 | tf_op jit(solution)/shard_map/ppermute | solution.py:290
  7.0 52.8 %collective-permute-start.6 = (bf16[48,64,128]{2,1,0:T(8,128)(2,1)}, bf16[48,64,128]{2,1,0:T(8,128)(2,1)}, u32[]{:S(2)}, u32[]{:S(2)}) collective-permute-start(bf16[48,64,128]{2,1,0:T(8,128)(2,1)} %pack_chunks.3.refs_4_), channel_id=1, source_target_pairs={{0,8},{8,0},{16,24},{24,16},{1,9},{9,1},{17,25},{25,17},{2,10},{10... | collective-permute-start | bytes 2359304 | tf_op jit(solution)/shard_map/ppermute | solution.py:293
  7.0 52.8 %copy-start.1 = (bf16[48,64,128]{2,1,0:T(8,128)(2,1)S(1)}, bf16[48,64,128]{2,1,0:T(8,128)(2,1)}, u32[]{:S(2)}) copy-start(bf16[48,64,128]{2,1,0:T(8,128)(2,1)} %pack_chunks.3.refs_4_) | copy-start | bytes 2359300
  24.7 35.0 %collective-permute-start.7 = (bf16[48,64,128]{2,1,0:T(8,128)(2,1)S(1)}, bf16[48,64,128]{2,1,0:T(8,128)(2,1)}, u32[]{:S(2)}, u32[]{:S(2)}) collective-permute-start(bf16[48,64,128]{2,1,0:T(8,128)(2,1)S(1)} %collective-permute-done.1.refs_6_), channel_id=1, source_target_pairs={{0,8},{8,0},{16,24},{24,16},{1,9},{9,1},{17,25},{25,17},{2,10},{10... | collective-permute-start | bytes 2359304 | tf_op jit(solution)/shard_map/ppermute | solution.py:293
  25.1 10.7 %collective-permute-start.4 = (bf16[1040,128]{1,0:T(8,128)(2,1)S(1)}, bf16[1040,128]{1,0:T(8,128)(2,1)S(1)}, u32[]{:S(2)}, u32[]{:S(2)}) collective-permute-start(bf16[1040,128]{1,0:T(8,128)(2,1)S(1)} %pad_maximum_fusion.refs_0_), channel_id=1, source_target_pairs={{0,6},{1,7},{2,0},{3,1},{4,2},{5,3},{6,4},{7,5},{8,14},{9,15},{10,... | collective-permute-start | bytes 798728 | tf_op jit(solution)/shard_map/ppermute | solution.py:309
  28.9 23.3 %collective-permute-start.3 = (bf16[1040,128]{1,0:T(8,128)(2,1)S(1)}, bf16[1040,128]{1,0:T(8,128)(2,1)S(1)}, u32[]{:S(2)}, u32[]{:S(2)}) collective-permute-start(bf16[1040,128]{1,0:T(8,128)(2,1)S(1)} %pad_maximum_fusion.refs_0_), channel_id=1, source_target_pairs={{0,4},{1,5},{2,6},{3,7},{4,0},{5,1},{6,2},{7,3},{8,12},{9,13},{10,... | collective-permute-start | bytes 798728 | tf_op jit(solution)/shard_map/ppermute | solution.py:309
  28.9 24.1 %collective-permute-start.2 = (bf16[1040,128]{1,0:T(8,128)(2,1)S(1)}, bf16[1040,128]{1,0:T(8,128)(2,1)S(1)}, u32[]{:S(2)}, u32[]{:S(2)}) collective-permute-start(bf16[1040,128]{1,0:T(8,128)(2,1)S(1)} %pad_maximum_fusion.refs_0_), channel_id=1, source_target_pairs={{0,2},{1,3},{2,4},{3,5},{4,6},{5,7},{6,0},{7,1},{8,10},{9,11},{10,... | collective-permute-start | bytes 798728 | tf_op jit(solution)/shard_map/ppermute | solution.py:309
  36.4 49.8 %collective-permute-start.10 = (bf16[48,64,128]{2,1,0:T(8,128)(2,1)}, bf16[48,64,128]{2,1,0:T(8,128)(2,1)}, u32[]{:S(2)}, u32[]{:S(2)}) collective-permute-start(bf16[48,64,128]{2,1,0:T(8,128)(2,1)} %get-tuple-element.35.refs_4_), channel_id=1, source_target_pairs={{0,8},{8,0},{16,24},{24,16},{1,9},{9,1},{17,25},{25,17},{2,10},{10... | collective-permute-start | bytes 2359304 | tf_op jit(solution)/shard_map/ppermute | solution.py:293
  56.6 106.0 %copy-start.2 = (bf16[4,1040,128]{2,1,0:T(8,128)(2,1)}, bf16[4,1040,128]{2,1,0:T(8,128)(2,1)S(1)}, u32[]{:S(2)}) copy-start(bf16[4,1040,128]{2,1,0:T(8,128)(2,1)S(1)} %join.1.refs_3_) | copy-start | bytes 3194884
  56.7 25.3 %collective-permute-start.9 = (bf16[4,1040,128]{2,1,0:T(8,128)(2,1)S(1)}, bf16[4,1040,128]{2,1,0:T(8,128)(2,1)}, u32[]{:S(2)}, u32[]{:S(2)}) collective-permute-start(bf16[4,1040,128]{2,1,0:T(8,128)(2,1)S(1)} %join.1.refs_3_), channel_id=1, source_target_pairs={{0,1},{1,0},{2,3},{3,2},{4,5},{5,4},{6,7},{7,6},{8,9},{9,8},{10,11... | collective-permute-start | bytes 3194888 | tf_op jit(solution)/shard_map/ppermute | solution.py:317
  58.2 19.2 %collective-permute-start.5 = (bf16[48,64,128]{2,1,0:T(8,128)(2,1)}, bf16[48,64,128]{2,1,0:T(8,128)(2,1)}, u32[]{:S(2)}, u32[]{:S(2)}) collective-permute-start(bf16[48,64,128]{2,1,0:T(8,128)(2,1)} %get-tuple-element.35.refs_4_), channel_id=1, source_target_pairs={{0,16},{8,24},{16,0},{24,8},{1,17},{9,25},{17,1},{25,9},{2,18},{10... | collective-permute-start | bytes 2359304 | tf_op jit(solution)/shard_map/ppermute | solution.py:290
  77.4 10.4 %collective-permute-start.11 = (bf16[48,64,128]{2,1,0:T(8,128)(2,1)}, bf16[48,64,128]{2,1,0:T(8,128)(2,1)}, u32[]{:S(2)}, u32[]{:S(2)}) collective-permute-start(bf16[48,64,128]{2,1,0:T(8,128)(2,1)} %collective-permute-done.5.refs_6_), channel_id=1, source_target_pairs={{0,8},{8,0},{16,24},{24,16},{1,9},{9,1},{17,25},{25,17},{2,10},{10... | collective-permute-start | bytes 2359304 | tf_op jit(solution)/shard_map/ppermute | solution.py:293
  77.4 36.4 %collective-permute-start.15 = (bf16[48,64,128]{2,1,0:T(8,128)(2,1)S(1)}, bf16[48,64,128]{2,1,0:T(8,128)(2,1)}, u32[]{:S(2)}, u32[]{:S(2)}) collective-permute-start(bf16[48,64,128]{2,1,0:T(8,128)(2,1)S(1)} %copy-done.4), channel_id=1, source_target_pairs={{0,8},{8,0},{16,24},{24,16},{1,9},{9,1},{17,25},{25,17},{2,10},{10... | collective-permute-start | bytes 2359304 | tf_op jit(solution)/shard_map/ppermute | solution.py:293
  77.9 34.3 %collective-permute-start.13 = (bf16[4,1040,128]{2,1,0:T(8,128)(2,1)S(1)}, bf16[4,1040,128]{2,1,0:T(8,128)(2,1)}, u32[]{:S(2)}, u32[]{:S(2)}) collective-permute-start(bf16[4,1040,128]{2,1,0:T(8,128)(2,1)S(1)} %join.1.refs_3_), channel_id=1, source_target_pairs={{0,8},{8,0},{16,24},{24,16},{1,9},{9,1},{17,25},{25,17},{2,10},{10... | collective-permute-start | bytes 3194888 | tf_op jit(solution)/shard_map/ppermute | solution.py:293
  82.0 31.8 %collective-permute-start.14 = (bf16[4,1040,128]{2,1,0:T(8,128)(2,1)}, bf16[4,1040,128]{2,1,0:T(8,128)(2,1)}, u32[]{:S(2)}, u32[]{:S(2)}) collective-permute-start(bf16[4,1040,128]{2,1,0:T(8,128)(2,1)} %collective-permute-done.9.refs_4_), channel_id=1, source_target_pairs={{0,8},{8,0},{16,24},{24,16},{1,9},{9,1},{17,25},{25,17},{2,10},{10... | collective-permute-start | bytes 3194888 | tf_op jit(solution)/shard_map/ppermute | solution.py:293
  82.0 25.3 %all-to-all-start.1 = ((bf16[8,384,128]{2,1,0:T(8,128)(2,1)}), bf16[8,384,128]{2,1,0:T(8,128)(2,1)}, u32[]{:S(2)}, u32[]{:S(2)}) async-start(bf16[8,384,128]{2,1,0:T(8,128)(2,1)} %chunk_products.4), calls=%async_computation.1 | async-start | bytes 1572864 | tf_op jit(solution)/shard_map/all_to_all | solution.py:336
  86.2 20.1 %collective-permute-start.8 = (bf16[48,64,128]{2,1,0:T(8,128)(2,1)S(1)}, bf16[48,64,128]{2,1,0:T(8,128)(2,1)}, u32[]{:S(2)}, u32[]{:S(2)}) collective-permute-start(bf16[48,64,128]{2,1,0:T(8,128)(2,1)S(1)} %copy-done.4), channel_id=1, source_target_pairs={{0,16},{8,24},{16,0},{24,8},{1,17},{9,25},{17,1},{25,9},{2,18},{10... | collective-permute-start | bytes 2359304 | tf_op jit(solution)/shard_map/ppermute | solution.py:290
  106.3 7.5 %collective-permute-start.16 = (bf16[48,64,128]{2,1,0:T(8,128)(2,1)}, bf16[48,64,128]{2,1,0:T(8,128)(2,1)}, u32[]{:S(2)}, u32[]{:S(2)}) collective-permute-start(bf16[48,64,128]{2,1,0:T(8,128)(2,1)} %collective-permute-done.8.refs_6_), channel_id=1, source_target_pairs={{0,8},{8,0},{16,24},{24,16},{1,9},{9,1},{17,25},{25,17},{2,10},{10... | collective-permute-start | bytes 2359304 | tf_op jit(solution)/shard_map/ppermute | solution.py:293
  107.3 25.6 %all-to-all-start.2 = ((bf16[8,384,128]{2,1,0:T(8,128)(2,1)}), bf16[8,384,128]{2,1,0:T(8,128)(2,1)}, u32[]{:S(2)}, u32[]{:S(2)}) async-start(bf16[8,384,128]{2,1,0:T(8,128)(2,1)} %chunk_products.5), calls=%async_computation.2 | async-start | bytes 1572864 | tf_op jit(solution)/shard_map/all_to_all | solution.py:336
  112.0 26.1 %collective-permute-start = (bf16[48,64,128]{2,1,0:T(8,128)(2,1)S(1)}, bf16[48,64,128]{2,1,0:T(8,128)(2,1)}, u32[]{:S(2)}, u32[]{:S(2)}) collective-permute-start(bf16[48,64,128]{2,1,0:T(8,128)(2,1)S(1)} %copy-done.3), channel_id=1, source_target_pairs={{0,8},{8,0},{16,24},{24,16},{1,9},{9,1},{17,25},{25,17},{2,10},{10... | collective-permute-start | bytes 2359304 | tf_op jit(solution)/shard_map/ppermute | solution.py:293
  112.3 19.8 %collective-permute-start.12 = (bf16[48,64,128]{2,1,0:T(8,128)(2,1)S(1)}, bf16[48,64,128]{2,1,0:T(8,128)(2,1)}, u32[]{:S(2)}, u32[]{:S(2)}) collective-permute-start(bf16[48,64,128]{2,1,0:T(8,128)(2,1)S(1)} %copy-done.3), channel_id=1, source_target_pairs={{0,16},{8,24},{16,0},{24,8},{1,17},{9,25},{17,1},{25,9},{2,18},{10... | collective-permute-start | bytes 2359304 | tf_op jit(solution)/shard_map/ppermute | solution.py:290
  132.1 6.0 %collective-permute-start.17 = (bf16[48,64,128]{2,1,0:T(8,128)(2,1)}, bf16[48,64,128]{2,1,0:T(8,128)(2,1)S(1)}, u32[]{:S(2)}, u32[]{:S(2)}) collective-permute-start(bf16[48,64,128]{2,1,0:T(8,128)(2,1)} %collective-permute-done.12.refs_6_), channel_id=1, source_target_pairs={{0,8},{8,0},{16,24},{24,16},{1,9},{9,1},{17,25},{25,17},{2,10},{10... | collective-permute-start | bytes 2359304 | tf_op jit(solution)/shard_map/ppermute | solution.py:293
  132.9 26.1 %all-to-all-start.3 = ((bf16[8,384,128]{2,1,0:T(8,128)(2,1)}), bf16[8,384,128]{2,1,0:T(8,128)(2,1)}, u32[]{:S(2)}, u32[]{:S(2)}) async-start(bf16[8,384,128]{2,1,0:T(8,128)(2,1)} %chunk_products.6), calls=%async_computation.3 | async-start | bytes 1572864 | tf_op jit(solution)/shard_map/all_to_all | solution.py:336
  159.0 24.0 %all-to-all-start = ((bf16[8,384,128]{2,1,0:T(8,128)(2,1)}), bf16[8,384,128]{2,1,0:T(8,128)(2,1)S(1)}, u32[]{:S(2)}, u32[]{:S(2)}) async-start(bf16[8,384,128]{2,1,0:T(8,128)(2,1)} %chunk_products.7), calls=%async_computation | async-start | bytes 1572864 | tf_op jit(solution)/shard_map/all_to_all | solution.py:336
  (14 other events, 164.1 us)

commit v5 on v4

--- a/solution.py
+++ b/solution.py
@@ -7,8 +7,8 @@
 from jax.experimental.pallas import tpu as pltpu
 from jax.sharding import PartitionSpec as P
 
-VMEM_LIMIT = 40 * 1024 * 1024
 VMEM_WHOLE = 58 * 1024 * 1024
+SMALL = pl.CostEstimate(flops=0, bytes_accessed=4096, transcendentals=0)
 
 
 def largest_divisor(total, most):
@@ -22,7 +22,7 @@
         chunk[...] = jnp.concatenate([source[:, :half, columns], source[:, half:, columns]], axis=-1)
 
 
-def pack_chunks(factors, width, begin, count, cost):
+def pack_chunks(factors, width, begin, count):
     orbitals, domain, part = factors.shape
     first = begin * width
     step = largest_divisor(orbitals, 12)
@@ -33,7 +33,7 @@
         in_specs=[pl.BlockSpec((step, domain, part), lambda i: (i, 0, 0))],
         out_specs=[pl.BlockSpec(packed, lambda i: (i, 0, 0))] * count,
         out_shape=[jax.ShapeDtypeStruct((orbitals,) + packed[1:], factors.dtype)] * count,
-        cost_estimate=pl.CostEstimate(flops=0, bytes_accessed=cost * factors.size, transcendentals=0),
+        cost_estimate=SMALL,
         compiler_params=pltpu.CompilerParams(vmem_limit_bytes=VMEM_WHOLE),
         name="pack_chunks",
     )(factors)
@@ -121,12 +121,8 @@
             ],
         ),
         out_shape=jax.ShapeDtypeStruct(out_shape, jnp.bfloat16),
-        cost_estimate=pl.CostEstimate(
-            flops=8 * amplitudes.size * lanes,
-            bytes_accessed=2 * amplitudes.size + 2 * total * half_domain * lanes,
-            transcendentals=0,
-        ),
-        compiler_params=pltpu.CompilerParams(vmem_limit_bytes=VMEM_LIMIT),
+        cost_estimate=SMALL,
+        compiler_params=pltpu.CompilerParams(vmem_limit_bytes=VMEM_WHOLE),
         name="chunk_products",
     )(slots, *[amplitudes.reshape(2, half, pairs, domain, domain)] * (2 * streams), *pieces)
     if split_rows:
@@ -145,8 +141,8 @@
     return pl.pallas_call(
         join_kernel,
         out_shape=jax.ShapeDtypeStruct(shape, pieces[0].dtype),
-        cost_estimate=pl.CostEstimate(flops=0, bytes_accessed=4 * len(pieces) * pieces[0].size, transcendentals=0),
-        compiler_params=pltpu.CompilerParams(vmem_limit_bytes=VMEM_LIMIT),
+        cost_estimate=SMALL,
+        compiler_params=pltpu.CompilerParams(vmem_limit_bytes=VMEM_WHOLE),
         name="join",
     )(*pieces)
 
@@ -223,11 +219,7 @@
             ],
         ),
         out_shape=[jax.ShapeDtypeStruct((tall, size), kind) for tall, kind in zip(heights, kinds)],
-        cost_estimate=pl.CostEstimate(
-            flops=4 * height * depth * size,
-            bytes_accessed=2 * depth * size + 8 * height * size,
-            transcendentals=0,
-        ),
+        cost_estimate=SMALL,
         compiler_params=pltpu.CompilerParams(vmem_limit_bytes=VMEM_WHOLE),
         name="first_shares",
     )(positions, *chunks, *sources)
@@ -263,11 +255,7 @@
         out_specs=pl.BlockSpec((2, height, step), lambda j: (0, 0, j)),
         out_shape=jax.ShapeDtypeStruct((2, height, size), jnp.bfloat16),
         scratch_shapes=[pltpu.VMEM((2 * height, depth), jnp.bfloat16)],
-        cost_estimate=pl.CostEstimate(
-            flops=4 * height * depth * size,
-            bytes_accessed=2 * depth * size + 12 * height * size,
-            transcendentals=0,
-        ),
+        cost_estimate=SMALL,
         compiler_params=pltpu.CompilerParams(vmem_limit_bytes=VMEM_WHOLE),
         name="last_share",
     )(chunk, metric, one, two)
@@ -308,9 +296,9 @@
         moves = [(g, (g + 2 * shift) % aux_count) for g in range(aux_count)]
         parts.append(lax.ppermute(load, "aux", moves))
 
-    packed = list(pack_chunks(factors, width, 0, 1, 2))
+    packed = list(pack_chunks(factors, width, 0, 1))
     if chunk_count > 1:
-        packed += pack_chunks(factors, width, 1, chunk_count - 1, 40)
+        packed += pack_chunks(factors, width, 1, chunk_count - 1)
         parts = after(parts, packed[1:])
 
     column = join(parts)
@@ -327,7 +315,7 @@
             own = after(own, [far_pieces, before_far.get(at, [])])
         far_pieces = [to_far(own, shift) for shift in range(1, far_count)]
         if chunk_count > 1:
-            far_pieces = after(far_pieces, made if at else packed[1:])
+            far_pieces = after(far_pieces, made if at else [packed[1:], column])
         pieces = []
         for piece in [packed[at]] + far_pieces:
             pieces += [piece, to_mate(piece)]

time: 194 us -> 197 us (1.015)
  waiting for transfers between devices: 63.3 us -> 58.7 us
  Pallas kernels: 86.5 us -> 90.3 us
  local copies, waits for them, and re-layouts: 10.2 us -> 12.7 us
    ppermute x1, waiting for transfers between devices: 4.03 us -> 30.4 us  [shards(): beside = lax.ppermute(column, 'aux', [(g, g ^ 1) for g in range(aux_count)])]
    ppermute x4, waiting for transfers between devices: 26.3 us -> 0.01 us  [to_far(): return lax.ppermute(array, 'orb', moves)]
    all_to_all x4, waiting for transfers between devices: 11.6 us -> 4.4 us  [shards(): lax.all_to_all(made, 'aux', split_axis=0, concat_axis=0, tiled=True)]
    ppermute x10, waiting for transfers between devices: 0.03 us -> 6.73 us  [to_mate(): return lax.ppermute(array, 'orb', [(g, g ^ 1) for g in range(orb_count)])]
    ppermute x3, waiting for transfers between devices: 21.4 us -> 17.1 us  [shards(): parts.append(lax.ppermute(load, 'aux', moves))]
    ppermute x4, starting transfers between devices: 7.59 us -> 5.39 us  [to_far(): return lax.ppermute(array, 'orb', moves)]
    pallas_call x1, Pallas kernels: 0.07 us -> 2.24 us  [join(): pl.pallas_call(join_kernel, out_shape=jax.ShapeDtypeStruct(shape, pieces[...]
    all_to_all x4, starting transfers between devices: 17.7 us -> 19.7 us  [shards(): lax.all_to_all(made, 'aux', split_axis=0, concat_axis=0, tiled=True)]
  transfers between devices with their start and end apart: 22 -> 22, of which waited for: 11 -> 11; matrix products, arithmetic and copies ran while one was open for 2% -> 2% of each run, Pallas kernels for 38% -> 39%
where the time goes in v5:
time: 197 us; the launch traced here: 196 us
  Pallas kernels  90.3 us (46%)
  waiting for transfers between devices  58.7 us (30%)
  starting transfers between devices  33.8 us (17%)
  local copies, waits for them, and re-layouts  12.7 us (6%)
    pallas_call x4, Pallas kernels, chunk_products(): pl.pallas_call(functools.partial(product_kernel, pairs, split_rows, strea...  55.4 us
    ppermute x1, waiting for transfers between devices, shards(): beside = lax.ppermute(column, 'aux', [(g, g ^ 1) for g in range(aux_count)])  30.4 us
    all_to_all x4, starting transfers between devices, shards(): lax.all_to_all(made, 'aux', split_axis=0, concat_axis=0, tiled=True)  19.7 us
    ppermute x3, waiting for transfers between devices, shards(): parts.append(lax.ppermute(load, 'aux', moves))  17.1 us
    pallas_call x1, Pallas kernels, first_shares(): pl.pallas_call(functools.partial(first_kernel, len(chunks), len(sources),...  15.4 us
    pallas_call x1, Pallas kernels, last_share(): pl.pallas_call(last_kernel, grid=(size // step,), in_specs=[pl.BlockSpec(...  9.04 us
    unnamed x52, local copies, waits for them, and re-layouts  9.02 us
    pallas_call x2, Pallas kernels, pack_chunks(): pl.pallas_call(functools.partial(pack_kernel, width, first), grid=(orbita...  8.2 us
  transfers between devices with their start and end apart: 22, of which 11 were waited for; matrix products, arithmetic and copies ran while one was open for 2% of the time, Pallas kernels for 39%

profile of v5, /device:TPU:0, one launch (start us, length us, event | category | flops | bytes accessed | tf_op | source)
XLA Modules:
  0.0 195.9 jit_solution(1297610245807210794)
XLA Ops:
  0.0 4.0 %pack_chunks.3.refs_4_ = bf16[48,64,128]{2,1,0:T(8,128)(2,1)} custom-call(bf16[48,128,256]{2,1,0:T(8,128)(2,1)} %source.3), custom_call_target="tpu_custom_call" | custom-call | bytes 4096 | tf_op jit(solution)/shard_map/pack_chunks/pallas_call | solution.py:30
  4.0 3.0 %collective-permute-start.1 = (bf16[48,64,128]{2,1,0:T(8,128)(2,1)}, bf16[48,64,128]{2,1,0:T(8,128)(2,1)S(1)}, u32[]{:S(2)}, u32[]{:S(2)}) collective-permute-start(bf16[48,64,128]{2,1,0:T(8,128)(2,1)} %pack_chunks.3.refs_4_), channel_id=1, source_target_pairs={{0,16},{8,24},{16,0},{24,8},{1,17},{9,25},{17,1},{25,9},{2,18},{10... | collective-permute-start | bytes 2359304 | tf_op jit(solution)/shard_map/ppermute | solution.py:278
  7.3 3.7 %collective-permute-start.4 = (bf16[1040,128]{1,0:T(8,128)(2,1)S(1)}, bf16[1040,128]{1,0:T(8,128)(2,1)S(1)}, u32[]{:S(2)}, u32[]{:S(2)}) collective-permute-start(bf16[1040,128]{1,0:T(8,128)(2,1)S(1)} %pad_maximum_fusion.refs_0_), channel_id=1, source_target_pairs={{0,6},{1,7},{2,0},{3,1},{4,2},{5,3},{6,4},{7,5},{8,14},{9,15},{10,... | collective-permute-start | bytes 798728 | tf_op jit(solution)/shard_map/ppermute | solution.py:297
  12.0 4.2 %pack_chunks.2 = (bf16[48,64,128]{2,1,0:T(8,128)(2,1)}, bf16[48,64,128]{2,1,0:T(8,128)(2,1)}, bf16[48,64,128]{2,1,0:T(8,128)(2,1)}) custom-call(bf16[48,128,256]{2,1,0:T(8,128)(2,1)} %source.3), custom_call_target="tpu_custom_call" | custom-call | bytes 4096 | tf_op jit(solution)/shard_map/pack_chunks/pallas_call | solution.py:30
  16.2 1.6 collective-permute-done.4.refs_3_
  17.9 15.5 %collective-permute-done.3.refs_2_ = bf16[1040,128]{1,0:T(8,128)(2,1)S(1)} collective-permute-done((bf16[1040,128]{1,0:T(8,128)(2,1)S(1)}, bf16[1040,128]{1,0:T(8,128)(2,1)S(1)}, u32[]{:S(2)}, u32[]{:S(2)}) %collective-permute-start.3) | collective-permute-done | bytes 266272 | tf_op jit(solution)/shard_map/ppermute | solution.py:297
  34.2 2.2 %join.1.refs_3_ = bf16[4,1040,128]{2,1,0:T(8,128)(2,1)} custom-call(bf16[1040,128]{1,0:T(8,128)(2,1)} %copy-done.9, bf16[1040,128]{1,0:T(8,128)(2,1)} %copy-done.21, bf16[1040,128]{1,0:T(8,128)(2,1)} %copy-done.20, bf16[1040,128]{1,0:T(8,128)(2,1)} %copy-done.19), custom_call_target="tpu_custom_call" | custom-call | bytes 4096 | tf_op jit(solution)/shard_map/join/pallas_call | solution.py:141
  39.6 13.9 %chunk_products.4 = bf16[8,384,128]{2,1,0:T(8,128)(2,1)} custom-call(s32[576]{0:T(1024)} %reshape.24.slots, bf16[2,24,12,128,128]{4,3,2,1,0:T(8,128)(2,1)} %bitcast.17, bf16[2,24,12,128,128]{4,3,2,1,0:T(8,128)(2,1)} %bitcast.18, bf16[2,24,12,128,128]{4,3,2,1,0:T(8,128)(2,1)} %bitcast.19, bf16[2,24,12,128,128]{4,3,2,1,0:T(8,128)(2,1)} %bitcast.20, ...), custom_call_target="tpu_custom_call" | custom-call | bytes 4096 | tf_op jit(solution)/shard_map/chunk_products/pallas_call | solution.py:106
  53.5 4.9 %all-to-all-start.1 = ((bf16[8,384,128]{2,1,0:T(8,128)(2,1)}), bf16[8,384,128]{2,1,0:T(8,128)(2,1)S(1)}, u32[]{:S(2)}, u32[]{:S(2)}) async-start(bf16[8,384,128]{2,1,0:T(8,128)(2,1)} %chunk_products.4), calls=%async_computation.1 | async-start | bytes 1572864 | tf_op jit(solution)/shard_map/all_to_all | solution.py:324
  58.4 2.0 %collective-permute-start.9 = (bf16[4,1040,128]{2,1,0:T(8,128)(2,1)S(1)}, bf16[4,1040,128]{2,1,0:T(8,128)(2,1)S(1)}, u32[]{:S(2)}, u32[]{:S(2)}) collective-permute-start(bf16[4,1040,128]{2,1,0:T(8,128)(2,1)S(1)} %copy-done.1), channel_id=1, source_target_pairs={{0,1},{1,0},{2,3},{3,2},{4,5},{5,4},{6,7},{7,6},{8,9},{9,8},{10,11... | collective-permute-start | bytes 3194888 | tf_op jit(solution)/shard_map/ppermute | solution.py:305
  61.9 30.4 %collective-permute-done.9.refs_4_ = bf16[4,1040,128]{2,1,0:T(8,128)(2,1)S(1)} collective-permute-done((bf16[4,1040,128]{2,1,0:T(8,128)(2,1)S(1)}, bf16[4,1040,128]{2,1,0:T(8,128)(2,1)S(1)}, u32[]{:S(2)}, u32[]{:S(2)}) %collective-permute-start.9) | collective-permute-done | bytes 1064992 | tf_op jit(solution)/shard_map/ppermute | solution.py:305
  95.0 13.8 %chunk_products.5 = bf16[8,384,128]{2,1,0:T(8,128)(2,1)} custom-call(s32[576]{0:T(1024)} %reshape.24.slots, bf16[2,24,12,128,128]{4,3,2,1,0:T(8,128)(2,1)} %bitcast.21, bf16[2,24,12,128,128]{4,3,2,1,0:T(8,128)(2,1)} %bitcast.22, bf16[2,24,12,128,128]{4,3,2,1,0:T(8,128)(2,1)} %bitcast.23, bf16[2,24,12,128,128]{4,3,2,1,0:T(8,128)(2,1)} %bitcast.24, ...), custom_call_target="tpu_custom_call" | custom-call | bytes 4096 | tf_op jit(solution)/shard_map/chunk_products/pallas_call | solution.py:106
  108.9 4.6 %all-to-all-start.2 = ((bf16[8,384,128]{2,1,0:T(8,128)(2,1)}), bf16[8,384,128]{2,1,0:T(8,128)(2,1)S(1)}, u32[]{:S(2)}, u32[]{:S(2)}) async-start(bf16[8,384,128]{2,1,0:T(8,128)(2,1)} %chunk_products.5), calls=%async_computation.2 | async-start | bytes 1572864 | tf_op jit(solution)/shard_map/all_to_all | solution.py:324
  115.4 1.5 collective-permute-done.13.refs_5_
  119.0 1.1 collective-permute-done.16.refs_7_
  121.0 13.8 %chunk_products.6 = bf16[8,384,128]{2,1,0:T(8,128)(2,1)} custom-call(s32[576]{0:T(1024)} %reshape.24.slots, bf16[2,24,12,128,128]{4,3,2,1,0:T(8,128)(2,1)} %bitcast.25, bf16[2,24,12,128,128]{4,3,2,1,0:T(8,128)(2,1)} %bitcast.26, bf16[2,24,12,128,128]{4,3,2,1,0:T(8,128)(2,1)} %bitcast.27, bf16[2,24,12,128,128]{4,3,2,1,0:T(8,128)(2,1)} %bitcast.28, ...), custom_call_target="tpu_custom_call" | custom-call | bytes 4096 | tf_op jit(solution)/shard_map/chunk_products/pallas_call | solution.py:106
  134.8 6.3 %all-to-all-start.3 = ((bf16[8,384,128]{2,1,0:T(8,128)(2,1)}), bf16[8,384,128]{2,1,0:T(8,128)(2,1)S(1)}, u32[]{:S(2)}, u32[]{:S(2)}) async-start(bf16[8,384,128]{2,1,0:T(8,128)(2,1)} %chunk_products.6), calls=%async_computation.3 | async-start | bytes 1572864 | tf_op jit(solution)/shard_map/all_to_all | solution.py:324
  141.7 2.0 %collective-permute-done.refs_5_ = bf16[48,64,128]{2,1,0:T(8,128)(2,1)S(1)} collective-permute-done((bf16[48,64,128]{2,1,0:T(8,128)(2,1)}, bf16[48,64,128]{2,1,0:T(8,128)(2,1)S(1)}, u32[]{:S(2)}, u32[]{:S(2)}) %collective-permute-start) | collective-permute-done | bytes 786464 | tf_op jit(solution)/shard_map/ppermute | solution.py:281
  145.7 13.8 %chunk_products.7 = bf16[8,384,128]{2,1,0:T(8,128)(2,1)} custom-call(s32[576]{0:T(1024)} %reshape.24.slots, bf16[2,24,12,128,128]{4,3,2,1,0:T(8,128)(2,1)} %bitcast.29, bf16[2,24,12,128,128]{4,3,2,1,0:T(8,128)(2,1)} %bitcast.30, bf16[2,24,12,128,128]{4,3,2,1,0:T(8,128)(2,1)} %bitcast.31, bf16[2,24,12,128,128]{4,3,2,1,0:T(8,128)(2,1)} %bitcast.32, ...), custom_call_target="tpu_custom_call" | custom-call | bytes 4096 | tf_op jit(solution)/shard_map/chunk_products/pallas_call | solution.py:106
  159.5 2.1 %all-to-all-done.3.refs_2_ = bf16[8,384,128]{2,1,0:T(8,128)(2,1)S(1)} async-done(((bf16[8,384,128]{2,1,0:T(8,128)(2,1)}), bf16[8,384,128]{2,1,0:T(8,128)(2,1)S(1)}, u32[]{:S(2)}, u32[]{:S(2)}) %all-to-all-start.3) | async-done | bytes 786464 | tf_op jit(solution)/shard_map/all_to_all | solution.py:324
  161.6 3.9 %all-to-all-start = ((bf16[8,384,128]{2,1,0:T(8,128)(2,1)}), bf16[8,384,128]{2,1,0:T(8,128)(2,1)S(1)}, u32[]{:S(2)}, u32[]{:S(2)}) async-start(bf16[8,384,128]{2,1,0:T(8,128)(2,1)} %chunk_products.7), calls=%async_computation | async-start | bytes 1572864 | tf_op jit(solution)/shard_map/all_to_all | solution.py:324
  168.3 15.4 %first_shares.1 = (f32[384,2048]{1,0:T(8,128)}, f32[384,2048]{1,0:T(8,128)}, bf16[512,2048]{1,0:T(8,128)(2,1)}) custom-call(s32[256]{0:T(256)} %reshape.29.positions, bf16[8,384,128]{2,1,0:T(8,128)(2,1)} %copy-done.3, bf16[8,384,128]{2,1,0:T(8,128)(2,1)} %copy-done.4, bf16[8,384,128]{2,1,0:T(8,128)(2,1)} %copy-done.5, bf16[4,1040,128]{2,1,0:T(8,128)(2,1)} %join.1.refs_3_, ...), custom_call_target="tpu_custom_call" | custom-call | bytes 4096 | tf_op jit(solution)/shard_map/first_shares/pallas_call | solution.py:209
  183.7 2.3 %all-to-all-done.chunk = bf16[8,384,128]{2,1,0:T(8,128)(2,1)S(1)} async-done(((bf16[8,384,128]{2,1,0:T(8,128)(2,1)}), bf16[8,384,128]{2,1,0:T(8,128)(2,1)S(1)}, u32[]{:S(2)}, u32[]{:S(2)}) %all-to-all-start) | async-done | bytes 786464 | tf_op jit(solution)/shard_map/all_to_all | solution.py:324
  186.9 9.0 %last_share.1 = bf16[2,384,2048]{2,1,0:T(8,128)(2,1)} custom-call(bf16[8,384,128]{2,1,0:T(8,128)(2,1)} %copy-done.2, bf16[512,2048]{1,0:T(8,128)(2,1)} %get-tuple-element.46.metric, f32[384,2048]{1,0:T(8,128)} %get-tuple-element.47.one, f32[384,2048]{1,0:T(8,128)} %get-tuple-element.48.two), custom_call_target="tpu_custom_call" | custom-call | bytes 4096 | tf_op jit(solution)/shard_map/last_share/pallas_call | solution.py:246
  (96 shorter events, 20.5 us)
Async XLA Ops:
  4.0 32.4 %collective-permute-start.1 = (bf16[48,64,128]{2,1,0:T(8,128)(2,1)}, bf16[48,64,128]{2,1,0:T(8,128)(2,1)S(1)}, u32[]{:S(2)}, u32[]{:S(2)}) collective-permute-start(bf16[48,64,128]{2,1,0:T(8,128)(2,1)} %pack_chunks.3.refs_4_), channel_id=1, source_target_pairs={{0,16},{8,24},{16,0},{24,8},{1,17},{9,25},{17,1},{25,9},{2,18},{10... | collective-permute-start | bytes 2359304 | tf_op jit(solution)/shard_map/ppermute | solution.py:278
  7.2 29.8 %copy-start.22 = (s32[48,12]{0,1:T(8,128)S(1)}, s32[48,12]{0,1:T(8,128)}, u32[]{:S(2)}) copy-start(s32[48,12]{0,1:T(8,128)} %param.7) | copy-start | bytes 6916
  7.3 26.1 %copy-start.9 = (bf16[1040,128]{1,0:T(8,128)(2,1)}, bf16[1040,128]{1,0:T(8,128)(2,1)S(1)}, u32[]{:S(2)}) copy-start(bf16[1040,128]{1,0:T(8,128)(2,1)S(1)} %pad_maximum_fusion.refs_0_) | copy-start | bytes 798724
  7.3 10.5 %collective-permute-start.4 = (bf16[1040,128]{1,0:T(8,128)(2,1)S(1)}, bf16[1040,128]{1,0:T(8,128)(2,1)S(1)}, u32[]{:S(2)}, u32[]{:S(2)}) collective-permute-start(bf16[1040,128]{1,0:T(8,128)(2,1)S(1)} %pad_maximum_fusion.refs_0_), channel_id=1, source_target_pairs={{0,6},{1,7},{2,0},{3,1},{4,2},{5,3},{6,4},{7,5},{8,14},{9,15},{10,... | collective-permute-start | bytes 798728 | tf_op jit(solution)/shard_map/ppermute | solution.py:297
  11.0 22.4 %collective-permute-start.3 = (bf16[1040,128]{1,0:T(8,128)(2,1)S(1)}, bf16[1040,128]{1,0:T(8,128)(2,1)S(1)}, u32[]{:S(2)}, u32[]{:S(2)}) collective-permute-start(bf16[1040,128]{1,0:T(8,128)(2,1)S(1)} %pad_maximum_fusion.refs_0_), channel_id=1, source_target_pairs={{0,4},{1,5},{2,6},{3,7},{4,0},{5,1},{6,2},{7,3},{8,12},{9,13},{10,... | collective-permute-start | bytes 798728 | tf_op jit(solution)/shard_map/ppermute | solution.py:297
  11.0 22.4 %collective-permute-start.2 = (bf16[1040,128]{1,0:T(8,128)(2,1)S(1)}, bf16[1040,128]{1,0:T(8,128)(2,1)S(1)}, u32[]{:S(2)}, u32[]{:S(2)}) collective-permute-start(bf16[1040,128]{1,0:T(8,128)(2,1)S(1)} %pad_maximum_fusion.refs_0_), channel_id=1, source_target_pairs={{0,2},{1,3},{2,4},{3,5},{4,6},{5,7},{6,0},{7,1},{8,10},{9,11},{10,... | collective-permute-start | bytes 798728 | tf_op jit(solution)/shard_map/ppermute | solution.py:297
  12.0 25.8 %collective-permute-start.6 = (bf16[48,64,128]{2,1,0:T(8,128)(2,1)}, bf16[48,64,128]{2,1,0:T(8,128)(2,1)S(1)}, u32[]{:S(2)}, u32[]{:S(2)}) collective-permute-start(bf16[48,64,128]{2,1,0:T(8,128)(2,1)} %pack_chunks.3.refs_4_), channel_id=1, source_target_pairs={{0,8},{8,0},{16,24},{24,16},{1,9},{9,1},{17,25},{25,17},{2,10},{10... | collective-permute-start | bytes 2359304 | tf_op jit(solution)/shard_map/ppermute | solution.py:281
  36.4 2.3 %collective-permute-start.7 = (bf16[48,64,128]{2,1,0:T(8,128)(2,1)S(1)}, bf16[48,64,128]{2,1,0:T(8,128)(2,1)S(1)}, u32[]{:S(2)}, u32[]{:S(2)}) collective-permute-start(bf16[48,64,128]{2,1,0:T(8,128)(2,1)S(1)} %collective-permute-done.1.refs_6_), channel_id=1, source_target_pairs={{0,8},{8,0},{16,24},{24,16},{1,9},{9,1},{17,25},{25,17},{2,10},{10... | collective-permute-start | bytes 2359304 | tf_op jit(solution)/shard_map/ppermute | solution.py:281
  36.4 24.0 %collective-permute-start.5 = (bf16[48,64,128]{2,1,0:T(8,128)(2,1)}, bf16[48,64,128]{2,1,0:T(8,128)(2,1)}, u32[]{:S(2)}, u32[]{:S(2)}) collective-permute-start(bf16[48,64,128]{2,1,0:T(8,128)(2,1)} %get-tuple-element.35.refs_4_), channel_id=1, source_target_pairs={{0,16},{8,24},{16,0},{24,8},{1,17},{9,25},{17,1},{25,9},{2,18},{10... | collective-permute-start | bytes 2359304 | tf_op jit(solution)/shard_map/ppermute | solution.py:278
  53.5 55.4 %all-to-all-start.1 = ((bf16[8,384,128]{2,1,0:T(8,128)(2,1)}), bf16[8,384,128]{2,1,0:T(8,128)(2,1)S(1)}, u32[]{:S(2)}, u32[]{:S(2)}) async-start(bf16[8,384,128]{2,1,0:T(8,128)(2,1)} %chunk_products.4), calls=%async_computation.1 | async-start | bytes 1572864 | tf_op jit(solution)/shard_map/all_to_all | solution.py:324
  58.4 33.9 %collective-permute-start.9 = (bf16[4,1040,128]{2,1,0:T(8,128)(2,1)S(1)}, bf16[4,1040,128]{2,1,0:T(8,128)(2,1)S(1)}, u32[]{:S(2)}, u32[]{:S(2)}) collective-permute-start(bf16[4,1040,128]{2,1,0:T(8,128)(2,1)S(1)} %copy-done.1), channel_id=1, source_target_pairs={{0,1},{1,0},{2,3},{3,2},{4,5},{5,4},{6,7},{7,6},{8,9},{9,8},{10,11... | collective-permute-start | bytes 3194888 | tf_op jit(solution)/shard_map/ppermute | solution.py:305
  60.4 32.8 %collective-permute-start.10 = (bf16[48,64,128]{2,1,0:T(8,128)(2,1)}, bf16[48,64,128]{2,1,0:T(8,128)(2,1)S(1)}, u32[]{:S(2)}, u32[]{:S(2)}) collective-permute-start(bf16[48,64,128]{2,1,0:T(8,128)(2,1)} %get-tuple-element.35.refs_4_), channel_id=1, source_target_pairs={{0,8},{8,0},{16,24},{24,16},{1,9},{9,1},{17,25},{25,17},{2,10},{10... | collective-permute-start | bytes 2359304 | tf_op jit(solution)/shard_map/ppermute | solution.py:281
  60.4 32.8 %collective-permute-start.11 = (bf16[48,64,128]{2,1,0:T(8,128)(2,1)}, bf16[48,64,128]{2,1,0:T(8,128)(2,1)S(1)}, u32[]{:S(2)}, u32[]{:S(2)}) collective-permute-start(bf16[48,64,128]{2,1,0:T(8,128)(2,1)} %collective-permute-done.5.refs_6_), channel_id=1, source_target_pairs={{0,8},{8,0},{16,24},{24,16},{1,9},{9,1},{17,25},{25,17},{2,10},{10... | collective-permute-start | bytes 2359304 | tf_op jit(solution)/shard_map/ppermute | solution.py:281
  61.0 53.1 %collective-permute-start.8 = (bf16[48,64,128]{2,1,0:T(8,128)(2,1)}, bf16[48,64,128]{2,1,0:T(8,128)(2,1)}, u32[]{:S(2)}, u32[]{:S(2)}) collective-permute-start(bf16[48,64,128]{2,1,0:T(8,128)(2,1)} %get-tuple-element.37.refs_4_), channel_id=1, source_target_pairs={{0,16},{8,24},{16,0},{24,8},{1,17},{9,25},{17,1},{25,9},{2,18},{10... | collective-permute-start | bytes 2359304 | tf_op jit(solution)/shard_map/ppermute | solution.py:278
  108.9 25.9 %all-to-all-start.2 = ((bf16[8,384,128]{2,1,0:T(8,128)(2,1)}), bf16[8,384,128]{2,1,0:T(8,128)(2,1)S(1)}, u32[]{:S(2)}, u32[]{:S(2)}) async-start(bf16[8,384,128]{2,1,0:T(8,128)(2,1)} %chunk_products.5), calls=%async_computation.2 | async-start | bytes 1572864 | tf_op jit(solution)/shard_map/all_to_all | solution.py:324
  113.4 3.5 %collective-permute-start.13 = (bf16[4,1040,128]{2,1,0:T(8,128)(2,1)S(1)}, bf16[4,1040,128]{2,1,0:T(8,128)(2,1)S(1)}, u32[]{:S(2)}, u32[]{:S(2)}) collective-permute-start(bf16[4,1040,128]{2,1,0:T(8,128)(2,1)S(1)} %copy-done.1), channel_id=1, source_target_pairs={{0,8},{8,0},{16,24},{24,16},{1,9},{9,1},{17,25},{25,17},{2,10},{10... | collective-permute-start | bytes 3194888 | tf_op jit(solution)/shard_map/ppermute | solution.py:281
  113.4 4.4 %collective-permute-start.14 = (bf16[4,1040,128]{2,1,0:T(8,128)(2,1)}, bf16[4,1040,128]{2,1,0:T(8,128)(2,1)S(1)}, u32[]{:S(2)}, u32[]{:S(2)}) collective-permute-start(bf16[4,1040,128]{2,1,0:T(8,128)(2,1)} %copy-done.6), channel_id=1, source_target_pairs={{0,8},{8,0},{16,24},{24,16},{1,9},{9,1},{17,25},{25,17},{2,10},{10... | collective-permute-start | bytes 3194888 | tf_op jit(solution)/shard_map/ppermute | solution.py:281
  114.0 5.0 %collective-permute-start.15 = (bf16[48,64,128]{2,1,0:T(8,128)(2,1)}, bf16[48,64,128]{2,1,0:T(8,128)(2,1)S(1)}, u32[]{:S(2)}, u32[]{:S(2)}) collective-permute-start(bf16[48,64,128]{2,1,0:T(8,128)(2,1)} %get-tuple-element.37.refs_4_), channel_id=1, source_target_pairs={{0,8},{8,0},{16,24},{24,16},{1,9},{9,1},{17,25},{25,17},{2,10},{10... | collective-permute-start | bytes 2359304 | tf_op jit(solution)/shard_map/ppermute | solution.py:281
  114.0 6.1 %collective-permute-start.16 = (bf16[48,64,128]{2,1,0:T(8,128)(2,1)}, bf16[48,64,128]{2,1,0:T(8,128)(2,1)S(1)}, u32[]{:S(2)}, u32[]{:S(2)}) collective-permute-start(bf16[48,64,128]{2,1,0:T(8,128)(2,1)} %collective-permute-done.8.refs_6_), channel_id=1, source_target_pairs={{0,8},{8,0},{16,24},{24,16},{1,9},{9,1},{17,25},{25,17},{2,10},{10... | collective-permute-start | bytes 2359304 | tf_op jit(solution)/shard_map/ppermute | solution.py:281
  114.5 26.7 %collective-permute-start.12 = (bf16[48,64,128]{2,1,0:T(8,128)(2,1)}, bf16[48,64,128]{2,1,0:T(8,128)(2,1)}, u32[]{:S(2)}, u32[]{:S(2)}) collective-permute-start(bf16[48,64,128]{2,1,0:T(8,128)(2,1)} %get-tuple-element.40.refs_4_), channel_id=1, source_target_pairs={{0,16},{8,24},{16,0},{24,8},{1,17},{9,25},{17,1},{25,9},{2,18},{10... | collective-permute-start | bytes 2359304 | tf_op jit(solution)/shard_map/ppermute | solution.py:278
  134.8 26.8 %all-to-all-start.3 = ((bf16[8,384,128]{2,1,0:T(8,128)(2,1)}), bf16[8,384,128]{2,1,0:T(8,128)(2,1)S(1)}, u32[]{:S(2)}, u32[]{:S(2)}) async-start(bf16[8,384,128]{2,1,0:T(8,128)(2,1)} %chunk_products.6), calls=%async_computation.3 | async-start | bytes 1572864 | tf_op jit(solution)/shard_map/all_to_all | solution.py:324
  141.2 2.5 %collective-permute-start = (bf16[48,64,128]{2,1,0:T(8,128)(2,1)}, bf16[48,64,128]{2,1,0:T(8,128)(2,1)S(1)}, u32[]{:S(2)}, u32[]{:S(2)}) collective-permute-start(bf16[48,64,128]{2,1,0:T(8,128)(2,1)} %get-tuple-element.40.refs_4_), channel_id=1, source_target_pairs={{0,8},{8,0},{16,24},{24,16},{1,9},{9,1},{17,25},{25,17},{2,10},{10... | collective-permute-start | bytes 2359304 | tf_op jit(solution)/shard_map/ppermute | solution.py:281
  141.2 3.6 %collective-permute-start.17 = (bf16[48,64,128]{2,1,0:T(8,128)(2,1)}, bf16[48,64,128]{2,1,0:T(8,128)(2,1)S(1)}, u32[]{:S(2)}, u32[]{:S(2)}) collective-permute-start(bf16[48,64,128]{2,1,0:T(8,128)(2,1)} %collective-permute-done.12.refs_6_), channel_id=1, source_target_pairs={{0,8},{8,0},{16,24},{24,16},{1,9},{9,1},{17,25},{25,17},{2,10},{10... | collective-permute-start | bytes 2359304 | tf_op jit(solution)/shard_map/ppermute | solution.py:281
  161.6 24.4 %all-to-all-start = ((bf16[8,384,128]{2,1,0:T(8,128)(2,1)}), bf16[8,384,128]{2,1,0:T(8,128)(2,1)S(1)}, u32[]{:S(2)}, u32[]{:S(2)}) async-start(bf16[8,384,128]{2,1,0:T(8,128)(2,1)} %chunk_products.7), calls=%async_computation | async-start | bytes 1572864 | tf_op jit(solution)/shard_map/all_to_all | solution.py:324
  (22 other events, 122.7 us)

commit v6 on v5

--- a/solution.py
+++ b/solution.py
@@ -8,6 +8,8 @@
 from jax.sharding import PartitionSpec as P
 
 VMEM_WHOLE = 58 * 1024 * 1024
+VMEM_MOST = 36 * 1024 * 1024
+VMEM_PART = 20 * 1024 * 1024
 SMALL = pl.CostEstimate(flops=0, bytes_accessed=4096, transcendentals=0)
 
 
@@ -122,7 +124,7 @@
         ),
         out_shape=jax.ShapeDtypeStruct(out_shape, jnp.bfloat16),
         cost_estimate=SMALL,
-        compiler_params=pltpu.CompilerParams(vmem_limit_bytes=VMEM_WHOLE),
+        compiler_params=pltpu.CompilerParams(vmem_limit_bytes=VMEM_PART),
         name="chunk_products",
     )(slots, *[amplitudes.reshape(2, half, pairs, domain, domain)] * (2 * streams), *pieces)
     if split_rows:
@@ -142,7 +144,7 @@
         join_kernel,
         out_shape=jax.ShapeDtypeStruct(shape, pieces[0].dtype),
         cost_estimate=SMALL,
-        compiler_params=pltpu.CompilerParams(vmem_limit_bytes=VMEM_WHOLE),
+        compiler_params=pltpu.CompilerParams(vmem_limit_bytes=VMEM_PART),
         name="join",
     )(*pieces)
 
@@ -220,7 +222,7 @@
         ),
         out_shape=[jax.ShapeDtypeStruct((tall, size), kind) for tall, kind in zip(heights, kinds)],
         cost_estimate=SMALL,
-        compiler_params=pltpu.CompilerParams(vmem_limit_bytes=VMEM_WHOLE),
+        compiler_params=pltpu.CompilerParams(vmem_limit_bytes=VMEM_MOST),
         name="first_shares",
     )(positions, *chunks, *sources)
 
@@ -256,7 +258,7 @@
         out_shape=jax.ShapeDtypeStruct((2, height, size), jnp.bfloat16),
         scratch_shapes=[pltpu.VMEM((2 * height, depth), jnp.bfloat16)],
         cost_estimate=SMALL,
-        compiler_params=pltpu.CompilerParams(vmem_limit_bytes=VMEM_WHOLE),
+        compiler_params=pltpu.CompilerParams(vmem_limit_bytes=VMEM_PART),
         name="last_share",
     )(chunk, metric, one, two)
 
@@ -305,17 +307,16 @@
     beside = lax.ppermute(column, "aux", [(g, g ^ 1) for g in range(aux_count)])
     sources = [column, beside, to_mate(column), to_mate(beside)]
 
-    before_far = {1: parts}
-    before_products = {1: beside, 2: sources[2:]}
+    before_products = {1: column, 2: beside, 3: sources[2:]}
     products = []
     far_pieces, made = [], None
     for at in range(chunk_count):
         own = packed[at]
         if at:
-            own = after(own, [far_pieces, before_far.get(at, [])])
+            own = after(own, far_pieces)
         far_pieces = [to_far(own, shift) for shift in range(1, far_count)]
         if chunk_count > 1:
-            far_pieces = after(far_pieces, made if at else [packed[1:], column])
+            far_pieces = after(far_pieces, made if at else [packed[1:], parts[1::2]])
         pieces = []
         for piece in [packed[at]] + far_pieces:
             pieces += [piece, to_mate(piece)]

time: 197 us -> 210 us (1.066)
  local copies, waits for them, and re-layouts: 12.7 us -> 52.1 us
  Pallas kernels: 90.3 us -> 68.1 us
  waiting for transfers between devices: 58.7 us -> 52.7 us
    unnamed x52 -> x68, local copies, waits for them, and re-layouts: 9.02 us -> 49.5 us
    pallas_call x4, Pallas kernels: 55.4 us -> 41.7 us  [chunk_products(): pl.pallas_call(functools.partial(product_kernel, pairs, split_rows, strea...]
    all_to_all x4, waiting for transfers between devices: 4.4 us -> 0.01 us  [shards(): lax.all_to_all(made, 'aux', split_axis=0, concat_axis=0, tiled=True)]
    pallas_call x1, Pallas kernels: 9.04 us -> 5.64 us  [last_share(): pl.pallas_call(last_kernel, grid=(size // step,), in_specs=[pl.BlockSpec(...]
    pallas_call x1, Pallas kernels: 15.4 us -> 12.6 us  [first_shares(): pl.pallas_call(functools.partial(first_kernel, len(chunks), len(sources),...]
    pallas_call x1, Pallas kernels: 2.24 us -> 0.07 us  [join(): pl.pallas_call(join_kernel, out_shape=jax.ShapeDtypeStruct(shape, pieces[...]
  transfers between devices with their start and end apart: 22 -> 22, of which waited for: 11 -> 8; matrix products, arithmetic and copies ran while one was open for 2% -> 1% of each run, Pallas kernels for 39% -> 28%
where the time goes in v6:
time: 210 us; the launch traced here: 208 us
  Pallas kernels  68.1 us (32%)
  waiting for transfers between devices  52.7 us (25%)
  local copies, waits for them, and re-layouts  52.1 us (25%)
  starting transfers between devices  35.1 us (17%)
    unnamed x68, local copies, waits for them, and re-layouts  49.5 us
    pallas_call x4, Pallas kernels, chunk_products(): pl.pallas_call(functools.partial(product_kernel, pairs, split_rows, strea...  41.7 us
    ppermute x1, waiting for transfers between devices, shards(): beside = lax.ppermute(column, 'aux', [(g, g ^ 1) for g in range(aux_count)])  29.8 us
    all_to_all x4, starting transfers between devices, shards(): lax.all_to_all(made, 'aux', split_axis=0, concat_axis=0, tiled=True)  20.8 us
    ppermute x3, waiting for transfers between devices, shards(): parts.append(lax.ppermute(load, 'aux', moves))  16.5 us
    pallas_call x1, Pallas kernels, first_shares(): pl.pallas_call(functools.partial(first_kernel, len(chunks), len(sources),...  12.6 us
    pallas_call x2, Pallas kernels, pack_chunks(): pl.pallas_call(functools.partial(pack_kernel, width, first), grid=(orbita...  8.14 us
    ppermute x10, waiting for transfers between devices, to_mate(): return lax.ppermute(array, 'orb', [(g, g ^ 1) for g in range(orb_count)])  6.4 us
  transfers between devices with their start and end apart: 22, of which 8 were waited for; matrix products, arithmetic and copies ran while one was open for 1% of the time, Pallas kernels for 28%

profile of v6, /device:TPU:0, one launch (start us, length us, event | category | flops | bytes accessed | tf_op | source)
XLA Modules:
  0.0 208.4 jit_solution(15220209946828144181)
XLA Ops:
  0.0 4.0 %pack_chunks.3.refs_4_ = bf16[48,64,128]{2,1,0:T(8,128)(2,1)} custom-call(bf16[48,128,256]{2,1,0:T(8,128)(2,1)} %source.3), custom_call_target="tpu_custom_call" | custom-call | bytes 4096 | tf_op jit(solution)/shard_map/pack_chunks/pallas_call | solution.py:32
  4.0 3.0 %collective-permute-start.7 = (bf16[48,64,128]{2,1,0:T(8,128)(2,1)}, bf16[48,64,128]{2,1,0:T(8,128)(2,1)S(1)}, u32[]{:S(2)}, u32[]{:S(2)}) collective-permute-start(bf16[48,64,128]{2,1,0:T(8,128)(2,1)} %pack_chunks.3.refs_4_), channel_id=1, source_target_pairs={{0,16},{8,24},{16,0},{24,8},{1,17},{9,25},{17,1},{25,9},{2,18},{10... | collective-permute-start | bytes 2359304 | tf_op jit(solution)/shard_map/ppermute | solution.py:280
  7.3 3.7 %collective-permute-start.2 = (bf16[1040,128]{1,0:T(8,128)(2,1)S(1)}, bf16[1040,128]{1,0:T(8,128)(2,1)S(1)}, u32[]{:S(2)}, u32[]{:S(2)}) collective-permute-start(bf16[1040,128]{1,0:T(8,128)(2,1)S(1)} %pad_maximum_fusion.refs_0_), channel_id=1, source_target_pairs={{0,6},{1,7},{2,0},{3,1},{4,2},{5,3},{6,4},{7,5},{8,14},{9,15},{10,... | collective-permute-start | bytes 798728 | tf_op jit(solution)/shard_map/ppermute | solution.py:299
  12.0 4.2 %pack_chunks.2 = (bf16[48,64,128]{2,1,0:T(8,128)(2,1)}, bf16[48,64,128]{2,1,0:T(8,128)(2,1)}, bf16[48,64,128]{2,1,0:T(8,128)(2,1)}) custom-call(bf16[48,128,256]{2,1,0:T(8,128)(2,1)} %source.3), custom_call_target="tpu_custom_call" | custom-call | bytes 4096 | tf_op jit(solution)/shard_map/pack_chunks/pallas_call | solution.py:32
  18.5 14.8 %collective-permute-done.1.refs_2_ = bf16[1040,128]{1,0:T(8,128)(2,1)S(1)} collective-permute-done((bf16[1040,128]{1,0:T(8,128)(2,1)S(1)}, bf16[1040,128]{1,0:T(8,128)(2,1)S(1)}, u32[]{:S(2)}, u32[]{:S(2)}) %collective-permute-start.1) | collective-permute-done | bytes 266272 | tf_op jit(solution)/shard_map/ppermute | solution.py:299
  37.2 6.4 %copy-done.1 = bf16[48,12,128,128]{3,2,1,0:T(8,128)(2,1)S(1)} copy-done((bf16[48,12,128,128]{3,2,1,0:T(8,128)(2,1)S(1)}, bf16[48,12,128,128]{3,2,1,0:T(8,128)(2,1)}, u32[]{:S(2)}) %copy-start.1) | copy-done | bytes 18874392
  44.7 10.4 %chunk_products.4 = bf16[8,384,128]{2,1,0:T(8,128)(2,1)} custom-call(s32[576]{0:T(1024)S(1)} %reshape.24.slots, bf16[2,24,12,128,128]{4,3,2,1,0:T(8,128)(2,1)S(1)} %bitcast.17, bf16[2,24,12,128,128]{4,3,2,1,0:T(8,128)(2,1)S(1)} %bitcast.18, bf16[2,24,12,128,128]{4,3,2,1,0:T(8,128)(2,1)S(1)} %bitcast.19, bf16[2,24,12,128,128]{4,3,2,1,0:T(8,128)(2,1)S(1)} %bitcast.20, ...), custom_call_target="tpu_custom_call" | custom-call | bytes 4096 | tf_op jit(solution)/shard_map/chunk_products/pallas_call | solution.py:108
  55.1 4.3 %all-to-all-start.1 = ((bf16[8,384,128]{2,1,0:T(8,128)(2,1)}), bf16[8,384,128]{2,1,0:T(8,128)(2,1)S(1)}, u32[]{:S(2)}, u32[]{:S(2)}) async-start(bf16[8,384,128]{2,1,0:T(8,128)(2,1)} %chunk_products.4), calls=%async_computation.1 | async-start | bytes 1572864 | tf_op jit(solution)/shard_map/all_to_all | solution.py:325
  63.7 6.4 %copy-done.2 = bf16[48,12,128,128]{3,2,1,0:T(8,128)(2,1)S(1)} copy-done((bf16[48,12,128,128]{3,2,1,0:T(8,128)(2,1)S(1)}, bf16[48,12,128,128]{3,2,1,0:T(8,128)(2,1)}, u32[]{:S(2)}) %copy-start.2) | copy-done | bytes 18874392
  70.1 10.4 %chunk_products.5 = bf16[8,384,128]{2,1,0:T(8,128)(2,1)} custom-call(s32[576]{0:T(1024)S(1)} %reshape.24.slots, bf16[2,24,12,128,128]{4,3,2,1,0:T(8,128)(2,1)S(1)} %bitcast.21, bf16[2,24,12,128,128]{4,3,2,1,0:T(8,128)(2,1)S(1)} %bitcast.22, bf16[2,24,12,128,128]{4,3,2,1,0:T(8,128)(2,1)S(1)} %bitcast.23, bf16[2,24,12,128,128]{4,3,2,1,0:T(8,128)(2,1)S(1)} %bitcast.24, ...), custom_call_target="tpu_custom_call" | custom-call | bytes 4096 | tf_op jit(solution)/shard_map/chunk_products/pallas_call | solution.py:108
  80.5 5.9 %all-to-all-start.2 = ((bf16[8,384,128]{2,1,0:T(8,128)(2,1)}), bf16[8,384,128]{2,1,0:T(8,128)(2,1)S(1)}, u32[]{:S(2)}, u32[]{:S(2)}) async-start(bf16[8,384,128]{2,1,0:T(8,128)(2,1)} %chunk_products.5), calls=%async_computation.2 | async-start | bytes 1572864 | tf_op jit(solution)/shard_map/all_to_all | solution.py:325
  86.4 2.0 collective-permute-start.4
  90.2 29.8 %collective-permute-done.4.refs_4_ = bf16[4,1040,128]{2,1,0:T(8,128)(2,1)S(1)} collective-permute-done((bf16[4,1040,128]{2,1,0:T(8,128)(2,1)S(1)}, bf16[4,1040,128]{2,1,0:T(8,128)(2,1)S(1)}, u32[]{:S(2)}, u32[]{:S(2)}) %collective-permute-start.4) | collective-permute-done | bytes 1064992 | tf_op jit(solution)/shard_map/ppermute | solution.py:307
  121.0 6.4 %copy-done.3 = bf16[48,12,128,128]{3,2,1,0:T(8,128)(2,1)S(1)} copy-done((bf16[48,12,128,128]{3,2,1,0:T(8,128)(2,1)S(1)}, bf16[48,12,128,128]{3,2,1,0:T(8,128)(2,1)}, u32[]{:S(2)}) %copy-start.3) | copy-done | bytes 18874392
  127.3 10.5 %chunk_products.6 = bf16[8,384,128]{2,1,0:T(8,128)(2,1)} custom-call(s32[576]{0:T(1024)S(1)} %reshape.24.slots, bf16[2,24,12,128,128]{4,3,2,1,0:T(8,128)(2,1)S(1)} %bitcast.25, bf16[2,24,12,128,128]{4,3,2,1,0:T(8,128)(2,1)S(1)} %bitcast.26, bf16[2,24,12,128,128]{4,3,2,1,0:T(8,128)(2,1)S(1)} %bitcast.27, bf16[2,24,12,128,128]{4,3,2,1,0:T(8,128)(2,1)S(1)} %bitcast.28, ...), custom_call_target="tpu_custom_call" | custom-call | bytes 4096 | tf_op jit(solution)/shard_map/chunk_products/pallas_call | solution.py:108
  137.9 4.6 %all-to-all-start.3 = ((bf16[8,384,128]{2,1,0:T(8,128)(2,1)}), bf16[8,384,128]{2,1,0:T(8,128)(2,1)}, u32[]{:S(2)}, u32[]{:S(2)}) async-start(bf16[8,384,128]{2,1,0:T(8,128)(2,1)} %chunk_products.6), calls=%async_computation.3 | async-start | bytes 1572864 | tf_op jit(solution)/shard_map/all_to_all | solution.py:325
  143.5 2.4 %collective-permute-done.3.refs_5_ = bf16[4,1040,128]{2,1,0:T(8,128)(2,1)S(1)} collective-permute-done((bf16[4,1040,128]{2,1,0:T(8,128)(2,1)S(1)}, bf16[4,1040,128]{2,1,0:T(8,128)(2,1)S(1)}, u32[]{:S(2)}, u32[]{:S(2)}) %collective-permute-start.3) | collective-permute-done | bytes 1064992 | tf_op jit(solution)/shard_map/ppermute | solution.py:283
  149.1 6.4 %copy-done.4 = bf16[48,12,128,128]{3,2,1,0:T(8,128)(2,1)S(1)} copy-done((bf16[48,12,128,128]{3,2,1,0:T(8,128)(2,1)S(1)}, bf16[48,12,128,128]{3,2,1,0:T(8,128)(2,1)}, u32[]{:S(2)}) %copy-start.4) | copy-done | bytes 18874392
  156.6 10.4 %chunk_products.7 = bf16[8,384,128]{2,1,0:T(8,128)(2,1)} custom-call(s32[576]{0:T(1024)S(1)} %reshape.24.slots, bf16[2,24,12,128,128]{4,3,2,1,0:T(8,128)(2,1)S(1)} %bitcast.29, bf16[2,24,12,128,128]{4,3,2,1,0:T(8,128)(2,1)S(1)} %bitcast.30, bf16[2,24,12,128,128]{4,3,2,1,0:T(8,128)(2,1)S(1)} %bitcast.31, bf16[2,24,12,128,128]{4,3,2,1,0:T(8,128)(2,1)S(1)} %bitcast.32, ...), custom_call_target="tpu_custom_call" | custom-call | bytes 4096 | tf_op jit(solution)/shard_map/chunk_products/pallas_call | solution.py:108
  167.0 6.0 %all-to-all-start = ((bf16[8,384,128]{2,1,0:T(8,128)(2,1)}), bf16[8,384,128]{2,1,0:T(8,128)(2,1)S(1)}, u32[]{:S(2)}, u32[]{:S(2)}) async-start(bf16[8,384,128]{2,1,0:T(8,128)(2,1)} %chunk_products.7), calls=%async_computation | async-start | bytes 1572864 | tf_op jit(solution)/shard_map/all_to_all | solution.py:325
  180.1 12.6 %first_shares.1 = (f32[384,2048]{1,0:T(8,128)S(1)}, f32[384,2048]{1,0:T(8,128)S(1)}, bf16[512,2048]{1,0:T(8,128)(2,1)S(1)}) custom-call(s32[256]{0:T(256)S(1)} %reshape.29.positions, bf16[8,384,128]{2,1,0:T(8,128)(2,1)S(1)} %all-to-all-done.1.refs_0_, bf16[8,384,128]{2,1,0:T(8,128)(2,1)S(1)} %copy-done.11, bf16[8,384,128]{2,1,0:T(8,128)(2,1)} %all-to-all-done.3.refs_2_, ...), custom_call_target="tpu_custom_call" | custom-call | bytes 4096 | tf_op jit(solution)/shard_map/first_shares/pallas_call | solution.py:211
  197.4 1.9 copy-done.7
  199.3 1.9 copy-done.9
  202.8 5.6 %last_share.1 = bf16[2,384,2048]{2,1,0:T(8,128)(2,1)} custom-call(bf16[8,384,128]{2,1,0:T(8,128)(2,1)S(1)} %all-to-all-done.chunk, bf16[512,2048]{1,0:T(8,128)(2,1)S(1)} %copy-done.13, f32[384,2048]{1,0:T(8,128)S(1)} %copy-done.7, f32[384,2048]{1,0:T(8,128)S(1)} %copy-done.9), custom_call_target="tpu_custom_call" | custom-call | bytes 4096 | tf_op jit(solution)/shard_map/last_share/pallas_call | solution.py:248
  (112 shorter events, 34.4 us)
Async XLA Ops:
  0.0 35.3 %copy-start.30 = (s32[48,12]{0,1:T(8,128)S(1)}, s32[48,12]{0,1:T(8,128)}, u32[]{:S(2)}) copy-start(s32[48,12]{0,1:T(8,128)} %param.7) | copy-start | bytes 6916
  4.0 33.2 %copy-start.5 = (bf16[48,64,128]{2,1,0:T(8,128)(2,1)S(1)}, bf16[48,64,128]{2,1,0:T(8,128)(2,1)}, u32[]{:S(2)}) copy-start(bf16[48,64,128]{2,1,0:T(8,128)(2,1)} %pack_chunks.3.refs_4_) | copy-start | bytes 2359300
  4.0 30.8 %collective-permute-start.7 = (bf16[48,64,128]{2,1,0:T(8,128)(2,1)}, bf16[48,64,128]{2,1,0:T(8,128)(2,1)S(1)}, u32[]{:S(2)}, u32[]{:S(2)}) collective-permute-start(bf16[48,64,128]{2,1,0:T(8,128)(2,1)} %pack_chunks.3.refs_4_), channel_id=1, source_target_pairs={{0,16},{8,24},{16,0},{24,8},{1,17},{9,25},{17,1},{25,9},{2,18},{10... | collective-permute-start | bytes 2359304 | tf_op jit(solution)/shard_map/ppermute | solution.py:280
  7.3 10.5 %collective-permute-start.2 = (bf16[1040,128]{1,0:T(8,128)(2,1)S(1)}, bf16[1040,128]{1,0:T(8,128)(2,1)S(1)}, u32[]{:S(2)}, u32[]{:S(2)}) collective-permute-start(bf16[1040,128]{1,0:T(8,128)(2,1)S(1)} %pad_maximum_fusion.refs_0_), channel_id=1, source_target_pairs={{0,6},{1,7},{2,0},{3,1},{4,2},{5,3},{6,4},{7,5},{8,14},{9,15},{10,... | collective-permute-start | bytes 798728 | tf_op jit(solution)/shard_map/ppermute | solution.py:299
  10.9 22.4 %collective-permute-start.1 = (bf16[1040,128]{1,0:T(8,128)(2,1)S(1)}, bf16[1040,128]{1,0:T(8,128)(2,1)S(1)}, u32[]{:S(2)}, u32[]{:S(2)}) collective-permute-start(bf16[1040,128]{1,0:T(8,128)(2,1)S(1)} %pad_maximum_fusion.refs_0_), channel_id=1, source_target_pairs={{0,4},{1,5},{2,6},{3,7},{4,0},{5,1},{6,2},{7,3},{8,12},{9,13},{10,... | collective-permute-start | bytes 798728 | tf_op jit(solution)/shard_map/ppermute | solution.py:299
  11.0 23.1 %collective-permute-start = (bf16[1040,128]{1,0:T(8,128)(2,1)S(1)}, bf16[1040,128]{1,0:T(8,128)(2,1)S(1)}, u32[]{:S(2)}, u32[]{:S(2)}) collective-permute-start(bf16[1040,128]{1,0:T(8,128)(2,1)S(1)} %pad_maximum_fusion.refs_0_), channel_id=1, source_target_pairs={{0,2},{1,3},{2,4},{3,5},{4,6},{5,7},{6,0},{7,1},{8,10},{9,11},{10,... | collective-permute-start | bytes 798728 | tf_op jit(solution)/shard_map/ppermute | solution.py:299
  12.0 23.5 %collective-permute-start.9 = (bf16[48,64,128]{2,1,0:T(8,128)(2,1)}, bf16[48,64,128]{2,1,0:T(8,128)(2,1)S(1)}, u32[]{:S(2)}, u32[]{:S(2)}) collective-permute-start(bf16[48,64,128]{2,1,0:T(8,128)(2,1)} %pack_chunks.3.refs_4_), channel_id=1, source_target_pairs={{0,8},{8,0},{16,24},{24,16},{1,9},{9,1},{17,25},{25,17},{2,10},{10... | collective-permute-start | bytes 2359304 | tf_op jit(solution)/shard_map/ppermute | solution.py:283
  34.8 2.4 %collective-permute-start.10 = (bf16[48,64,128]{2,1,0:T(8,128)(2,1)S(1)}, bf16[48,64,128]{2,1,0:T(8,128)(2,1)}, u32[]{:S(2)}, u32[]{:S(2)}) collective-permute-start(bf16[48,64,128]{2,1,0:T(8,128)(2,1)S(1)} %collective-permute-done.7.refs_6_), channel_id=1, source_target_pairs={{0,8},{8,0},{16,24},{24,16},{1,9},{9,1},{17,25},{25,17},{2,10},{10... | collective-permute-start | bytes 2359304 | tf_op jit(solution)/shard_map/ppermute | solution.py:283
  34.8 24.8 %collective-permute-start.8 = (bf16[48,64,128]{2,1,0:T(8,128)(2,1)}, bf16[48,64,128]{2,1,0:T(8,128)(2,1)}, u32[]{:S(2)}, u32[]{:S(2)}) collective-permute-start(bf16[48,64,128]{2,1,0:T(8,128)(2,1)} %get-tuple-element.37.refs_4_), channel_id=1, source_target_pairs={{0,16},{8,24},{16,0},{24,8},{1,17},{9,25},{17,1},{25,9},{2,18},{10... | collective-permute-start | bytes 2359304 | tf_op jit(solution)/shard_map/ppermute | solution.py:280
  55.1 25.3 %all-to-all-start.1 = ((bf16[8,384,128]{2,1,0:T(8,128)(2,1)}), bf16[8,384,128]{2,1,0:T(8,128)(2,1)S(1)}, u32[]{:S(2)}, u32[]{:S(2)}) async-start(bf16[8,384,128]{2,1,0:T(8,128)(2,1)} %chunk_products.4), calls=%async_computation.1 | async-start | bytes 1572864 | tf_op jit(solution)/shard_map/all_to_all | solution.py:325
  59.4 4.3 %collective-permute-start.12 = (bf16[48,64,128]{2,1,0:T(8,128)(2,1)S(1)}, bf16[48,64,128]{2,1,0:T(8,128)(2,1)S(1)}, u32[]{:S(2)}, u32[]{:S(2)}) collective-permute-start(bf16[48,64,128]{2,1,0:T(8,128)(2,1)S(1)} %copy-done.21), channel_id=1, source_target_pairs={{0,8},{8,0},{16,24},{24,16},{1,9},{9,1},{17,25},{25,17},{2,10},{10... | collective-permute-start | bytes 2359304 | tf_op jit(solution)/shard_map/ppermute | solution.py:283
  59.5 4.2 %collective-permute-start.13 = (bf16[48,64,128]{2,1,0:T(8,128)(2,1)}, bf16[48,64,128]{2,1,0:T(8,128)(2,1)S(1)}, u32[]{:S(2)}, u32[]{:S(2)}) collective-permute-start(bf16[48,64,128]{2,1,0:T(8,128)(2,1)} %collective-permute-done.8.refs_6_), channel_id=1, source_target_pairs={{0,8},{8,0},{16,24},{24,16},{1,9},{9,1},{17,25},{25,17},{2,10},{10... | collective-permute-start | bytes 2359304 | tf_op jit(solution)/shard_map/ppermute | solution.py:283
  60.0 28.4 %collective-permute-start.11 = (bf16[48,64,128]{2,1,0:T(8,128)(2,1)}, bf16[48,64,128]{2,1,0:T(8,128)(2,1)}, u32[]{:S(2)}, u32[]{:S(2)}) collective-permute-start(bf16[48,64,128]{2,1,0:T(8,128)(2,1)} %get-tuple-element.39.refs_4_), channel_id=1, source_target_pairs={{0,16},{8,24},{16,0},{24,8},{1,17},{9,25},{17,1},{25,9},{2,18},{10... | collective-permute-start | bytes 2359304 | tf_op jit(solution)/shard_map/ppermute | solution.py:280
  80.5 57.4 %all-to-all-start.2 = ((bf16[8,384,128]{2,1,0:T(8,128)(2,1)}), bf16[8,384,128]{2,1,0:T(8,128)(2,1)S(1)}, u32[]{:S(2)}, u32[]{:S(2)}) async-start(bf16[8,384,128]{2,1,0:T(8,128)(2,1)} %chunk_products.5), calls=%async_computation.2 | async-start | bytes 1572864 | tf_op jit(solution)/shard_map/all_to_all | solution.py:325
  86.4 33.6 %collective-permute-start.4 = (bf16[4,1040,128]{2,1,0:T(8,128)(2,1)S(1)}, bf16[4,1040,128]{2,1,0:T(8,128)(2,1)S(1)}, u32[]{:S(2)}, u32[]{:S(2)}) collective-permute-start(bf16[4,1040,128]{2,1,0:T(8,128)(2,1)S(1)} %join.1.refs_3_), channel_id=1, source_target_pairs={{0,1},{1,0},{2,3},{3,2},{4,5},{5,4},{6,7},{7,6},{8,9},{9,8},{10,11... | collective-permute-start | bytes 3194888 | tf_op jit(solution)/shard_map/ppermute | solution.py:307
  88.4 31.5 %collective-permute-start.15 = (bf16[48,64,128]{2,1,0:T(8,128)(2,1)}, bf16[48,64,128]{2,1,0:T(8,128)(2,1)S(1)}, u32[]{:S(2)}, u32[]{:S(2)}) collective-permute-start(bf16[48,64,128]{2,1,0:T(8,128)(2,1)} %get-tuple-element.39.refs_4_), channel_id=1, source_target_pairs={{0,8},{8,0},{16,24},{24,16},{1,9},{9,1},{17,25},{25,17},{2,10},{10... | collective-permute-start | bytes 2359304 | tf_op jit(solution)/shard_map/ppermute | solution.py:283
  88.4 32.5 %collective-permute-start.16 = (bf16[48,64,128]{2,1,0:T(8,128)(2,1)}, bf16[48,64,128]{2,1,0:T(8,128)(2,1)S(1)}, u32[]{:S(2)}, u32[]{:S(2)}) collective-permute-start(bf16[48,64,128]{2,1,0:T(8,128)(2,1)} %collective-permute-done.11.refs_6_), channel_id=1, source_target_pairs={{0,8},{8,0},{16,24},{24,16},{1,9},{9,1},{17,25},{25,17},{2,10},{10... | collective-permute-start | bytes 2359304 | tf_op jit(solution)/shard_map/ppermute | solution.py:283
  89.0 54.1 %collective-permute-start.14 = (bf16[48,64,128]{2,1,0:T(8,128)(2,1)}, bf16[48,64,128]{2,1,0:T(8,128)(2,1)}, u32[]{:S(2)}, u32[]{:S(2)}) collective-permute-start(bf16[48,64,128]{2,1,0:T(8,128)(2,1)} %get-tuple-element.42.refs_4_), channel_id=1, source_target_pairs={{0,16},{8,24},{16,0},{24,8},{1,17},{9,25},{17,1},{25,9},{2,18},{10... | collective-permute-start | bytes 2359304 | tf_op jit(solution)/shard_map/ppermute | solution.py:280
  137.9 29.1 %all-to-all-start.3 = ((bf16[8,384,128]{2,1,0:T(8,128)(2,1)}), bf16[8,384,128]{2,1,0:T(8,128)(2,1)}, u32[]{:S(2)}, u32[]{:S(2)}) async-start(bf16[8,384,128]{2,1,0:T(8,128)(2,1)} %chunk_products.6), calls=%async_computation.3 | async-start | bytes 1572864 | tf_op jit(solution)/shard_map/all_to_all | solution.py:325
  142.4 3.5 %collective-permute-start.3 = (bf16[4,1040,128]{2,1,0:T(8,128)(2,1)S(1)}, bf16[4,1040,128]{2,1,0:T(8,128)(2,1)S(1)}, u32[]{:S(2)}, u32[]{:S(2)}) collective-permute-start(bf16[4,1040,128]{2,1,0:T(8,128)(2,1)S(1)} %join.1.refs_3_), channel_id=1, source_target_pairs={{0,8},{8,0},{16,24},{24,16},{1,9},{9,1},{17,25},{25,17},{2,10},{10... | collective-permute-start | bytes 3194888 | tf_op jit(solution)/shard_map/ppermute | solution.py:283
  142.4 4.4 %collective-permute-start.5 = (bf16[4,1040,128]{2,1,0:T(8,128)(2,1)}, bf16[4,1040,128]{2,1,0:T(8,128)(2,1)S(1)}, u32[]{:S(2)}, u32[]{:S(2)}) collective-permute-start(bf16[4,1040,128]{2,1,0:T(8,128)(2,1)} %copy-done.14), channel_id=1, source_target_pairs={{0,8},{8,0},{16,24},{24,16},{1,9},{9,1},{17,25},{25,17},{2,10},{10... | collective-permute-start | bytes 3194888 | tf_op jit(solution)/shard_map/ppermute | solution.py:283
  142.9 5.0 %collective-permute-start.6 = (bf16[48,64,128]{2,1,0:T(8,128)(2,1)}, bf16[48,64,128]{2,1,0:T(8,128)(2,1)S(1)}, u32[]{:S(2)}, u32[]{:S(2)}) collective-permute-start(bf16[48,64,128]{2,1,0:T(8,128)(2,1)} %get-tuple-element.42.refs_4_), channel_id=1, source_target_pairs={{0,8},{8,0},{16,24},{24,16},{1,9},{9,1},{17,25},{25,17},{2,10},{10... | collective-permute-start | bytes 2359304 | tf_op jit(solution)/shard_map/ppermute | solution.py:283
  143.0 6.1 %collective-permute-start.17 = (bf16[48,64,128]{2,1,0:T(8,128)(2,1)}, bf16[48,64,128]{2,1,0:T(8,128)(2,1)S(1)}, u32[]{:S(2)}, u32[]{:S(2)}) collective-permute-start(bf16[48,64,128]{2,1,0:T(8,128)(2,1)} %collective-permute-done.14.refs_6_), channel_id=1, source_target_pairs={{0,8},{8,0},{16,24},{24,16},{1,9},{9,1},{17,25},{25,17},{2,10},{10... | collective-permute-start | bytes 2359304 | tf_op jit(solution)/shard_map/ppermute | solution.py:283
  167.0 30.4 %all-to-all-start = ((bf16[8,384,128]{2,1,0:T(8,128)(2,1)}), bf16[8,384,128]{2,1,0:T(8,128)(2,1)S(1)}, u32[]{:S(2)}, u32[]{:S(2)}) async-start(bf16[8,384,128]{2,1,0:T(8,128)(2,1)} %chunk_products.7), calls=%async_computation | async-start | bytes 1572864 | tf_op jit(solution)/shard_map/all_to_all | solution.py:325
  (30 other events, 110.7 us)

commit v7 on v6

--- a/solution.py
+++ b/solution.py
@@ -8,9 +8,10 @@
 from jax.sharding import PartitionSpec as P
 
 VMEM_WHOLE = 58 * 1024 * 1024
-VMEM_MOST = 36 * 1024 * 1024
-VMEM_PART = 20 * 1024 * 1024
+VMEM_MOST = 44 * 1024 * 1024
+VMEM_PART = 44 * 1024 * 1024
 SMALL = pl.CostEstimate(flops=0, bytes_accessed=4096, transcendentals=0)
+LARGE = pl.CostEstimate(flops=40_000_000_000, bytes_accessed=4096, transcendentals=0)
 
 
 def largest_divisor(total, most):
@@ -91,7 +92,7 @@
             out[q] = both
 
 
-def chunk_products(slots, amplitudes, pieces, owners):
+def chunk_products(slots, amplitudes, pieces, owners, cost):
     orbitals, pairs, domain, _ = amplitudes.shape
     group, half_domain, lanes = pieces[0].shape
     total = group * len(pieces)
@@ -123,7 +124,7 @@
             ],
         ),
         out_shape=jax.ShapeDtypeStruct(out_shape, jnp.bfloat16),
-        cost_estimate=SMALL,
+        cost_estimate=cost,
         compiler_params=pltpu.CompilerParams(vmem_limit_bytes=VMEM_PART),
         name="chunk_products",
     )(slots, *[amplitudes.reshape(2, half, pairs, domain, domain)] * (2 * streams), *pieces)
@@ -301,7 +302,7 @@
     packed = list(pack_chunks(factors, width, 0, 1))
     if chunk_count > 1:
         packed += pack_chunks(factors, width, 1, chunk_count - 1)
-        parts = after(parts, packed[1:])
+        parts = [after(part, packed[1:]) for part in parts]
 
     column = join(parts)
     beside = lax.ppermute(column, "aux", [(g, g ^ 1) for g in range(aux_count)])
@@ -321,7 +322,7 @@
         for piece in [packed[at]] + far_pieces:
             pieces += [piece, to_mate(piece)]
         places = after(slots, before_products[at]) if at in before_products else slots
-        made = chunk_products(places, amplitudes, pieces, aux_count)
+        made = chunk_products(places, amplitudes, pieces, aux_count, LARGE if at < 2 else SMALL)
         products.append(lax.all_to_all(made, "aux", split_axis=0, concat_axis=0, tiled=True))
 
     positions = jnp.concatenate([source[:, half_tiles * span, : 2 * half_tiles] for source in sources])

time: 210 us -> 204 us (0.971)
  local copies, waits for them, and re-layouts: 52.1 us -> 20.3 us
  waiting for transfers between devices: 52.7 us -> 64.5 us
  Pallas kernels: 68.1 us -> 79.6 us
  starting transfers between devices: 35.1 us -> 38.1 us
    unnamed x68 -> x42, local copies, waits for them, and re-layouts: 49.5 us -> 17.7 us
    pallas_call x4, Pallas kernels: 41.7 us -> 52.5 us  [chunk_products(): pl.pallas_call(functools.partial(product_kernel, pairs, split_rows, strea...]
    ppermute x4, waiting for transfers between devices: 0.01 us -> 6.38 us  [to_far(): return lax.ppermute(array, 'orb', moves)]
    all_to_all x4, waiting for transfers between devices: 0.01 us -> 4.11 us  [shards(): lax.all_to_all(made, 'aux', split_axis=0, concat_axis=0, tiled=True)]
    ppermute x3, waiting for transfers between devices: 16.5 us -> 20.6 us  [shards(): parts.append(lax.ppermute(load, 'aux', moves))]
    ppermute x10, waiting for transfers between devices: 6.4 us -> 3.78 us  [to_mate(): return lax.ppermute(array, 'orb', [(g, g ^ 1) for g in range(orb_count)])]
    ppermute x4, starting transfers between devices: 5.5 us -> 7.74 us  [to_far(): return lax.ppermute(array, 'orb', moves)]
  transfers between devices with their start and end apart: 22 -> 22, of which waited for: 8 -> 11; matrix products, arithmetic and copies ran while one was open for 1% -> 1% of each run, Pallas kernels for 28% -> 34%
where the time goes in v7:
time: 204 us; the launch traced here: 203 us
  Pallas kernels  79.6 us (39%)
  waiting for transfers between devices  64.5 us (32%)
  starting transfers between devices  38.1 us (19%)
  local copies, waits for them, and re-layouts  20.3 us (10%)
    pallas_call x4, Pallas kernels, chunk_products(): pl.pallas_call(functools.partial(product_kernel, pairs, split_rows, strea...  52.5 us
    ppermute x1, waiting for transfers between devices, shards(): beside = lax.ppermute(column, 'aux', [(g, g ^ 1) for g in range(aux_count)])  29.7 us
    ppermute x3, waiting for transfers between devices, shards(): parts.append(lax.ppermute(load, 'aux', moves))  20.6 us
    all_to_all x4, starting transfers between devices, shards(): lax.all_to_all(made, 'aux', split_axis=0, concat_axis=0, tiled=True)  19.9 us
    unnamed x42, local copies, waits for them, and re-layouts  17.7 us
    pallas_call x1, Pallas kernels, first_shares(): pl.pallas_call(functools.partial(first_kernel, len(chunks), len(sources),...  13.1 us
    pallas_call x2, Pallas kernels, pack_chunks(): pl.pallas_call(functools.partial(pack_kernel, width, first), grid=(orbita...  8.18 us
    ppermute x4, starting transfers between devices, to_far(): return lax.ppermute(array, 'orb', moves)  7.74 us
  transfers between devices with their start and end apart: 22, of which 11 were waited for; matrix products, arithmetic and copies ran while one was open for 1% of the time, Pallas kernels for 34%

profile of v7, /device:TPU:0, one launch (start us, length us, event | category | flops | bytes accessed | tf_op | source)
XLA Modules:
  0.0 202.9 jit_solution(2028206006031653711)
XLA Ops:
  0.0 4.0 %pack_chunks.3.refs_4_ = bf16[48,64,128]{2,1,0:T(8,128)(2,1)} custom-call(bf16[48,128,256]{2,1,0:T(8,128)(2,1)} %source.3), custom_call_target="tpu_custom_call" | custom-call | bytes 4096 | tf_op jit(solution)/shard_map/pack_chunks/pallas_call | solution.py:33
  4.0 3.0 %collective-permute-start.7 = (bf16[48,64,128]{2,1,0:T(8,128)(2,1)}, bf16[48,64,128]{2,1,0:T(8,128)(2,1)}, u32[]{:S(2)}, u32[]{:S(2)}) collective-permute-start(bf16[48,64,128]{2,1,0:T(8,128)(2,1)} %pack_chunks.3.refs_4_), channel_id=1, source_target_pairs={{0,16},{8,24},{16,0},{24,8},{1,17},{9,25},{17,1},{25,9},{2,18},{10... | collective-permute-start | bytes 2359304 | tf_op jit(solution)/shard_map/ppermute | solution.py:281
  7.3 3.7 %collective-permute-start.2 = (bf16[1040,128]{1,0:T(8,128)(2,1)S(1)}, bf16[1040,128]{1,0:T(8,128)(2,1)S(1)}, u32[]{:S(2)}, u32[]{:S(2)}) collective-permute-start(bf16[1040,128]{1,0:T(8,128)(2,1)S(1)} %pad_maximum_fusion.refs_0_), channel_id=1, source_target_pairs={{0,6},{1,7},{2,0},{3,1},{4,2},{5,3},{6,4},{7,5},{8,14},{9,15},{10,... | collective-permute-start | bytes 798728 | tf_op jit(solution)/shard_map/ppermute | solution.py:300
  11.0 4.2 %pack_chunks.2 = (bf16[48,64,128]{2,1,0:T(8,128)(2,1)}, bf16[48,64,128]{2,1,0:T(8,128)(2,1)}, bf16[48,64,128]{2,1,0:T(8,128)(2,1)}) custom-call(bf16[48,128,256]{2,1,0:T(8,128)(2,1)} %source.3), custom_call_target="tpu_custom_call" | custom-call | bytes 4096 | tf_op jit(solution)/shard_map/pack_chunks/pallas_call | solution.py:33
  15.2 2.6 %collective-permute-done.2.refs_3_ = bf16[1040,128]{1,0:T(8,128)(2,1)S(1)} collective-permute-done((bf16[1040,128]{1,0:T(8,128)(2,1)S(1)}, bf16[1040,128]{1,0:T(8,128)(2,1)S(1)}, u32[]{:S(2)}, u32[]{:S(2)}) %collective-permute-start.2) | collective-permute-done | bytes 266272 | tf_op jit(solution)/shard_map/ppermute | solution.py:300
  17.8 5.1 %collective-permute-done.refs_1_ = bf16[1040,128]{1,0:T(8,128)(2,1)S(1)} collective-permute-done((bf16[1040,128]{1,0:T(8,128)(2,1)S(1)}, bf16[1040,128]{1,0:T(8,128)(2,1)S(1)}, u32[]{:S(2)}, u32[]{:S(2)}) %collective-permute-start) | collective-permute-done | bytes 266272 | tf_op jit(solution)/shard_map/ppermute | solution.py:300
  22.9 1.9 collective-permute-done.7.refs_6_
  27.5 13.5 %chunk_products.4 = bf16[8,384,128]{2,1,0:T(8,128)(2,1)} custom-call(s32[576]{0:T(1024)S(1)} %reshape.24.slots, bf16[2,24,12,128,128]{4,3,2,1,0:T(8,128)(2,1)} %bitcast.17, bf16[2,24,12,128,128]{4,3,2,1,0:T(8,128)(2,1)} %bitcast.18, bf16[2,24,12,128,128]{4,3,2,1,0:T(8,128)(2,1)} %bitcast.19, bf16[2,24,12,128,128]{4,3,2,1,0:T(8,128)(2,1)} %bitcast.20, ...), custom_call_target="tpu_custom_call" | custom-call | flops 40000000000 | bytes 4096 | tf_op jit(solution)/shard_map/chunk_products/pallas_call | solution.py:109
  41.0 4.4 %collective-permute-done.8.refs_6_ = bf16[48,64,128]{2,1,0:T(8,128)(2,1)} collective-permute-done((bf16[48,64,128]{2,1,0:T(8,128)(2,1)}, bf16[48,64,128]{2,1,0:T(8,128)(2,1)}, u32[]{:S(2)}, u32[]{:S(2)}) %collective-permute-start.8) | collective-permute-done | bytes 786464 | tf_op jit(solution)/shard_map/ppermute | solution.py:281
  45.5 2.7 %collective-permute-start.1 = (bf16[1040,128]{1,0:T(8,128)(2,1)S(1)}, bf16[1040,128]{1,0:T(8,128)(2,1)S(1)}, u32[]{:S(2)}, u32[]{:S(2)}) collective-permute-start(bf16[1040,128]{1,0:T(8,128)(2,1)S(1)} %pad_maximum_fusion.refs_0_), channel_id=1, source_target_pairs={{0,4},{1,5},{2,6},{3,7},{4,0},{5,1},{6,2},{7,3},{8,12},{9,13},{10,... | collective-permute-start | bytes 798728 | tf_op jit(solution)/shard_map/ppermute | solution.py:300
  48.2 12.8 %collective-permute-done.1.refs_2_ = bf16[1040,128]{1,0:T(8,128)(2,1)S(1)} collective-permute-done((bf16[1040,128]{1,0:T(8,128)(2,1)S(1)}, bf16[1040,128]{1,0:T(8,128)(2,1)S(1)}, u32[]{:S(2)}, u32[]{:S(2)}) %collective-permute-start.1) | collective-permute-done | bytes 266272 | tf_op jit(solution)/shard_map/ppermute | solution.py:300
  61.1 5.8 %all-to-all-start.1 = ((bf16[8,384,128]{2,1,0:T(8,128)(2,1)}), bf16[8,384,128]{2,1,0:T(8,128)(2,1)S(1)}, u32[]{:S(2)}, u32[]{:S(2)}) async-start(bf16[8,384,128]{2,1,0:T(8,128)(2,1)} %chunk_products.4), calls=%async_computation.1 | async-start | bytes 1572864 | tf_op jit(solution)/shard_map/all_to_all | solution.py:326
  69.5 12.7 %chunk_products.5 = bf16[8,384,128]{2,1,0:T(8,128)(2,1)S(1)} custom-call(s32[576]{0:T(1024)S(1)} %reshape.24.slots, bf16[2,24,12,128,128]{4,3,2,1,0:T(8,128)(2,1)} %bitcast.21, bf16[2,24,12,128,128]{4,3,2,1,0:T(8,128)(2,1)} %bitcast.22, bf16[2,24,12,128,128]{4,3,2,1,0:T(8,128)(2,1)} %bitcast.23, bf16[2,24,12,128,128]{4,3,2,1,0:T(8,128)(2,1)} %bitcast.24, ...), custom_call_target="tpu_custom_call" | custom-call | flops 40000000000 | bytes 4096 | tf_op jit(solution)/shard_map/chunk_products/pallas_call | solution.py:109
  83.1 4.1 %all-to-all-done.1.refs_0_ = bf16[8,384,128]{2,1,0:T(8,128)(2,1)S(1)} async-done(((bf16[8,384,128]{2,1,0:T(8,128)(2,1)}), bf16[8,384,128]{2,1,0:T(8,128)(2,1)S(1)}, u32[]{:S(2)}, u32[]{:S(2)}) %all-to-all-start.1) | async-done | bytes 786464 | tf_op jit(solution)/shard_map/all_to_all | solution.py:326
  87.2 3.6 %all-to-all-start.2 = ((bf16[8,384,128]{2,1,0:T(8,128)(2,1)}), bf16[8,384,128]{2,1,0:T(8,128)(2,1)S(1)}, u32[]{:S(2)}, u32[]{:S(2)}) async-start(bf16[8,384,128]{2,1,0:T(8,128)(2,1)} %copy-done.14), calls=%async_computation.2 | async-start | bytes 1572864 | tf_op jit(solution)/shard_map/all_to_all | solution.py:326
  90.8 2.0 collective-permute-start.4
  94.8 29.7 %collective-permute-done.4.refs_4_ = bf16[4,1040,128]{2,1,0:T(8,128)(2,1)S(1)} collective-permute-done((bf16[4,1040,128]{2,1,0:T(8,128)(2,1)S(1)}, bf16[4,1040,128]{2,1,0:T(8,128)(2,1)S(1)}, u32[]{:S(2)}, u32[]{:S(2)}) %collective-permute-start.4) | collective-permute-done | bytes 1064992 | tf_op jit(solution)/shard_map/ppermute | solution.py:308
  125.6 13.2 %chunk_products.6 = bf16[8,384,128]{2,1,0:T(8,128)(2,1)} custom-call(s32[576]{0:T(1024)S(1)} %reshape.24.slots, bf16[2,24,12,128,128]{4,3,2,1,0:T(8,128)(2,1)} %bitcast.25, bf16[2,24,12,128,128]{4,3,2,1,0:T(8,128)(2,1)} %bitcast.26, bf16[2,24,12,128,128]{4,3,2,1,0:T(8,128)(2,1)} %bitcast.27, bf16[2,24,12,128,128]{4,3,2,1,0:T(8,128)(2,1)} %bitcast.28, ...), custom_call_target="tpu_custom_call" | custom-call | bytes 4096 | tf_op jit(solution)/shard_map/chunk_products/pallas_call | solution.py:109
  138.8 4.6 %all-to-all-start.3 = ((bf16[8,384,128]{2,1,0:T(8,128)(2,1)}), bf16[8,384,128]{2,1,0:T(8,128)(2,1)}, u32[]{:S(2)}, u32[]{:S(2)}) async-start(bf16[8,384,128]{2,1,0:T(8,128)(2,1)} %chunk_products.6), calls=%async_computation.3 | async-start | bytes 1572864 | tf_op jit(solution)/shard_map/all_to_all | solution.py:326
  144.4 2.4 %collective-permute-done.3.refs_5_ = bf16[4,1040,128]{2,1,0:T(8,128)(2,1)S(1)} collective-permute-done((bf16[4,1040,128]{2,1,0:T(8,128)(2,1)S(1)}, bf16[4,1040,128]{2,1,0:T(8,128)(2,1)S(1)}, u32[]{:S(2)}, u32[]{:S(2)}) %collective-permute-start.3) | collective-permute-done | bytes 1064992 | tf_op jit(solution)/shard_map/ppermute | solution.py:284
  151.2 13.1 %chunk_products.7 = bf16[8,384,128]{2,1,0:T(8,128)(2,1)} custom-call(s32[576]{0:T(1024)S(1)} %reshape.24.slots, bf16[2,24,12,128,128]{4,3,2,1,0:T(8,128)(2,1)} %bitcast.29, bf16[2,24,12,128,128]{4,3,2,1,0:T(8,128)(2,1)} %bitcast.30, bf16[2,24,12,128,128]{4,3,2,1,0:T(8,128)(2,1)} %bitcast.31, bf16[2,24,12,128,128]{4,3,2,1,0:T(8,128)(2,1)} %bitcast.32, ...), custom_call_target="tpu_custom_call" | custom-call | bytes 4096 | tf_op jit(solution)/shard_map/chunk_products/pallas_call | solution.py:109
  164.2 6.0 %all-to-all-start = ((bf16[8,384,128]{2,1,0:T(8,128)(2,1)}), bf16[8,384,128]{2,1,0:T(8,128)(2,1)S(1)}, u32[]{:S(2)}, u32[]{:S(2)}) async-start(bf16[8,384,128]{2,1,0:T(8,128)(2,1)} %chunk_products.7), calls=%async_computation | async-start | bytes 1572864 | tf_op jit(solution)/shard_map/all_to_all | solution.py:326
  177.3 13.1 %first_shares.1 = (f32[384,2048]{1,0:T(8,128)}, f32[384,2048]{1,0:T(8,128)}, bf16[512,2048]{1,0:T(8,128)(2,1)S(1)}) custom-call(s32[256]{0:T(256)S(1)} %reshape.29.positions, bf16[8,384,128]{2,1,0:T(8,128)(2,1)S(1)} %all-to-all-done.1.refs_0_, bf16[8,384,128]{2,1,0:T(8,128)(2,1)S(1)} %copy-done.4, bf16[8,384,128]{2,1,0:T(8,128)(2,1)} %all-to-all-done.3.refs_2_, ...), custom_call_target="tpu_custom_call" | custom-call | bytes 4096 | tf_op jit(solution)/shard_map/first_shares/pallas_call | solution.py:212
  197.2 5.6 %last_share.1 = bf16[2,384,2048]{2,1,0:T(8,128)(2,1)} custom-call(bf16[8,384,128]{2,1,0:T(8,128)(2,1)S(1)} %all-to-all-done.chunk, bf16[512,2048]{1,0:T(8,128)(2,1)S(1)} %copy-done.6, f32[384,2048]{1,0:T(8,128)S(1)} %copy-done.1, f32[384,2048]{1,0:T(8,128)S(1)} %copy-done.2), custom_call_target="tpu_custom_call" | custom-call | bytes 4096 | tf_op jit(solution)/shard_map/last_share/pallas_call | solution.py:249
  (86 shorter events, 28.7 us)
Async XLA Ops:
  0.0 25.4 %copy-start.17 = (s32[48,12]{0,1:T(8,128)S(1)}, s32[48,12]{0,1:T(8,128)}, u32[]{:S(2)}) copy-start(s32[48,12]{0,1:T(8,128)} %param.7) | copy-start | bytes 6916
  4.0 20.9 %collective-permute-start.7 = (bf16[48,64,128]{2,1,0:T(8,128)(2,1)}, bf16[48,64,128]{2,1,0:T(8,128)(2,1)}, u32[]{:S(2)}, u32[]{:S(2)}) collective-permute-start(bf16[48,64,128]{2,1,0:T(8,128)(2,1)} %pack_chunks.3.refs_4_), channel_id=1, source_target_pairs={{0,16},{8,24},{16,0},{24,8},{1,17},{9,25},{17,1},{25,9},{2,18},{10... | collective-permute-start | bytes 2359304 | tf_op jit(solution)/shard_map/ppermute | solution.py:281
  7.3 10.5 %collective-permute-start.2 = (bf16[1040,128]{1,0:T(8,128)(2,1)S(1)}, bf16[1040,128]{1,0:T(8,128)(2,1)S(1)}, u32[]{:S(2)}, u32[]{:S(2)}) collective-permute-start(bf16[1040,128]{1,0:T(8,128)(2,1)S(1)} %pad_maximum_fusion.refs_0_), channel_id=1, source_target_pairs={{0,6},{1,7},{2,0},{3,1},{4,2},{5,3},{6,4},{7,5},{8,14},{9,15},{10,... | collective-permute-start | bytes 798728 | tf_op jit(solution)/shard_map/ppermute | solution.py:300
  11.0 12.0 %collective-permute-start = (bf16[1040,128]{1,0:T(8,128)(2,1)S(1)}, bf16[1040,128]{1,0:T(8,128)(2,1)S(1)}, u32[]{:S(2)}, u32[]{:S(2)}) collective-permute-start(bf16[1040,128]{1,0:T(8,128)(2,1)S(1)} %pad_maximum_fusion.refs_0_), channel_id=1, source_target_pairs={{0,2},{1,3},{2,4},{3,5},{4,6},{5,7},{6,0},{7,1},{8,10},{9,11},{10,... | collective-permute-start | bytes 798728 | tf_op jit(solution)/shard_map/ppermute | solution.py:300
  11.0 16.4 %collective-permute-start.9 = (bf16[48,64,128]{2,1,0:T(8,128)(2,1)}, bf16[48,64,128]{2,1,0:T(8,128)(2,1)}, u32[]{:S(2)}, u32[]{:S(2)}) collective-permute-start(bf16[48,64,128]{2,1,0:T(8,128)(2,1)} %pack_chunks.3.refs_4_), channel_id=1, source_target_pairs={{0,8},{8,0},{16,24},{24,16},{1,9},{9,1},{17,25},{25,17},{2,10},{10... | collective-permute-start | bytes 2359304 | tf_op jit(solution)/shard_map/ppermute | solution.py:284
  24.9 2.6 %collective-permute-start.10 = (bf16[48,64,128]{2,1,0:T(8,128)(2,1)}, bf16[48,64,128]{2,1,0:T(8,128)(2,1)}, u32[]{:S(2)}, u32[]{:S(2)}) collective-permute-start(bf16[48,64,128]{2,1,0:T(8,128)(2,1)} %collective-permute-done.7.refs_6_), channel_id=1, source_target_pairs={{0,8},{8,0},{16,24},{24,16},{1,9},{9,1},{17,25},{25,17},{2,10},{10... | collective-permute-start | bytes 2359304 | tf_op jit(solution)/shard_map/ppermute | solution.py:284
  24.9 43.4 %collective-permute-start.12 = (bf16[48,64,128]{2,1,0:T(8,128)(2,1)}, bf16[48,64,128]{2,1,0:T(8,128)(2,1)}, u32[]{:S(2)}, u32[]{:S(2)}) collective-permute-start(bf16[48,64,128]{2,1,0:T(8,128)(2,1)} %get-tuple-element.37.refs_4_), channel_id=1, source_target_pairs={{0,8},{8,0},{16,24},{24,16},{1,9},{9,1},{17,25},{25,17},{2,10},{10... | collective-permute-start | bytes 2359304 | tf_op jit(solution)/shard_map/ppermute | solution.py:284
  25.6 19.8 %collective-permute-start.8 = (bf16[48,64,128]{2,1,0:T(8,128)(2,1)}, bf16[48,64,128]{2,1,0:T(8,128)(2,1)}, u32[]{:S(2)}, u32[]{:S(2)}) collective-permute-start(bf16[48,64,128]{2,1,0:T(8,128)(2,1)} %get-tuple-element.37.refs_4_), channel_id=1, source_target_pairs={{0,16},{8,24},{16,0},{24,8},{1,17},{9,25},{17,1},{25,9},{2,18},{10... | collective-permute-start | bytes 2359304 | tf_op jit(solution)/shard_map/ppermute | solution.py:281
  45.5 22.9 %collective-permute-start.13 = (bf16[48,64,128]{2,1,0:T(8,128)(2,1)}, bf16[48,64,128]{2,1,0:T(8,128)(2,1)}, u32[]{:S(2)}, u32[]{:S(2)}) collective-permute-start(bf16[48,64,128]{2,1,0:T(8,128)(2,1)} %collective-permute-done.8.refs_6_), channel_id=1, source_target_pairs={{0,8},{8,0},{16,24},{24,16},{1,9},{9,1},{17,25},{25,17},{2,10},{10... | collective-permute-start | bytes 2359304 | tf_op jit(solution)/shard_map/ppermute | solution.py:284
  45.5 15.5 %collective-permute-start.1 = (bf16[1040,128]{1,0:T(8,128)(2,1)S(1)}, bf16[1040,128]{1,0:T(8,128)(2,1)S(1)}, u32[]{:S(2)}, u32[]{:S(2)}) collective-permute-start(bf16[1040,128]{1,0:T(8,128)(2,1)S(1)} %pad_maximum_fusion.refs_0_), channel_id=1, source_target_pairs={{0,4},{1,5},{2,6},{3,7},{4,0},{5,1},{6,2},{7,3},{8,12},{9,13},{10,... | collective-permute-start | bytes 798728 | tf_op jit(solution)/shard_map/ppermute | solution.py:300
  61.1 26.2 %all-to-all-start.1 = ((bf16[8,384,128]{2,1,0:T(8,128)(2,1)}), bf16[8,384,128]{2,1,0:T(8,128)(2,1)S(1)}, u32[]{:S(2)}, u32[]{:S(2)}) async-start(bf16[8,384,128]{2,1,0:T(8,128)(2,1)} %chunk_products.4), calls=%async_computation.1 | async-start | bytes 1572864 | tf_op jit(solution)/shard_map/all_to_all | solution.py:326
  66.8 26.0 %collective-permute-start.11 = (bf16[48,64,128]{2,1,0:T(8,128)(2,1)}, bf16[48,64,128]{2,1,0:T(8,128)(2,1)}, u32[]{:S(2)}, u32[]{:S(2)}) collective-permute-start(bf16[48,64,128]{2,1,0:T(8,128)(2,1)} %get-tuple-element.39.refs_4_), channel_id=1, source_target_pairs={{0,16},{8,24},{16,0},{24,8},{1,17},{9,25},{17,1},{25,9},{2,18},{10... | collective-permute-start | bytes 2359304 | tf_op jit(solution)/shard_map/ppermute | solution.py:281
  87.2 51.6 %all-to-all-start.2 = ((bf16[8,384,128]{2,1,0:T(8,128)(2,1)}), bf16[8,384,128]{2,1,0:T(8,128)(2,1)S(1)}, u32[]{:S(2)}, u32[]{:S(2)}) async-start(bf16[8,384,128]{2,1,0:T(8,128)(2,1)} %copy-done.14), calls=%async_computation.2 | async-start | bytes 1572864 | tf_op jit(solution)/shard_map/all_to_all | solution.py:326
  90.8 33.8 %collective-permute-start.4 = (bf16[4,1040,128]{2,1,0:T(8,128)(2,1)S(1)}, bf16[4,1040,128]{2,1,0:T(8,128)(2,1)S(1)}, u32[]{:S(2)}, u32[]{:S(2)}) collective-permute-start(bf16[4,1040,128]{2,1,0:T(8,128)(2,1)S(1)} %join.1.refs_3_), channel_id=1, source_target_pairs={{0,1},{1,0},{2,3},{3,2},{4,5},{5,4},{6,7},{7,6},{8,9},{9,8},{10,11... | collective-permute-start | bytes 3194888 | tf_op jit(solution)/shard_map/ppermute | solution.py:308
  92.8 32.7 %collective-permute-start.15 = (bf16[48,64,128]{2,1,0:T(8,128)(2,1)}, bf16[48,64,128]{2,1,0:T(8,128)(2,1)S(1)}, u32[]{:S(2)}, u32[]{:S(2)}) collective-permute-start(bf16[48,64,128]{2,1,0:T(8,128)(2,1)} %get-tuple-element.39.refs_4_), channel_id=1, source_target_pairs={{0,8},{8,0},{16,24},{24,16},{1,9},{9,1},{17,25},{25,17},{2,10},{10... | collective-permute-start | bytes 2359304 | tf_op jit(solution)/shard_map/ppermute | solution.py:284
  92.8 32.7 %collective-permute-start.16 = (bf16[48,64,128]{2,1,0:T(8,128)(2,1)}, bf16[48,64,128]{2,1,0:T(8,128)(2,1)S(1)}, u32[]{:S(2)}, u32[]{:S(2)}) collective-permute-start(bf16[48,64,128]{2,1,0:T(8,128)(2,1)} %collective-permute-done.11.refs_6_), channel_id=1, source_target_pairs={{0,8},{8,0},{16,24},{24,16},{1,9},{9,1},{17,25},{25,17},{2,10},{10... | collective-permute-start | bytes 2359304 | tf_op jit(solution)/shard_map/ppermute | solution.py:284
  93.3 50.6 %collective-permute-start.14 = (bf16[48,64,128]{2,1,0:T(8,128)(2,1)}, bf16[48,64,128]{2,1,0:T(8,128)(2,1)}, u32[]{:S(2)}, u32[]{:S(2)}) collective-permute-start(bf16[48,64,128]{2,1,0:T(8,128)(2,1)} %get-tuple-element.42.refs_4_), channel_id=1, source_target_pairs={{0,16},{8,24},{16,0},{24,8},{1,17},{9,25},{17,1},{25,9},{2,18},{10... | collective-permute-start | bytes 2359304 | tf_op jit(solution)/shard_map/ppermute | solution.py:281
  138.8 25.4 %copy-start.3 = (bf16[8,384,128]{2,1,0:T(8,128)(2,1)}, bf16[8,384,128]{2,1,0:T(8,128)(2,1)S(1)}, u32[]{:S(2)}) copy-start(bf16[8,384,128]{2,1,0:T(8,128)(2,1)S(1)} %all-to-all-done.2.refs_1_) | copy-start | bytes 2359300
  138.8 25.4 %all-to-all-start.3 = ((bf16[8,384,128]{2,1,0:T(8,128)(2,1)}), bf16[8,384,128]{2,1,0:T(8,128)(2,1)}, u32[]{:S(2)}, u32[]{:S(2)}) async-start(bf16[8,384,128]{2,1,0:T(8,128)(2,1)} %chunk_products.6), calls=%async_computation.3 | async-start | bytes 1572864 | tf_op jit(solution)/shard_map/all_to_all | solution.py:326
  143.4 3.5 %collective-permute-start.3 = (bf16[4,1040,128]{2,1,0:T(8,128)(2,1)S(1)}, bf16[4,1040,128]{2,1,0:T(8,128)(2,1)S(1)}, u32[]{:S(2)}, u32[]{:S(2)}) collective-permute-start(bf16[4,1040,128]{2,1,0:T(8,128)(2,1)S(1)} %join.1.refs_3_), channel_id=1, source_target_pairs={{0,8},{8,0},{16,24},{24,16},{1,9},{9,1},{17,25},{25,17},{2,10},{10... | collective-permute-start | bytes 3194888 | tf_op jit(solution)/shard_map/ppermute | solution.py:284
  143.4 4.5 %collective-permute-start.5 = (bf16[4,1040,128]{2,1,0:T(8,128)(2,1)}, bf16[4,1040,128]{2,1,0:T(8,128)(2,1)S(1)}, u32[]{:S(2)}, u32[]{:S(2)}) collective-permute-start(bf16[4,1040,128]{2,1,0:T(8,128)(2,1)} %copy-done.7), channel_id=1, source_target_pairs={{0,8},{8,0},{16,24},{24,16},{1,9},{9,1},{17,25},{25,17},{2,10},{10... | collective-permute-start | bytes 3194888 | tf_op jit(solution)/shard_map/ppermute | solution.py:284
  143.9 5.0 %collective-permute-start.6 = (bf16[48,64,128]{2,1,0:T(8,128)(2,1)}, bf16[48,64,128]{2,1,0:T(8,128)(2,1)S(1)}, u32[]{:S(2)}, u32[]{:S(2)}) collective-permute-start(bf16[48,64,128]{2,1,0:T(8,128)(2,1)} %get-tuple-element.42.refs_4_), channel_id=1, source_target_pairs={{0,8},{8,0},{16,24},{24,16},{1,9},{9,1},{17,25},{25,17},{2,10},{10... | collective-permute-start | bytes 2359304 | tf_op jit(solution)/shard_map/ppermute | solution.py:284
  144.0 6.1 %collective-permute-start.17 = (bf16[48,64,128]{2,1,0:T(8,128)(2,1)}, bf16[48,64,128]{2,1,0:T(8,128)(2,1)S(1)}, u32[]{:S(2)}, u32[]{:S(2)}) collective-permute-start(bf16[48,64,128]{2,1,0:T(8,128)(2,1)} %collective-permute-done.14.refs_6_), channel_id=1, source_target_pairs={{0,8},{8,0},{16,24},{24,16},{1,9},{9,1},{17,25},{25,17},{2,10},{10... | collective-permute-start | bytes 2359304 | tf_op jit(solution)/shard_map/ppermute | solution.py:284
  164.2 27.6 %all-to-all-start = ((bf16[8,384,128]{2,1,0:T(8,128)(2,1)}), bf16[8,384,128]{2,1,0:T(8,128)(2,1)S(1)}, u32[]{:S(2)}, u32[]{:S(2)}) async-start(bf16[8,384,128]{2,1,0:T(8,128)(2,1)} %chunk_products.7), calls=%async_computation | async-start | bytes 1572864 | tf_op jit(solution)/shard_map/all_to_all | solution.py:326
  (17 other events, 55.5 us)

commit v8 on v6

--- a/solution.py
+++ b/solution.py
@@ -8,8 +8,8 @@
 from jax.sharding import PartitionSpec as P
 
 VMEM_WHOLE = 58 * 1024 * 1024
-VMEM_MOST = 36 * 1024 * 1024
-VMEM_PART = 20 * 1024 * 1024
+VMEM_MOST = 44 * 1024 * 1024
+VMEM_PART = 44 * 1024 * 1024
 SMALL = pl.CostEstimate(flops=0, bytes_accessed=4096, transcendentals=0)
 
 
@@ -133,22 +133,6 @@
     return result.reshape(owners, half * rows, lanes)
 
 
-def join_kernel(*refs):
-    for at, piece in enumerate(refs[:-1]):
-        refs[-1][at] = piece[...]
-
-
-def join(pieces):
-    shape = (len(pieces),) + pieces[0].shape
-    return pl.pallas_call(
-        join_kernel,
-        out_shape=jax.ShapeDtypeStruct(shape, pieces[0].dtype),
-        cost_estimate=SMALL,
-        compiler_params=pltpu.CompilerParams(vmem_limit_bytes=VMEM_PART),
-        name="join",
-    )(*pieces)
-
-
 def place_tiles(chunks, owners, tiles_each, positions, sources, dense):
     devices, _, span = sources[0].shape
     width = span // 2
@@ -293,21 +277,14 @@
     spot_rows = -(-spots.size // (16 * span)) * 16
     spots = jnp.pad(spots, (0, spot_rows * span - spots.size)).reshape(spot_rows, span)
     load = jnp.concatenate([tiles, spots], axis=0)
-    parts = [load]
-    for shift in range(1, aux_count // 2):
-        moves = [(g, (g + 2 * shift) % aux_count) for g in range(aux_count)]
-        parts.append(lax.ppermute(load, "aux", moves))
+    first = lax.all_gather(load[None], "aux", axis=0, tiled=True)
+    sources = [first, to_mate(first)]
 
     packed = list(pack_chunks(factors, width, 0, 1))
     if chunk_count > 1:
         packed += pack_chunks(factors, width, 1, chunk_count - 1)
-        parts = after(parts, packed[1:])
-
-    column = join(parts)
-    beside = lax.ppermute(column, "aux", [(g, g ^ 1) for g in range(aux_count)])
-    sources = [column, beside, to_mate(column), to_mate(beside)]
-
-    before_products = {1: column, 2: beside, 3: sources[2:]}
+
+    before_products = {3: sources}
     products = []
     far_pieces, made = [], None
     for at in range(chunk_count):
@@ -316,7 +293,7 @@
             own = after(own, far_pieces)
         far_pieces = [to_far(own, shift) for shift in range(1, far_count)]
         if chunk_count > 1:
-            far_pieces = after(far_pieces, made if at else [packed[1:], parts[1::2]])
+            far_pieces = after(far_pieces, made if at else packed[1:])
         pieces = []
         for piece in [packed[at]] + far_pieces:
             pieces += [piece, to_mate(piece)]

time: 210 us -> 170 us (0.81)
  local copies, waits for them, and re-layouts: 52.1 us -> 16.4 us
  waiting for transfers between devices: 52.7 us -> 32.5 us
  between operations: 0.25 us -> 13.6 us
  Pallas kernels: 68.1 us -> 80.3 us
  starting transfers between devices: 35.1 us -> 24.8 us
    ppermute x4 -> x0, waiting for transfers between devices: 46.3 us -> none  [the longest x1 29.8 us: shards(): beside = lax.ppermute(column, 'aux', [(g, g ^ 1) for g in range(aux_count)])]
    unnamed x68 -> x34, local copies, waits for them, and re-layouts: 49.5 us -> 14.5 us
    ppermute x4, waiting for transfers between devices: 0.01 us -> 13.6 us  [to_far(): return lax.ppermute(array, 'orb', moves)]
    all_to_all x4, waiting for transfers between devices: 0.01 us -> 11.5 us  [shards(): lax.all_to_all(made, 'aux', split_axis=0, concat_axis=0, tiled=True)]
    pallas_call x4, Pallas kernels: 41.7 us -> 52.9 us  [chunk_products(): pl.pallas_call(functools.partial(product_kernel, pairs, split_rows, strea...]
    ppermute x4 -> x0, starting transfers between devices: 6.69 us -> none  [the longest x3 4.67 us: shards(): parts.append(lax.ppermute(load, 'aux', moves))]
    all_to_all x4, starting transfers between devices: 20.8 us -> 16.5 us  [shards(): lax.all_to_all(made, 'aux', split_axis=0, concat_axis=0, tiled=True)]
    ppermute x10 -> x9, waiting for transfers between devices: 6.4 us -> 7.43 us  [to_mate(): return lax.ppermute(array, 'orb', [(g, g ^ 1) for g in range(orb_count)])]
  transfers between devices with their start and end apart: 22 -> 18, of which waited for: 8 -> 11; matrix products, arithmetic and copies ran while one was open for 1% -> 1% of each run, Pallas kernels for 28% -> 44%
where the time goes in v8:
time: 170 us; the launch traced here: 169 us
  Pallas kernels  80.3 us (47%)
  waiting for transfers between devices  32.5 us (19%)
  starting transfers between devices  24.8 us (15%)
  local copies, waits for them, and re-layouts  16.4 us (10%)
  between operations  13.6 us (8%)
    pallas_call x4, Pallas kernels, chunk_products(): pl.pallas_call(functools.partial(product_kernel, pairs, split_rows, strea...  52.9 us
    all_to_all x4, starting transfers between devices, shards(): lax.all_to_all(made, 'aux', split_axis=0, concat_axis=0, tiled=True)  16.5 us
    unnamed x34, local copies, waits for them, and re-layouts  14.5 us
    pallas_call x1, Pallas kernels, first_shares(): pl.pallas_call(functools.partial(first_kernel, len(chunks), len(sources),...  13.7 us
    ppermute x4, waiting for transfers between devices, to_far(): return lax.ppermute(array, 'orb', moves)  13.6 us
    all_to_all x4, waiting for transfers between devices, shards(): lax.all_to_all(made, 'aux', split_axis=0, concat_axis=0, tiled=True)  11.5 us
    pallas_call x2, Pallas kernels, pack_chunks(): pl.pallas_call(functools.partial(pack_kernel, width, first), grid=(orbita...  8.1 us
    ppermute x9, waiting for transfers between devices, to_mate(): return lax.ppermute(array, 'orb', [(g, g ^ 1) for g in range(orb_count)])  7.43 us
  transfers between devices with their start and end apart: 18, of which 11 were waited for; matrix products, arithmetic and copies ran while one was open for 1% of the time, Pallas kernels for 44%

profile of v8, /device:TPU:0, one launch (start us, length us, event | category | flops | bytes accessed | tf_op | source)
XLA Modules:
  0.0 169.2 jit_solution(4641291331254021425)
XLA Ops:
  8.4 3.9 %pack_chunks.3.refs_4_ = bf16[48,64,128]{2,1,0:T(8,128)(2,1)} custom-call(bf16[48,128,256]{2,1,0:T(8,128)(2,1)} %source.3), custom_call_target="tpu_custom_call" | custom-call | bytes 4096 | tf_op jit(solution)/shard_map/pack_chunks/pallas_call | solution.py:32
  12.3 3.0 %collective-permute-start.2 = (bf16[48,64,128]{2,1,0:T(8,128)(2,1)}, bf16[48,64,128]{2,1,0:T(8,128)(2,1)S(1)}, u32[]{:S(2)}, u32[]{:S(2)}) collective-permute-start(bf16[48,64,128]{2,1,0:T(8,128)(2,1)} %pack_chunks.3.refs_4_), channel_id=1, source_target_pairs={{0,16},{8,24},{16,0},{24,8},{1,17},{9,25},{17,1},{25,9},{2,18},{10... | collective-permute-start | bytes 2359304 | tf_op jit(solution)/shard_map/ppermute | solution.py:264
  15.3 4.2 %pack_chunks.2 = (bf16[48,64,128]{2,1,0:T(8,128)(2,1)}, bf16[48,64,128]{2,1,0:T(8,128)(2,1)}, bf16[48,64,128]{2,1,0:T(8,128)(2,1)}) custom-call(bf16[48,128,256]{2,1,0:T(8,128)(2,1)} %source.3), custom_call_target="tpu_custom_call" | custom-call | bytes 4096 | tf_op jit(solution)/shard_map/pack_chunks/pallas_call | solution.py:32
  19.5 13.6 %collective-permute-done.2.refs_6_ = bf16[48,64,128]{2,1,0:T(8,128)(2,1)S(1)} collective-permute-done((bf16[48,64,128]{2,1,0:T(8,128)(2,1)}, bf16[48,64,128]{2,1,0:T(8,128)(2,1)S(1)}, u32[]{:S(2)}, u32[]{:S(2)}) %collective-permute-start.2) | collective-permute-done | bytes 786464 | tf_op jit(solution)/shard_map/ppermute | solution.py:264
  34.0 1.7 collective-permute-start.3
  39.1 13.1 %chunk_products.4 = bf16[8,384,128]{2,1,0:T(8,128)(2,1)} custom-call(s32[576]{0:T(1024)S(1)} %reshape.24.slots, bf16[2,24,12,128,128]{4,3,2,1,0:T(8,128)(2,1)} %bitcast.15, bf16[2,24,12,128,128]{4,3,2,1,0:T(8,128)(2,1)} %bitcast.16, bf16[2,24,12,128,128]{4,3,2,1,0:T(8,128)(2,1)} %bitcast.17, bf16[2,24,12,128,128]{4,3,2,1,0:T(8,128)(2,1)} %bitcast.18, ...), custom_call_target="tpu_custom_call" | custom-call | bytes 4096 | tf_op jit(solution)/shard_map/chunk_products/pallas_call | solution.py:108
  52.2 5.8 %all-to-all-start.1 = ((bf16[8,384,128]{2,1,0:T(8,128)(2,1)}), bf16[8,384,128]{2,1,0:T(8,128)(2,1)S(1)}, u32[]{:S(2)}, u32[]{:S(2)}) async-start(bf16[8,384,128]{2,1,0:T(8,128)(2,1)} %chunk_products.4), calls=%async_computation.1 | async-start | bytes 1572864 | tf_op jit(solution)/shard_map/all_to_all | solution.py:302
  61.7 13.1 %chunk_products.5 = bf16[8,384,128]{2,1,0:T(8,128)(2,1)} custom-call(s32[576]{0:T(1024)S(1)} %reshape.24.slots, bf16[2,24,12,128,128]{4,3,2,1,0:T(8,128)(2,1)} %bitcast.19, bf16[2,24,12,128,128]{4,3,2,1,0:T(8,128)(2,1)} %bitcast.20, bf16[2,24,12,128,128]{4,3,2,1,0:T(8,128)(2,1)} %bitcast.21, bf16[2,24,12,128,128]{4,3,2,1,0:T(8,128)(2,1)} %bitcast.22, ...), custom_call_target="tpu_custom_call" | custom-call | bytes 4096 | tf_op jit(solution)/shard_map/chunk_products/pallas_call | solution.py:108
  74.8 4.1 %all-to-all-done.1.refs_0_ = bf16[8,384,128]{2,1,0:T(8,128)(2,1)S(1)} async-done(((bf16[8,384,128]{2,1,0:T(8,128)(2,1)}), bf16[8,384,128]{2,1,0:T(8,128)(2,1)S(1)}, u32[]{:S(2)}, u32[]{:S(2)}) %all-to-all-start.1) | async-done | bytes 786464 | tf_op jit(solution)/shard_map/all_to_all | solution.py:302
  78.9 3.5 %all-to-all-start.2 = ((bf16[8,384,128]{2,1,0:T(8,128)(2,1)}), bf16[8,384,128]{2,1,0:T(8,128)(2,1)S(1)}, u32[]{:S(2)}, u32[]{:S(2)}) async-start(bf16[8,384,128]{2,1,0:T(8,128)(2,1)} %chunk_products.5), calls=%async_computation.2 | async-start | bytes 1572864 | tf_op jit(solution)/shard_map/all_to_all | solution.py:302
  86.3 13.5 %chunk_products.6 = bf16[8,384,128]{2,1,0:T(8,128)(2,1)} custom-call(s32[576]{0:T(1024)S(1)} %reshape.24.slots, bf16[2,24,12,128,128]{4,3,2,1,0:T(8,128)(2,1)} %bitcast.23, bf16[2,24,12,128,128]{4,3,2,1,0:T(8,128)(2,1)} %bitcast.24, bf16[2,24,12,128,128]{4,3,2,1,0:T(8,128)(2,1)} %bitcast.25, bf16[2,24,12,128,128]{4,3,2,1,0:T(8,128)(2,1)} %bitcast.26, ...), custom_call_target="tpu_custom_call" | custom-call | bytes 4096 | tf_op jit(solution)/shard_map/chunk_products/pallas_call | solution.py:108
  99.8 2.8 %all-to-all-done.2.refs_1_ = bf16[8,384,128]{2,1,0:T(8,128)(2,1)S(1)} async-done(((bf16[8,384,128]{2,1,0:T(8,128)(2,1)}), bf16[8,384,128]{2,1,0:T(8,128)(2,1)S(1)}, u32[]{:S(2)}, u32[]{:S(2)}) %all-to-all-start.2) | async-done | bytes 786464 | tf_op jit(solution)/shard_map/all_to_all | solution.py:302
  102.6 3.6 %all-to-all-start.3 = ((bf16[8,384,128]{2,1,0:T(8,128)(2,1)}), bf16[8,384,128]{2,1,0:T(8,128)(2,1)S(1)}, u32[]{:S(2)}, u32[]{:S(2)}) async-start(bf16[8,384,128]{2,1,0:T(8,128)(2,1)} %chunk_products.6), calls=%async_computation.3 | async-start | bytes 1572864 | tf_op jit(solution)/shard_map/all_to_all | solution.py:302
  106.8 2.0 %collective-permute-done.1.refs_5_ = bf16[48,64,128]{2,1,0:T(8,128)(2,1)S(1)} collective-permute-done((bf16[48,64,128]{2,1,0:T(8,128)(2,1)}, bf16[48,64,128]{2,1,0:T(8,128)(2,1)S(1)}, u32[]{:S(2)}, u32[]{:S(2)}) %collective-permute-start.1) | collective-permute-done | bytes 786464 | tf_op jit(solution)/shard_map/ppermute | solution.py:267
  109.9 13.2 %chunk_products.7 = bf16[8,384,128]{2,1,0:T(8,128)(2,1)} custom-call(s32[576]{0:T(1024)S(1)} %reshape.24.slots, bf16[2,24,12,128,128]{4,3,2,1,0:T(8,128)(2,1)} %bitcast.27, bf16[2,24,12,128,128]{4,3,2,1,0:T(8,128)(2,1)} %bitcast.28, bf16[2,24,12,128,128]{4,3,2,1,0:T(8,128)(2,1)} %bitcast.29, bf16[2,24,12,128,128]{4,3,2,1,0:T(8,128)(2,1)} %bitcast.30, ...), custom_call_target="tpu_custom_call" | custom-call | bytes 4096 | tf_op jit(solution)/shard_map/chunk_products/pallas_call | solution.py:108
  123.1 3.4 %all-to-all-done.3.refs_2_ = bf16[8,384,128]{2,1,0:T(8,128)(2,1)S(1)} async-done(((bf16[8,384,128]{2,1,0:T(8,128)(2,1)}), bf16[8,384,128]{2,1,0:T(8,128)(2,1)S(1)}, u32[]{:S(2)}, u32[]{:S(2)}) %all-to-all-start.3) | async-done | bytes 786464 | tf_op jit(solution)/shard_map/all_to_all | solution.py:302
  127.5 3.5 %all-to-all-start = ((bf16[8,384,128]{2,1,0:T(8,128)(2,1)}), bf16[8,384,128]{2,1,0:T(8,128)(2,1)S(1)}, u32[]{:S(2)}, u32[]{:S(2)}) async-start(bf16[8,384,128]{2,1,0:T(8,128)(2,1)} %chunk_products.7), calls=%async_computation | async-start | bytes 1572864 | tf_op jit(solution)/shard_map/all_to_all | solution.py:302
  133.7 1.6 copy-done.6
  135.3 13.7 %first_shares.1 = (f32[384,2048]{1,0:T(8,128)}, f32[384,2048]{1,0:T(8,128)}, bf16[512,2048]{1,0:T(8,128)(2,1)S(1)}) custom-call(s32[256]{0:T(256)S(1)} %reshape.29.positions, bf16[8,384,128]{2,1,0:T(8,128)(2,1)S(1)} %all-to-all-done.1.refs_0_, bf16[8,384,128]{2,1,0:T(8,128)(2,1)S(1)} %all-to-all-done.2.refs_1_, bf16[8,384,128]{2,1,0:T(8,128)(2,1)S(1)} %copy-done.5, ...), custom_call_target="tpu_custom_call" | custom-call | bytes 4096 | tf_op jit(solution)/shard_map/first_shares/pallas_call | solution.py:195
  149.0 1.4 copy-done.7
  151.4 1.9 %copy-done.2 = f32[384,2048]{1,0:T(8,128)S(1)} copy-done((f32[384,2048]{1,0:T(8,128)S(1)}, f32[384,2048]{1,0:T(8,128)}, u32[]{:S(2)}) %copy-start.2) | copy-done | bytes 3145752
  153.3 1.9 %copy-done.3 = f32[384,2048]{1,0:T(8,128)S(1)} copy-done((f32[384,2048]{1,0:T(8,128)S(1)}, f32[384,2048]{1,0:T(8,128)}, u32[]{:S(2)}) %copy-start.3) | copy-done | bytes 3145752
  155.2 1.6 copy-done.8
  156.8 5.6 %last_share.1 = bf16[2,384,2048]{2,1,0:T(8,128)(2,1)} custom-call(bf16[8,384,128]{2,1,0:T(8,128)(2,1)S(1)} %all-to-all-done.chunk, bf16[512,2048]{1,0:T(8,128)(2,1)S(1)} %copy-done.8, f32[384,2048]{1,0:T(8,128)S(1)} %copy-done.2, f32[384,2048]{1,0:T(8,128)S(1)} %copy-done.3), custom_call_target="tpu_custom_call" | custom-call | bytes 4096 | tf_op jit(solution)/shard_map/last_share/pallas_call | solution.py:232
  (68 shorter events, 19.9 us)
Async XLA Ops:
  6.5 76.5 %all-gather.3.cloned.1.call-start = ((), (), s32[]{:S(2)}) async-start(), calls=%async_computation.4 | async-start | bytes 2396160 | tf_op jit(solution)/shard_map/all_gather | solution.py:280
  8.4 27.3 %copy-start.15 = (s32[48,12]{0,1:T(8,128)S(1)}, s32[48,12]{0,1:T(8,128)}, u32[]{:S(2)}) copy-start(s32[48,12]{0,1:T(8,128)} %param.7) | copy-start | bytes 6916
  12.3 24.5 %copy-start.1 = (bf16[48,64,128]{2,1,0:T(8,128)(2,1)S(1)}, bf16[48,64,128]{2,1,0:T(8,128)(2,1)}, u32[]{:S(2)}) copy-start(bf16[48,64,128]{2,1,0:T(8,128)(2,1)} %pack_chunks.3.refs_4_) | copy-start | bytes 2359300
  12.3 20.8 %collective-permute-start.2 = (bf16[48,64,128]{2,1,0:T(8,128)(2,1)}, bf16[48,64,128]{2,1,0:T(8,128)(2,1)S(1)}, u32[]{:S(2)}, u32[]{:S(2)}) collective-permute-start(bf16[48,64,128]{2,1,0:T(8,128)(2,1)} %pack_chunks.3.refs_4_), channel_id=1, source_target_pairs={{0,16},{8,24},{16,0},{24,8},{1,17},{9,25},{17,1},{25,9},{2,18},{10... | collective-permute-start | bytes 2359304 | tf_op jit(solution)/shard_map/ppermute | solution.py:264
  15.3 20.6 %collective-permute-start.4 = (bf16[48,64,128]{2,1,0:T(8,128)(2,1)}, bf16[48,64,128]{2,1,0:T(8,128)(2,1)S(1)}, u32[]{:S(2)}, u32[]{:S(2)}) collective-permute-start(bf16[48,64,128]{2,1,0:T(8,128)(2,1)} %pack_chunks.3.refs_4_), channel_id=1, source_target_pairs={{0,8},{8,0},{16,24},{24,16},{1,9},{9,1},{17,25},{25,17},{2,10},{10... | collective-permute-start | bytes 2359304 | tf_op jit(solution)/shard_map/ppermute | solution.py:267
  33.1 3.7 %collective-permute-start.5 = (bf16[48,64,128]{2,1,0:T(8,128)(2,1)S(1)}, bf16[48,64,128]{2,1,0:T(8,128)(2,1)}, u32[]{:S(2)}, u32[]{:S(2)}) collective-permute-start(bf16[48,64,128]{2,1,0:T(8,128)(2,1)S(1)} %collective-permute-done.2.refs_6_), channel_id=1, source_target_pairs={{0,8},{8,0},{16,24},{24,16},{1,9},{9,1},{17,25},{25,17},{2,10},{10... | collective-permute-start | bytes 2359304 | tf_op jit(solution)/shard_map/ppermute | solution.py:267
  34.0 24.2 %collective-permute-start.3 = (bf16[48,64,128]{2,1,0:T(8,128)(2,1)}, bf16[48,64,128]{2,1,0:T(8,128)(2,1)}, u32[]{:S(2)}, u32[]{:S(2)}) collective-permute-start(bf16[48,64,128]{2,1,0:T(8,128)(2,1)} %get-tuple-element.27.refs_4_), channel_id=1, source_target_pairs={{0,16},{8,24},{16,0},{24,8},{1,17},{9,25},{17,1},{25,9},{2,18},{10... | collective-permute-start | bytes 2359304 | tf_op jit(solution)/shard_map/ppermute | solution.py:264
  39.1 18.9 %copy-start.10 = (bf16[48,64,128]{2,1,0:T(8,128)(2,1)S(1)}, bf16[48,64,128]{2,1,0:T(8,128)(2,1)}, u32[]{:S(2)}) copy-start(bf16[48,64,128]{2,1,0:T(8,128)(2,1)} %get-tuple-element.27.refs_4_) | copy-start | bytes 2359300
  39.1 19.5 %copy-start.9 = (bf16[48,64,128]{2,1,0:T(8,128)(2,1)S(1)}, bf16[48,64,128]{2,1,0:T(8,128)(2,1)}, u32[]{:S(2)}) copy-start(bf16[48,64,128]{2,1,0:T(8,128)(2,1)} %get-tuple-element.29.refs_4_) | copy-start | bytes 2359300
  52.2 26.7 %all-to-all-start.1 = ((bf16[8,384,128]{2,1,0:T(8,128)(2,1)}), bf16[8,384,128]{2,1,0:T(8,128)(2,1)S(1)}, u32[]{:S(2)}, u32[]{:S(2)}) async-start(bf16[8,384,128]{2,1,0:T(8,128)(2,1)} %chunk_products.4), calls=%async_computation.1 | async-start | bytes 1572864 | tf_op jit(solution)/shard_map/all_to_all | solution.py:302
  58.1 2.6 %collective-permute-start.7 = (bf16[48,64,128]{2,1,0:T(8,128)(2,1)S(1)}, bf16[48,64,128]{2,1,0:T(8,128)(2,1)S(1)}, u32[]{:S(2)}, u32[]{:S(2)}) collective-permute-start(bf16[48,64,128]{2,1,0:T(8,128)(2,1)S(1)} %copy-done.10), channel_id=1, source_target_pairs={{0,8},{8,0},{16,24},{24,16},{1,9},{9,1},{17,25},{25,17},{2,10},{10... | collective-permute-start | bytes 2359304 | tf_op jit(solution)/shard_map/ppermute | solution.py:267
  58.1 3.6 %collective-permute-start.8 = (bf16[48,64,128]{2,1,0:T(8,128)(2,1)}, bf16[48,64,128]{2,1,0:T(8,128)(2,1)S(1)}, u32[]{:S(2)}, u32[]{:S(2)}) collective-permute-start(bf16[48,64,128]{2,1,0:T(8,128)(2,1)} %collective-permute-done.3.refs_6_), channel_id=1, source_target_pairs={{0,8},{8,0},{16,24},{24,16},{1,9},{9,1},{17,25},{25,17},{2,10},{10... | collective-permute-start | bytes 2359304 | tf_op jit(solution)/shard_map/ppermute | solution.py:267
  58.6 23.9 %collective-permute-start.6 = (bf16[48,64,128]{2,1,0:T(8,128)(2,1)S(1)}, bf16[48,64,128]{2,1,0:T(8,128)(2,1)}, u32[]{:S(2)}, u32[]{:S(2)}) collective-permute-start(bf16[48,64,128]{2,1,0:T(8,128)(2,1)S(1)} %copy-done.9), channel_id=1, source_target_pairs={{0,16},{8,24},{16,0},{24,8},{1,17},{9,25},{17,1},{25,9},{2,18},{10... | collective-permute-start | bytes 2359304 | tf_op jit(solution)/shard_map/ppermute | solution.py:264
  78.9 23.7 %all-to-all-start.2 = ((bf16[8,384,128]{2,1,0:T(8,128)(2,1)}), bf16[8,384,128]{2,1,0:T(8,128)(2,1)S(1)}, u32[]{:S(2)}, u32[]{:S(2)}) async-start(bf16[8,384,128]{2,1,0:T(8,128)(2,1)} %chunk_products.5), calls=%async_computation.2 | async-start | bytes 1572864 | tf_op jit(solution)/shard_map/all_to_all | solution.py:302
  82.5 2.7 %collective-permute-start.10 = (bf16[48,64,128]{2,1,0:T(8,128)(2,1)S(1)}, bf16[48,64,128]{2,1,0:T(8,128)(2,1)}, u32[]{:S(2)}, u32[]{:S(2)}) collective-permute-start(bf16[48,64,128]{2,1,0:T(8,128)(2,1)S(1)} %copy-done.9), channel_id=1, source_target_pairs={{0,8},{8,0},{16,24},{24,16},{1,9},{9,1},{17,25},{25,17},{2,10},{10... | collective-permute-start | bytes 2359304 | tf_op jit(solution)/shard_map/ppermute | solution.py:267
  82.6 3.7 %collective-permute-start.11 = (bf16[48,64,128]{2,1,0:T(8,128)(2,1)}, bf16[48,64,128]{2,1,0:T(8,128)(2,1)}, u32[]{:S(2)}, u32[]{:S(2)}) collective-permute-start(bf16[48,64,128]{2,1,0:T(8,128)(2,1)} %collective-permute-done.6.refs_6_), channel_id=1, source_target_pairs={{0,8},{8,0},{16,24},{24,16},{1,9},{9,1},{17,25},{25,17},{2,10},{10... | collective-permute-start | bytes 2359304 | tf_op jit(solution)/shard_map/ppermute | solution.py:267
  83.1 23.7 %collective-permute-start = (bf16[8,1040,128]{2,1,0:T(8,128)(2,1)}, bf16[8,1040,128]{2,1,0:T(8,128)(2,1)}, u32[]{:S(2)}, u32[]{:S(2)}) collective-permute-start(bf16[8,1040,128]{2,1,0:T(8,128)(2,1)} %bitcast.12), channel_id=1, source_target_pairs={{0,8},{8,0},{16,24},{24,16},{1,9},{9,1},{17,25},{25,17},{2,10},{10... | collective-permute-start | bytes 6389768 | tf_op jit(solution)/shard_map/ppermute | solution.py:267
  83.2 23.1 %collective-permute-start.9 = (bf16[48,64,128]{2,1,0:T(8,128)(2,1)}, bf16[48,64,128]{2,1,0:T(8,128)(2,1)}, u32[]{:S(2)}, u32[]{:S(2)}) collective-permute-start(bf16[48,64,128]{2,1,0:T(8,128)(2,1)} %get-tuple-element.31.refs_4_), channel_id=1, source_target_pairs={{0,16},{8,24},{16,0},{24,8},{1,17},{9,25},{17,1},{25,9},{2,18},{10... | collective-permute-start | bytes 2359304 | tf_op jit(solution)/shard_map/ppermute | solution.py:264
  102.6 23.9 %all-to-all-start.3 = ((bf16[8,384,128]{2,1,0:T(8,128)(2,1)}), bf16[8,384,128]{2,1,0:T(8,128)(2,1)S(1)}, u32[]{:S(2)}, u32[]{:S(2)}) async-start(bf16[8,384,128]{2,1,0:T(8,128)(2,1)} %chunk_products.6), calls=%async_computation.3 | async-start | bytes 1572864 | tf_op jit(solution)/shard_map/all_to_all | solution.py:302
  106.2 2.6 %collective-permute-start.1 = (bf16[48,64,128]{2,1,0:T(8,128)(2,1)}, bf16[48,64,128]{2,1,0:T(8,128)(2,1)S(1)}, u32[]{:S(2)}, u32[]{:S(2)}) collective-permute-start(bf16[48,64,128]{2,1,0:T(8,128)(2,1)} %get-tuple-element.31.refs_4_), channel_id=1, source_target_pairs={{0,8},{8,0},{16,24},{24,16},{1,9},{9,1},{17,25},{25,17},{2,10},{10... | collective-permute-start | bytes 2359304 | tf_op jit(solution)/shard_map/ppermute | solution.py:267
  106.3 3.6 %collective-permute-start.12 = (bf16[48,64,128]{2,1,0:T(8,128)(2,1)}, bf16[48,64,128]{2,1,0:T(8,128)(2,1)S(1)}, u32[]{:S(2)}, u32[]{:S(2)}) collective-permute-start(bf16[48,64,128]{2,1,0:T(8,128)(2,1)} %collective-permute-done.9.refs_6_), channel_id=1, source_target_pairs={{0,8},{8,0},{16,24},{24,16},{1,9},{9,1},{17,25},{25,17},{2,10},{10... | collective-permute-start | bytes 2359304 | tf_op jit(solution)/shard_map/ppermute | solution.py:267
  127.5 23.9 %all-to-all-start = ((bf16[8,384,128]{2,1,0:T(8,128)(2,1)}), bf16[8,384,128]{2,1,0:T(8,128)(2,1)S(1)}, u32[]{:S(2)}, u32[]{:S(2)}) async-start(bf16[8,384,128]{2,1,0:T(8,128)(2,1)} %chunk_products.7), calls=%async_computation | async-start | bytes 1572864 | tf_op jit(solution)/shard_map/all_to_all | solution.py:302
  151.4 1.9 %copy-start.2 = (f32[384,2048]{1,0:T(8,128)S(1)}, f32[384,2048]{1,0:T(8,128)}, u32[]{:S(2)}) copy-start(f32[384,2048]{1,0:T(8,128)} %get-tuple-element.37.one) | copy-start | bytes 9437188
  153.3 1.9 %copy-start.3 = (f32[384,2048]{1,0:T(8,128)S(1)}, f32[384,2048]{1,0:T(8,128)}, u32[]{:S(2)}) copy-start(f32[384,2048]{1,0:T(8,128)} %get-tuple-element.38.two) | copy-start | bytes 9437188
  (10 other events, 11.7 us)
Sparse Core Ops, SparseCore 0:
  9.5 52.5 all-gather.2

commit v9 on v8

--- a/solution.py
+++ b/solution.py
@@ -8,7 +8,8 @@
 from jax.sharding import PartitionSpec as P
 
 VMEM_WHOLE = 58 * 1024 * 1024
-VMEM_MOST = 44 * 1024 * 1024
+VMEM_MOST = 30 * 1024 * 1024
+VMEM_LAST = 16 * 1024 * 1024
 VMEM_PART = 44 * 1024 * 1024
 SMALL = pl.CostEstimate(flops=0, bytes_accessed=4096, transcendentals=0)
 
@@ -175,14 +176,12 @@
         place_tiles(dense.shape[0] // (depth // count), owners, tiles_each, positions, sources, dense)
         unpack_rows(chunks, rows)
 
-    step = outs[0].shape[-1]
+    step = dense.shape[1] // pl.num_programs(0)
     columns = pl.ds(pl.multiple_of(pl.program_id(0) * step, step), step)
-    if len(outs) > 2:
-        outs[2][...] = dense[depth:, columns]
-    for side in range(2):
-        part = rows[side * height : (side + 1) * height]
-        sums = jnp.dot(part, dense[:depth, columns], preferred_element_type=jnp.float32)
-        outs[side][...] = sums.astype(outs[side].dtype)
+    if len(outs) > 1:
+        outs[1][:, columns] = dense[depth:, columns]
+    sums = jnp.dot(rows[...], dense[:depth, columns], preferred_element_type=jnp.float32)
+    outs[0][:, columns] = sums.astype(outs[0].dtype)
 
 
 def first_shares(chunks, positions, sources, tiles_each, size, dtype):
@@ -190,61 +189,60 @@
     depth = len(chunks) * owners * lanes // 2
     step = largest_divisor(size, 256)
     whole = lambda j, s: (0, 0, 0)
-    heights = [height] * 2 + ([size - depth] if depth < size else [])
-    kinds = [dtype] * 2 + [sources[0].dtype]
+    heights = [2 * height] + ([size - depth] if depth < size else [])
+    kinds = [dtype, sources[0].dtype]
     return pl.pallas_call(
         functools.partial(first_kernel, len(chunks), len(sources), tiles_each),
         grid_spec=pltpu.PrefetchScalarGridSpec(
             num_scalar_prefetch=1,
             grid=(size // step,),
             in_specs=[pl.BlockSpec(array.shape, whole) for array in [*chunks, *sources]],
-            out_specs=[pl.BlockSpec((tall, step), lambda j, s: (0, j)) for tall in heights],
+            out_specs=[pl.BlockSpec(memory_space=pltpu.VMEM)] * len(heights),
             scratch_shapes=[
                 pltpu.VMEM((size, size), sources[0].dtype),
                 pltpu.VMEM((2 * height, depth), jnp.bfloat16),
             ],
         ),
-        out_shape=[jax.ShapeDtypeStruct((tall, size), kind) for tall, kind in zip(heights, kinds)],
+        out_shape=[pltpu.VMEM((tall, size), kind) for tall, kind in zip(heights, kinds)],
         cost_estimate=SMALL,
         compiler_params=pltpu.CompilerParams(vmem_limit_bytes=VMEM_MOST),
         name="first_shares",
     )(positions, *chunks, *sources)
 
 
-def last_kernel(chunk, metric, one, two, out, rows):
+def last_kernel(chunk, metric, before, out, rows):
     height = chunk.shape[1]
 
     @pl.when(pl.program_id(0) == 0)
     def _():
         unpack_rows([chunk], rows)
 
-    for side, before in enumerate((one, two)):
-        part = rows[side * height : (side + 1) * height]
-        sums = jnp.dot(part, metric[...], preferred_element_type=jnp.float32)
-        out[side] = (sums + before[...]).astype(out.dtype)
-
-
-def last_share(chunk, metric, one, two):
+    step = out.shape[-1]
+    columns = pl.ds(pl.multiple_of(pl.program_id(0) * step, step), step)
+    sums = jnp.dot(rows[...], metric[:, columns], preferred_element_type=jnp.float32) + before[:, columns]
+    out[0] = sums[:height].astype(out.dtype)
+    out[1] = sums[height:].astype(out.dtype)
+
+
+def last_share(chunk, metric, before):
     owners, height, lanes = chunk.shape
     depth, size = metric.shape
     step = largest_divisor(size, 256)
-    tall = pl.BlockSpec((height, step), lambda j: (0, j))
     return pl.pallas_call(
         last_kernel,
         grid=(size // step,),
         in_specs=[
             pl.BlockSpec(chunk.shape, lambda j: (0, 0, 0)),
-            pl.BlockSpec((depth, step), lambda j: (0, j)),
-            tall,
-            tall,
+            pl.BlockSpec(memory_space=pltpu.VMEM),
+            pl.BlockSpec(memory_space=pltpu.VMEM),
         ],
         out_specs=pl.BlockSpec((2, height, step), lambda j: (0, 0, j)),
         out_shape=jax.ShapeDtypeStruct((2, height, size), jnp.bfloat16),
         scratch_shapes=[pltpu.VMEM((2 * height, depth), jnp.bfloat16)],
         cost_estimate=SMALL,
-        compiler_params=pltpu.CompilerParams(vmem_limit_bytes=VMEM_PART),
+        compiler_params=pltpu.CompilerParams(vmem_limit_bytes=VMEM_LAST),
         name="last_share",
-    )(chunk, metric, one, two)
+    )(chunk, metric, before)
 
 
 def after(value, others):
@@ -306,10 +304,11 @@
     size = part * aux_count
     if chunk_count > 1:
         ready = after(products[:-1], made)
-        one, two, metric = first_shares(ready, positions, sources, half_tiles, size, jnp.float32)
-        result = last_share(products[-1], metric, one, two)
+        before, metric = first_shares(ready, positions, sources, half_tiles, size, jnp.float32)
+        result = last_share(products[-1], metric, before)
     else:
-        result = jnp.stack(first_shares(products, positions, sources, half_tiles, size, jnp.bfloat16))
+        result = first_shares(products, positions, sources, half_tiles, size, jnp.bfloat16)[0]
+        result = result.reshape(2, group // 2, domain // aux_count, size)
     return result.reshape(group, domain // aux_count, size)
 
 

time: 170 us -> 170 us (level)
  local copies, waits for them, and re-layouts: 16.4 us -> 18.1 us
  transfers between devices with their start and end apart: 18 -> 18, of which waited for: 11 -> 10; matrix products, arithmetic and copies ran while one was open for 1% -> 1% of each run, Pallas kernels for 44% -> 44%
where the time goes in v9:
time: 170 us; the launch traced here: 168 us
  Pallas kernels  78.9 us (46%)
  waiting for transfers between devices  31.6 us (19%)
  starting transfers between devices  24.8 us (15%)
  local copies, waits for them, and re-layouts  18.1 us (11%)
  between operations  13.6 us (8%)
    pallas_call x4, Pallas kernels, chunk_products(): pl.pallas_call(functools.partial(product_kernel, pairs, split_rows, strea...  52.9 us
    all_to_all x4, starting transfers between devices, shards(): lax.all_to_all(made, 'aux', split_axis=0, concat_axis=0, tiled=True)  16.5 us
    unnamed x34, local copies, waits for them, and re-layouts  16.1 us
    ppermute x4, waiting for transfers between devices, to_far(): return lax.ppermute(array, 'orb', moves)  13.6 us
    pallas_call x1, Pallas kernels, first_shares(): pl.pallas_call(functools.partial(first_kernel, len(chunks), len(sources),...  12.8 us
    all_to_all x4, waiting for transfers between devices, shards(): lax.all_to_all(made, 'aux', split_axis=0, concat_axis=0, tiled=True)  10.4 us
    pallas_call x2, Pallas kernels, pack_chunks(): pl.pallas_call(functools.partial(pack_kernel, width, first), grid=(orbita...  8.12 us
    ppermute x9, waiting for transfers between devices, to_mate(): return lax.ppermute(array, 'orb', [(g, g ^ 1) for g in range(orb_count)])  7.47 us
  transfers between devices with their start and end apart: 18, of which 10 were waited for; matrix products, arithmetic and copies ran while one was open for 1% of the time, Pallas kernels for 44%

profile of v9, /device:TPU:0, one launch (start us, length us, event | category | flops | bytes accessed | tf_op | source)
XLA Modules:
  0.0 168.5 jit_solution(15066702314884996451)
XLA Ops:
  8.4 3.9 %pack_chunks.3.refs_4_ = bf16[48,64,128]{2,1,0:T(8,128)(2,1)} custom-call(bf16[48,128,256]{2,1,0:T(8,128)(2,1)} %source.3), custom_call_target="tpu_custom_call" | custom-call | bytes 4096 | tf_op jit(solution)/shard_map/pack_chunks/pallas_call | solution.py:33
  12.3 3.0 %collective-permute-start.2 = (bf16[48,64,128]{2,1,0:T(8,128)(2,1)}, bf16[48,64,128]{2,1,0:T(8,128)(2,1)S(1)}, u32[]{:S(2)}, u32[]{:S(2)}) collective-permute-start(bf16[48,64,128]{2,1,0:T(8,128)(2,1)} %pack_chunks.3.refs_4_), channel_id=1, source_target_pairs={{0,16},{8,24},{16,0},{24,8},{1,17},{9,25},{17,1},{25,9},{2,18},{10... | collective-permute-start | bytes 2359304 | tf_op jit(solution)/shard_map/ppermute | solution.py:262
  15.3 4.2 %pack_chunks.2 = (bf16[48,64,128]{2,1,0:T(8,128)(2,1)}, bf16[48,64,128]{2,1,0:T(8,128)(2,1)}, bf16[48,64,128]{2,1,0:T(8,128)(2,1)}) custom-call(bf16[48,128,256]{2,1,0:T(8,128)(2,1)} %source.3), custom_call_target="tpu_custom_call" | custom-call | bytes 4096 | tf_op jit(solution)/shard_map/pack_chunks/pallas_call | solution.py:33
  19.5 13.6 %collective-permute-done.2.refs_6_ = bf16[48,64,128]{2,1,0:T(8,128)(2,1)S(1)} collective-permute-done((bf16[48,64,128]{2,1,0:T(8,128)(2,1)}, bf16[48,64,128]{2,1,0:T(8,128)(2,1)S(1)}, u32[]{:S(2)}, u32[]{:S(2)}) %collective-permute-start.2) | collective-permute-done | bytes 786464 | tf_op jit(solution)/shard_map/ppermute | solution.py:262
  34.0 1.7 collective-permute-start.3
  39.2 13.1 %chunk_products.4 = bf16[8,384,128]{2,1,0:T(8,128)(2,1)} custom-call(s32[576]{0:T(1024)S(1)} %reshape.24.slots, bf16[2,24,12,128,128]{4,3,2,1,0:T(8,128)(2,1)} %bitcast.15, bf16[2,24,12,128,128]{4,3,2,1,0:T(8,128)(2,1)} %bitcast.16, bf16[2,24,12,128,128]{4,3,2,1,0:T(8,128)(2,1)} %bitcast.17, bf16[2,24,12,128,128]{4,3,2,1,0:T(8,128)(2,1)} %bitcast.18, ...), custom_call_target="tpu_custom_call" | custom-call | bytes 4096 | tf_op jit(solution)/shard_map/chunk_products/pallas_call | solution.py:109
  52.3 5.8 %all-to-all-start.1 = ((bf16[8,384,128]{2,1,0:T(8,128)(2,1)}), bf16[8,384,128]{2,1,0:T(8,128)(2,1)S(1)}, u32[]{:S(2)}, u32[]{:S(2)}) async-start(bf16[8,384,128]{2,1,0:T(8,128)(2,1)} %chunk_products.4), calls=%async_computation.1 | async-start | bytes 1572864 | tf_op jit(solution)/shard_map/all_to_all | solution.py:300
  59.3 1.4 collective-permute-done.7.refs_5_
  61.8 13.1 %chunk_products.5 = bf16[8,384,128]{2,1,0:T(8,128)(2,1)} custom-call(s32[576]{0:T(1024)S(1)} %reshape.24.slots, bf16[2,24,12,128,128]{4,3,2,1,0:T(8,128)(2,1)} %bitcast.19, bf16[2,24,12,128,128]{4,3,2,1,0:T(8,128)(2,1)} %bitcast.20, bf16[2,24,12,128,128]{4,3,2,1,0:T(8,128)(2,1)} %bitcast.21, bf16[2,24,12,128,128]{4,3,2,1,0:T(8,128)(2,1)} %bitcast.22, ...), custom_call_target="tpu_custom_call" | custom-call | bytes 4096 | tf_op jit(solution)/shard_map/chunk_products/pallas_call | solution.py:109
  74.9 4.1 %all-to-all-done.1.refs_0_ = bf16[8,384,128]{2,1,0:T(8,128)(2,1)S(1)} async-done(((bf16[8,384,128]{2,1,0:T(8,128)(2,1)}), bf16[8,384,128]{2,1,0:T(8,128)(2,1)S(1)}, u32[]{:S(2)}, u32[]{:S(2)}) %all-to-all-start.1) | async-done | bytes 786464 | tf_op jit(solution)/shard_map/all_to_all | solution.py:300
  79.0 3.5 %all-to-all-start.2 = ((bf16[8,384,128]{2,1,0:T(8,128)(2,1)}), bf16[8,384,128]{2,1,0:T(8,128)(2,1)S(1)}, u32[]{:S(2)}, u32[]{:S(2)}) async-start(bf16[8,384,128]{2,1,0:T(8,128)(2,1)} %chunk_products.5), calls=%async_computation.2 | async-start | bytes 1572864 | tf_op jit(solution)/shard_map/all_to_all | solution.py:300
  86.4 13.5 %chunk_products.6 = bf16[8,384,128]{2,1,0:T(8,128)(2,1)} custom-call(s32[576]{0:T(1024)S(1)} %reshape.24.slots, bf16[2,24,12,128,128]{4,3,2,1,0:T(8,128)(2,1)} %bitcast.23, bf16[2,24,12,128,128]{4,3,2,1,0:T(8,128)(2,1)} %bitcast.24, bf16[2,24,12,128,128]{4,3,2,1,0:T(8,128)(2,1)} %bitcast.25, bf16[2,24,12,128,128]{4,3,2,1,0:T(8,128)(2,1)} %bitcast.26, ...), custom_call_target="tpu_custom_call" | custom-call | bytes 4096 | tf_op jit(solution)/shard_map/chunk_products/pallas_call | solution.py:109
  99.8 2.8 %all-to-all-done.2.refs_1_ = bf16[8,384,128]{2,1,0:T(8,128)(2,1)S(1)} async-done(((bf16[8,384,128]{2,1,0:T(8,128)(2,1)}), bf16[8,384,128]{2,1,0:T(8,128)(2,1)S(1)}, u32[]{:S(2)}, u32[]{:S(2)}) %all-to-all-start.2) | async-done | bytes 786464 | tf_op jit(solution)/shard_map/all_to_all | solution.py:300
  102.7 3.6 %all-to-all-start.3 = ((bf16[8,384,128]{2,1,0:T(8,128)(2,1)}), bf16[8,384,128]{2,1,0:T(8,128)(2,1)S(1)}, u32[]{:S(2)}, u32[]{:S(2)}) async-start(bf16[8,384,128]{2,1,0:T(8,128)(2,1)} %chunk_products.6), calls=%async_computation.3 | async-start | bytes 1572864 | tf_op jit(solution)/shard_map/all_to_all | solution.py:300
  106.8 2.0 %collective-permute-done.1.refs_5_ = bf16[48,64,128]{2,1,0:T(8,128)(2,1)S(1)} collective-permute-done((bf16[48,64,128]{2,1,0:T(8,128)(2,1)}, bf16[48,64,128]{2,1,0:T(8,128)(2,1)S(1)}, u32[]{:S(2)}, u32[]{:S(2)}) %collective-permute-start.1) | collective-permute-done | bytes 786464 | tf_op jit(solution)/shard_map/ppermute | solution.py:265
  109.9 13.2 %chunk_products.7 = bf16[8,384,128]{2,1,0:T(8,128)(2,1)} custom-call(s32[576]{0:T(1024)S(1)} %reshape.24.slots, bf16[2,24,12,128,128]{4,3,2,1,0:T(8,128)(2,1)} %bitcast.27, bf16[2,24,12,128,128]{4,3,2,1,0:T(8,128)(2,1)} %bitcast.28, bf16[2,24,12,128,128]{4,3,2,1,0:T(8,128)(2,1)} %bitcast.29, bf16[2,24,12,128,128]{4,3,2,1,0:T(8,128)(2,1)} %bitcast.30, ...), custom_call_target="tpu_custom_call" | custom-call | bytes 4096 | tf_op jit(solution)/shard_map/chunk_products/pallas_call | solution.py:109
  123.2 3.5 %all-to-all-done.3.refs_2_ = bf16[8,384,128]{2,1,0:T(8,128)(2,1)S(1)} async-done(((bf16[8,384,128]{2,1,0:T(8,128)(2,1)}), bf16[8,384,128]{2,1,0:T(8,128)(2,1)S(1)}, u32[]{:S(2)}, u32[]{:S(2)}) %all-to-all-start.3) | async-done | bytes 786464 | tf_op jit(solution)/shard_map/all_to_all | solution.py:300
  127.5 3.5 %all-to-all-start = ((bf16[8,384,128]{2,1,0:T(8,128)(2,1)}), bf16[8,384,128]{2,1,0:T(8,128)(2,1)S(1)}, u32[]{:S(2)}, u32[]{:S(2)}) async-start(bf16[8,384,128]{2,1,0:T(8,128)(2,1)} %chunk_products.7), calls=%async_computation | async-start | bytes 1572864 | tf_op jit(solution)/shard_map/all_to_all | solution.py:300
  133.7 1.6 copy-done.6
  135.3 12.8 %first_shares.1 = (f32[768,2048]{1,0:T(8,128)S(1)}, bf16[512,2048]{1,0:T(8,128)(2,1)S(1)}) custom-call(s32[256]{0:T(256)S(1)} %reshape.29.positions, bf16[8,384,128]{2,1,0:T(8,128)(2,1)S(1)} %all-to-all-done.1.refs_0_, bf16[8,384,128]{2,1,0:T(8,128)(2,1)S(1)} %all-to-all-done.2.refs_1_, bf16[8,384,128]{2,1,0:T(8,128)(2,1)S(1)} %copy-done.5, ...), custom_call_target="tpu_custom_call" | custom-call | bytes 4096 | tf_op jit(solution)/shard_map/first_shares/pallas_call | solution.py:194
  148.1 2.6 %copy-done.1 = f32[768,2048]{1,0:T(8,128)} copy-done((f32[768,2048]{1,0:T(8,128)}, f32[768,2048]{1,0:T(8,128)S(1)}, u32[]{:S(2)}) %copy-start.1) | copy-done | bytes 6291480
  152.1 2.8 %copy-done.2 = f32[768,2048]{1,0:T(8,128)S(1)} copy-done((f32[768,2048]{1,0:T(8,128)S(1)}, f32[768,2048]{1,0:T(8,128)}, u32[]{:S(2)}) %copy-start.2) | copy-done | bytes 6291480
  154.9 1.6 copy-done.8
  156.4 5.2 %last_share.1 = bf16[2,384,2048]{2,1,0:T(8,128)(2,1)} custom-call(bf16[8,384,128]{2,1,0:T(8,128)(2,1)S(1)} %all-to-all-done.chunk, bf16[512,2048]{1,0:T(8,128)(2,1)S(1)} %copy-done.8, f32[768,2048]{1,0:T(8,128)S(1)} %copy-done.2), custom_call_target="tpu_custom_call" | custom-call | bytes 4096 | tf_op jit(solution)/shard_map/last_share/pallas_call | solution.py:231
  (68 shorter events, 18.9 us)
Async XLA Ops:
  6.5 76.6 %all-gather.3.cloned.1.call-start = ((), (), s32[]{:S(2)}) async-start(), calls=%async_computation.4 | async-start | bytes 2396160 | tf_op jit(solution)/shard_map/all_gather | solution.py:278
  8.4 27.3 %copy-start.15 = (s32[48,12]{0,1:T(8,128)S(1)}, s32[48,12]{0,1:T(8,128)}, u32[]{:S(2)}) copy-start(s32[48,12]{0,1:T(8,128)} %param.7) | copy-start | bytes 6916
  12.3 24.6 %copy-start.3 = (bf16[48,64,128]{2,1,0:T(8,128)(2,1)S(1)}, bf16[48,64,128]{2,1,0:T(8,128)(2,1)}, u32[]{:S(2)}) copy-start(bf16[48,64,128]{2,1,0:T(8,128)(2,1)} %pack_chunks.3.refs_4_) | copy-start | bytes 2359300
  12.3 20.8 %collective-permute-start.2 = (bf16[48,64,128]{2,1,0:T(8,128)(2,1)}, bf16[48,64,128]{2,1,0:T(8,128)(2,1)S(1)}, u32[]{:S(2)}, u32[]{:S(2)}) collective-permute-start(bf16[48,64,128]{2,1,0:T(8,128)(2,1)} %pack_chunks.3.refs_4_), channel_id=1, source_target_pairs={{0,16},{8,24},{16,0},{24,8},{1,17},{9,25},{17,1},{25,9},{2,18},{10... | collective-permute-start | bytes 2359304 | tf_op jit(solution)/shard_map/ppermute | solution.py:262
  15.3 20.6 %collective-permute-start.4 = (bf16[48,64,128]{2,1,0:T(8,128)(2,1)}, bf16[48,64,128]{2,1,0:T(8,128)(2,1)S(1)}, u32[]{:S(2)}, u32[]{:S(2)}) collective-permute-start(bf16[48,64,128]{2,1,0:T(8,128)(2,1)} %pack_chunks.3.refs_4_), channel_id=1, source_target_pairs={{0,8},{8,0},{16,24},{24,16},{1,9},{9,1},{17,25},{25,17},{2,10},{10... | collective-permute-start | bytes 2359304 | tf_op jit(solution)/shard_map/ppermute | solution.py:265
  33.1 3.8 %collective-permute-start.5 = (bf16[48,64,128]{2,1,0:T(8,128)(2,1)S(1)}, bf16[48,64,128]{2,1,0:T(8,128)(2,1)}, u32[]{:S(2)}, u32[]{:S(2)}) collective-permute-start(bf16[48,64,128]{2,1,0:T(8,128)(2,1)S(1)} %collective-permute-done.2.refs_6_), channel_id=1, source_target_pairs={{0,8},{8,0},{16,24},{24,16},{1,9},{9,1},{17,25},{25,17},{2,10},{10... | collective-permute-start | bytes 2359304 | tf_op jit(solution)/shard_map/ppermute | solution.py:265
  34.0 24.2 %collective-permute-start.3 = (bf16[48,64,128]{2,1,0:T(8,128)(2,1)}, bf16[48,64,128]{2,1,0:T(8,128)(2,1)}, u32[]{:S(2)}, u32[]{:S(2)}) collective-permute-start(bf16[48,64,128]{2,1,0:T(8,128)(2,1)} %get-tuple-element.26.refs_4_), channel_id=1, source_target_pairs={{0,16},{8,24},{16,0},{24,8},{1,17},{9,25},{17,1},{25,9},{2,18},{10... | collective-permute-start | bytes 2359304 | tf_op jit(solution)/shard_map/ppermute | solution.py:262
  39.2 18.9 %copy-start.10 = (bf16[48,64,128]{2,1,0:T(8,128)(2,1)S(1)}, bf16[48,64,128]{2,1,0:T(8,128)(2,1)}, u32[]{:S(2)}) copy-start(bf16[48,64,128]{2,1,0:T(8,128)(2,1)} %get-tuple-element.26.refs_4_) | copy-start | bytes 2359300
  39.2 19.5 %copy-start.9 = (bf16[48,64,128]{2,1,0:T(8,128)(2,1)S(1)}, bf16[48,64,128]{2,1,0:T(8,128)(2,1)}, u32[]{:S(2)}) copy-start(bf16[48,64,128]{2,1,0:T(8,128)(2,1)} %get-tuple-element.28.refs_4_) | copy-start | bytes 2359300
  52.3 26.7 %all-to-all-start.1 = ((bf16[8,384,128]{2,1,0:T(8,128)(2,1)}), bf16[8,384,128]{2,1,0:T(8,128)(2,1)S(1)}, u32[]{:S(2)}, u32[]{:S(2)}) async-start(bf16[8,384,128]{2,1,0:T(8,128)(2,1)} %chunk_products.4), calls=%async_computation.1 | async-start | bytes 1572864 | tf_op jit(solution)/shard_map/all_to_all | solution.py:300
  58.1 2.6 %collective-permute-start.7 = (bf16[48,64,128]{2,1,0:T(8,128)(2,1)S(1)}, bf16[48,64,128]{2,1,0:T(8,128)(2,1)S(1)}, u32[]{:S(2)}, u32[]{:S(2)}) collective-permute-start(bf16[48,64,128]{2,1,0:T(8,128)(2,1)S(1)} %copy-done.10), channel_id=1, source_target_pairs={{0,8},{8,0},{16,24},{24,16},{1,9},{9,1},{17,25},{25,17},{2,10},{10... | collective-permute-start | bytes 2359304 | tf_op jit(solution)/shard_map/ppermute | solution.py:265
  58.2 3.6 %collective-permute-start.8 = (bf16[48,64,128]{2,1,0:T(8,128)(2,1)}, bf16[48,64,128]{2,1,0:T(8,128)(2,1)S(1)}, u32[]{:S(2)}, u32[]{:S(2)}) collective-permute-start(bf16[48,64,128]{2,1,0:T(8,128)(2,1)} %collective-permute-done.3.refs_6_), channel_id=1, source_target_pairs={{0,8},{8,0},{16,24},{24,16},{1,9},{9,1},{17,25},{25,17},{2,10},{10... | collective-permute-start | bytes 2359304 | tf_op jit(solution)/shard_map/ppermute | solution.py:265
  58.7 23.9 %collective-permute-start.6 = (bf16[48,64,128]{2,1,0:T(8,128)(2,1)S(1)}, bf16[48,64,128]{2,1,0:T(8,128)(2,1)}, u32[]{:S(2)}, u32[]{:S(2)}) collective-permute-start(bf16[48,64,128]{2,1,0:T(8,128)(2,1)S(1)} %copy-done.9), channel_id=1, source_target_pairs={{0,16},{8,24},{16,0},{24,8},{1,17},{9,25},{17,1},{25,9},{2,18},{10... | collective-permute-start | bytes 2359304 | tf_op jit(solution)/shard_map/ppermute | solution.py:262
  79.0 23.7 %all-to-all-start.2 = ((bf16[8,384,128]{2,1,0:T(8,128)(2,1)}), bf16[8,384,128]{2,1,0:T(8,128)(2,1)S(1)}, u32[]{:S(2)}, u32[]{:S(2)}) async-start(bf16[8,384,128]{2,1,0:T(8,128)(2,1)} %chunk_products.5), calls=%async_computation.2 | async-start | bytes 1572864 | tf_op jit(solution)/shard_map/all_to_all | solution.py:300
  82.5 2.7 %collective-permute-start.10 = (bf16[48,64,128]{2,1,0:T(8,128)(2,1)S(1)}, bf16[48,64,128]{2,1,0:T(8,128)(2,1)}, u32[]{:S(2)}, u32[]{:S(2)}) collective-permute-start(bf16[48,64,128]{2,1,0:T(8,128)(2,1)S(1)} %copy-done.9), channel_id=1, source_target_pairs={{0,8},{8,0},{16,24},{24,16},{1,9},{9,1},{17,25},{25,17},{2,10},{10... | collective-permute-start | bytes 2359304 | tf_op jit(solution)/shard_map/ppermute | solution.py:265
  82.6 3.7 %collective-permute-start.11 = (bf16[48,64,128]{2,1,0:T(8,128)(2,1)}, bf16[48,64,128]{2,1,0:T(8,128)(2,1)}, u32[]{:S(2)}, u32[]{:S(2)}) collective-permute-start(bf16[48,64,128]{2,1,0:T(8,128)(2,1)} %collective-permute-done.6.refs_6_), channel_id=1, source_target_pairs={{0,8},{8,0},{16,24},{24,16},{1,9},{9,1},{17,25},{25,17},{2,10},{10... | collective-permute-start | bytes 2359304 | tf_op jit(solution)/shard_map/ppermute | solution.py:265
  83.1 23.7 %collective-permute-start = (bf16[8,1040,128]{2,1,0:T(8,128)(2,1)}, bf16[8,1040,128]{2,1,0:T(8,128)(2,1)}, u32[]{:S(2)}, u32[]{:S(2)}) collective-permute-start(bf16[8,1040,128]{2,1,0:T(8,128)(2,1)} %bitcast.12), channel_id=1, source_target_pairs={{0,8},{8,0},{16,24},{24,16},{1,9},{9,1},{17,25},{25,17},{2,10},{10... | collective-permute-start | bytes 6389768 | tf_op jit(solution)/shard_map/ppermute | solution.py:265
  83.2 23.1 %collective-permute-start.9 = (bf16[48,64,128]{2,1,0:T(8,128)(2,1)}, bf16[48,64,128]{2,1,0:T(8,128)(2,1)}, u32[]{:S(2)}, u32[]{:S(2)}) collective-permute-start(bf16[48,64,128]{2,1,0:T(8,128)(2,1)} %get-tuple-element.30.refs_4_), channel_id=1, source_target_pairs={{0,16},{8,24},{16,0},{24,8},{1,17},{9,25},{17,1},{25,9},{2,18},{10... | collective-permute-start | bytes 2359304 | tf_op jit(solution)/shard_map/ppermute | solution.py:262
  102.7 23.9 %all-to-all-start.3 = ((bf16[8,384,128]{2,1,0:T(8,128)(2,1)}), bf16[8,384,128]{2,1,0:T(8,128)(2,1)S(1)}, u32[]{:S(2)}, u32[]{:S(2)}) async-start(bf16[8,384,128]{2,1,0:T(8,128)(2,1)} %chunk_products.6), calls=%async_computation.3 | async-start | bytes 1572864 | tf_op jit(solution)/shard_map/all_to_all | solution.py:300
  106.2 2.6 %collective-permute-start.1 = (bf16[48,64,128]{2,1,0:T(8,128)(2,1)}, bf16[48,64,128]{2,1,0:T(8,128)(2,1)S(1)}, u32[]{:S(2)}, u32[]{:S(2)}) collective-permute-start(bf16[48,64,128]{2,1,0:T(8,128)(2,1)} %get-tuple-element.30.refs_4_), channel_id=1, source_target_pairs={{0,8},{8,0},{16,24},{24,16},{1,9},{9,1},{17,25},{25,17},{2,10},{10... | collective-permute-start | bytes 2359304 | tf_op jit(solution)/shard_map/ppermute | solution.py:265
  106.3 3.6 %collective-permute-start.12 = (bf16[48,64,128]{2,1,0:T(8,128)(2,1)}, bf16[48,64,128]{2,1,0:T(8,128)(2,1)S(1)}, u32[]{:S(2)}, u32[]{:S(2)}) collective-permute-start(bf16[48,64,128]{2,1,0:T(8,128)(2,1)} %collective-permute-done.9.refs_6_), channel_id=1, source_target_pairs={{0,8},{8,0},{16,24},{24,16},{1,9},{9,1},{17,25},{25,17},{2,10},{10... | collective-permute-start | bytes 2359304 | tf_op jit(solution)/shard_map/ppermute | solution.py:265
  127.5 24.6 %all-to-all-start = ((bf16[8,384,128]{2,1,0:T(8,128)(2,1)}), bf16[8,384,128]{2,1,0:T(8,128)(2,1)S(1)}, u32[]{:S(2)}, u32[]{:S(2)}) async-start(bf16[8,384,128]{2,1,0:T(8,128)(2,1)} %chunk_products.7), calls=%async_computation | async-start | bytes 1572864 | tf_op jit(solution)/shard_map/all_to_all | solution.py:300
  148.1 2.6 %copy-start.1 = (f32[768,2048]{1,0:T(8,128)}, f32[768,2048]{1,0:T(8,128)S(1)}, u32[]{:S(2)}) copy-start(f32[768,2048]{1,0:T(8,128)S(1)} %get-tuple-element.36.before) | copy-start | bytes 18874372
  152.1 2.8 %copy-start.2 = (f32[768,2048]{1,0:T(8,128)S(1)}, f32[768,2048]{1,0:T(8,128)}, u32[]{:S(2)}) copy-start(f32[768,2048]{1,0:T(8,128)} %copy-done.1) | copy-start | bytes 18874372
  (10 other events, 11.7 us)
Sparse Core Ops, SparseCore 0:
  9.5 52.5 all-gather.2

commit v10 on v9

--- a/solution.py
+++ b/solution.py
@@ -28,16 +28,17 @@
 def pack_chunks(factors, width, begin, count):
     orbitals, domain, part = factors.shape
     first = begin * width
+    lanes = min(part, 2 * width) if first + count * width <= 2 * width else part
     step = largest_divisor(orbitals, 12)
     packed = (step, domain // 2, 2 * width)
     return pl.pallas_call(
         functools.partial(pack_kernel, width, first),
         grid=(orbitals // step,),
-        in_specs=[pl.BlockSpec((step, domain, part), lambda i: (i, 0, 0))],
+        in_specs=[pl.BlockSpec((step, domain, lanes), lambda i: (i, 0, 0))],
         out_specs=[pl.BlockSpec(packed, lambda i: (i, 0, 0))] * count,
         out_shape=[jax.ShapeDtypeStruct((orbitals,) + packed[1:], factors.dtype)] * count,
         cost_estimate=SMALL,
-        compiler_params=pltpu.CompilerParams(vmem_limit_bytes=VMEM_WHOLE),
+        compiler_params=pltpu.CompilerParams(vmem_limit_bytes=VMEM_PART if begin else VMEM_WHOLE),
         name="pack_chunks",
     )(factors)
 

time: 170 us -> 170 us (level)
  waiting for transfers between devices: 31.6 us -> 34.3 us
  local copies, waits for them, and re-layouts: 18.1 us -> 15.8 us
  Pallas kernels: 78.9 us -> 77.1 us
    all_to_all x4, waiting for transfers between devices: 10.4 us -> 13.4 us  [shards(): lax.all_to_all(made, 'aux', split_axis=0, concat_axis=0, tiled=True)]
    pallas_call x2, Pallas kernels: 8.12 us -> 5.64 us  [pack_chunks(): pl.pallas_call(functools.partial(pack_kernel, width, first), grid=(orbita...]
    unnamed x34 -> x24, local copies, waits for them, and re-layouts: 16.1 us -> 13.9 us
  transfers between devices with their start and end apart: 18 -> 18, of which waited for: 10 -> 11; matrix products, arithmetic and copies ran while one was open for 1% -> 1% of each run, Pallas kernels for 44% -> 43%
where the time goes in v10:
time: 170 us; the launch traced here: 169 us
  Pallas kernels  77.1 us (45%)
  waiting for transfers between devices  34.3 us (20%)
  starting transfers between devices  26.2 us (15%)
  local copies, waits for them, and re-layouts  15.8 us (9%)
  between operations  13.6 us (8%)
    pallas_call x4, Pallas kernels, chunk_products(): pl.pallas_call(functools.partial(product_kernel, pairs, split_rows, strea...  53.6 us
    all_to_all x4, starting transfers between devices, shards(): lax.all_to_all(made, 'aux', split_axis=0, concat_axis=0, tiled=True)  16.8 us
    ppermute x4, waiting for transfers between devices, to_far(): return lax.ppermute(array, 'orb', moves)  13.9 us
    unnamed x24, local copies, waits for them, and re-layouts  13.9 us
    all_to_all x4, waiting for transfers between devices, shards(): lax.all_to_all(made, 'aux', split_axis=0, concat_axis=0, tiled=True)  13.4 us
    pallas_call x1, Pallas kernels, first_shares(): pl.pallas_call(functools.partial(first_kernel, len(chunks), len(sources),...  12.7 us
    ppermute x4, starting transfers between devices, to_far(): return lax.ppermute(array, 'orb', moves)  7.72 us
    ppermute x9, waiting for transfers between devices, to_mate(): return lax.ppermute(array, 'orb', [(g, g ^ 1) for g in range(orb_count)])  6.99 us
  transfers between devices with their start and end apart: 18, of which 11 were waited for; matrix products, arithmetic and copies ran while one was open for 1% of the time, Pallas kernels for 43%

profile of v10, /device:TPU:0, one launch (start us, length us, event | category | flops | bytes accessed | tf_op | source)
XLA Modules:
  0.0 168.6 jit_solution(6884932842947372217)
XLA Ops:
  8.4 3.6 %pack_chunks.3.refs_4_ = bf16[48,64,128]{2,1,0:T(8,128)(2,1)} custom-call(bf16[48,128,256]{2,1,0:T(8,128)(2,1)} %source.3), custom_call_target="tpu_custom_call" | custom-call | bytes 4096 | tf_op jit(solution)/shard_map/pack_chunks/pallas_call | solution.py:34
  12.0 3.0 %collective-permute-start.2 = (bf16[48,64,128]{2,1,0:T(8,128)(2,1)}, bf16[48,64,128]{2,1,0:T(8,128)(2,1)}, u32[]{:S(2)}, u32[]{:S(2)}) collective-permute-start(bf16[48,64,128]{2,1,0:T(8,128)(2,1)} %pack_chunks.3.refs_4_), channel_id=1, source_target_pairs={{0,16},{8,24},{16,0},{24,8},{1,17},{9,25},{17,1},{25,9},{2,18},{10... | collective-permute-start | bytes 2359304 | tf_op jit(solution)/shard_map/ppermute | solution.py:263
  15.0 1.9 %copy-done.1 = bf16[48,128,256]{2,1,0:T(8,128)(2,1)S(1)} copy-done((bf16[48,128,256]{2,1,0:T(8,128)(2,1)S(1)}, bf16[48,128,256]{2,1,0:T(8,128)(2,1)}, u32[]{:S(2)}) %copy-start.1) | copy-done | bytes 3145752
  16.9 2.0 %pack_chunks.2 = (bf16[48,64,128]{2,1,0:T(8,128)(2,1)S(1)}, bf16[48,64,128]{2,1,0:T(8,128)(2,1)S(1)}, bf16[48,64,128]{2,1,0:T(8,128)(2,1)}) custom-call(bf16[48,128,256]{2,1,0:T(8,128)(2,1)S(1)} %copy-done.1), custom_call_target="tpu_custom_call" | custom-call | bytes 4096 | tf_op jit(solution)/shard_map/pack_chunks/pallas_call | solution.py:34
  18.9 13.9 %collective-permute-done.2.refs_6_ = bf16[48,64,128]{2,1,0:T(8,128)(2,1)} collective-permute-done((bf16[48,64,128]{2,1,0:T(8,128)(2,1)}, bf16[48,64,128]{2,1,0:T(8,128)(2,1)}, u32[]{:S(2)}, u32[]{:S(2)}) %collective-permute-start.2) | collective-permute-done | bytes 786464 | tf_op jit(solution)/shard_map/ppermute | solution.py:263
  32.8 1.7 %collective-permute-start.3 = (bf16[48,64,128]{2,1,0:T(8,128)(2,1)S(1)}, bf16[48,64,128]{2,1,0:T(8,128)(2,1)}, u32[]{:S(2)}, u32[]{:S(2)}) collective-permute-start(bf16[48,64,128]{2,1,0:T(8,128)(2,1)S(1)} %get-tuple-element.26.refs_4_), channel_id=1, source_target_pairs={{0,16},{8,24},{16,0},{24,8},{1,17},{9,25},{17,1},{25,9},{2,18},{10... | collective-permute-start | bytes 2359304 | tf_op jit(solution)/shard_map/ppermute | solution.py:263
  35.5 13.7 %chunk_products.4 = bf16[8,384,128]{2,1,0:T(8,128)(2,1)} custom-call(s32[576]{0:T(1024)S(1)} %reshape.24.slots, bf16[2,24,12,128,128]{4,3,2,1,0:T(8,128)(2,1)} %bitcast.15, bf16[2,24,12,128,128]{4,3,2,1,0:T(8,128)(2,1)} %bitcast.16, bf16[2,24,12,128,128]{4,3,2,1,0:T(8,128)(2,1)} %bitcast.17, bf16[2,24,12,128,128]{4,3,2,1,0:T(8,128)(2,1)} %bitcast.18, ...), custom_call_target="tpu_custom_call" | custom-call | bytes 4096 | tf_op jit(solution)/shard_map/chunk_products/pallas_call | solution.py:110
  49.2 6.1 %all-to-all-start.1 = ((bf16[8,384,128]{2,1,0:T(8,128)(2,1)}), bf16[8,384,128]{2,1,0:T(8,128)(2,1)S(1)}, u32[]{:S(2)}, u32[]{:S(2)}) async-start(bf16[8,384,128]{2,1,0:T(8,128)(2,1)} %chunk_products.4), calls=%async_computation.1 | async-start | bytes 1572864 | tf_op jit(solution)/shard_map/all_to_all | solution.py:301
  58.9 13.1 %chunk_products.5 = bf16[8,384,128]{2,1,0:T(8,128)(2,1)} custom-call(s32[576]{0:T(1024)S(1)} %reshape.24.slots, bf16[2,24,12,128,128]{4,3,2,1,0:T(8,128)(2,1)} %bitcast.19, bf16[2,24,12,128,128]{4,3,2,1,0:T(8,128)(2,1)} %bitcast.20, bf16[2,24,12,128,128]{4,3,2,1,0:T(8,128)(2,1)} %bitcast.21, bf16[2,24,12,128,128]{4,3,2,1,0:T(8,128)(2,1)} %bitcast.22, ...), custom_call_target="tpu_custom_call" | custom-call | bytes 4096 | tf_op jit(solution)/shard_map/chunk_products/pallas_call | solution.py:110
  72.0 6.7 %all-to-all-done.1.refs_0_ = bf16[8,384,128]{2,1,0:T(8,128)(2,1)S(1)} async-done(((bf16[8,384,128]{2,1,0:T(8,128)(2,1)}), bf16[8,384,128]{2,1,0:T(8,128)(2,1)S(1)}, u32[]{:S(2)}, u32[]{:S(2)}) %all-to-all-start.1) | async-done | bytes 786464 | tf_op jit(solution)/shard_map/all_to_all | solution.py:301
  78.8 3.5 %all-to-all-start.2 = ((bf16[8,384,128]{2,1,0:T(8,128)(2,1)}), bf16[8,384,128]{2,1,0:T(8,128)(2,1)S(1)}, u32[]{:S(2)}, u32[]{:S(2)}) async-start(bf16[8,384,128]{2,1,0:T(8,128)(2,1)} %chunk_products.5), calls=%async_computation.2 | async-start | bytes 1572864 | tf_op jit(solution)/shard_map/all_to_all | solution.py:301
  86.1 13.5 %chunk_products.6 = bf16[8,384,128]{2,1,0:T(8,128)(2,1)} custom-call(s32[576]{0:T(1024)S(1)} %reshape.24.slots, bf16[2,24,12,128,128]{4,3,2,1,0:T(8,128)(2,1)} %bitcast.23, bf16[2,24,12,128,128]{4,3,2,1,0:T(8,128)(2,1)} %bitcast.24, bf16[2,24,12,128,128]{4,3,2,1,0:T(8,128)(2,1)} %bitcast.25, bf16[2,24,12,128,128]{4,3,2,1,0:T(8,128)(2,1)} %bitcast.26, ...), custom_call_target="tpu_custom_call" | custom-call | bytes 4096 | tf_op jit(solution)/shard_map/chunk_products/pallas_call | solution.py:110
  99.6 3.1 %all-to-all-done.2.refs_1_ = bf16[8,384,128]{2,1,0:T(8,128)(2,1)S(1)} async-done(((bf16[8,384,128]{2,1,0:T(8,128)(2,1)}), bf16[8,384,128]{2,1,0:T(8,128)(2,1)S(1)}, u32[]{:S(2)}, u32[]{:S(2)}) %all-to-all-start.2) | async-done | bytes 786464 | tf_op jit(solution)/shard_map/all_to_all | solution.py:301
  102.8 3.6 %all-to-all-start.3 = ((bf16[8,384,128]{2,1,0:T(8,128)(2,1)}), bf16[8,384,128]{2,1,0:T(8,128)(2,1)S(1)}, u32[]{:S(2)}, u32[]{:S(2)}) async-start(bf16[8,384,128]{2,1,0:T(8,128)(2,1)} %chunk_products.6), calls=%async_computation.3 | async-start | bytes 1572864 | tf_op jit(solution)/shard_map/all_to_all | solution.py:301
  106.9 2.0 %collective-permute-done.1.refs_5_ = bf16[48,64,128]{2,1,0:T(8,128)(2,1)S(1)} collective-permute-done((bf16[48,64,128]{2,1,0:T(8,128)(2,1)}, bf16[48,64,128]{2,1,0:T(8,128)(2,1)S(1)}, u32[]{:S(2)}, u32[]{:S(2)}) %collective-permute-start.1) | collective-permute-done | bytes 786464 | tf_op jit(solution)/shard_map/ppermute | solution.py:266
  110.0 13.2 %chunk_products.7 = bf16[8,384,128]{2,1,0:T(8,128)(2,1)} custom-call(s32[576]{0:T(1024)S(1)} %reshape.24.slots, bf16[2,24,12,128,128]{4,3,2,1,0:T(8,128)(2,1)} %bitcast.27, bf16[2,24,12,128,128]{4,3,2,1,0:T(8,128)(2,1)} %bitcast.28, bf16[2,24,12,128,128]{4,3,2,1,0:T(8,128)(2,1)} %bitcast.29, bf16[2,24,12,128,128]{4,3,2,1,0:T(8,128)(2,1)} %bitcast.30, ...), custom_call_target="tpu_custom_call" | custom-call | bytes 4096 | tf_op jit(solution)/shard_map/chunk_products/pallas_call | solution.py:110
  123.3 3.5 %all-to-all-done.3.refs_2_ = bf16[8,384,128]{2,1,0:T(8,128)(2,1)S(1)} async-done(((bf16[8,384,128]{2,1,0:T(8,128)(2,1)}), bf16[8,384,128]{2,1,0:T(8,128)(2,1)S(1)}, u32[]{:S(2)}, u32[]{:S(2)}) %all-to-all-start.3) | async-done | bytes 786464 | tf_op jit(solution)/shard_map/all_to_all | solution.py:301
  127.6 3.5 %all-to-all-start = ((bf16[8,384,128]{2,1,0:T(8,128)(2,1)}), bf16[8,384,128]{2,1,0:T(8,128)(2,1)S(1)}, u32[]{:S(2)}, u32[]{:S(2)}) async-start(bf16[8,384,128]{2,1,0:T(8,128)(2,1)} %chunk_products.7), calls=%async_computation | async-start | bytes 1572864 | tf_op jit(solution)/shard_map/all_to_all | solution.py:301
  133.9 1.6 copy-done.7
  135.5 12.7 %first_shares.1 = (f32[768,2048]{1,0:T(8,128)S(1)}, bf16[512,2048]{1,0:T(8,128)(2,1)S(1)}) custom-call(s32[256]{0:T(256)S(1)} %reshape.29.positions, bf16[8,384,128]{2,1,0:T(8,128)(2,1)S(1)} %all-to-all-done.1.refs_0_, bf16[8,384,128]{2,1,0:T(8,128)(2,1)S(1)} %all-to-all-done.2.refs_1_, bf16[8,384,128]{2,1,0:T(8,128)(2,1)S(1)} %copy-done.6, ...), custom_call_target="tpu_custom_call" | custom-call | bytes 4096 | tf_op jit(solution)/shard_map/first_shares/pallas_call | solution.py:195
  148.2 2.6 %copy-done.2 = f32[768,2048]{1,0:T(8,128)} copy-done((f32[768,2048]{1,0:T(8,128)}, f32[768,2048]{1,0:T(8,128)S(1)}, u32[]{:S(2)}) %copy-start.2) | copy-done | bytes 6291480
  152.2 2.8 %copy-done.3 = f32[768,2048]{1,0:T(8,128)S(1)} copy-done((f32[768,2048]{1,0:T(8,128)S(1)}, f32[768,2048]{1,0:T(8,128)}, u32[]{:S(2)}) %copy-start.3) | copy-done | bytes 6291480
  155.0 1.6 copy-done.9
  156.6 5.2 %last_share.1 = bf16[2,384,2048]{2,1,0:T(8,128)(2,1)} custom-call(bf16[8,384,128]{2,1,0:T(8,128)(2,1)S(1)} %all-to-all-done.chunk, bf16[512,2048]{1,0:T(8,128)(2,1)S(1)} %copy-done.9, f32[768,2048]{1,0:T(8,128)S(1)} %copy-done.3), custom_call_target="tpu_custom_call" | custom-call | bytes 4096 | tf_op jit(solution)/shard_map/last_share/pallas_call | solution.py:232
  (58 shorter events, 16.7 us)
Async XLA Ops:
  6.5 76.4 %all-gather.3.cloned.1.call-start = ((), (), s32[]{:S(2)}) async-start(), calls=%async_computation.4 | async-start | bytes 2396160 | tf_op jit(solution)/shard_map/all_gather | solution.py:279
  8.4 26.2 %copy-start.10 = (s32[48,12]{0,1:T(8,128)S(1)}, s32[48,12]{0,1:T(8,128)}, u32[]{:S(2)}) copy-start(s32[48,12]{0,1:T(8,128)} %param.7) | copy-start | bytes 6916
  12.0 20.8 %collective-permute-start.2 = (bf16[48,64,128]{2,1,0:T(8,128)(2,1)}, bf16[48,64,128]{2,1,0:T(8,128)(2,1)}, u32[]{:S(2)}, u32[]{:S(2)}) collective-permute-start(bf16[48,64,128]{2,1,0:T(8,128)(2,1)} %pack_chunks.3.refs_4_), channel_id=1, source_target_pairs={{0,16},{8,24},{16,0},{24,8},{1,17},{9,25},{17,1},{25,9},{2,18},{10... | collective-permute-start | bytes 2359304 | tf_op jit(solution)/shard_map/ppermute | solution.py:263
  15.0 19.8 %collective-permute-start.4 = (bf16[48,64,128]{2,1,0:T(8,128)(2,1)}, bf16[48,64,128]{2,1,0:T(8,128)(2,1)}, u32[]{:S(2)}, u32[]{:S(2)}) collective-permute-start(bf16[48,64,128]{2,1,0:T(8,128)(2,1)} %pack_chunks.3.refs_4_), channel_id=1, source_target_pairs={{0,8},{8,0},{16,24},{24,16},{1,9},{9,1},{17,25},{25,17},{2,10},{10... | collective-permute-start | bytes 2359304 | tf_op jit(solution)/shard_map/ppermute | solution.py:266
  15.0 1.9 %copy-start.1 = (bf16[48,128,256]{2,1,0:T(8,128)(2,1)S(1)}, bf16[48,128,256]{2,1,0:T(8,128)(2,1)}, u32[]{:S(2)}) copy-start(bf16[48,128,256]{2,1,0:T(8,128)(2,1)} %source.3) | copy-start | bytes 9437188
  16.9 18.6 %copy-start.4 = (bf16[48,64,128]{2,1,0:T(8,128)(2,1)S(1)}, bf16[48,64,128]{2,1,0:T(8,128)(2,1)}, u32[]{:S(2)}) copy-start(bf16[48,64,128]{2,1,0:T(8,128)(2,1)} %pack_chunks.3.refs_4_) | copy-start | bytes 2359300
  32.8 2.6 %collective-permute-start.5 = (bf16[48,64,128]{2,1,0:T(8,128)(2,1)}, bf16[48,64,128]{2,1,0:T(8,128)(2,1)}, u32[]{:S(2)}, u32[]{:S(2)}) collective-permute-start(bf16[48,64,128]{2,1,0:T(8,128)(2,1)} %collective-permute-done.2.refs_6_), channel_id=1, source_target_pairs={{0,8},{8,0},{16,24},{24,16},{1,9},{9,1},{17,25},{25,17},{2,10},{10... | collective-permute-start | bytes 2359304 | tf_op jit(solution)/shard_map/ppermute | solution.py:266
  32.8 22.5 %collective-permute-start.3 = (bf16[48,64,128]{2,1,0:T(8,128)(2,1)S(1)}, bf16[48,64,128]{2,1,0:T(8,128)(2,1)}, u32[]{:S(2)}, u32[]{:S(2)}) collective-permute-start(bf16[48,64,128]{2,1,0:T(8,128)(2,1)S(1)} %get-tuple-element.26.refs_4_), channel_id=1, source_target_pairs={{0,16},{8,24},{16,0},{24,8},{1,17},{9,25},{17,1},{25,9},{2,18},{10... | collective-permute-start | bytes 2359304 | tf_op jit(solution)/shard_map/ppermute | solution.py:263
  49.2 29.5 %all-to-all-start.1 = ((bf16[8,384,128]{2,1,0:T(8,128)(2,1)}), bf16[8,384,128]{2,1,0:T(8,128)(2,1)S(1)}, u32[]{:S(2)}, u32[]{:S(2)}) async-start(bf16[8,384,128]{2,1,0:T(8,128)(2,1)} %chunk_products.4), calls=%async_computation.1 | async-start | bytes 1572864 | tf_op jit(solution)/shard_map/all_to_all | solution.py:301
  55.3 2.6 %collective-permute-start.7 = (bf16[48,64,128]{2,1,0:T(8,128)(2,1)S(1)}, bf16[48,64,128]{2,1,0:T(8,128)(2,1)S(1)}, u32[]{:S(2)}, u32[]{:S(2)}) collective-permute-start(bf16[48,64,128]{2,1,0:T(8,128)(2,1)S(1)} %get-tuple-element.26.refs_4_), channel_id=1, source_target_pairs={{0,8},{8,0},{16,24},{24,16},{1,9},{9,1},{17,25},{25,17},{2,10},{10... | collective-permute-start | bytes 2359304 | tf_op jit(solution)/shard_map/ppermute | solution.py:266
  55.3 3.6 %collective-permute-start.8 = (bf16[48,64,128]{2,1,0:T(8,128)(2,1)}, bf16[48,64,128]{2,1,0:T(8,128)(2,1)S(1)}, u32[]{:S(2)}, u32[]{:S(2)}) collective-permute-start(bf16[48,64,128]{2,1,0:T(8,128)(2,1)} %collective-permute-done.3.refs_6_), channel_id=1, source_target_pairs={{0,8},{8,0},{16,24},{24,16},{1,9},{9,1},{17,25},{25,17},{2,10},{10... | collective-permute-start | bytes 2359304 | tf_op jit(solution)/shard_map/ppermute | solution.py:266
  55.8 26.6 %collective-permute-start.6 = (bf16[48,64,128]{2,1,0:T(8,128)(2,1)S(1)}, bf16[48,64,128]{2,1,0:T(8,128)(2,1)}, u32[]{:S(2)}, u32[]{:S(2)}) collective-permute-start(bf16[48,64,128]{2,1,0:T(8,128)(2,1)S(1)} %get-tuple-element.28.refs_4_), channel_id=1, source_target_pairs={{0,16},{8,24},{16,0},{24,8},{1,17},{9,25},{17,1},{25,9},{2,18},{10... | collective-permute-start | bytes 2359304 | tf_op jit(solution)/shard_map/ppermute | solution.py:263
  78.8 24.0 %all-to-all-start.2 = ((bf16[8,384,128]{2,1,0:T(8,128)(2,1)}), bf16[8,384,128]{2,1,0:T(8,128)(2,1)S(1)}, u32[]{:S(2)}, u32[]{:S(2)}) async-start(bf16[8,384,128]{2,1,0:T(8,128)(2,1)} %chunk_products.5), calls=%async_computation.2 | async-start | bytes 1572864 | tf_op jit(solution)/shard_map/all_to_all | solution.py:301
  82.3 2.7 %collective-permute-start.10 = (bf16[48,64,128]{2,1,0:T(8,128)(2,1)S(1)}, bf16[48,64,128]{2,1,0:T(8,128)(2,1)}, u32[]{:S(2)}, u32[]{:S(2)}) collective-permute-start(bf16[48,64,128]{2,1,0:T(8,128)(2,1)S(1)} %get-tuple-element.28.refs_4_), channel_id=1, source_target_pairs={{0,8},{8,0},{16,24},{24,16},{1,9},{9,1},{17,25},{25,17},{2,10},{10... | collective-permute-start | bytes 2359304 | tf_op jit(solution)/shard_map/ppermute | solution.py:266
  82.4 3.7 %collective-permute-start.11 = (bf16[48,64,128]{2,1,0:T(8,128)(2,1)}, bf16[48,64,128]{2,1,0:T(8,128)(2,1)}, u32[]{:S(2)}, u32[]{:S(2)}) collective-permute-start(bf16[48,64,128]{2,1,0:T(8,128)(2,1)} %collective-permute-done.6.refs_6_), channel_id=1, source_target_pairs={{0,8},{8,0},{16,24},{24,16},{1,9},{9,1},{17,25},{25,17},{2,10},{10... | collective-permute-start | bytes 2359304 | tf_op jit(solution)/shard_map/ppermute | solution.py:266
  82.9 24.0 %collective-permute-start = (bf16[8,1040,128]{2,1,0:T(8,128)(2,1)}, bf16[8,1040,128]{2,1,0:T(8,128)(2,1)}, u32[]{:S(2)}, u32[]{:S(2)}) collective-permute-start(bf16[8,1040,128]{2,1,0:T(8,128)(2,1)} %bitcast.12), channel_id=1, source_target_pairs={{0,8},{8,0},{16,24},{24,16},{1,9},{9,1},{17,25},{25,17},{2,10},{10... | collective-permute-start | bytes 6389768 | tf_op jit(solution)/shard_map/ppermute | solution.py:266
  83.0 23.5 %collective-permute-start.9 = (bf16[48,64,128]{2,1,0:T(8,128)(2,1)}, bf16[48,64,128]{2,1,0:T(8,128)(2,1)}, u32[]{:S(2)}, u32[]{:S(2)}) collective-permute-start(bf16[48,64,128]{2,1,0:T(8,128)(2,1)} %get-tuple-element.30.refs_4_), channel_id=1, source_target_pairs={{0,16},{8,24},{16,0},{24,8},{1,17},{9,25},{17,1},{25,9},{2,18},{10... | collective-permute-start | bytes 2359304 | tf_op jit(solution)/shard_map/ppermute | solution.py:263
  102.8 24.0 %all-to-all-start.3 = ((bf16[8,384,128]{2,1,0:T(8,128)(2,1)}), bf16[8,384,128]{2,1,0:T(8,128)(2,1)S(1)}, u32[]{:S(2)}, u32[]{:S(2)}) async-start(bf16[8,384,128]{2,1,0:T(8,128)(2,1)} %chunk_products.6), calls=%async_computation.3 | async-start | bytes 1572864 | tf_op jit(solution)/shard_map/all_to_all | solution.py:301
  106.4 2.5 %collective-permute-start.1 = (bf16[48,64,128]{2,1,0:T(8,128)(2,1)}, bf16[48,64,128]{2,1,0:T(8,128)(2,1)S(1)}, u32[]{:S(2)}, u32[]{:S(2)}) collective-permute-start(bf16[48,64,128]{2,1,0:T(8,128)(2,1)} %get-tuple-element.30.refs_4_), channel_id=1, source_target_pairs={{0,8},{8,0},{16,24},{24,16},{1,9},{9,1},{17,25},{25,17},{2,10},{10... | collective-permute-start | bytes 2359304 | tf_op jit(solution)/shard_map/ppermute | solution.py:266
  106.4 3.6 %collective-permute-start.12 = (bf16[48,64,128]{2,1,0:T(8,128)(2,1)}, bf16[48,64,128]{2,1,0:T(8,128)(2,1)S(1)}, u32[]{:S(2)}, u32[]{:S(2)}) collective-permute-start(bf16[48,64,128]{2,1,0:T(8,128)(2,1)} %collective-permute-done.9.refs_6_), channel_id=1, source_target_pairs={{0,8},{8,0},{16,24},{24,16},{1,9},{9,1},{17,25},{25,17},{2,10},{10... | collective-permute-start | bytes 2359304 | tf_op jit(solution)/shard_map/ppermute | solution.py:266
  127.6 24.6 %all-to-all-start = ((bf16[8,384,128]{2,1,0:T(8,128)(2,1)}), bf16[8,384,128]{2,1,0:T(8,128)(2,1)S(1)}, u32[]{:S(2)}, u32[]{:S(2)}) async-start(bf16[8,384,128]{2,1,0:T(8,128)(2,1)} %chunk_products.7), calls=%async_computation | async-start | bytes 1572864 | tf_op jit(solution)/shard_map/all_to_all | solution.py:301
  133.9 1.6 copy-start.7
  148.2 2.6 %copy-start.2 = (f32[768,2048]{1,0:T(8,128)}, f32[768,2048]{1,0:T(8,128)S(1)}, u32[]{:S(2)}) copy-start(f32[768,2048]{1,0:T(8,128)S(1)} %get-tuple-element.36.before) | copy-start | bytes 18874372
  152.2 2.8 %copy-start.3 = (f32[768,2048]{1,0:T(8,128)S(1)}, f32[768,2048]{1,0:T(8,128)}, u32[]{:S(2)}) copy-start(f32[768,2048]{1,0:T(8,128)} %copy-done.2) | copy-start | bytes 18874372
  (5 other events, 6.0 us)
Sparse Core Ops, SparseCore 0:
  9.5 54.2 all-gather.2

commit v11 on v10

--- a/solution.py
+++ b/solution.py
@@ -9,7 +9,6 @@
 
 VMEM_WHOLE = 58 * 1024 * 1024
 VMEM_MOST = 30 * 1024 * 1024
-VMEM_LAST = 16 * 1024 * 1024
 VMEM_PART = 44 * 1024 * 1024
 SMALL = pl.CostEstimate(flops=0, bytes_accessed=4096, transcendentals=0)
 
@@ -180,9 +179,9 @@
     step = dense.shape[1] // pl.num_programs(0)
     columns = pl.ds(pl.multiple_of(pl.program_id(0) * step, step), step)
     if len(outs) > 1:
-        outs[1][:, columns] = dense[depth:, columns]
+        outs[1][...] = dense[depth:, columns]
     sums = jnp.dot(rows[...], dense[:depth, columns], preferred_element_type=jnp.float32)
-    outs[0][:, columns] = sums.astype(outs[0].dtype)
+    outs[0][...] = sums.astype(outs[0].dtype)
 
 
 def first_shares(chunks, positions, sources, tiles_each, size, dtype):
@@ -198,13 +197,13 @@
             num_scalar_prefetch=1,
             grid=(size // step,),
             in_specs=[pl.BlockSpec(array.shape, whole) for array in [*chunks, *sources]],
-            out_specs=[pl.BlockSpec(memory_space=pltpu.VMEM)] * len(heights),
+            out_specs=[pl.BlockSpec((tall, step), lambda j, s: (0, j)) for tall in heights],
             scratch_shapes=[
                 pltpu.VMEM((size, size), sources[0].dtype),
                 pltpu.VMEM((2 * height, depth), jnp.bfloat16),
             ],
         ),
-        out_shape=[pltpu.VMEM((tall, size), kind) for tall, kind in zip(heights, kinds)],
+        out_shape=[jax.ShapeDtypeStruct((tall, size), kind) for tall, kind in zip(heights, kinds)],
         cost_estimate=SMALL,
         compiler_params=pltpu.CompilerParams(vmem_limit_bytes=VMEM_MOST),
         name="first_shares",
@@ -212,36 +211,34 @@
 
 
 def last_kernel(chunk, metric, before, out, rows):
-    height = chunk.shape[1]
-
     @pl.when(pl.program_id(0) == 0)
     def _():
         unpack_rows([chunk], rows)
 
-    step = out.shape[-1]
-    columns = pl.ds(pl.multiple_of(pl.program_id(0) * step, step), step)
-    sums = jnp.dot(rows[...], metric[:, columns], preferred_element_type=jnp.float32) + before[:, columns]
-    out[0] = sums[:height].astype(out.dtype)
-    out[1] = sums[height:].astype(out.dtype)
+    step = out.shape[0]
+    part = rows[pl.ds(pl.multiple_of(pl.program_id(0) * step, step), step), :]
+    sums = jnp.dot(part, metric[...], preferred_element_type=jnp.float32) + before[...]
+    out[...] = sums.astype(out.dtype)
 
 
 def last_share(chunk, metric, before):
-    owners, height, lanes = chunk.shape
-    depth, size = metric.shape
-    step = largest_divisor(size, 256)
+    height, size = before.shape
+    depth = metric.shape[0]
+    step = largest_divisor(height // 16, 12) * 16
+    rows = pl.BlockSpec((step, size), lambda j: (j, 0))
     return pl.pallas_call(
         last_kernel,
-        grid=(size // step,),
+        grid=(height // step,),
         in_specs=[
             pl.BlockSpec(chunk.shape, lambda j: (0, 0, 0)),
-            pl.BlockSpec(memory_space=pltpu.VMEM),
-            pl.BlockSpec(memory_space=pltpu.VMEM),
+            pl.BlockSpec((depth, size), lambda j: (0, 0)),
+            rows,
         ],
-        out_specs=pl.BlockSpec((2, height, step), lambda j: (0, 0, j)),
-        out_shape=jax.ShapeDtypeStruct((2, height, size), jnp.bfloat16),
-        scratch_shapes=[pltpu.VMEM((2 * height, depth), jnp.bfloat16)],
+        out_specs=rows,
+        out_shape=jax.ShapeDtypeStruct((height, size), jnp.bfloat16),
+        scratch_shapes=[pltpu.VMEM((height, depth), jnp.bfloat16)],
         cost_estimate=SMALL,
-        compiler_params=pltpu.CompilerParams(vmem_limit_bytes=VMEM_LAST),
+        compiler_params=pltpu.CompilerParams(vmem_limit_bytes=VMEM_WHOLE),
         name="last_share",
     )(chunk, metric, before)
 
@@ -309,7 +306,6 @@
         result = last_share(products[-1], metric, before)
     else:
         result = first_shares(products, positions, sources, half_tiles, size, jnp.bfloat16)[0]
-        result = result.reshape(2, group // 2, domain // aux_count, size)
     return result.reshape(group, domain // aux_count, size)
 
 

time: 170 us -> 166 us (0.976)
  local copies, waits for them, and re-layouts: 15.8 us -> 9.49 us
  Pallas kernels: 77.1 us -> 79.7 us
    unnamed x24 -> x16, local copies, waits for them, and re-layouts: 13.9 us -> 7.57 us
    pallas_call x1, Pallas kernels: 5.17 us -> 7.25 us  [last_share(): pl.pallas_call(last_kernel, grid=(height // step,), in_specs=[pl.BlockSpe...]
  transfers between devices with their start and end apart: 18 -> 18, of which waited for: 11 -> 11; matrix products, arithmetic and copies ran while one was open for 1% -> 1% of each run, Pallas kernels for 43% -> 44%
where the time goes in v11:
time: 166 us
  Pallas kernels  79.7 us (48%)
  waiting for transfers between devices  34.3 us (21%)
  starting transfers between devices  26.9 us (16%)
  between operations  13.6 us (8%)
  local copies, waits for them, and re-layouts  9.49 us (6%)
    pallas_call x4, Pallas kernels, chunk_products(): pl.pallas_call(functools.partial(product_kernel, pairs, split_rows, strea...  53.6 us
    all_to_all x4, starting transfers between devices, shards(): lax.all_to_all(made, 'aux', split_axis=0, concat_axis=0, tiled=True)  17.5 us
    ppermute x4, waiting for transfers between devices, to_far(): return lax.ppermute(array, 'orb', moves)  13.9 us
    all_to_all x4, waiting for transfers between devices, shards(): lax.all_to_all(made, 'aux', split_axis=0, concat_axis=0, tiled=True)  13.4 us
    pallas_call x1, Pallas kernels, first_shares(): pl.pallas_call(functools.partial(first_kernel, len(chunks), len(sources),...  13.2 us
    ppermute x4, starting transfers between devices, to_far(): return lax.ppermute(array, 'orb', moves)  7.72 us
    unnamed x16, local copies, waits for them, and re-layouts  7.57 us
    pallas_call x1, Pallas kernels, last_share(): pl.pallas_call(last_kernel, grid=(height // step,), in_specs=[pl.BlockSpe...  7.25 us
  transfers between devices with their start and end apart: 18, of which 11 were waited for; matrix products, arithmetic and copies ran while one was open for 1% of the time, Pallas kernels for 44%

profile of v11, /device:TPU:0, one launch (start us, length us, event | category | flops | bytes accessed | tf_op | source)
XLA Modules:
  0.0 165.5 jit_solution(9510695907404956139)
XLA Ops:
  8.4 3.6 %pack_chunks.3.refs_4_ = bf16[48,64,128]{2,1,0:T(8,128)(2,1)} custom-call(bf16[48,128,256]{2,1,0:T(8,128)(2,1)} %source.3), custom_call_target="tpu_custom_call" | custom-call | bytes 4096 | tf_op jit(solution)/shard_map/pack_chunks/pallas_call | solution.py:33
  12.0 3.0 %collective-permute-start.2 = (bf16[48,64,128]{2,1,0:T(8,128)(2,1)}, bf16[48,64,128]{2,1,0:T(8,128)(2,1)}, u32[]{:S(2)}, u32[]{:S(2)}) collective-permute-start(bf16[48,64,128]{2,1,0:T(8,128)(2,1)} %pack_chunks.3.refs_4_), channel_id=1, source_target_pairs={{0,16},{8,24},{16,0},{24,8},{1,17},{9,25},{17,1},{25,9},{2,18},{10... | collective-permute-start | bytes 2359304 | tf_op jit(solution)/shard_map/ppermute | solution.py:260
  15.0 1.9 %copy-done.1 = bf16[48,128,256]{2,1,0:T(8,128)(2,1)S(1)} copy-done((bf16[48,128,256]{2,1,0:T(8,128)(2,1)S(1)}, bf16[48,128,256]{2,1,0:T(8,128)(2,1)}, u32[]{:S(2)}) %copy-start.1) | copy-done | bytes 3145752
  16.9 2.0 %pack_chunks.2 = (bf16[48,64,128]{2,1,0:T(8,128)(2,1)S(1)}, bf16[48,64,128]{2,1,0:T(8,128)(2,1)S(1)}, bf16[48,64,128]{2,1,0:T(8,128)(2,1)}) custom-call(bf16[48,128,256]{2,1,0:T(8,128)(2,1)S(1)} %copy-done.1), custom_call_target="tpu_custom_call" | custom-call | bytes 4096 | tf_op jit(solution)/shard_map/pack_chunks/pallas_call | solution.py:33
  18.9 13.9 %collective-permute-done.2.refs_6_ = bf16[48,64,128]{2,1,0:T(8,128)(2,1)} collective-permute-done((bf16[48,64,128]{2,1,0:T(8,128)(2,1)}, bf16[48,64,128]{2,1,0:T(8,128)(2,1)}, u32[]{:S(2)}, u32[]{:S(2)}) %collective-permute-start.2) | collective-permute-done | bytes 786464 | tf_op jit(solution)/shard_map/ppermute | solution.py:260
  32.8 1.7 %collective-permute-start.3 = (bf16[48,64,128]{2,1,0:T(8,128)(2,1)S(1)}, bf16[48,64,128]{2,1,0:T(8,128)(2,1)}, u32[]{:S(2)}, u32[]{:S(2)}) collective-permute-start(bf16[48,64,128]{2,1,0:T(8,128)(2,1)S(1)} %get-tuple-element.26.refs_4_), channel_id=1, source_target_pairs={{0,16},{8,24},{16,0},{24,8},{1,17},{9,25},{17,1},{25,9},{2,18},{10... | collective-permute-start | bytes 2359304 | tf_op jit(solution)/shard_map/ppermute | solution.py:260
  35.5 13.7 %chunk_products.4 = bf16[8,384,128]{2,1,0:T(8,128)(2,1)} custom-call(s32[576]{0:T(1024)S(1)} %reshape.24.slots, bf16[2,24,12,128,128]{4,3,2,1,0:T(8,128)(2,1)} %bitcast.15, bf16[2,24,12,128,128]{4,3,2,1,0:T(8,128)(2,1)} %bitcast.16, bf16[2,24,12,128,128]{4,3,2,1,0:T(8,128)(2,1)} %bitcast.17, bf16[2,24,12,128,128]{4,3,2,1,0:T(8,128)(2,1)} %bitcast.18, ...), custom_call_target="tpu_custom_call" | custom-call | bytes 4096 | tf_op jit(solution)/shard_map/chunk_products/pallas_call | solution.py:109
  49.2 6.1 %all-to-all-start.1 = ((bf16[8,384,128]{2,1,0:T(8,128)(2,1)}), bf16[8,384,128]{2,1,0:T(8,128)(2,1)S(1)}, u32[]{:S(2)}, u32[]{:S(2)}) async-start(bf16[8,384,128]{2,1,0:T(8,128)(2,1)} %chunk_products.4), calls=%async_computation.1 | async-start | bytes 1572864 | tf_op jit(solution)/shard_map/all_to_all | solution.py:298
  55.8 1.5 collective-permute-start.6
  58.9 13.1 %chunk_products.5 = bf16[8,384,128]{2,1,0:T(8,128)(2,1)} custom-call(s32[576]{0:T(1024)S(1)} %reshape.24.slots, bf16[2,24,12,128,128]{4,3,2,1,0:T(8,128)(2,1)} %bitcast.19, bf16[2,24,12,128,128]{4,3,2,1,0:T(8,128)(2,1)} %bitcast.20, bf16[2,24,12,128,128]{4,3,2,1,0:T(8,128)(2,1)} %bitcast.21, bf16[2,24,12,128,128]{4,3,2,1,0:T(8,128)(2,1)} %bitcast.22, ...), custom_call_target="tpu_custom_call" | custom-call | bytes 4096 | tf_op jit(solution)/shard_map/chunk_products/pallas_call | solution.py:109
  72.0 6.8 %all-to-all-done.1.refs_0_ = bf16[8,384,128]{2,1,0:T(8,128)(2,1)S(1)} async-done(((bf16[8,384,128]{2,1,0:T(8,128)(2,1)}), bf16[8,384,128]{2,1,0:T(8,128)(2,1)S(1)}, u32[]{:S(2)}, u32[]{:S(2)}) %all-to-all-start.1) | async-done | bytes 786464 | tf_op jit(solution)/shard_map/all_to_all | solution.py:298
  78.8 3.5 %all-to-all-start.2 = ((bf16[8,384,128]{2,1,0:T(8,128)(2,1)}), bf16[8,384,128]{2,1,0:T(8,128)(2,1)S(1)}, u32[]{:S(2)}, u32[]{:S(2)}) async-start(bf16[8,384,128]{2,1,0:T(8,128)(2,1)} %chunk_products.5), calls=%async_computation.2 | async-start | bytes 1572864 | tf_op jit(solution)/shard_map/all_to_all | solution.py:298
  83.0 1.5 collective-permute-start.9
  86.1 13.5 %chunk_products.6 = bf16[8,384,128]{2,1,0:T(8,128)(2,1)} custom-call(s32[576]{0:T(1024)S(1)} %reshape.24.slots, bf16[2,24,12,128,128]{4,3,2,1,0:T(8,128)(2,1)} %bitcast.23, bf16[2,24,12,128,128]{4,3,2,1,0:T(8,128)(2,1)} %bitcast.24, bf16[2,24,12,128,128]{4,3,2,1,0:T(8,128)(2,1)} %bitcast.25, bf16[2,24,12,128,128]{4,3,2,1,0:T(8,128)(2,1)} %bitcast.26, ...), custom_call_target="tpu_custom_call" | custom-call | bytes 4096 | tf_op jit(solution)/shard_map/chunk_products/pallas_call | solution.py:109
  99.6 3.1 %all-to-all-done.2.refs_1_ = bf16[8,384,128]{2,1,0:T(8,128)(2,1)S(1)} async-done(((bf16[8,384,128]{2,1,0:T(8,128)(2,1)}), bf16[8,384,128]{2,1,0:T(8,128)(2,1)S(1)}, u32[]{:S(2)}, u32[]{:S(2)}) %all-to-all-start.2) | async-done | bytes 786464 | tf_op jit(solution)/shard_map/all_to_all | solution.py:298
  102.8 3.6 %all-to-all-start.3 = ((bf16[8,384,128]{2,1,0:T(8,128)(2,1)}), bf16[8,384,128]{2,1,0:T(8,128)(2,1)S(1)}, u32[]{:S(2)}, u32[]{:S(2)}) async-start(bf16[8,384,128]{2,1,0:T(8,128)(2,1)} %chunk_products.6), calls=%async_computation.3 | async-start | bytes 1572864 | tf_op jit(solution)/shard_map/all_to_all | solution.py:298
  106.9 2.0 %collective-permute-done.1.refs_5_ = bf16[48,64,128]{2,1,0:T(8,128)(2,1)S(1)} collective-permute-done((bf16[48,64,128]{2,1,0:T(8,128)(2,1)}, bf16[48,64,128]{2,1,0:T(8,128)(2,1)S(1)}, u32[]{:S(2)}, u32[]{:S(2)}) %collective-permute-start.1) | collective-permute-done | bytes 786464 | tf_op jit(solution)/shard_map/ppermute | solution.py:263
  110.0 13.2 %chunk_products.7 = bf16[8,384,128]{2,1,0:T(8,128)(2,1)} custom-call(s32[576]{0:T(1024)S(1)} %reshape.24.slots, bf16[2,24,12,128,128]{4,3,2,1,0:T(8,128)(2,1)} %bitcast.27, bf16[2,24,12,128,128]{4,3,2,1,0:T(8,128)(2,1)} %bitcast.28, bf16[2,24,12,128,128]{4,3,2,1,0:T(8,128)(2,1)} %bitcast.29, bf16[2,24,12,128,128]{4,3,2,1,0:T(8,128)(2,1)} %bitcast.30, ...), custom_call_target="tpu_custom_call" | custom-call | bytes 4096 | tf_op jit(solution)/shard_map/chunk_products/pallas_call | solution.py:109
  123.3 3.5 %all-to-all-done.3.refs_2_ = bf16[8,384,128]{2,1,0:T(8,128)(2,1)S(1)} async-done(((bf16[8,384,128]{2,1,0:T(8,128)(2,1)}), bf16[8,384,128]{2,1,0:T(8,128)(2,1)S(1)}, u32[]{:S(2)}, u32[]{:S(2)}) %all-to-all-start.3) | async-done | bytes 786464 | tf_op jit(solution)/shard_map/all_to_all | solution.py:298
  126.8 4.2 %all-to-all-start = ((bf16[8,384,128]{2,1,0:T(8,128)(2,1)}), bf16[8,384,128]{2,1,0:T(8,128)(2,1)}, u32[]{:S(2)}, u32[]{:S(2)}) async-start(bf16[8,384,128]{2,1,0:T(8,128)(2,1)} %chunk_products.7), calls=%async_computation | async-start | bytes 1572864 | tf_op jit(solution)/shard_map/all_to_all | solution.py:298
  132.5 1.6 copy-done.4
  134.1 13.2 %first_shares.1 = (f32[768,2048]{1,0:T(8,128)S(1)}, bf16[512,2048]{1,0:T(8,128)(2,1)S(1)}) custom-call(s32[256]{0:T(256)S(1)} %reshape.29.positions, bf16[8,384,128]{2,1,0:T(8,128)(2,1)S(1)} %all-to-all-done.1.refs_0_, bf16[8,384,128]{2,1,0:T(8,128)(2,1)S(1)} %all-to-all-done.2.refs_1_, bf16[8,384,128]{2,1,0:T(8,128)(2,1)S(1)} %all-to-all-done.3.refs_2_, ...), custom_call_target="tpu_custom_call" | custom-call | bytes 4096 | tf_op jit(solution)/shard_map/first_shares/pallas_call | solution.py:194
  147.4 2.6 %copy-done.2 = f32[768,2048]{1,0:T(8,128)} copy-done((f32[768,2048]{1,0:T(8,128)}, f32[768,2048]{1,0:T(8,128)S(1)}, u32[]{:S(2)}) %copy-start.2) | copy-done | bytes 6291480
  151.4 7.3 %last_share.1 = bf16[768,2048]{1,0:T(8,128)(2,1)} custom-call(bf16[8,384,128]{2,1,0:T(8,128)(2,1)} %all-to-all-done.chunk, bf16[512,2048]{1,0:T(8,128)(2,1)} %copy-done.5, f32[768,2048]{1,0:T(8,128)} %copy-done.2), custom_call_target="tpu_custom_call" | custom-call | bytes 4096 | tf_op jit(solution)/shard_map/last_share/pallas_call | solution.py:229
  (50 shorter events, 11.7 us)
Async XLA Ops:
  6.5 76.4 %all-gather.3.cloned.1.call-start = ((), (), s32[]{:S(2)}) async-start(), calls=%async_computation.4 | async-start | bytes 2396160 | tf_op jit(solution)/shard_map/all_gather | solution.py:276
  8.4 26.2 %copy-start.6 = (s32[48,12]{0,1:T(8,128)S(1)}, s32[48,12]{0,1:T(8,128)}, u32[]{:S(2)}) copy-start(s32[48,12]{0,1:T(8,128)} %param.7) | copy-start | bytes 6916
  12.0 20.8 %collective-permute-start.2 = (bf16[48,64,128]{2,1,0:T(8,128)(2,1)}, bf16[48,64,128]{2,1,0:T(8,128)(2,1)}, u32[]{:S(2)}, u32[]{:S(2)}) collective-permute-start(bf16[48,64,128]{2,1,0:T(8,128)(2,1)} %pack_chunks.3.refs_4_), channel_id=1, source_target_pairs={{0,16},{8,24},{16,0},{24,8},{1,17},{9,25},{17,1},{25,9},{2,18},{10... | collective-permute-start | bytes 2359304 | tf_op jit(solution)/shard_map/ppermute | solution.py:260
  15.0 19.8 %collective-permute-start.4 = (bf16[48,64,128]{2,1,0:T(8,128)(2,1)}, bf16[48,64,128]{2,1,0:T(8,128)(2,1)}, u32[]{:S(2)}, u32[]{:S(2)}) collective-permute-start(bf16[48,64,128]{2,1,0:T(8,128)(2,1)} %pack_chunks.3.refs_4_), channel_id=1, source_target_pairs={{0,8},{8,0},{16,24},{24,16},{1,9},{9,1},{17,25},{25,17},{2,10},{10... | collective-permute-start | bytes 2359304 | tf_op jit(solution)/shard_map/ppermute | solution.py:263
  15.0 1.9 %copy-start.1 = (bf16[48,128,256]{2,1,0:T(8,128)(2,1)S(1)}, bf16[48,128,256]{2,1,0:T(8,128)(2,1)}, u32[]{:S(2)}) copy-start(bf16[48,128,256]{2,1,0:T(8,128)(2,1)} %source.3) | copy-start | bytes 9437188
  16.9 18.6 %copy-start.3 = (bf16[48,64,128]{2,1,0:T(8,128)(2,1)S(1)}, bf16[48,64,128]{2,1,0:T(8,128)(2,1)}, u32[]{:S(2)}) copy-start(bf16[48,64,128]{2,1,0:T(8,128)(2,1)} %pack_chunks.3.refs_4_) | copy-start | bytes 2359300
  32.8 2.6 %collective-permute-start.5 = (bf16[48,64,128]{2,1,0:T(8,128)(2,1)}, bf16[48,64,128]{2,1,0:T(8,128)(2,1)}, u32[]{:S(2)}, u32[]{:S(2)}) collective-permute-start(bf16[48,64,128]{2,1,0:T(8,128)(2,1)} %collective-permute-done.2.refs_6_), channel_id=1, source_target_pairs={{0,8},{8,0},{16,24},{24,16},{1,9},{9,1},{17,25},{25,17},{2,10},{10... | collective-permute-start | bytes 2359304 | tf_op jit(solution)/shard_map/ppermute | solution.py:263
  32.8 22.5 %collective-permute-start.3 = (bf16[48,64,128]{2,1,0:T(8,128)(2,1)S(1)}, bf16[48,64,128]{2,1,0:T(8,128)(2,1)}, u32[]{:S(2)}, u32[]{:S(2)}) collective-permute-start(bf16[48,64,128]{2,1,0:T(8,128)(2,1)S(1)} %get-tuple-element.26.refs_4_), channel_id=1, source_target_pairs={{0,16},{8,24},{16,0},{24,8},{1,17},{9,25},{17,1},{25,9},{2,18},{10... | collective-permute-start | bytes 2359304 | tf_op jit(solution)/shard_map/ppermute | solution.py:260
  49.2 29.6 %all-to-all-start.1 = ((bf16[8,384,128]{2,1,0:T(8,128)(2,1)}), bf16[8,384,128]{2,1,0:T(8,128)(2,1)S(1)}, u32[]{:S(2)}, u32[]{:S(2)}) async-start(bf16[8,384,128]{2,1,0:T(8,128)(2,1)} %chunk_products.4), calls=%async_computation.1 | async-start | bytes 1572864 | tf_op jit(solution)/shard_map/all_to_all | solution.py:298
  55.3 2.6 %collective-permute-start.7 = (bf16[48,64,128]{2,1,0:T(8,128)(2,1)S(1)}, bf16[48,64,128]{2,1,0:T(8,128)(2,1)S(1)}, u32[]{:S(2)}, u32[]{:S(2)}) collective-permute-start(bf16[48,64,128]{2,1,0:T(8,128)(2,1)S(1)} %get-tuple-element.26.refs_4_), channel_id=1, source_target_pairs={{0,8},{8,0},{16,24},{24,16},{1,9},{9,1},{17,25},{25,17},{2,10},{10... | collective-permute-start | bytes 2359304 | tf_op jit(solution)/shard_map/ppermute | solution.py:263
  55.3 3.6 %collective-permute-start.8 = (bf16[48,64,128]{2,1,0:T(8,128)(2,1)}, bf16[48,64,128]{2,1,0:T(8,128)(2,1)S(1)}, u32[]{:S(2)}, u32[]{:S(2)}) collective-permute-start(bf16[48,64,128]{2,1,0:T(8,128)(2,1)} %collective-permute-done.3.refs_6_), channel_id=1, source_target_pairs={{0,8},{8,0},{16,24},{24,16},{1,9},{9,1},{17,25},{25,17},{2,10},{10... | collective-permute-start | bytes 2359304 | tf_op jit(solution)/shard_map/ppermute | solution.py:263
  55.8 26.6 %collective-permute-start.6 = (bf16[48,64,128]{2,1,0:T(8,128)(2,1)S(1)}, bf16[48,64,128]{2,1,0:T(8,128)(2,1)}, u32[]{:S(2)}, u32[]{:S(2)}) collective-permute-start(bf16[48,64,128]{2,1,0:T(8,128)(2,1)S(1)} %get-tuple-element.28.refs_4_), channel_id=1, source_target_pairs={{0,16},{8,24},{16,0},{24,8},{1,17},{9,25},{17,1},{25,9},{2,18},{10... | collective-permute-start | bytes 2359304 | tf_op jit(solution)/shard_map/ppermute | solution.py:260
  78.8 24.0 %all-to-all-start.2 = ((bf16[8,384,128]{2,1,0:T(8,128)(2,1)}), bf16[8,384,128]{2,1,0:T(8,128)(2,1)S(1)}, u32[]{:S(2)}, u32[]{:S(2)}) async-start(bf16[8,384,128]{2,1,0:T(8,128)(2,1)} %chunk_products.5), calls=%async_computation.2 | async-start | bytes 1572864 | tf_op jit(solution)/shard_map/all_to_all | solution.py:298
  82.3 2.7 %collective-permute-start.10 = (bf16[48,64,128]{2,1,0:T(8,128)(2,1)S(1)}, bf16[48,64,128]{2,1,0:T(8,128)(2,1)}, u32[]{:S(2)}, u32[]{:S(2)}) collective-permute-start(bf16[48,64,128]{2,1,0:T(8,128)(2,1)S(1)} %get-tuple-element.28.refs_4_), channel_id=1, source_target_pairs={{0,8},{8,0},{16,24},{24,16},{1,9},{9,1},{17,25},{25,17},{2,10},{10... | collective-permute-start | bytes 2359304 | tf_op jit(solution)/shard_map/ppermute | solution.py:263
  82.4 3.7 %collective-permute-start.11 = (bf16[48,64,128]{2,1,0:T(8,128)(2,1)}, bf16[48,64,128]{2,1,0:T(8,128)(2,1)}, u32[]{:S(2)}, u32[]{:S(2)}) collective-permute-start(bf16[48,64,128]{2,1,0:T(8,128)(2,1)} %collective-permute-done.6.refs_6_), channel_id=1, source_target_pairs={{0,8},{8,0},{16,24},{24,16},{1,9},{9,1},{17,25},{25,17},{2,10},{10... | collective-permute-start | bytes 2359304 | tf_op jit(solution)/shard_map/ppermute | solution.py:263
  82.9 24.0 %collective-permute-start = (bf16[8,1040,128]{2,1,0:T(8,128)(2,1)}, bf16[8,1040,128]{2,1,0:T(8,128)(2,1)}, u32[]{:S(2)}, u32[]{:S(2)}) collective-permute-start(bf16[8,1040,128]{2,1,0:T(8,128)(2,1)} %bitcast.12), channel_id=1, source_target_pairs={{0,8},{8,0},{16,24},{24,16},{1,9},{9,1},{17,25},{25,17},{2,10},{10... | collective-permute-start | bytes 6389768 | tf_op jit(solution)/shard_map/ppermute | solution.py:263
  83.0 23.4 %collective-permute-start.9 = (bf16[48,64,128]{2,1,0:T(8,128)(2,1)}, bf16[48,64,128]{2,1,0:T(8,128)(2,1)}, u32[]{:S(2)}, u32[]{:S(2)}) collective-permute-start(bf16[48,64,128]{2,1,0:T(8,128)(2,1)} %get-tuple-element.30.refs_4_), channel_id=1, source_target_pairs={{0,16},{8,24},{16,0},{24,8},{1,17},{9,25},{17,1},{25,9},{2,18},{10... | collective-permute-start | bytes 2359304 | tf_op jit(solution)/shard_map/ppermute | solution.py:260
  102.8 24.0 %all-to-all-start.3 = ((bf16[8,384,128]{2,1,0:T(8,128)(2,1)}), bf16[8,384,128]{2,1,0:T(8,128)(2,1)S(1)}, u32[]{:S(2)}, u32[]{:S(2)}) async-start(bf16[8,384,128]{2,1,0:T(8,128)(2,1)} %chunk_products.6), calls=%async_computation.3 | async-start | bytes 1572864 | tf_op jit(solution)/shard_map/all_to_all | solution.py:298
  106.4 2.5 %collective-permute-start.1 = (bf16[48,64,128]{2,1,0:T(8,128)(2,1)}, bf16[48,64,128]{2,1,0:T(8,128)(2,1)S(1)}, u32[]{:S(2)}, u32[]{:S(2)}) collective-permute-start(bf16[48,64,128]{2,1,0:T(8,128)(2,1)} %get-tuple-element.30.refs_4_), channel_id=1, source_target_pairs={{0,8},{8,0},{16,24},{24,16},{1,9},{9,1},{17,25},{25,17},{2,10},{10... | collective-permute-start | bytes 2359304 | tf_op jit(solution)/shard_map/ppermute | solution.py:263
  106.4 3.6 %collective-permute-start.12 = (bf16[48,64,128]{2,1,0:T(8,128)(2,1)}, bf16[48,64,128]{2,1,0:T(8,128)(2,1)S(1)}, u32[]{:S(2)}, u32[]{:S(2)}) collective-permute-start(bf16[48,64,128]{2,1,0:T(8,128)(2,1)} %collective-permute-done.9.refs_6_), channel_id=1, source_target_pairs={{0,8},{8,0},{16,24},{24,16},{1,9},{9,1},{17,25},{25,17},{2,10},{10... | collective-permute-start | bytes 2359304 | tf_op jit(solution)/shard_map/ppermute | solution.py:263
  126.8 24.6 %all-to-all-start = ((bf16[8,384,128]{2,1,0:T(8,128)(2,1)}), bf16[8,384,128]{2,1,0:T(8,128)(2,1)}, u32[]{:S(2)}, u32[]{:S(2)}) async-start(bf16[8,384,128]{2,1,0:T(8,128)(2,1)} %chunk_products.7), calls=%async_computation | async-start | bytes 1572864 | tf_op jit(solution)/shard_map/all_to_all | solution.py:298
  132.5 1.6 copy-start.4
  147.4 2.6 %copy-start.2 = (f32[768,2048]{1,0:T(8,128)}, f32[768,2048]{1,0:T(8,128)S(1)}, u32[]{:S(2)}) copy-start(f32[768,2048]{1,0:T(8,128)S(1)} %get-tuple-element.36.before) | copy-start | bytes 18874372
  150.0 1.4 copy-start.5
  (1 other events, 1.1 us)
Sparse Core Ops, SparseCore 0:
  9.5 54.2 all-gather.2
